TPU v7x, 32 devices: a whole 2x2x4 slice. The times are simulated.
32 devices in a mesh: ens: 4 (over y, x), cols: 8 (over z, core).
Axes of the slice: x: 2, y: 2, z: 4, core: 2. Of those that a mesh axis runs over, the one named last changes fastest.
Arguments:
- static_control: float32 [16, 16, 4096], P(None, 'cols'), may hold values from -6 to 6
- ensemble_control: float32 [32, 16, 16, 4096], P('ens', None, 'cols'), may hold values from -6 to 6
- perturbations: bfloat16 [32, 16, 16, 4096], P('ens', None, 'cols'), may hold values from -6 to 6
- vertical_root: float32 [16, 16], replicated, may hold values from 0 to 1.5
- vertical_local: float32 [16, 16], replicated, may hold values from 0 to 1.5
- face_north: float32 [16, 4096], P('cols'), may hold values from 0.02 to 0.24
- face_east: float32 [16, 4096], P('cols'), may hold values from 0.02 to 0.24
- innovation: float32 [524288], P('cols'), may hold values from -6 to 6
- obs_weight: float32 [524288], P('cols'), may hold values from 0.5 to 4
- obs_slot: int32 [524288], P('cols'), may hold values from 0 to 8191
- send_index: int32 [64, 1024], P('cols'), may hold values from 0 to 131071
- send_count: int32 [64], P('cols'), may hold values from 256 to 1024, as said below
Outputs:
- static_grad: float32 [16, 16, 4096], P(None, 'cols')
- ensemble_grad: float32 [32, 16, 16, 4096], P('ens', None, 'cols')
Inputs may be any that keep to these rules, and one draw needn't show every extreme that they name: `send_count`: in every draw one observation owner, drawn from the seed, receives full lists (count 1024) from every column owner; all other counts are drawn independently.
All inputs are finite; a program needn't handle non-finite values.
Results may differ from a plain program's by a relative error of at most 0.0003.
Values sent between devices are 32-bit elements; how exact they have to be, the bound alone decides.
No kernel may reach another device: no remote copies, remote signals or barrier semaphores. Data moves between devices by JAX's collectives and lax.ppermute only.
A program may use at most 128 MiB of HBM per device.

v0:
```python
import functools
import math

import jax
import jax.numpy as jnp
from jax import lax
from jax.experimental import pallas as pl
from jax.experimental.pallas import tpu as pltpu
from jax.sharding import PartitionSpec as P

NDIFF = 4
LANES = 128
FINE = 32
MIB = 1 << 20

f32 = jnp.float32
bf16 = jnp.bfloat16
SMEM = pl.BlockSpec(memory_space=pltpu.SMEM)
VMEM = pl.BlockSpec(memory_space=pltpu.VMEM)


def tiled(field):
    *lead, rows, lon = field.shape
    field = field.reshape(*lead, rows, lon // LANES, LANES)
    return jnp.swapaxes(field, -3, -2).reshape(*lead, rows * lon // LANES, LANES)


def untiled(field, rows):
    *lead, count, lanes = field.shape
    field = field.reshape(*lead, count // rows, rows, lanes)
    return jnp.swapaxes(field, -3, -2).reshape(*lead, rows, count // rows * lanes)


def params(limit, **more):
    return pltpu.CompilerParams(vmem_limit_bytes=limit * MIB, **more)


def halves(x):
    high = x.astype(bf16)
    return high, (x - high.astype(f32)).astype(bf16)


def one_hot(index, count):
    ids = lax.broadcasted_iota(jnp.int32, (count, index.shape[1]), 0)
    return jnp.where(ids == index, f32(1), f32(0)).astype(bf16)


def over(x, size):
    if size & (size - 1):
        return lax.div(x, jnp.int32(size)), lax.rem(x, jnp.int32(size))
    return lax.shift_right_logical(x, jnp.int32(size.bit_length() - 1)), x & (size - 1)


def prepare_kernel(lev_share, rows, where_ref, root_ref, count_ref, static_ref, north_ref, east_ref, index_ref, out_ref, row_ref, lane_ref):
    levels, per_level, _ = static_ref.shape
    first = where_ref[0] * lev_share
    for j in range(lev_share):
        total = root_ref[first + j, 0] * static_ref[0]
        for m in range(1, levels):
            total = total + root_ref[first + j, m] * static_ref[m]
        out_ref[j] = total
    out_ref[lev_share] = north_ref[...]
    out_ref[lev_share + 1] = east_ref[...]
    lists, capacity = index_ref.shape
    lon = per_level // rows * LANES
    pieces = capacity // LANES
    slot = lax.broadcasted_iota(jnp.int32, (1, capacity), 1)
    for q in range(lists):
        cell = index_ref[q : q + 1, :]
        rest, lane = over(cell, LANES)
        rest, block = over(rest, lon // LANES)
        level, row = over(rest, rows)
        grid_row = jnp.where(slot < count_ref[q], level * per_level + block * rows + row, -1)
        for c in range(pieces):
            row_ref[q * pieces + c : q * pieces + c + 1, :] = grid_row[:, c * LANES : (c + 1) * LANES]
            lane_ref[q * pieces + c : q * pieces + c + 1, :] = lane[:, c * LANES : (c + 1) * LANES]


def slots_kernel(n_cols, cap_rows, where_ref, slot_ref, weight_ref, innov_ref, out_ref, acc_ref, fold_ref):
    coarse = acc_ref.shape[0]
    obs_rows = slot_ref.shape[0]
    group = min(8, obs_rows)
    acc_ref[...] = jnp.zeros_like(acc_ref)

    def step(i, carry):
        at = pl.ds(pl.multiple_of(i * group, group), group)
        slot = slot_ref[at, :]
        weight = weight_ref[at, :]
        amount = weight * innov_ref[at, :]
        upper, lower = over(slot, FINE)
        terms = [t.astype(f32) for t in halves(weight) + halves(amount)]
        fine_ids = lax.broadcasted_iota(jnp.int32, (FINE, LANES), 0)
        left, right = [], []
        for r in range(group):
            left.append(one_hot(upper[r : r + 1, :], coarse))
            mask = fine_ids == lower[r : r + 1, :]
            right.append(
                jnp.concatenate([jnp.where(mask, t[r : r + 1, :], f32(0)).astype(bf16) for t in terms], axis=0)
            )
        acc_ref[...] += lax.dot_general(
            jnp.concatenate(left, axis=1),
            jnp.concatenate(right, axis=1),
            (((1,), (1,)), ((), ())),
            preferred_element_type=f32,
        )
        return carry

    lax.fori_loop(0, obs_rows // group, step, 0)
    acc = acc_ref[...]
    fold_ref[...] = acc + pltpu.roll(acc, LANES - FINE, 1)
    per_row = LANES // FINE
    lane = lax.broadcasted_iota(jnp.int32, (coarse // per_row, LANES), 1)
    weights = jnp.zeros((coarse // per_row, LANES), f32)
    amounts = jnp.zeros((coarse // per_row, LANES), f32)
    for c in range(per_row):
        piece = fold_ref[pl.ds(c, coarse // per_row, stride=per_row), :]
        here = lane // FINE == c
        weights = jnp.where(here, pltpu.roll(piece, c * FINE, 1) if c else piece, weights)
        shift = (c * FINE - 2 * FINE) % LANES
        amounts = jnp.where(here, pltpu.roll(piece, shift, 1) if shift else piece, amounts)
    for p in range(n_cols):
        out_ref[p, 0] = weights[p * cap_rows : (p + 1) * cap_rows]
        out_ref[p, 1] = amounts[p * cap_rows : (p + 1) * cap_rows]


def splat(matrix_ref, out_ref, scale, transpose):
    levels = matrix_ref.shape[0]
    for l in range(levels):
        for m in range(levels):
            entry = matrix_ref[m, l] if transpose else matrix_ref[l, m]
            out_ref[l, m] = jnp.full((8, LANES), entry * f32(scale), f32)


def forward_kernel(scale, local_ref, control_ref, pert_ref, out_ref, splat_ref):
    levels, per_level, _ = out_ref.shape

    @pl.when(pl.program_id(0) == 0)
    def _():
        splat(local_ref, splat_ref, scale, False)
        out_ref[...] = jnp.zeros_like(out_ref)

    def chunk(j, carry):
        at = pl.ds(pl.multiple_of(j * 16, 16), 16)
        control = [control_ref[0, m, at, :].reshape(2, 8, LANES) for m in range(levels)]
        for l in range(levels):
            total = splat_ref[l, 0][None] * control[0]
            for m in range(1, levels):
                total = total + splat_ref[l, m][None] * control[m]
            pert = pert_ref[0, l, at, :].astype(f32)
            out_ref[l, at, :] += pert * total.reshape(16, LANES)
        return carry

    lax.fori_loop(0, per_level // 16, chunk, 0)


def member_kernel(scale, local_ref, adjoint_ref, control_ref, pert_ref, out_ref, splat_ref):
    levels, per_level, _ = adjoint_ref.shape

    @pl.when(pl.program_id(0) == 0)
    def _():
        splat(local_ref, splat_ref, scale, True)

    def chunk(j, carry):
        at = pl.ds(pl.multiple_of(j * 16, 16), 16)
        weighted = [
            (pert_ref[0, l, at, :].astype(f32) * adjoint_ref[l, at, :]).reshape(2, 8, LANES) for l in range(levels)
        ]
        for m in range(levels):
            total = splat_ref[m, 0][None] * weighted[0]
            for l in range(1, levels):
                total = total + splat_ref[m, l][None] * weighted[l]
            out_ref[0, m, at, :] = control_ref[0, m, at, :] + total.reshape(16, LANES)
        return carry

    lax.fori_loop(0, per_level // 16, chunk, 0)


def eastern(x):
    lane = lax.broadcasted_iota(jnp.int32, x.shape, 1)
    near = pltpu.roll(x, LANES - 1, 1)
    return jnp.where(lane == LANES - 1, pltpu.roll(near, x.shape[0] - 1, 0), near)


def western(x):
    lane = lax.broadcasted_iota(jnp.int32, x.shape, 1)
    near = pltpu.roll(x, 1, 1)
    return jnp.where(lane == 0, pltpu.roll(near, 1, 0), near)


def diffuse_rows(tiles, level, coef_ref, rows):
    blocks = tiles[0].shape[1] // rows
    field = [t[level, pl.ds(r, blocks, stride=rows), :] for t in tiles for r in range(rows)]
    for step in range(NDIFF):
        field = [
            coef_ref[0, i + step] * field[i]
            + coef_ref[1, i + step] * field[i - 1]
            + coef_ref[2, i + step] * field[i + 1]
            + coef_ref[3, i + step] * eastern(field[i])
            + coef_ref[4, i + step] * western(field[i])
            for i in range(1, len(field) - 1)
        ]
        field = list(field)
    return field


def first_diffusion_kernel(lev_share, rows, where_ref, *refs):
    tiles, (out_ref, coef_ref) = refs[:-2], refs[-2:]
    blocks = tiles[0].shape[1] // rows
    side = len(tiles) // 2
    north = [t[lev_share, pl.ds(r, blocks, stride=rows), :] for t in tiles for r in range(rows)]
    east = [t[lev_share + 1, pl.ds(r, blocks, stride=rows), :] for t in tiles for r in range(rows)]
    for i in range(1, len(north) - 1):
        south = north[i + 1]
        if (i + 1) % rows == 0 and i < side * rows:
            south = south * jnp.where(where_ref[1] == side - (i + 1) // rows, f32(0), f32(1))
        west = western(east[i])
        coef_ref[0, i] = 1.0 - north[i] - south - east[i] - west
        coef_ref[1, i] = north[i]
        coef_ref[2, i] = south
        coef_ref[3, i] = east[i]
        coef_ref[4, i] = west
    for i in (0, len(north) - 1):
        for c in range(5):
            coef_ref[c, i] = jnp.zeros_like(north[0])

    def body(level, carry):
        final = diffuse_rows(tiles, level, coef_ref, rows)
        for r in range(rows):
            out_ref[level, pl.ds(r, blocks, stride=rows), :] = final[r]
        return carry

    lax.fori_loop(0, lev_share, body, 0)


def second_diffusion_kernel(rows, coef_ref, *refs):
    tiles, out_ref = refs[:-1], refs[-1]
    copies, lev_share = out_ref.shape[:2]
    blocks = tiles[0].shape[1] // rows

    def body(level, carry):
        final = diffuse_rows(tiles, level, coef_ref, rows)
        for copy in range(copies):
            for r in range(rows):
                out_ref[copy, level, pl.ds(r, blocks, stride=rows), :] = final[r]
        return carry

    lax.fori_loop(0, lev_share, body, 0)


def lookup_kernel(where_ref, part_ref, static_ref, row_ref, lane_ref, slots_ref, out_ref, field_ref, turned_ref):
    cells = part_ref.shape[0]
    own = static_ref.shape[0]
    n_lists, _, cap_rows, _ = slots_ref.shape
    field_ref[...] = part_ref[...]
    at = pl.ds(pl.multiple_of(where_ref[0] * own, own), own)
    field_ref[at, :] += static_ref[...]

    def turn(t, carry):
        at = pl.ds(pl.multiple_of(t * LANES, LANES), LANES)
        high, low = halves(field_ref[at, :].T)
        turned_ref[0:LANES, at] = high
        turned_ref[LANES : 2 * LANES, at] = low
        return carry

    lax.fori_loop(0, cells // LANES, turn, 0)
    lane_ids = lax.broadcasted_iota(jnp.int32, (LANES, LANES), 0)

    def look(q, carry):
        at = pl.ds(pl.multiple_of(q * cap_rows, cap_rows), cap_rows)
        rows = row_ref[at, :]
        lanes = lane_ref[at, :]
        found = []
        for c in range(cap_rows):
            got = jnp.dot(turned_ref[...], one_hot(rows[c : c + 1, :], cells), preferred_element_type=f32)
            got = got[:LANES] + got[LANES:]
            found.append(jnp.sum(jnp.where(lane_ids == lanes[c : c + 1, :], got, f32(0)), axis=0, keepdims=True))
        out_ref[0, at, :] = jnp.concatenate(found, axis=0)
        out_ref[1, at, :] = slots_ref[q, 0]
        out_ref[2, at, :] = slots_ref[q, 1]
        return carry

    lax.fori_loop(0, n_lists, look, 0)


def scatter_kernel(cap_rows, where_ref, row_ref, lane_ref, *refs):
    shares, (out_ref, own_ref, acc_ref) = refs[:-3], refs[-3:]
    cells = out_ref.shape[0]
    own = own_ref.shape[0]
    acc_ref[...] = jnp.zeros_like(acc_ref)
    lane_ids = lax.broadcasted_iota(jnp.int32, (LANES, LANES), 0)

    def put(q, carry):
        at = pl.ds(pl.multiple_of(q * cap_rows, cap_rows), cap_rows)
        value, weight, amount = (functools.reduce(jnp.add, [s[t, at, :] for s in shares]) for t in range(3))
        high, low = (h.astype(f32) for h in halves(value * weight - amount))
        rows = row_ref[at, :]
        lanes = lane_ref[at, :]
        left, right = [], []
        for c in range(cap_rows):
            left.append(one_hot(rows[c : c + 1, :], cells))
            mask = lane_ids == lanes[c : c + 1, :]
            right.append(
                jnp.concatenate(
                    [jnp.where(mask, h[c : c + 1, :], f32(0)).astype(bf16) for h in (high, low)], axis=0
                )
            )
        acc_ref[...] += lax.dot_general(
            jnp.concatenate(left, axis=1),
            jnp.concatenate(right, axis=1),
            (((1,), (1,)), ((), ())),
            preferred_element_type=f32,
        )
        return carry

    lax.fori_loop(0, row_ref.shape[0] // cap_rows, put, 0)
    out_ref[...] = acc_ref[:, :LANES] + acc_ref[:, LANES:]
    own_ref[...] = out_ref[pl.ds(pl.multiple_of(where_ref[0] * own, own), own), :]


def static_kernel(root_ref, static_ref, smooth_ref, out_ref):
    levels, per_level, _ = static_ref.shape

    def chunk(j, carry):
        at = pl.ds(pl.multiple_of(j * 16, 16), 16)
        smooth = [smooth_ref[l, at, :] for l in range(levels)]
        for m in range(levels):
            total = static_ref[m, at, :]
            for l in range(levels):
                total = total + root_ref[l, m] * smooth[l]
            out_ref[m, at, :] = total
        return carry

    lax.fori_loop(0, per_level // 16, chunk, 0)


def neighbours(x, axis):
    count = lax.axis_size(axis)
    by = (2, 1, -1, -2)
    return [lax.ppermute(x, axis, [(i, i + d) for i in range(count) if 0 <= i + d < count]) for d in by]


def local(
    static_control,
    ensemble_control,
    perturbations,
    vertical_root,
    vertical_local,
    face_north,
    face_east,
    innovation,
    obs_weight,
    obs_slot,
    send_index,
    send_count,
):
    n_ens = lax.axis_size("ens")
    n_cols = lax.axis_size("cols")
    members, levels, rows, lon = ensemble_control.shape
    per_level = rows * lon // LANES
    cells = levels * per_level
    lev_share = levels // n_ens
    own = lev_share * per_level
    lists, capacity = send_index.shape
    cap_rows = capacity // LANES
    entry_rows = lists * cap_rows
    member_scale = 1.0 / math.sqrt(members * n_ens - 1)
    where = jnp.stack([lax.axis_index("ens"), lax.axis_index("cols")]).astype(jnp.int32)

    static = tiled(static_control)
    control = tiled(ensemble_control)
    pert = tiled(perturbations)
    north = tiled(face_north)
    east = tiled(face_east)

    packed, entry_row, entry_lane = pl.pallas_call(
        functools.partial(prepare_kernel, lev_share, rows),
        in_specs=[SMEM, SMEM, SMEM, VMEM, VMEM, VMEM, VMEM],
        out_specs=[VMEM] * 3,
        out_shape=[
            jax.ShapeDtypeStruct((lev_share + 2, per_level, LANES), f32),
            jax.ShapeDtypeStruct((entry_rows, LANES), jnp.int32),
            jax.ShapeDtypeStruct((entry_rows, LANES), jnp.int32),
        ],
        compiler_params=params(16),
        name="prepare",
    )(where, vertical_root, send_count, static, north, east, send_index)
    packs = neighbours(packed, "cols")

    obs_rows = obs_slot.shape[0] // LANES
    share_rows = obs_rows // n_ens
    obs_spec = pl.BlockSpec((share_rows, LANES), lambda i, at: (at[0], 0))
    coarse = n_cols * capacity // FINE
    slots = pl.pallas_call(
        functools.partial(slots_kernel, n_cols, cap_rows),
        grid_spec=pltpu.PrefetchScalarGridSpec(
            num_scalar_prefetch=1,
            grid=(1,),
            in_specs=[obs_spec] * 3,
            out_specs=pl.BlockSpec((n_cols, 2, cap_rows, LANES), lambda i, at: (0, 0, 0, 0)),
            scratch_shapes=[pltpu.VMEM((coarse, LANES), f32), pltpu.VMEM((coarse, LANES), f32)],
        ),
        out_shape=jax.ShapeDtypeStruct((n_cols, 2, cap_rows, LANES), f32),
        compiler_params=params(32),
        cost_estimate=pl.CostEstimate(flops=2 * 128 * coarse * share_rows * LANES, bytes_accessed=12 * share_rows * LANES, transcendentals=0),
        name="slot_sums",
    )(
        where,
        obs_slot.reshape(obs_rows, LANES),
        obs_weight.reshape(obs_rows, LANES),
        innovation.reshape(obs_rows, LANES),
    )
    slots = lax.all_to_all(slots, "cols", split_axis=0, concat_axis=0, tiled=True)

    member_spec = pl.BlockSpec((1, levels, per_level, LANES), lambda k: (k, 0, 0, 0))
    whole_spec = pl.BlockSpec((levels, per_level, LANES), lambda k: (0, 0, 0))
    splat_shape = pltpu.VMEM((levels, levels, 8, LANES), f32)
    member_cost = pl.CostEstimate(flops=2 * members * levels * cells * LANES, bytes_accessed=members * cells * LANES * 6, transcendentals=0)
    part = pl.pallas_call(
        functools.partial(forward_kernel, member_scale),
        grid=(members,),
        in_specs=[SMEM, member_spec, member_spec],
        out_specs=whole_spec,
        out_shape=jax.ShapeDtypeStruct((levels, per_level, LANES), f32),
        scratch_shapes=[splat_shape],
        compiler_params=params(32),
        cost_estimate=member_cost,
        name="members_forward",
    )(vertical_local, control, pert)

    tiles = [packs[0], packs[1], packed, packs[2], packs[3]]
    blocks = per_level // rows
    increment, coefs = pl.pallas_call(
        functools.partial(first_diffusion_kernel, lev_share, rows),
        in_specs=[SMEM] + [VMEM] * 5,
        out_specs=[VMEM] * 2,
        out_shape=[
            jax.ShapeDtypeStruct((lev_share, per_level, LANES), f32),
            jax.ShapeDtypeStruct((5, 5 * rows, blocks, LANES), f32),
        ],
        compiler_params=params(32),
        name="diffuse_forward",
    )(where, *tiles)

    share = pl.pallas_call(
        lookup_kernel,
        in_specs=[SMEM] + [VMEM] * 5,
        out_specs=VMEM,
        out_shape=jax.ShapeDtypeStruct((3, entry_rows, LANES), f32),
        scratch_shapes=[pltpu.VMEM((cells, LANES), f32), pltpu.VMEM((2 * LANES, cells), bf16)],
        compiler_params=params(32),
        name="lookup",
    )(where, part.reshape(cells, LANES), increment.reshape(own, LANES), entry_row, entry_lane, slots)
    shares = [share] + [
        lax.ppermute(share, "ens", [((i + d) % n_ens, i) for i in range(n_ens)]) for d in range(1, n_ens)
    ]

    adjoint, adjoint_own = pl.pallas_call(
        functools.partial(scatter_kernel, cap_rows),
        in_specs=[SMEM] + [VMEM] * (2 + n_ens),
        out_specs=[VMEM] * 2,
        out_shape=[jax.ShapeDtypeStruct((cells, LANES), f32), jax.ShapeDtypeStruct((own, LANES), f32)],
        scratch_shapes=[pltpu.VMEM((cells, 2 * LANES), f32)],
        compiler_params=params(32),
        name="scatter",
    )(where, entry_row, entry_lane, *shares)
    adjoint_own = adjoint_own.reshape(lev_share, per_level, LANES)
    around = neighbours(adjoint_own, "cols")

    smooth = pl.pallas_call(
        functools.partial(second_diffusion_kernel, rows),
        in_specs=[VMEM] * 6,
        out_specs=VMEM,
        out_shape=jax.ShapeDtypeStruct((n_ens, lev_share, per_level, LANES), f32),
        compiler_params=params(32),
        name="diffuse_adjoint",
    )(coefs, around[0], around[1], adjoint_own, around[2], around[3])
    smooth = lax.all_to_all(smooth, "ens", split_axis=0, concat_axis=0, tiled=True)

    ensemble_grad = pl.pallas_call(
        functools.partial(member_kernel, member_scale),
        grid=(members,),
        in_specs=[SMEM, whole_spec, member_spec, member_spec],
        out_specs=member_spec,
        out_shape=jax.ShapeDtypeStruct((members, levels, per_level, LANES), f32),
        scratch_shapes=[splat_shape],
        compiler_params=params(32),
        cost_estimate=member_cost,
        name="members_gradient",
    )(vertical_local, adjoint.reshape(levels, per_level, LANES), control, pert)

    static_grad = pl.pallas_call(
        static_kernel,
        in_specs=[SMEM, VMEM, VMEM],
        out_specs=VMEM,
        out_shape=jax.ShapeDtypeStruct((levels, per_level, LANES), f32),
        compiler_params=params(16),
        name="static_gradient",
    )(vertical_root, static, smooth.reshape(levels, per_level, LANES))
    return (untiled(static_grad, rows), untiled(ensemble_grad, rows))


def solution(mesh):
    placed = (
        P(None, "cols", None),
        P("ens", None, "cols", None),
        P("ens", None, "cols", None),
        P(),
        P(),
        P("cols", None),
        P("cols", None),
        P("cols"),
        P("cols"),
        P("cols"),
        P("cols", None),
        P("cols"),
    )
    return jax.shard_map(
        local,
        mesh=mesh,
        in_specs=placed,
        out_specs=(P(None, "cols", None), P("ens", None, "cols", None)),
        check_vma=False,
    )
```

profile of v0, /device:TPU:0, one launch (start us, length us, event | category | flops | bytes accessed | tf_op | source)
XLA Modules:
  0.0 111.1 jit_solution(3913061156292242776)
XLA Ops:
  0.7 1.2 %copy-done.3 = f32[16,2,4096]{2,1,0:T(2,128)S(1)} copy-done((f32[16,2,4096]{2,1,0:T(2,128)S(1)}, f32[16,2,4096]{2,1,0:T(2,128)}, u32[]{:S(2)}) %copy-start.3) | copy-done | bytes 524312
  6.5 1.3 %collective-permute-start.3 = (f32[6,64,128]{2,1,0:T(8,128)S(1)}, f32[6,64,128]{2,1,0:T(8,128)S(1)}, u32[]{:S(2)}, u32[]{:S(2)}) collective-permute-start(f32[6,64,128]{2,1,0:T(8,128)S(1)} %get-tuple-element.9.refs_2_), channel_id=1, source_target_pairs={{2,0},{3,1},{4,2},{5,3},{6,4},{7,5},{10,8},{11,9},{12,10},{13,11},... | collective-permute-start | bytes 589832 | tf_op jit(solution)/shard_map/ppermute | solution.py:339
  7.8 1.3 %collective-permute-start.2 = (f32[6,64,128]{2,1,0:T(8,128)S(1)}, f32[6,64,128]{2,1,0:T(8,128)S(1)}, u32[]{:S(2)}, u32[]{:S(2)}) collective-permute-start(f32[6,64,128]{2,1,0:T(8,128)S(1)} %get-tuple-element.9.refs_2_), channel_id=1, source_target_pairs={{1,0},{2,1},{3,2},{4,3},{5,4},{6,5},{7,6},{9,8},{10,9},{11,10},{12... | collective-permute-start | bytes 589832 | tf_op jit(solution)/shard_map/ppermute | solution.py:339
  9.1 3.0 %collective-permute-start.1 = (f32[6,64,128]{2,1,0:T(8,128)S(1)}, f32[6,64,128]{2,1,0:T(8,128)S(1)}, u32[]{:S(2)}, u32[]{:S(2)}) collective-permute-start(f32[6,64,128]{2,1,0:T(8,128)S(1)} %get-tuple-element.9.refs_2_), channel_id=1, source_target_pairs={{0,1},{1,2},{2,3},{3,4},{4,5},{5,6},{6,7},{8,9},{9,10},{10,11},{11... | collective-permute-start | bytes 589832 | tf_op jit(solution)/shard_map/ppermute | solution.py:339
  12.1 6.2 %collective-permute-start = (f32[6,64,128]{2,1,0:T(8,128)S(1)}, f32[6,64,128]{2,1,0:T(8,128)}, u32[]{:S(2)}, u32[]{:S(2)}) collective-permute-start(f32[6,64,128]{2,1,0:T(8,128)S(1)} %get-tuple-element.9.refs_2_), channel_id=1, source_target_pairs={{0,2},{1,3},{2,4},{3,5},{4,6},{5,7},{8,10},{9,11},{10,12},{11,13},... | collective-permute-start | bytes 589832 | tf_op jit(solution)/shard_map/ppermute | solution.py:339
  18.3 0.9 copy-done.26
  19.3 0.9 copy-done.27
  20.2 0.9 copy-done.28
  21.2 6.4 %slot_sums.1 = f32[8,2,8,128]{3,2,1,0:T(8,128)} custom-call(s32[2]{0:T(128)S(1)} %pad_add_fusion.where_ref, s32[512,128]{1,0:T(8,128)S(1)} %bitcast.62, f32[512,128]{1,0:T(8,128)S(1)} %bitcast.63, f32[512,128]{1,0:T(8,128)S(1)} %bitcast.64), custom_call_target="tpu_custom_call" | custom-call | flops 1073741824 | bytes 196608 | tf_op jit(solution)/shard_map/slot_sums/pallas_call | solution.py:393
  27.5 3.7 %all-to-all-start = ((f32[8,2,8,128]{3,2,1,0:T(8,128)}), f32[8,2,8,128]{3,2,1,0:T(8,128)S(1)}, u32[]{:S(2)}, u32[]{:S(2)}) async-start(f32[8,2,8,128]{3,2,1,0:T(8,128)} %slot_sums.1), calls=%async_computation | async-start | bytes 131072 | tf_op jit(solution)/shard_map/all_to_all | solution.py:412
  31.2 2.2 %copy-done = f32[8,16,2,4096]{3,2,1,0:T(2,128)S(1)} copy-done((f32[8,16,2,4096]{3,2,1,0:T(2,128)S(1)}, f32[8,16,2,4096]{3,2,1,0:T(2,128)}, u32[]{:S(2)}) %copy-start) | copy-done | bytes 4194328
  33.4 6.4 %members_forward.1 = f32[16,64,128]{2,1,0:T(8,128)S(1)} custom-call(f32[16,16]{1,0:T(8,128)S(1)} %copy-done.19, f32[8,16,64,128]{3,2,1,0:T(8,128)S(1)} %bitcast.45, bf16[8,16,64,128]{3,2,1,0:T(8,128)(2,1)S(1)} %bitcast.47), custom_call_target="tpu_custom_call" | custom-call | flops 33554432 | bytes 6291456 | tf_op jit(solution)/shard_map/members_forward/pallas_call | solution.py:418
  41.9 0.9 copy-done.8
  45.6 2.4 %diffuse_forward.1 = (f32[4,64,128]{2,1,0:T(8,128)S(1)}, f32[5,10,32,128]{3,2,1,0:T(8,128)S(1)}) custom-call(s32[2]{0:T(128)S(1)} %pad_add_fusion.where_ref, f32[6,64,128]{2,1,0:T(8,128)} %collective-permute-done.refs_0_, f32[6,64,128]{2,1,0:T(8,128)S(1)} %copy-done.14, f32[6,64,128]{2,1,0:T(8,128)S(1)} %copy-done.8, f32[6,64,128]{2,1,0:T(8,128)S(1)} %copy-done.12, ...), custom_call_target="tpu_custom_call" | custom-call | tf_op jit(solution)/shard_map/diffuse_forward/pallas_call | solution.py:432
  50.3 11.7 %lookup.1.refs_0_ = f32[3,64,128]{2,1,0:T(8,128)S(1)} custom-call(s32[2]{0:T(128)S(1)} %pad_add_fusion.where_ref, f32[1024,128]{1,0:T(8,128)S(1)} %bitcast.52, f32[256,128]{1,0:T(8,128)S(1)} %bitcast.54, s32[64,128]{1,0:T(8,128)S(1)} %get-tuple-element.11.row_ref, s32[64,128]{1,0:T(8,128)S(1)} %copy-done.16, f32[8,2,8,128]{3,2,1,0:T(8,128)S(1)} %all-to-all-done.slots_ref), custom_call_target="tpu_custom_call" | custom-call | tf_op jit(solution)/shard_map/lookup/pallas_call | solution.py:444
  62.1 1.7 %collective-permute-start.6 = (f32[3,64,128]{2,1,0:T(8,128)S(1)}, f32[3,64,128]{2,1,0:T(8,128)S(1)}, u32[]{:S(2)}, u32[]{:S(2)}) collective-permute-start(f32[3,64,128]{2,1,0:T(8,128)S(1)} %lookup.1.refs_0_), channel_id=1, source_target_pairs={{24,0},{0,8},{8,16},{16,24},{25,1},{1,9},{9,17},{17,25},{26,2},{2,... | collective-permute-start | bytes 294920 | tf_op jit(solution)/shard_map/ppermute | solution.py:454
  63.8 1.5 %collective-permute-start.5 = (f32[3,64,128]{2,1,0:T(8,128)S(1)}, f32[3,64,128]{2,1,0:T(8,128)S(1)}, u32[]{:S(2)}, u32[]{:S(2)}) collective-permute-start(f32[3,64,128]{2,1,0:T(8,128)S(1)} %lookup.1.refs_0_), channel_id=1, source_target_pairs={{16,0},{24,8},{0,16},{8,24},{17,1},{25,9},{1,17},{9,25},{18,2},{26... | collective-permute-start | bytes 294920 | tf_op jit(solution)/shard_map/ppermute | solution.py:454
  65.3 1.4 %collective-permute-start.4 = (f32[3,64,128]{2,1,0:T(8,128)S(1)}, f32[3,64,128]{2,1,0:T(8,128)S(1)}, u32[]{:S(2)}, u32[]{:S(2)}) collective-permute-start(f32[3,64,128]{2,1,0:T(8,128)S(1)} %lookup.1.refs_0_), channel_id=1, source_target_pairs={{8,0},{16,8},{24,16},{0,24},{9,1},{17,9},{25,17},{1,25},{10,2},{18... | collective-permute-start | bytes 294920 | tf_op jit(solution)/shard_map/ppermute | solution.py:454
  66.7 2.0 %collective-permute-done.6.refs_3_ = f32[3,64,128]{2,1,0:T(8,128)S(1)} collective-permute-done((f32[3,64,128]{2,1,0:T(8,128)S(1)}, f32[3,64,128]{2,1,0:T(8,128)S(1)}, u32[]{:S(2)}, u32[]{:S(2)}) %collective-permute-start.6) | collective-permute-done | bytes 98336 | tf_op jit(solution)/shard_map/ppermute | solution.py:454
  68.8 2.1 %collective-permute-done.5.refs_2_ = f32[3,64,128]{2,1,0:T(8,128)S(1)} collective-permute-done((f32[3,64,128]{2,1,0:T(8,128)S(1)}, f32[3,64,128]{2,1,0:T(8,128)S(1)}, u32[]{:S(2)}, u32[]{:S(2)}) %collective-permute-start.5) | collective-permute-done | bytes 98336 | tf_op jit(solution)/shard_map/ppermute | solution.py:454
  70.9 6.8 %scatter.1 = (f32[1024,128]{1,0:T(8,128)S(1)}, f32[256,128]{1,0:T(8,128)S(1)}) custom-call(s32[2]{0:T(128)S(1)} %pad_add_fusion.where_ref, s32[64,128]{1,0:T(8,128)S(1)} %get-tuple-element.11.row_ref, s32[64,128]{1,0:T(8,128)S(1)} %copy-done.16, f32[3,64,128]{2,1,0:T(8,128)S(1)} %lookup.1.refs_0_, f32[3,64,128]{2,1,0:T(8,128)S(1)} %collective-permute-done.4.refs_1_, ...), custom_call_target="tpu_custom_call" | custom-call | tf_op jit(solution)/shard_map/scatter/pallas_call | solution.py:457
  78.5 1.3 %collective-permute-start.10 = (f32[4,64,128]{2,1,0:T(8,128)S(1)}, f32[4,64,128]{2,1,0:T(8,128)S(1)}, u32[]{:S(2)}, u32[]{:S(2)}) collective-permute-start(f32[4,64,128]{2,1,0:T(8,128)S(1)} %bitcast.55), channel_id=1, source_target_pairs={{2,0},{3,1},{4,2},{5,3},{6,4},{7,5},{10,8},{11,9},{12,10},{13,11},... | collective-permute-start | bytes 393224 | tf_op jit(solution)/shard_map/ppermute | solution.py:339
  79.8 1.3 %collective-permute-start.9 = (f32[4,64,128]{2,1,0:T(8,128)S(1)}, f32[4,64,128]{2,1,0:T(8,128)S(1)}, u32[]{:S(2)}, u32[]{:S(2)}) collective-permute-start(f32[4,64,128]{2,1,0:T(8,128)S(1)} %bitcast.56), channel_id=1, source_target_pairs={{1,0},{2,1},{3,2},{4,3},{5,4},{6,5},{7,6},{9,8},{10,9},{11,10},{12... | collective-permute-start | bytes 393224 | tf_op jit(solution)/shard_map/ppermute | solution.py:339
  81.1 3.0 %collective-permute-start.8 = (f32[4,64,128]{2,1,0:T(8,128)S(1)}, f32[4,64,128]{2,1,0:T(8,128)S(1)}, u32[]{:S(2)}, u32[]{:S(2)}) collective-permute-start(f32[4,64,128]{2,1,0:T(8,128)S(1)} %bitcast.57), channel_id=1, source_target_pairs={{0,1},{1,2},{2,3},{3,4},{4,5},{5,6},{6,7},{8,9},{9,10},{10,11},{11... | collective-permute-start | bytes 393224 | tf_op jit(solution)/shard_map/ppermute | solution.py:339
  84.2 4.6 %collective-permute-start.7 = (f32[4,64,128]{2,1,0:T(8,128)S(1)}, f32[4,64,128]{2,1,0:T(8,128)S(1)}, u32[]{:S(2)}, u32[]{:S(2)}) collective-permute-start(f32[4,64,128]{2,1,0:T(8,128)S(1)} %bitcast.58), channel_id=1, source_target_pairs={{0,2},{1,3},{2,4},{3,5},{4,6},{5,7},{8,10},{9,11},{10,12},{11,13},... | collective-permute-start | bytes 393224 | tf_op jit(solution)/shard_map/ppermute | solution.py:339
  88.8 3.8 %collective-permute-done.7.refs_0_ = f32[4,64,128]{2,1,0:T(8,128)S(1)} collective-permute-done((f32[4,64,128]{2,1,0:T(8,128)S(1)}, f32[4,64,128]{2,1,0:T(8,128)S(1)}, u32[]{:S(2)}, u32[]{:S(2)}) %collective-permute-start.7) | collective-permute-done | bytes 131104 | tf_op jit(solution)/shard_map/ppermute | solution.py:339
  92.6 2.2 %diffuse_adjoint.1 = f32[4,4,64,128]{3,2,1,0:T(8,128)} custom-call(f32[5,10,32,128]{3,2,1,0:T(8,128)S(1)} %get-tuple-element.10.coef_ref, f32[4,64,128]{2,1,0:T(8,128)S(1)} %collective-permute-done.7.refs_0_, f32[4,64,128]{2,1,0:T(8,128)S(1)} %collective-permute-done.8.refs_1_, f32[4,64,128]{2,1,0:T(8,128)S(1)} %bitcast.59, ...), custom_call_target="tpu_custom_call" | custom-call | tf_op jit(solution)/shard_map/diffuse_adjoint/pallas_call | solution.py:469
  94.8 3.5 %all-to-all-start.1 = ((f32[4,4,64,128]{3,2,1,0:T(8,128)}), f32[4,4,64,128]{3,2,1,0:T(8,128)S(1)}, u32[]{:S(2)}, u32[]{:S(2)}) async-start(f32[4,4,64,128]{3,2,1,0:T(8,128)} %diffuse_adjoint.1), calls=%async_computation.1 | async-start | bytes 1048576 | tf_op jit(solution)/shard_map/all_to_all | solution.py:477
  98.3 2.2 %copy-done.1 = f32[8,16,2,4096]{3,2,1,0:T(2,128)S(1)} copy-done((f32[8,16,2,4096]{3,2,1,0:T(2,128)S(1)}, f32[8,16,2,4096]{3,2,1,0:T(2,128)}, u32[]{:S(2)}) %copy-start.1) | copy-done | bytes 4194328
  100.5 1.0 copy-done.6
  101.5 7.4 %members_gradient.1 = f32[8,16,64,128]{3,2,1,0:T(8,128)} custom-call(f32[16,16]{1,0:T(8,128)S(1)} %copy-done.19, f32[16,64,128]{2,1,0:T(8,128)S(1)} %bitcast.53, f32[8,16,64,128]{3,2,1,0:T(8,128)S(1)} %bitcast.46, bf16[8,16,64,128]{3,2,1,0:T(8,128)(2,1)S(1)} %bitcast.48), custom_call_target="tpu_custom_call" | custom-call | flops 33554432 | bytes 6291456 | tf_op jit(solution)/shard_map/members_gradient/pallas_call | solution.py:479
  108.9 2.2 %static_gradient.1 = f32[16,64,128]{2,1,0:T(8,128)} custom-call(f32[16,16]{1,0:T(8,128)S(1)} %copy-done.21, f32[16,64,128]{2,1,0:T(8,128)S(1)} %bitcast.50, f32[16,64,128]{2,1,0:T(8,128)S(1)} %bitcast.51), custom_call_target="tpu_custom_call" | custom-call | tf_op jit(solution)/shard_map/static_gradient/pallas_call | solution.py:491
  (62 shorter events, 12.7 us)
Async XLA Ops:
  0.6 30.6 %copy-start.2 = (bf16[8,16,2,4096]{3,2,1,0:T(2,128)(2,1)S(1)}, bf16[8,16,2,4096]{3,2,1,0:T(2,128)(2,1)}, u32[]{:S(2)}) copy-start(bf16[8,16,2,4096]{3,2,1,0:T(2,128)(2,1)} %param.14) | copy-start | bytes 6291460
  0.7 1.2 %copy-start.3 = (f32[16,2,4096]{2,1,0:T(2,128)S(1)}, f32[16,2,4096]{2,1,0:T(2,128)}, u32[]{:S(2)}) copy-start(f32[16,2,4096]{2,1,0:T(2,128)} %param.12) | copy-start | bytes 1572868
  5.5 25.7 %copy-start.19 = (f32[16,16]{1,0:T(8,128)S(1)}, f32[16,16]{1,0:T(8,128)}, u32[]{:S(2)}) copy-start(f32[16,16]{1,0:T(8,128)} %local_ref.3) | copy-start | bytes 3076
  6.4 24.8 %copy-start.15 = (s32[64,128]{1,0:T(8,128)}, s32[64,128]{1,0:T(8,128)S(1)}, u32[]{:S(2)}) copy-start(s32[64,128]{1,0:T(8,128)S(1)} %get-tuple-element.12.lane_ref) | copy-start | bytes 98308
  6.4 33.4 %copy-start.7 = (f32[6,64,128]{2,1,0:T(8,128)}, f32[6,64,128]{2,1,0:T(8,128)S(1)}, u32[]{:S(2)}) copy-start(f32[6,64,128]{2,1,0:T(8,128)S(1)} %get-tuple-element.9.refs_2_) | copy-start | bytes 589828
  6.5 33.4 %collective-permute-start.3 = (f32[6,64,128]{2,1,0:T(8,128)S(1)}, f32[6,64,128]{2,1,0:T(8,128)S(1)}, u32[]{:S(2)}, u32[]{:S(2)}) collective-permute-start(f32[6,64,128]{2,1,0:T(8,128)S(1)} %get-tuple-element.9.refs_2_), channel_id=1, source_target_pairs={{2,0},{3,1},{4,2},{5,3},{6,4},{7,5},{10,8},{11,9},{12,10},{13,11},... | collective-permute-start | bytes 589832 | tf_op jit(solution)/shard_map/ppermute | solution.py:339
  7.8 32.7 %collective-permute-start.2 = (f32[6,64,128]{2,1,0:T(8,128)S(1)}, f32[6,64,128]{2,1,0:T(8,128)S(1)}, u32[]{:S(2)}, u32[]{:S(2)}) collective-permute-start(f32[6,64,128]{2,1,0:T(8,128)S(1)} %get-tuple-element.9.refs_2_), channel_id=1, source_target_pairs={{1,0},{2,1},{3,2},{4,3},{5,4},{6,5},{7,6},{9,8},{10,9},{11,10},{12... | collective-permute-start | bytes 589832 | tf_op jit(solution)/shard_map/ppermute | solution.py:339
  9.1 32.1 %collective-permute-start.1 = (f32[6,64,128]{2,1,0:T(8,128)S(1)}, f32[6,64,128]{2,1,0:T(8,128)S(1)}, u32[]{:S(2)}, u32[]{:S(2)}) collective-permute-start(f32[6,64,128]{2,1,0:T(8,128)S(1)} %get-tuple-element.9.refs_2_), channel_id=1, source_target_pairs={{0,1},{1,2},{2,3},{3,4},{4,5},{5,6},{6,7},{8,9},{9,10},{10,11},{11... | collective-permute-start | bytes 589832 | tf_op jit(solution)/shard_map/ppermute | solution.py:339
  12.1 29.8 %collective-permute-start = (f32[6,64,128]{2,1,0:T(8,128)S(1)}, f32[6,64,128]{2,1,0:T(8,128)}, u32[]{:S(2)}, u32[]{:S(2)}) collective-permute-start(f32[6,64,128]{2,1,0:T(8,128)S(1)} %get-tuple-element.9.refs_2_), channel_id=1, source_target_pairs={{0,2},{1,3},{2,4},{3,5},{4,6},{5,7},{8,10},{9,11},{10,12},{11,13},... | collective-permute-start | bytes 589832 | tf_op jit(solution)/shard_map/ppermute | solution.py:339
  18.3 0.9 copy-start.26
  19.3 0.9 copy-start.27
  20.2 0.9 copy-start.28
  27.5 21.1 %all-to-all-start = ((f32[8,2,8,128]{3,2,1,0:T(8,128)}), f32[8,2,8,128]{3,2,1,0:T(8,128)S(1)}, u32[]{:S(2)}, u32[]{:S(2)}) async-start(f32[8,2,8,128]{3,2,1,0:T(8,128)} %slot_sums.1), calls=%async_computation | async-start | bytes 131072 | tf_op jit(solution)/shard_map/all_to_all | solution.py:412
  31.2 2.2 %copy-start = (f32[8,16,2,4096]{3,2,1,0:T(2,128)S(1)}, f32[8,16,2,4096]{3,2,1,0:T(2,128)}, u32[]{:S(2)}) copy-start(f32[8,16,2,4096]{3,2,1,0:T(2,128)} %param.13) | copy-start | bytes 12582916
  41.9 0.9 copy-start.8
  42.8 0.9 copy-start.10
  43.7 0.9 copy-start.12
  44.6 0.9 copy-start.14
  49.4 0.9 copy-start.18
  62.1 6.7 %collective-permute-start.6 = (f32[3,64,128]{2,1,0:T(8,128)S(1)}, f32[3,64,128]{2,1,0:T(8,128)S(1)}, u32[]{:S(2)}, u32[]{:S(2)}) collective-permute-start(f32[3,64,128]{2,1,0:T(8,128)S(1)} %lookup.1.refs_0_), channel_id=1, source_target_pairs={{24,0},{0,8},{8,16},{16,24},{25,1},{1,9},{9,17},{17,25},{26,2},{2,... | collective-permute-start | bytes 294920 | tf_op jit(solution)/shard_map/ppermute | solution.py:454
  63.8 7.0 %collective-permute-start.5 = (f32[3,64,128]{2,1,0:T(8,128)S(1)}, f32[3,64,128]{2,1,0:T(8,128)S(1)}, u32[]{:S(2)}, u32[]{:S(2)}) collective-permute-start(f32[3,64,128]{2,1,0:T(8,128)S(1)} %lookup.1.refs_0_), channel_id=1, source_target_pairs={{16,0},{24,8},{0,16},{8,24},{17,1},{25,9},{1,17},{9,25},{18,2},{26... | collective-permute-start | bytes 294920 | tf_op jit(solution)/shard_map/ppermute | solution.py:454
  65.3 5.6 %collective-permute-start.4 = (f32[3,64,128]{2,1,0:T(8,128)S(1)}, f32[3,64,128]{2,1,0:T(8,128)S(1)}, u32[]{:S(2)}, u32[]{:S(2)}) collective-permute-start(f32[3,64,128]{2,1,0:T(8,128)S(1)} %lookup.1.refs_0_), channel_id=1, source_target_pairs={{8,0},{16,8},{24,16},{0,24},{9,1},{17,9},{25,17},{1,25},{10,2},{18... | collective-permute-start | bytes 294920 | tf_op jit(solution)/shard_map/ppermute | solution.py:454
  77.7 0.8 copy-start.5
  78.5 10.2 %collective-permute-start.10 = (f32[4,64,128]{2,1,0:T(8,128)S(1)}, f32[4,64,128]{2,1,0:T(8,128)S(1)}, u32[]{:S(2)}, u32[]{:S(2)}) collective-permute-start(f32[4,64,128]{2,1,0:T(8,128)S(1)} %bitcast.55), channel_id=1, source_target_pairs={{2,0},{3,1},{4,2},{5,3},{6,4},{7,5},{10,8},{11,9},{12,10},{13,11},... | collective-permute-start | bytes 393224 | tf_op jit(solution)/shard_map/ppermute | solution.py:339
  79.8 8.9 %collective-permute-start.9 = (f32[4,64,128]{2,1,0:T(8,128)S(1)}, f32[4,64,128]{2,1,0:T(8,128)S(1)}, u32[]{:S(2)}, u32[]{:S(2)}) collective-permute-start(f32[4,64,128]{2,1,0:T(8,128)S(1)} %bitcast.56), channel_id=1, source_target_pairs={{1,0},{2,1},{3,2},{4,3},{5,4},{6,5},{7,6},{9,8},{10,9},{11,10},{12... | collective-permute-start | bytes 393224 | tf_op jit(solution)/shard_map/ppermute | solution.py:339
  81.1 7.6 %collective-permute-start.8 = (f32[4,64,128]{2,1,0:T(8,128)S(1)}, f32[4,64,128]{2,1,0:T(8,128)S(1)}, u32[]{:S(2)}, u32[]{:S(2)}) collective-permute-start(f32[4,64,128]{2,1,0:T(8,128)S(1)} %bitcast.57), channel_id=1, source_target_pairs={{0,1},{1,2},{2,3},{3,4},{4,5},{5,6},{6,7},{8,9},{9,10},{10,11},{11... | collective-permute-start | bytes 393224 | tf_op jit(solution)/shard_map/ppermute | solution.py:339
  84.2 8.4 %collective-permute-start.7 = (f32[4,64,128]{2,1,0:T(8,128)S(1)}, f32[4,64,128]{2,1,0:T(8,128)S(1)}, u32[]{:S(2)}, u32[]{:S(2)}) collective-permute-start(f32[4,64,128]{2,1,0:T(8,128)S(1)} %bitcast.58), channel_id=1, source_target_pairs={{0,2},{1,3},{2,4},{3,5},{4,6},{5,7},{8,10},{9,11},{10,12},{11,13},... | collective-permute-start | bytes 393224 | tf_op jit(solution)/shard_map/ppermute | solution.py:339
  94.8 14.1 %all-to-all-start.1 = ((f32[4,4,64,128]{3,2,1,0:T(8,128)}), f32[4,4,64,128]{3,2,1,0:T(8,128)S(1)}, u32[]{:S(2)}, u32[]{:S(2)}) async-start(f32[4,4,64,128]{3,2,1,0:T(8,128)} %diffuse_adjoint.1), calls=%async_computation.1 | async-start | bytes 1048576 | tf_op jit(solution)/shard_map/all_to_all | solution.py:477
  98.3 2.2 %copy-start.1 = (f32[8,16,2,4096]{3,2,1,0:T(2,128)S(1)}, f32[8,16,2,4096]{3,2,1,0:T(2,128)}, u32[]{:S(2)}) copy-start(f32[8,16,2,4096]{3,2,1,0:T(2,128)} %param.13) | copy-start | bytes 12582916
  100.5 1.0 copy-start.6
  101.5 7.4 %copy-start.4 = (f32[16,2,4096]{2,1,0:T(2,128)S(1)}, f32[16,2,4096]{2,1,0:T(2,128)}, u32[]{:S(2)}) copy-start(f32[16,2,4096]{2,1,0:T(2,128)} %param.12) | copy-start | bytes 1572868
  101.5 7.4 %copy-start.21 = (f32[16,16]{1,0:T(8,128)S(1)}, f32[16,16]{1,0:T(8,128)}, u32[]{:S(2)}) copy-start(f32[16,16]{1,0:T(8,128)} %root_ref.3) | copy-start | bytes 3076
  (10 other events, 7.1 us)
where the time goes:
time: 112 us; the launch traced here: 111 us
  Pallas kernels  46.4 us (41%)
  starting transfers between devices  33.8 us (30%)
  local copies, waits for them, and re-layouts  21.9 us (20%)
  waiting for transfers between devices  8.06 us (7%)
    ppermute x8, starting transfers between devices, neighbours(): lax.ppermute(x, axis, [(i, i + d) for i in range(count) if 0 <= i + d < c...  22 us
    unnamed x58, local copies, waits for them, and re-layouts  21.9 us
    pallas_call x1, Pallas kernels, local(): pl.pallas_call(lookup_kernel, in_specs=[SMEM] + [VMEM] * 5, out_specs=VME...  11.7 us
    pallas_call x1, Pallas kernels, local(): pl.pallas_call(functools.partial(member_kernel, member_scale), grid=(memb...  7.4 us
    pallas_call x1, Pallas kernels, local(): pl.pallas_call(functools.partial(scatter_kernel, cap_rows), in_specs=[SME...  6.8 us
    pallas_call x1, Pallas kernels, local(): pl.pallas_call(functools.partial(forward_kernel, member_scale), grid=(mem...  6.37 us
    pallas_call x1, Pallas kernels, local(): pl.pallas_call(functools.partial(slots_kernel, n_cols, cap_rows), grid_sp...  6.36 us
    ppermute x3, starting transfers between devices, local(): lax.ppermute(share, 'ens', [((i + d) % n_ens, i) for i in range(n_ens)])  4.65 us
  transfers between devices with their start and end apart: 13, of which 4 were waited for; matrix products, arithmetic and copies ran while one was open for 0% of the time, Pallas kernels for 20%

commit v1 on v0

--- a/solution.py
+++ b/solution.py
@@ -40,9 +40,27 @@
     return high, (x - high.astype(f32)).astype(bf16)
 
 
-def one_hot(index, count):
-    ids = lax.broadcasted_iota(jnp.int32, (count, index.shape[1]), 0)
-    return jnp.where(ids == index, f32(1), f32(0)).astype(bf16)
+def in_hbm(x):
+    return pltpu.with_memory_space_constraint(x, pltpu.HBM)
+
+
+def spread(row, dtype):
+    return jnp.broadcast_to(row, (16, row.shape[1])).astype(dtype)
+
+
+def matches(index, count):
+    ids = lax.broadcasted_iota(jnp.int32, (count, index.shape[1]), 0).astype(jnp.int16)
+    return ids.reshape(count // 16, 16, index.shape[1]) == spread(index, jnp.int16)[None]
+
+
+def placed_at(index, count, amount=None):
+    where = matches(index, count)
+    amount = bf16(1) if amount is None else spread(amount, bf16)[None]
+    return jnp.where(where, amount, bf16(0)).reshape(count, index.shape[1])
+
+
+def product_nt(left, right):
+    return lax.dot_general(left, right, (((1,), (1,)), ((), ())), preferred_element_type=f32)
 
 
 def over(x, size):
@@ -71,9 +89,14 @@
         rest, block = over(rest, lon // LANES)
         level, row = over(rest, rows)
         grid_row = jnp.where(slot < count_ref[q], level * per_level + block * rows + row, -1)
+        code = (grid_row * LANES + lane).astype(f32)
         for c in range(pieces):
-            row_ref[q * pieces + c : q * pieces + c + 1, :] = grid_row[:, c * LANES : (c + 1) * LANES]
-            lane_ref[q * pieces + c : q * pieces + c + 1, :] = lane[:, c * LANES : (c + 1) * LANES]
+            at = q * pieces + c
+            row_ref[at : at + 1, :] = grid_row[:, c * LANES : (c + 1) * LANES]
+            lane_ref[at : at + 1, :] = lane[:, c * LANES : (c + 1) * LANES]
+            plane = lev_share + 2 + at // per_level
+            at = at % per_level
+            out_ref[plane, at : at + 1, :] = code[:, c * LANES : (c + 1) * LANES]
 
 
 def slots_kernel(n_cols, cap_rows, where_ref, slot_ref, weight_ref, innov_ref, out_ref, acc_ref, fold_ref):
@@ -89,20 +112,20 @@
         amount = weight * innov_ref[at, :]
         upper, lower = over(slot, FINE)
         terms = [t.astype(f32) for t in halves(weight) + halves(amount)]
-        fine_ids = lax.broadcasted_iota(jnp.int32, (FINE, LANES), 0)
         left, right = [], []
         for r in range(group):
-            left.append(one_hot(upper[r : r + 1, :], coarse))
-            mask = fine_ids == lower[r : r + 1, :]
-            right.append(
-                jnp.concatenate([jnp.where(mask, t[r : r + 1, :], f32(0)).astype(bf16) for t in terms], axis=0)
-            )
-        acc_ref[...] += lax.dot_general(
-            jnp.concatenate(left, axis=1),
-            jnp.concatenate(right, axis=1),
-            (((1,), (1,)), ((), ())),
-            preferred_element_type=f32,
-        )
+            left.append(placed_at(upper[r : r + 1, :], coarse))
+            mask = matches(lower[r : r + 1, :], FINE)
+            right += [
+                jnp.concatenate(
+                    [
+                        jnp.where(mask, spread(t[r : r + 1, :], bf16)[None], bf16(0)).reshape(FINE, LANES)
+                        for t in terms
+                    ],
+                    axis=0,
+                )
+            ]
+        acc_ref[...] += product_nt(jnp.concatenate(left, axis=1), jnp.concatenate(right, axis=1))
         return carry
 
     lax.fori_loop(0, obs_rows // group, step, 0)
@@ -232,10 +255,34 @@
     lax.fori_loop(0, lev_share, body, 0)
 
 
-def second_diffusion_kernel(rows, coef_ref, *refs):
-    tiles, out_ref = refs[:-1], refs[-1]
-    copies, lev_share = out_ref.shape[:2]
-    blocks = tiles[0].shape[1] // rows
+def second_diffusion_kernel(rows, cap_rows, where_ref, coef_ref, own_ref, *refs):
+    sides, out_ref, acc_ref, tile_ref = refs[:-3], refs[-3], refs[-2], refs[-1]
+    around = len(sides) // 2
+    codes, amounts = sides[:around], sides[around:]
+    copies, lev_share, per_level, _ = out_ref.shape
+    own = lev_share * per_level
+    entry_rows = amounts[0].shape[0]
+    planes = entry_rows // per_level
+    lists = entry_rows // cap_rows
+    blocks = per_level // rows
+    first = where_ref[0] * own
+
+    for n in range(around):
+        acc_ref[...] = jnp.zeros_like(acc_ref)
+
+        def step(q, carry):
+            at = pl.multiple_of(q * cap_rows, cap_rows)
+            plane = lev_share + 2 + at // per_level
+            code = codes[n][plane, pl.ds(pl.multiple_of(at % per_level, cap_rows), cap_rows), :].astype(jnp.int32)
+            row = lax.shift_right_arithmetic(code, jnp.int32(LANES.bit_length() - 1)) - first
+            put(acc_ref, row, code & (LANES - 1), amounts[n][pl.ds(at, cap_rows), :])
+            return carry
+
+        lax.fori_loop(0, lists, step, 0)
+        tile_ref[n] = (acc_ref[:, :LANES] + acc_ref[:, LANES:]).reshape(lev_share, per_level, LANES)
+
+    half = around // 2
+    tiles = [tile_ref.at[n] for n in range(half)] + [own_ref] + [tile_ref.at[n] for n in range(half, around)]
 
     def body(level, carry):
         final = diffuse_rows(tiles, level, coef_ref, rows)
@@ -247,34 +294,43 @@
     lax.fori_loop(0, lev_share, body, 0)
 
 
-def lookup_kernel(where_ref, part_ref, static_ref, row_ref, lane_ref, slots_ref, out_ref, field_ref, turned_ref):
+def lookup_kernel(where_ref, part_ref, static_ref, row_ref, lane_ref, slots_ref, out_ref, field_ref, terms_ref):
     cells = part_ref.shape[0]
     own = static_ref.shape[0]
     n_lists, _, cap_rows, _ = slots_ref.shape
     field_ref[...] = part_ref[...]
     at = pl.ds(pl.multiple_of(where_ref[0] * own, own), own)
     field_ref[at, :] += static_ref[...]
-
-    def turn(t, carry):
-        at = pl.ds(pl.multiple_of(t * LANES, LANES), LANES)
-        high, low = halves(field_ref[at, :].T)
-        turned_ref[0:LANES, at] = high
-        turned_ref[LANES : 2 * LANES, at] = low
-        return carry
-
-    lax.fori_loop(0, cells // LANES, turn, 0)
-    lane_ids = lax.broadcasted_iota(jnp.int32, (LANES, LANES), 0)
+    high, low = halves(field_ref[...])
+    terms_ref[:, :LANES] = high
+    terms_ref[:, LANES:] = low
+    ids16 = lax.broadcasted_iota(jnp.int32, (LANES, cells), 1).astype(jnp.int16)
+    ids = lax.broadcasted_iota(jnp.int32, (LANES, LANES), 1)
+    ones = jnp.ones((16, 2 * LANES), bf16)
 
     def look(q, carry):
         at = pl.ds(pl.multiple_of(q * cap_rows, cap_rows), cap_rows)
-        rows = row_ref[at, :]
-        lanes = lane_ref[at, :]
-        found = []
+        rows = row_ref[at, :].astype(f32).T
+        lanes = lane_ref[at, :].astype(f32).T
+        picks = []
         for c in range(cap_rows):
-            got = jnp.dot(turned_ref[...], one_hot(rows[c : c + 1, :], cells), preferred_element_type=f32)
-            got = got[:LANES] + got[LANES:]
-            found.append(jnp.sum(jnp.where(lane_ids == lanes[c : c + 1, :], got, f32(0)), axis=0, keepdims=True))
-        out_ref[0, at, :] = jnp.concatenate(found, axis=0)
+            column = jnp.broadcast_to(rows[:, c : c + 1], (LANES, LANES)).astype(jnp.int32).astype(jnp.int16)
+            column = jnp.concatenate([column] * (cells // LANES), axis=1)
+            picks.append(jnp.where(ids16 == column, bf16(1), bf16(0)))
+        got = jnp.dot(jnp.concatenate(picks, axis=0), terms_ref[...], preferred_element_type=f32)
+        kept = []
+        for c in range(cap_rows):
+            mask = ids == jnp.broadcast_to(lanes[:, c : c + 1], (LANES, LANES)).astype(jnp.int32)
+            mine = got[c * LANES : (c + 1) * LANES]
+            kept.append(
+                jnp.concatenate(
+                    [jnp.where(mask, mine[:, :LANES], f32(0)), jnp.where(mask, mine[:, LANES:], f32(0))], axis=1
+                ).astype(bf16)
+            )
+        total = product_nt(ones, jnp.concatenate(kept, axis=0))
+        out_ref[0, at, :] = jnp.concatenate(
+            [total[0:1, c * LANES : (c + 1) * LANES] for c in range(cap_rows)], axis=0
+        )
         out_ref[1, at, :] = slots_ref[q, 0]
         out_ref[2, at, :] = slots_ref[q, 1]
         return carry
@@ -282,37 +338,35 @@
     lax.fori_loop(0, n_lists, look, 0)
 
 
-def scatter_kernel(cap_rows, where_ref, row_ref, lane_ref, *refs):
-    shares, (out_ref, own_ref, acc_ref) = refs[:-3], refs[-3:]
-    cells = out_ref.shape[0]
+def put(acc_ref, rows, lanes, amounts):
+    high, low = (h.astype(f32) for h in halves(amounts))
+    left, right = [], []
+    for c in range(rows.shape[0]):
+        piece = slice(c, c + 1)
+        left.append(placed_at(rows[piece, :], acc_ref.shape[0]))
+        mask = matches(lanes[piece, :], LANES)
+        right.append(
+            jnp.concatenate(
+                [
+                    jnp.where(mask, spread(h[piece, :], bf16)[None], bf16(0)).reshape(LANES, LANES)
+                    for h in (high, low)
+                ],
+                axis=0,
+            )
+        )
+    acc_ref[...] += product_nt(jnp.concatenate(left, axis=1), jnp.concatenate(right, axis=1))
+
+
+def scatter_kernel(cap_rows, where_ref, row_ref, lane_ref, amount_ref, out_ref, own_ref, acc_ref):
     own = own_ref.shape[0]
     acc_ref[...] = jnp.zeros_like(acc_ref)
-    lane_ids = lax.broadcasted_iota(jnp.int32, (LANES, LANES), 0)
-
-    def put(q, carry):
+
+    def step(q, carry):
         at = pl.ds(pl.multiple_of(q * cap_rows, cap_rows), cap_rows)
-        value, weight, amount = (functools.reduce(jnp.add, [s[t, at, :] for s in shares]) for t in range(3))
-        high, low = (h.astype(f32) for h in halves(value * weight - amount))
-        rows = row_ref[at, :]
-        lanes = lane_ref[at, :]
-        left, right = [], []
-        for c in range(cap_rows):
-            left.append(one_hot(rows[c : c + 1, :], cells))
-            mask = lane_ids == lanes[c : c + 1, :]
-            right.append(
-                jnp.concatenate(
-                    [jnp.where(mask, h[c : c + 1, :], f32(0)).astype(bf16) for h in (high, low)], axis=0
-                )
-            )
-        acc_ref[...] += lax.dot_general(
-            jnp.concatenate(left, axis=1),
-            jnp.concatenate(right, axis=1),
-            (((1,), (1,)), ((), ())),
-            preferred_element_type=f32,
-        )
-        return carry
-
-    lax.fori_loop(0, row_ref.shape[0] // cap_rows, put, 0)
+        put(acc_ref, row_ref[at, :], lane_ref[at, :], amount_ref[at, :])
+        return carry
+
+    lax.fori_loop(0, row_ref.shape[0] // cap_rows, step, 0)
     out_ref[...] = acc_ref[:, :LANES] + acc_ref[:, LANES:]
     own_ref[...] = out_ref[pl.ds(pl.multiple_of(where_ref[0] * own, own), own), :]
 
@@ -333,10 +387,9 @@
     lax.fori_loop(0, per_level // 16, chunk, 0)
 
 
-def neighbours(x, axis):
-    count = lax.axis_size(axis)
-    by = (2, 1, -1, -2)
-    return [lax.ppermute(x, axis, [(i, i + d) for i in range(count) if 0 <= i + d < count]) for d in by]
+def shifted(x, by):
+    count = lax.axis_size("cols")
+    return lax.ppermute(x, "cols", [(i, i + by) for i in range(count) if 0 <= i + by < count])
 
 
 def local(
@@ -366,25 +419,42 @@
     member_scale = 1.0 / math.sqrt(members * n_ens - 1)
     where = jnp.stack([lax.axis_index("ens"), lax.axis_index("cols")]).astype(jnp.int32)
 
-    static = tiled(static_control)
-    control = tiled(ensemble_control)
-    pert = tiled(perturbations)
-    north = tiled(face_north)
-    east = tiled(face_east)
-
+    static = in_hbm(tiled(static_control))
+    control = in_hbm(tiled(ensemble_control))
+    pert = in_hbm(tiled(perturbations))
+
+    planes = lev_share + 2 + entry_rows // per_level
+    whole = lambda *shape: pl.BlockSpec(shape, lambda i: (0,) * len(shape))
     packed, entry_row, entry_lane = pl.pallas_call(
         functools.partial(prepare_kernel, lev_share, rows),
-        in_specs=[SMEM, SMEM, SMEM, VMEM, VMEM, VMEM, VMEM],
+        grid=(1,),
+        in_specs=[
+            SMEM,
+            SMEM,
+            SMEM,
+            whole(levels, per_level, LANES),
+            whole(per_level, LANES),
+            whole(per_level, LANES),
+            whole(lists, capacity),
+        ],
         out_specs=[VMEM] * 3,
         out_shape=[
-            jax.ShapeDtypeStruct((lev_share + 2, per_level, LANES), f32),
-            jax.ShapeDtypeStruct((entry_rows, LANES), jnp.int32),
-            jax.ShapeDtypeStruct((entry_rows, LANES), jnp.int32),
+            pltpu.VMEM((planes, per_level, LANES), f32),
+            pltpu.VMEM((entry_rows, LANES), jnp.int32),
+            pltpu.VMEM((entry_rows, LANES), jnp.int32),
         ],
-        compiler_params=params(16),
+        compiler_params=params(8),
         name="prepare",
-    )(where, vertical_root, send_count, static, north, east, send_index)
-    packs = neighbours(packed, "cols")
+    )(
+        where,
+        in_hbm(vertical_root),
+        in_hbm(send_count),
+        static,
+        in_hbm(tiled(face_north)),
+        in_hbm(tiled(face_east)),
+        in_hbm(send_index),
+    )
+    packs = {by: shifted(packed, by) for by in (2, -2)}
 
     obs_rows = obs_slot.shape[0] // LANES
     share_rows = obs_rows // n_ens
@@ -396,106 +466,120 @@
             num_scalar_prefetch=1,
             grid=(1,),
             in_specs=[obs_spec] * 3,
-            out_specs=pl.BlockSpec((n_cols, 2, cap_rows, LANES), lambda i, at: (0, 0, 0, 0)),
+            out_specs=VMEM,
             scratch_shapes=[pltpu.VMEM((coarse, LANES), f32), pltpu.VMEM((coarse, LANES), f32)],
         ),
-        out_shape=jax.ShapeDtypeStruct((n_cols, 2, cap_rows, LANES), f32),
-        compiler_params=params(32),
-        cost_estimate=pl.CostEstimate(flops=2 * 128 * coarse * share_rows * LANES, bytes_accessed=12 * share_rows * LANES, transcendentals=0),
+        out_shape=pltpu.VMEM((n_cols, 2, cap_rows, LANES), f32),
+        compiler_params=params(16),
         name="slot_sums",
     )(
         where,
-        obs_slot.reshape(obs_rows, LANES),
-        obs_weight.reshape(obs_rows, LANES),
-        innovation.reshape(obs_rows, LANES),
+        in_hbm(obs_slot.reshape(obs_rows, LANES)),
+        in_hbm(obs_weight.reshape(obs_rows, LANES)),
+        in_hbm(innovation.reshape(obs_rows, LANES)),
     )
+    packed_again, slots = lax.optimization_barrier((packed, slots))
+    packs |= {by: shifted(packed_again, by) for by in (1, -1)}
     slots = lax.all_to_all(slots, "cols", split_axis=0, concat_axis=0, tiled=True)
 
     member_spec = pl.BlockSpec((1, levels, per_level, LANES), lambda k: (k, 0, 0, 0))
-    whole_spec = pl.BlockSpec((levels, per_level, LANES), lambda k: (0, 0, 0))
     splat_shape = pltpu.VMEM((levels, levels, 8, LANES), f32)
-    member_cost = pl.CostEstimate(flops=2 * members * levels * cells * LANES, bytes_accessed=members * cells * LANES * 6, transcendentals=0)
+    member_cost = pl.CostEstimate(
+        flops=2 * members * levels * cells * LANES,
+        bytes_accessed=members * cells * LANES * 6,
+        transcendentals=0,
+    )
     part = pl.pallas_call(
         functools.partial(forward_kernel, member_scale),
         grid=(members,),
         in_specs=[SMEM, member_spec, member_spec],
-        out_specs=whole_spec,
-        out_shape=jax.ShapeDtypeStruct((levels, per_level, LANES), f32),
+        out_specs=VMEM,
+        out_shape=pltpu.VMEM((levels, per_level, LANES), f32),
         scratch_shapes=[splat_shape],
-        compiler_params=params(32),
+        compiler_params=params(8),
         cost_estimate=member_cost,
         name="members_forward",
-    )(vertical_local, control, pert)
-
-    tiles = [packs[0], packs[1], packed, packs[2], packs[3]]
+    )(in_hbm(vertical_local), control, pert)
+
     blocks = per_level // rows
     increment, coefs = pl.pallas_call(
         functools.partial(first_diffusion_kernel, lev_share, rows),
         in_specs=[SMEM] + [VMEM] * 5,
         out_specs=[VMEM] * 2,
         out_shape=[
-            jax.ShapeDtypeStruct((lev_share, per_level, LANES), f32),
-            jax.ShapeDtypeStruct((5, 5 * rows, blocks, LANES), f32),
+            pltpu.VMEM((lev_share, per_level, LANES), f32),
+            pltpu.VMEM((5, 5 * rows, blocks, LANES), f32),
         ],
-        compiler_params=params(32),
+        compiler_params=params(8),
         name="diffuse_forward",
-    )(where, *tiles)
+    )(where, packs[2], packs[1], packed, packs[-1], packs[-2])
 
     share = pl.pallas_call(
         lookup_kernel,
         in_specs=[SMEM] + [VMEM] * 5,
         out_specs=VMEM,
-        out_shape=jax.ShapeDtypeStruct((3, entry_rows, LANES), f32),
-        scratch_shapes=[pltpu.VMEM((cells, LANES), f32), pltpu.VMEM((2 * LANES, cells), bf16)],
-        compiler_params=params(32),
+        out_shape=pltpu.VMEM((3, entry_rows, LANES), f32),
+        scratch_shapes=[pltpu.VMEM((cells, LANES), f32), pltpu.VMEM((cells, 2 * LANES), bf16)],
+        compiler_params=params(16),
         name="lookup",
     )(where, part.reshape(cells, LANES), increment.reshape(own, LANES), entry_row, entry_lane, slots)
-    shares = [share] + [
-        lax.ppermute(share, "ens", [((i + d) % n_ens, i) for i in range(n_ens)]) for d in range(1, n_ens)
-    ]
+    total = share
+    for d in range(1, n_ens):
+        total = total + lax.ppermute(share, "ens", [((i + d) % n_ens, i) for i in range(n_ens)])
+    amounts = total[0] * total[1] - total[2]
+    amounts_around = [shifted(amounts, by) for by in (2, 1, -1, -2)]
 
     adjoint, adjoint_own = pl.pallas_call(
         functools.partial(scatter_kernel, cap_rows),
-        in_specs=[SMEM] + [VMEM] * (2 + n_ens),
+        in_specs=[SMEM] + [VMEM] * 3,
         out_specs=[VMEM] * 2,
-        out_shape=[jax.ShapeDtypeStruct((cells, LANES), f32), jax.ShapeDtypeStruct((own, LANES), f32)],
+        out_shape=[pltpu.VMEM((cells, LANES), f32), pltpu.VMEM((own, LANES), f32)],
         scratch_shapes=[pltpu.VMEM((cells, 2 * LANES), f32)],
-        compiler_params=params(32),
+        compiler_params=params(16),
         name="scatter",
-    )(where, entry_row, entry_lane, *shares)
-    adjoint_own = adjoint_own.reshape(lev_share, per_level, LANES)
-    around = neighbours(adjoint_own, "cols")
+    )(where, entry_row, entry_lane, amounts)
 
     smooth = pl.pallas_call(
-        functools.partial(second_diffusion_kernel, rows),
-        in_specs=[VMEM] * 6,
+        functools.partial(second_diffusion_kernel, rows, cap_rows),
+        in_specs=[SMEM] + [VMEM] * 10,
         out_specs=VMEM,
-        out_shape=jax.ShapeDtypeStruct((n_ens, lev_share, per_level, LANES), f32),
-        compiler_params=params(32),
+        out_shape=pltpu.VMEM((n_ens, lev_share, per_level, LANES), f32),
+        scratch_shapes=[pltpu.VMEM((own, 2 * LANES), f32), pltpu.VMEM((4, lev_share, per_level, LANES), f32)],
+        compiler_params=params(16),
         name="diffuse_adjoint",
-    )(coefs, around[0], around[1], adjoint_own, around[2], around[3])
+    )(
+        where,
+        coefs,
+        adjoint_own.reshape(lev_share, per_level, LANES),
+        packs[2],
+        packs[1],
+        packs[-1],
+        packs[-2],
+        *amounts_around,
+    )
     smooth = lax.all_to_all(smooth, "ens", split_axis=0, concat_axis=0, tiled=True)
 
     ensemble_grad = pl.pallas_call(
         functools.partial(member_kernel, member_scale),
         grid=(members,),
-        in_specs=[SMEM, whole_spec, member_spec, member_spec],
+        in_specs=[SMEM, VMEM, member_spec, member_spec],
         out_specs=member_spec,
         out_shape=jax.ShapeDtypeStruct((members, levels, per_level, LANES), f32),
         scratch_shapes=[splat_shape],
-        compiler_params=params(32),
+        compiler_params=params(8),
         cost_estimate=member_cost,
         name="members_gradient",
-    )(vertical_local, adjoint.reshape(levels, per_level, LANES), control, pert)
+    )(in_hbm(vertical_local), adjoint.reshape(levels, per_level, LANES), control, pert)
 
     static_grad = pl.pallas_call(
         static_kernel,
-        in_specs=[SMEM, VMEM, VMEM],
-        out_specs=VMEM,
+        grid=(1,),
+        in_specs=[SMEM, whole(levels, per_level, LANES), VMEM],
+        out_specs=whole(levels, per_level, LANES),
         out_shape=jax.ShapeDtypeStruct((levels, per_level, LANES), f32),
-        compiler_params=params(16),
+        compiler_params=params(8),
         name="static_gradient",
-    )(vertical_root, static, smooth.reshape(levels, per_level, LANES))
+    )(in_hbm(vertical_root), static, smooth.reshape(levels, per_level, LANES))
     return (untiled(static_grad, rows), untiled(ensemble_grad, rows))
 
 

time: 112 us -> 101 us (0.902)
  local copies, waits for them, and re-layouts: 21.9 us -> 0 us
  Pallas kernels: 46.4 us -> 61.2 us
  waiting for transfers between devices: 8.06 us -> 3.86 us
    unnamed x58 -> x0, local copies, waits for them, and re-layouts: 21.9 us -> none
    pallas_call x3, Pallas kernels: 5.29 us -> 17.8 us  [the longest x1 13.9 us: local(): pl.pallas_call(functools.partial(second_diffusion_kernel, rows, cap_rows)...]
    ppermute x8, waiting for transfers between devices: 3.85 us -> 0.02 us  [shifted(): lax.ppermute(x, 'cols', [(i, i + by) for i in range(count) if 0 <= i + by...]
    pallas_call x1, Pallas kernels: 7.4 us -> 9.62 us  [local(): pl.pallas_call(functools.partial(member_kernel, member_scale), grid=(memb...]
    pallas_call x1, Pallas kernels: 11.7 us -> 9.61 us  [local(): pl.pallas_call(lookup_kernel, in_specs=[SMEM] + [VMEM] * 5, out_specs=VME...]
    pallas_call x1, Pallas kernels: 6.37 us -> 8.25 us  [local(): pl.pallas_call(functools.partial(forward_kernel, member_scale), grid=(mem...]
  transfers between devices with their start and end apart: 13 -> 13, of which waited for: 4 -> 3; matrix products, arithmetic and copies ran while one was open for 0% -> 0% of each run, Pallas kernels for 20% -> 27%
where the time goes in v1:
time: 101 us; the launch traced here: 99.8 us
  Pallas kernels  61.2 us (61%)
  starting transfers between devices  33.8 us (33%)
  waiting for transfers between devices  3.86 us (4%)
    ppermute x8, starting transfers between devices, shifted(): lax.ppermute(x, 'cols', [(i, i + by) for i in range(count) if 0 <= i + by...  21.4 us
    pallas_call x1, Pallas kernels, local(): pl.pallas_call(functools.partial(second_diffusion_kernel, rows, cap_rows)...  13.9 us
    pallas_call x1, Pallas kernels, local(): pl.pallas_call(functools.partial(member_kernel, member_scale), grid=(memb...  9.62 us
    pallas_call x1, Pallas kernels, local(): pl.pallas_call(lookup_kernel, in_specs=[SMEM] + [VMEM] * 5, out_specs=VME...  9.61 us
    pallas_call x1, Pallas kernels, local(): pl.pallas_call(functools.partial(forward_kernel, member_scale), grid=(mem...  8.25 us
    pallas_call x1, Pallas kernels, local(): pl.pallas_call(functools.partial(slots_kernel, n_cols, cap_rows), grid_sp...  7.22 us
    pallas_call x1, Pallas kernels, local(): pl.pallas_call(functools.partial(scatter_kernel, cap_rows), in_specs=[SME...  6.63 us
    all_to_all x1, starting transfers between devices, local(): lax.all_to_all(slots, 'cols', split_axis=0, concat_axis=0, tiled=True)  4.56 us
  transfers between devices with their start and end apart: 13, of which 3 were waited for; matrix products, arithmetic and copies ran while one was open for 0% of the time, Pallas kernels for 27%

profile of v1, /device:TPU:0, one launch (start us, length us, event | category | flops | bytes accessed | tf_op | source)
XLA Modules:
  0.0 99.8 jit_solution(14264660016777565056)
XLA Ops:
  0.6 0.1 pad_add_fusion.where_ref
  0.7 7.2 %slot_sums.1 = f32[8,2,8,128]{3,2,1,0:T(8,128)} custom-call(s32[2]{0:T(128)S(1)} %pad_add_fusion.where_ref, s32[512,128]{1,0:T(8,128)} %bitcast.60, f32[512,128]{1,0:T(8,128)} %bitcast.61, f32[512,128]{1,0:T(8,128)} %bitcast.62), custom_call_target="tpu_custom_call" | custom-call | tf_op jit(solution)/shard_map/slot_sums/pallas_call | solution.py:463
  7.9 1.3 %prepare.1 = (f32[7,64,128]{2,1,0:T(8,128)S(1)}, s32[64,128]{1,0:T(8,128)S(1)}, s32[64,128]{1,0:T(8,128)S(1)}) custom-call(s32[2]{0:T(128)S(1)} %pad_add_fusion.where_ref, f32[16,16]{1,0:T(8,128)} %root_ref.3, s32[8]{0:T(128)} %count_ref.1, f32[16,64,128]{2,1,0:T(8,128)} %bitcast.57, f32[64,128]{1,0:T(8,128)} %bitcast.63, f32[64,128]{1,0:T(8,128)} %bitcast.64, ...), custom_call_target="tpu_custom_call" | custom-call | tf_op jit(solution)/shard_map/prepare/pallas_call | solution.py:428
  9.3 1.3 %collective-permute-start.2 = (f32[7,64,128]{2,1,0:T(8,128)S(1)}, f32[7,64,128]{2,1,0:T(8,128)S(1)}, u32[]{:S(2)}, u32[]{:S(2)}) collective-permute-start(f32[7,64,128]{2,1,0:T(8,128)S(1)} %get-tuple-element.12.refs_2_), channel_id=1, source_target_pairs={{1,0},{2,1},{3,2},{4,3},{5,4},{6,5},{7,6},{9,8},{10,9},{11,10},{12... | collective-permute-start | bytes 688136 | tf_op jit(solution)/shard_map/ppermute | solution.py:392
  10.6 3.0 %collective-permute-start.1 = (f32[7,64,128]{2,1,0:T(8,128)S(1)}, f32[7,64,128]{2,1,0:T(8,128)S(1)}, u32[]{:S(2)}, u32[]{:S(2)}) collective-permute-start(f32[7,64,128]{2,1,0:T(8,128)S(1)} %get-tuple-element.12.refs_2_), channel_id=1, source_target_pairs={{0,1},{1,2},{2,3},{3,4},{4,5},{5,6},{6,7},{8,9},{9,10},{10,11},{11... | collective-permute-start | bytes 688136 | tf_op jit(solution)/shard_map/ppermute | solution.py:392
  13.6 1.3 %collective-permute-start.3 = (f32[7,64,128]{2,1,0:T(8,128)S(1)}, f32[7,64,128]{2,1,0:T(8,128)S(1)}, u32[]{:S(2)}, u32[]{:S(2)}) collective-permute-start(f32[7,64,128]{2,1,0:T(8,128)S(1)} %get-tuple-element.12.refs_2_), channel_id=1, source_target_pairs={{2,0},{3,1},{4,2},{5,3},{6,4},{7,5},{10,8},{11,9},{12,10},{13,11},... | collective-permute-start | bytes 688136 | tf_op jit(solution)/shard_map/ppermute | solution.py:392
  14.9 5.6 %collective-permute-start = (f32[7,64,128]{2,1,0:T(8,128)S(1)}, f32[7,64,128]{2,1,0:T(8,128)S(1)}, u32[]{:S(2)}, u32[]{:S(2)}) collective-permute-start(f32[7,64,128]{2,1,0:T(8,128)S(1)} %get-tuple-element.12.refs_2_), channel_id=1, source_target_pairs={{0,2},{1,3},{2,4},{3,5},{4,6},{5,7},{8,10},{9,11},{10,12},{11,13},... | collective-permute-start | bytes 688136 | tf_op jit(solution)/shard_map/ppermute | solution.py:392
  20.5 4.6 %all-to-all-start = ((f32[8,2,8,128]{3,2,1,0:T(8,128)}), f32[8,2,8,128]{3,2,1,0:T(8,128)S(1)}, u32[]{:S(2)}, u32[]{:S(2)}) async-start(f32[8,2,8,128]{3,2,1,0:T(8,128)} %slot_sums.1), calls=%async_computation | async-start | bytes 131072 | tf_op jit(solution)/shard_map/all_to_all | solution.py:483
  25.0 8.3 %members_forward.1 = f32[16,64,128]{2,1,0:T(8,128)S(1)} custom-call(f32[16,16]{1,0:T(8,128)} %local_ref.3, f32[8,16,64,128]{3,2,1,0:T(8,128)} %bitcast.52, bf16[8,16,64,128]{3,2,1,0:T(8,128)(2,1)} %bitcast.54), custom_call_target="tpu_custom_call" | custom-call | flops 33554432 | bytes 6291456 | tf_op jit(solution)/shard_map/members_forward/pallas_call | solution.py:492
  33.3 0.0 collective-permute-done.2.refs_3_.refs_2_
  33.3 0.0 collective-permute-done.1.refs_1_
  33.3 0.0 collective-permute-done.refs_0_
  33.3 2.0 %diffuse_forward.1 = (f32[4,64,128]{2,1,0:T(8,128)S(1)}, f32[5,10,32,128]{3,2,1,0:T(8,128)S(1)}) custom-call(s32[2]{0:T(128)S(1)} %pad_add_fusion.where_ref, f32[7,64,128]{2,1,0:T(8,128)S(1)} %collective-permute-done.refs_0_, f32[7,64,128]{2,1,0:T(8,128)S(1)} %collective-permute-done.1.refs_1_, f32[7,64,128]{2,1,0:T(8,128)S(1)} %get-tuple-element.12.refs_2_, ...), custom_call_target="tpu_custom_call" | custom-call | tf_op jit(solution)/shard_map/diffuse_forward/pallas_call | solution.py:505
  35.4 9.6 %lookup.1 = f32[3,64,128]{2,1,0:T(8,128)S(1)} custom-call(s32[2]{0:T(128)S(1)} %pad_add_fusion.where_ref, f32[1024,128]{1,0:T(8,128)S(1)} %bitcast.48, f32[256,128]{1,0:T(8,128)S(1)} %bitcast.51, s32[64,128]{1,0:T(8,128)S(1)} %get-tuple-element.14.row_ref, s32[64,128]{1,0:T(8,128)S(1)} %get-tuple-element.15.lane_ref, f32[8,2,8,128]{3,2,1,0:T(8,128)S(1)} %all-to-all-done.slots_ref), custom_call_target="tpu_custom_call" | custom-call | tf_op jit(solution)/shard_map/lookup/pallas_call | solution.py:517
  45.0 1.5 %collective-permute-start.6 = (f32[3,64,128]{2,1,0:T(8,128)S(1)}, f32[3,64,128]{2,1,0:T(8,128)S(1)}, u32[]{:S(2)}, u32[]{:S(2)}) collective-permute-start(f32[3,64,128]{2,1,0:T(8,128)S(1)} %lookup.1), channel_id=1, source_target_pairs={{24,0},{0,8},{8,16},{16,24},{25,1},{1,9},{9,17},{17,25},{26,2},{2,... | collective-permute-start | bytes 294920 | tf_op jit(solution)/shard_map/ppermute | solution.py:528
  46.5 1.5 %collective-permute-start.5 = (f32[3,64,128]{2,1,0:T(8,128)S(1)}, f32[3,64,128]{2,1,0:T(8,128)S(1)}, u32[]{:S(2)}, u32[]{:S(2)}) collective-permute-start(f32[3,64,128]{2,1,0:T(8,128)S(1)} %lookup.1), channel_id=1, source_target_pairs={{16,0},{24,8},{0,16},{8,24},{17,1},{25,9},{1,17},{9,25},{18,2},{26... | collective-permute-start | bytes 294920 | tf_op jit(solution)/shard_map/ppermute | solution.py:528
  48.0 1.4 %collective-permute-start.4 = (f32[3,64,128]{2,1,0:T(8,128)S(1)}, f32[3,64,128]{2,1,0:T(8,128)S(1)}, u32[]{:S(2)}, u32[]{:S(2)}) collective-permute-start(f32[3,64,128]{2,1,0:T(8,128)S(1)} %lookup.1), channel_id=1, source_target_pairs={{8,0},{16,8},{24,16},{0,24},{9,1},{17,9},{25,17},{1,25},{10,2},{18... | collective-permute-start | bytes 294920 | tf_op jit(solution)/shard_map/ppermute | solution.py:528
  49.4 2.0 %collective-permute-done.6 = f32[3,64,128]{2,1,0:T(8,128)S(1)} collective-permute-done((f32[3,64,128]{2,1,0:T(8,128)S(1)}, f32[3,64,128]{2,1,0:T(8,128)S(1)}, u32[]{:S(2)}, u32[]{:S(2)}) %collective-permute-start.6) | collective-permute-done | bytes 98336 | tf_op jit(solution)/shard_map/ppermute | solution.py:528
  51.5 1.7 %collective-permute-done.5 = f32[3,64,128]{2,1,0:T(8,128)S(1)} collective-permute-done((f32[3,64,128]{2,1,0:T(8,128)S(1)}, f32[3,64,128]{2,1,0:T(8,128)S(1)}, u32[]{:S(2)}, u32[]{:S(2)}) %collective-permute-start.5) | collective-permute-done | bytes 98336 | tf_op jit(solution)/shard_map/ppermute | solution.py:528
  53.2 0.1 collective-permute-done.4
  53.3 1.3 %collective-permute-start.10 = (f32[64,128]{1,0:T(8,128)S(1)}, f32[64,128]{1,0:T(8,128)S(1)}, u32[]{:S(2)}, u32[]{:S(2)}) collective-permute-start(f32[64,128]{1,0:T(8,128)S(1)} %fusion.amount_ref), channel_id=1, source_target_pairs={{2,0},{3,1},{4,2},{5,3},{6,4},{7,5},{10,8},{11,9},{12,10},{13,11},... | collective-permute-start | bytes 98312 | tf_op jit(solution)/shard_map/ppermute | solution.py:392
  54.6 1.3 %collective-permute-start.9 = (f32[64,128]{1,0:T(8,128)S(1)}, f32[64,128]{1,0:T(8,128)S(1)}, u32[]{:S(2)}, u32[]{:S(2)}) collective-permute-start(f32[64,128]{1,0:T(8,128)S(1)} %fusion.amount_ref), channel_id=1, source_target_pairs={{1,0},{2,1},{3,2},{4,3},{5,4},{6,5},{7,6},{9,8},{10,9},{11,10},{12... | collective-permute-start | bytes 98312 | tf_op jit(solution)/shard_map/ppermute | solution.py:392
  55.9 3.0 %collective-permute-start.8 = (f32[64,128]{1,0:T(8,128)S(1)}, f32[64,128]{1,0:T(8,128)S(1)}, u32[]{:S(2)}, u32[]{:S(2)}) collective-permute-start(f32[64,128]{1,0:T(8,128)S(1)} %fusion.amount_ref), channel_id=1, source_target_pairs={{0,1},{1,2},{2,3},{3,4},{4,5},{5,6},{6,7},{8,9},{9,10},{10,11},{11... | collective-permute-start | bytes 98312 | tf_op jit(solution)/shard_map/ppermute | solution.py:392
  59.0 4.6 %collective-permute-start.7 = (f32[64,128]{1,0:T(8,128)S(1)}, f32[64,128]{1,0:T(8,128)S(1)}, u32[]{:S(2)}, u32[]{:S(2)}) collective-permute-start(f32[64,128]{1,0:T(8,128)S(1)} %fusion.amount_ref), channel_id=1, source_target_pairs={{0,2},{1,3},{2,4},{3,5},{4,6},{5,7},{8,10},{9,11},{10,12},{11,13},... | collective-permute-start | bytes 98312 | tf_op jit(solution)/shard_map/ppermute | solution.py:392
  63.5 6.6 %scatter.1 = (f32[1024,128]{1,0:T(8,128)S(1)}, f32[256,128]{1,0:T(8,128)S(1)}) custom-call(s32[2]{0:T(128)S(1)} %pad_add_fusion.where_ref, s32[64,128]{1,0:T(8,128)S(1)} %get-tuple-element.14.row_ref, s32[64,128]{1,0:T(8,128)S(1)} %get-tuple-element.15.lane_ref, f32[64,128]{1,0:T(8,128)S(1)} %fusion.amount_ref), custom_call_target="tpu_custom_call" | custom-call | tf_op jit(solution)/shard_map/scatter/pallas_call | solution.py:532
  70.2 0.0 collective-permute-done.10.refs_7_
  70.2 0.0 collective-permute-done.9.refs_6_
  70.2 0.0 collective-permute-done.7.refs_4_
  70.2 13.9 %diffuse_adjoint.1 = f32[4,4,64,128]{3,2,1,0:T(8,128)} custom-call(s32[2]{0:T(128)S(1)} %pad_add_fusion.where_ref, f32[5,10,32,128]{3,2,1,0:T(8,128)S(1)} %get-tuple-element.13.coef_ref, f32[4,64,128]{2,1,0:T(8,128)S(1)} %bitcast.50, f32[7,64,128]{2,1,0:T(8,128)S(1)} %collective-permute-done.refs_0_, f32[7,64,128]{2,1,0:T(8,128)S(1)} %collective-permute-done.1.refs_1_, ...), custom_call_target="tpu_custom_call" | custom-call | tf_op jit(solution)/shard_map/diffuse_adjoint/pallas_call | solution.py:542
  84.1 3.5 %all-to-all-start.1 = ((f32[4,4,64,128]{3,2,1,0:T(8,128)}), f32[4,4,64,128]{3,2,1,0:T(8,128)S(1)}, u32[]{:S(2)}, u32[]{:S(2)}) async-start(f32[4,4,64,128]{3,2,1,0:T(8,128)} %diffuse_adjoint.1), calls=%async_computation.1 | async-start | bytes 1048576 | tf_op jit(solution)/shard_map/all_to_all | solution.py:560
  87.6 9.6 %members_gradient.1 = f32[8,16,64,128]{3,2,1,0:T(8,128)} custom-call(f32[16,16]{1,0:T(8,128)} %local_ref.3, f32[16,64,128]{2,1,0:T(8,128)S(1)} %bitcast.49, f32[8,16,64,128]{3,2,1,0:T(8,128)} %bitcast.53, bf16[8,16,64,128]{3,2,1,0:T(8,128)(2,1)} %bitcast.55), custom_call_target="tpu_custom_call" | custom-call | flops 33554432 | bytes 6291456 | tf_op jit(solution)/shard_map/members_gradient/pallas_call | solution.py:562
  97.2 2.6 %static_gradient.1 = f32[16,64,128]{2,1,0:T(8,128)} custom-call(f32[16,16]{1,0:T(8,128)} %root_ref.3, f32[16,64,128]{2,1,0:T(8,128)} %bitcast.58, f32[16,64,128]{2,1,0:T(8,128)S(1)} %bitcast.47), custom_call_target="tpu_custom_call" | custom-call | tf_op jit(solution)/shard_map/static_gradient/pallas_call | solution.py:574
  (6 shorter events, 0.0 us)
Async XLA Ops:
  9.3 24.0 %collective-permute-start.2 = (f32[7,64,128]{2,1,0:T(8,128)S(1)}, f32[7,64,128]{2,1,0:T(8,128)S(1)}, u32[]{:S(2)}, u32[]{:S(2)}) collective-permute-start(f32[7,64,128]{2,1,0:T(8,128)S(1)} %get-tuple-element.12.refs_2_), channel_id=1, source_target_pairs={{1,0},{2,1},{3,2},{4,3},{5,4},{6,5},{7,6},{9,8},{10,9},{11,10},{12... | collective-permute-start | bytes 688136 | tf_op jit(solution)/shard_map/ppermute | solution.py:392
  10.6 22.8 %collective-permute-start.1 = (f32[7,64,128]{2,1,0:T(8,128)S(1)}, f32[7,64,128]{2,1,0:T(8,128)S(1)}, u32[]{:S(2)}, u32[]{:S(2)}) collective-permute-start(f32[7,64,128]{2,1,0:T(8,128)S(1)} %get-tuple-element.12.refs_2_), channel_id=1, source_target_pairs={{0,1},{1,2},{2,3},{3,4},{4,5},{5,6},{6,7},{8,9},{9,10},{10,11},{11... | collective-permute-start | bytes 688136 | tf_op jit(solution)/shard_map/ppermute | solution.py:392
  13.6 19.7 %collective-permute-start.3 = (f32[7,64,128]{2,1,0:T(8,128)S(1)}, f32[7,64,128]{2,1,0:T(8,128)S(1)}, u32[]{:S(2)}, u32[]{:S(2)}) collective-permute-start(f32[7,64,128]{2,1,0:T(8,128)S(1)} %get-tuple-element.12.refs_2_), channel_id=1, source_target_pairs={{2,0},{3,1},{4,2},{5,3},{6,4},{7,5},{10,8},{11,9},{12,10},{13,11},... | collective-permute-start | bytes 688136 | tf_op jit(solution)/shard_map/ppermute | solution.py:392
  14.9 18.4 %collective-permute-start = (f32[7,64,128]{2,1,0:T(8,128)S(1)}, f32[7,64,128]{2,1,0:T(8,128)S(1)}, u32[]{:S(2)}, u32[]{:S(2)}) collective-permute-start(f32[7,64,128]{2,1,0:T(8,128)S(1)} %get-tuple-element.12.refs_2_), channel_id=1, source_target_pairs={{0,2},{1,3},{2,4},{3,5},{4,6},{5,7},{8,10},{9,11},{10,12},{11,13},... | collective-permute-start | bytes 688136 | tf_op jit(solution)/shard_map/ppermute | solution.py:392
  20.5 14.9 %all-to-all-start = ((f32[8,2,8,128]{3,2,1,0:T(8,128)}), f32[8,2,8,128]{3,2,1,0:T(8,128)S(1)}, u32[]{:S(2)}, u32[]{:S(2)}) async-start(f32[8,2,8,128]{3,2,1,0:T(8,128)} %slot_sums.1), calls=%async_computation | async-start | bytes 131072 | tf_op jit(solution)/shard_map/all_to_all | solution.py:483
  45.0 6.5 %collective-permute-start.6 = (f32[3,64,128]{2,1,0:T(8,128)S(1)}, f32[3,64,128]{2,1,0:T(8,128)S(1)}, u32[]{:S(2)}, u32[]{:S(2)}) collective-permute-start(f32[3,64,128]{2,1,0:T(8,128)S(1)} %lookup.1), channel_id=1, source_target_pairs={{24,0},{0,8},{8,16},{16,24},{25,1},{1,9},{9,17},{17,25},{26,2},{2,... | collective-permute-start | bytes 294920 | tf_op jit(solution)/shard_map/ppermute | solution.py:528
  46.5 6.7 %collective-permute-start.5 = (f32[3,64,128]{2,1,0:T(8,128)S(1)}, f32[3,64,128]{2,1,0:T(8,128)S(1)}, u32[]{:S(2)}, u32[]{:S(2)}) collective-permute-start(f32[3,64,128]{2,1,0:T(8,128)S(1)} %lookup.1), channel_id=1, source_target_pairs={{16,0},{24,8},{0,16},{8,24},{17,1},{25,9},{1,17},{9,25},{18,2},{26... | collective-permute-start | bytes 294920 | tf_op jit(solution)/shard_map/ppermute | solution.py:528
  48.0 5.3 %collective-permute-start.4 = (f32[3,64,128]{2,1,0:T(8,128)S(1)}, f32[3,64,128]{2,1,0:T(8,128)S(1)}, u32[]{:S(2)}, u32[]{:S(2)}) collective-permute-start(f32[3,64,128]{2,1,0:T(8,128)S(1)} %lookup.1), channel_id=1, source_target_pairs={{8,0},{16,8},{24,16},{0,24},{9,1},{17,9},{25,17},{1,25},{10,2},{18... | collective-permute-start | bytes 294920 | tf_op jit(solution)/shard_map/ppermute | solution.py:528
  53.3 16.8 %collective-permute-start.10 = (f32[64,128]{1,0:T(8,128)S(1)}, f32[64,128]{1,0:T(8,128)S(1)}, u32[]{:S(2)}, u32[]{:S(2)}) collective-permute-start(f32[64,128]{1,0:T(8,128)S(1)} %fusion.amount_ref), channel_id=1, source_target_pairs={{2,0},{3,1},{4,2},{5,3},{6,4},{7,5},{10,8},{11,9},{12,10},{13,11},... | collective-permute-start | bytes 98312 | tf_op jit(solution)/shard_map/ppermute | solution.py:392
  54.6 15.6 %collective-permute-start.9 = (f32[64,128]{1,0:T(8,128)S(1)}, f32[64,128]{1,0:T(8,128)S(1)}, u32[]{:S(2)}, u32[]{:S(2)}) collective-permute-start(f32[64,128]{1,0:T(8,128)S(1)} %fusion.amount_ref), channel_id=1, source_target_pairs={{1,0},{2,1},{3,2},{4,3},{5,4},{6,5},{7,6},{9,8},{10,9},{11,10},{12... | collective-permute-start | bytes 98312 | tf_op jit(solution)/shard_map/ppermute | solution.py:392
  55.9 14.3 %collective-permute-start.8 = (f32[64,128]{1,0:T(8,128)S(1)}, f32[64,128]{1,0:T(8,128)S(1)}, u32[]{:S(2)}, u32[]{:S(2)}) collective-permute-start(f32[64,128]{1,0:T(8,128)S(1)} %fusion.amount_ref), channel_id=1, source_target_pairs={{0,1},{1,2},{2,3},{3,4},{4,5},{5,6},{6,7},{8,9},{9,10},{10,11},{11... | collective-permute-start | bytes 98312 | tf_op jit(solution)/shard_map/ppermute | solution.py:392
  59.0 11.2 %collective-permute-start.7 = (f32[64,128]{1,0:T(8,128)S(1)}, f32[64,128]{1,0:T(8,128)S(1)}, u32[]{:S(2)}, u32[]{:S(2)}) collective-permute-start(f32[64,128]{1,0:T(8,128)S(1)} %fusion.amount_ref), channel_id=1, source_target_pairs={{0,2},{1,3},{2,4},{3,5},{4,6},{5,7},{8,10},{9,11},{10,12},{11,13},... | collective-permute-start | bytes 98312 | tf_op jit(solution)/shard_map/ppermute | solution.py:392
  84.1 13.1 %all-to-all-start.1 = ((f32[4,4,64,128]{3,2,1,0:T(8,128)}), f32[4,4,64,128]{3,2,1,0:T(8,128)S(1)}, u32[]{:S(2)}, u32[]{:S(2)}) async-start(f32[4,4,64,128]{3,2,1,0:T(8,128)} %diffuse_adjoint.1), calls=%async_computation.1 | async-start | bytes 1048576 | tf_op jit(solution)/shard_map/all_to_all | solution.py:560

commit v2 on v1

v2 whole, which is shorter than its diff:
```python
import functools
import math

import jax
import jax.numpy as jnp
from jax import lax
from jax.experimental import pallas as pl
from jax.experimental.pallas import tpu as pltpu
from jax.sharding import PartitionSpec as P

NDIFF = 4
LANES = 128
FINE = 32
MIB = 1 << 20

f32 = jnp.float32
bf16 = jnp.bfloat16
SMEM = pl.BlockSpec(memory_space=pltpu.SMEM)
VMEM = pl.BlockSpec(memory_space=pltpu.VMEM)


def tiled(field):
    *lead, rows, lon = field.shape
    field = field.reshape(*lead, rows, lon // LANES, LANES)
    return jnp.swapaxes(field, -3, -2).reshape(*lead, rows * lon // LANES, LANES)


def untiled(field, rows):
    *lead, count, lanes = field.shape
    field = field.reshape(*lead, count // rows, rows, lanes)
    return jnp.swapaxes(field, -3, -2).reshape(*lead, rows, count // rows * lanes)


def params(limit, **more):
    return pltpu.CompilerParams(vmem_limit_bytes=limit * MIB, **more)


def halves(x):
    high = x.astype(bf16)
    return high, (x - high.astype(f32)).astype(bf16)


def in_hbm(x):
    return pltpu.with_memory_space_constraint(x, pltpu.HBM)


def spread(row, dtype):
    return jnp.broadcast_to(row, (16, row.shape[1])).astype(dtype)


def matches(index, count):
    ids = lax.broadcasted_iota(jnp.int32, (count, index.shape[1]), 0).astype(jnp.int16)
    return ids.reshape(count // 16, 16, index.shape[1]) == spread(index, jnp.int16)[None]


def placed_at(index, count, amount=None):
    where = matches(index, count)
    amount = bf16(1) if amount is None else spread(amount, bf16)[None]
    return jnp.where(where, amount, bf16(0)).reshape(count, index.shape[1])


def product_nt(left, right):
    return lax.dot_general(left, right, (((1,), (1,)), ((), ())), preferred_element_type=f32)


def over(x, size):
    if size & (size - 1):
        return lax.div(x, jnp.int32(size)), lax.rem(x, jnp.int32(size))
    return lax.shift_right_logical(x, jnp.int32(size.bit_length() - 1)), x & (size - 1)


def prepare_kernel(lev_share, rows, root_ref, count_ref, static_ref, north_ref, east_ref, index_ref, out_ref, row_ref, lane_ref):
    levels, per_level, _ = static_ref.shape
    first = lax.axis_index("ens") * lev_share
    for j in range(lev_share):
        total = root_ref[first + j, 0] * static_ref[0]
        for m in range(1, levels):
            total = total + root_ref[first + j, m] * static_ref[m]
        out_ref[j] = total
    out_ref[lev_share] = north_ref[...]
    out_ref[lev_share + 1] = east_ref[...]
    lists, capacity = index_ref.shape
    lon = per_level // rows * LANES
    pieces = capacity // LANES
    slot = lax.broadcasted_iota(jnp.int32, (1, capacity), 1)
    for q in range(lists):
        cell = index_ref[q : q + 1, :]
        rest, lane = over(cell, LANES)
        rest, block = over(rest, lon // LANES)
        level, row = over(rest, rows)
        grid_row = jnp.where(slot < count_ref[q], level * per_level + block * rows + row, -1)
        for c in range(pieces):
            at = q * pieces + c
            row_ref[at : at + 1, :] = grid_row[:, c * LANES : (c + 1) * LANES]
            lane_ref[at : at + 1, :] = lane[:, c * LANES : (c + 1) * LANES]


def level_product(matrix, transpose):
    levels = matrix.shape[0]
    size = levels * 16
    pick = lax.broadcasted_iota(jnp.int32, (size, levels), 0) // 16
    pick = jnp.where(pick == lax.broadcasted_iota(jnp.int32, (size, levels), 1), f32(1), f32(0)).astype(bf16)
    same = (
        lax.broadcasted_iota(jnp.int32, (size, size), 0) % 16 == lax.broadcasted_iota(jnp.int32, (size, size), 1) % 16
    )
    out = []
    for half in halves(matrix):
        if transpose:
            wide = product_nt(pick, half)
        else:
            wide = jnp.dot(pick, half, preferred_element_type=f32)
        wide = product_nt(wide.astype(bf16), pick)
        out.append(jnp.where(same, wide, f32(0)).astype(bf16))
    return jnp.concatenate([out[0], out[0], out[1]], axis=1)


def three_terms(x):
    high, low = halves(x)
    return jnp.concatenate([high, low, high], axis=0)


def slots_kernel(n_cols, cap_rows, scale, *refs):
    sources, (out_ref, *kept), matrices, (acc_ref, fold_ref, *landed), sems = (
        refs[:8],
        refs[8:12],
        refs[12:15],
        refs[15:22],
        refs[22],
    )
    coarse = acc_ref.shape[0]
    obs_rows = landed[0].shape[0]
    group = min(8, obs_rows)
    first = pl.multiple_of(lax.axis_index("ens") * obs_rows, obs_rows)
    copies = [
        pltpu.make_async_copy(sources[i].at[pl.ds(first, obs_rows), :], landed[i], sems.at[i]) for i in range(3)
    ]
    copies += [pltpu.make_async_copy(sources[3 + i], landed[3 + i], sems.at[3 + i]) for i in range(2)]
    copies += [pltpu.make_async_copy(sources[5 + i], kept[i], sems.at[5 + i]) for i in range(3)]
    for copy in copies:
        copy.start()
    acc_ref[...] = jnp.zeros_like(acc_ref)
    for copy in copies[:5]:
        copy.wait()
    slot_ref, weight_ref, innov_ref, local_ref, root_ref = landed

    def step(i, carry):
        at = pl.ds(pl.multiple_of(i * group, group), group)
        slot = slot_ref[at, :]
        weight = weight_ref[at, :]
        amount = weight * innov_ref[at, :]
        upper, lower = over(slot, FINE)
        terms = [t.astype(f32) for t in halves(weight) + halves(amount)]
        left, right = [], []
        for r in range(group):
            left.append(placed_at(upper[r : r + 1, :], coarse))
            mask = matches(lower[r : r + 1, :], FINE)
            right.append(
                jnp.concatenate(
                    [
                        jnp.where(mask, spread(t[r : r + 1, :], bf16)[None], bf16(0)).reshape(FINE, LANES)
                        for t in terms
                    ],
                    axis=0,
                )
            )
        acc_ref[...] += product_nt(jnp.concatenate(left, axis=1), jnp.concatenate(right, axis=1))
        return carry

    lax.fori_loop(0, obs_rows // group, step, 0)
    acc = acc_ref[...]
    fold_ref[...] = acc + pltpu.roll(acc, LANES - FINE, 1)
    per_row = LANES // FINE
    lane = lax.broadcasted_iota(jnp.int32, (coarse // per_row, LANES), 1)
    weights = jnp.zeros((coarse // per_row, LANES), f32)
    amounts = jnp.zeros((coarse // per_row, LANES), f32)
    for c in range(per_row):
        piece = fold_ref[pl.ds(c, coarse // per_row, stride=per_row), :]
        here = lane // FINE == c
        weights = jnp.where(here, pltpu.roll(piece, c * FINE, 1) if c else piece, weights)
        shift = (c * FINE - 2 * FINE) % LANES
        amounts = jnp.where(here, pltpu.roll(piece, shift, 1) if shift else piece, amounts)
    for p in range(n_cols):
        out_ref[p, 0] = weights[p * cap_rows : (p + 1) * cap_rows]
        out_ref[p, 1] = amounts[p * cap_rows : (p + 1) * cap_rows]
    matrices[0][...] = level_product(local_ref[...] * f32(scale), False)
    matrices[1][...] = level_product(local_ref[...] * f32(scale), True)
    matrices[2][...] = level_product(root_ref[...], True)
    for copy in copies[5:]:
        copy.wait()


def forward_kernel(matrix_ref, control_ref, pert_ref, out_ref):
    members, levels, per_level, _ = control_ref.shape
    pair = 2 - members % 2

    def chunk(j, carry):
        at = pl.ds(pl.multiple_of(j * 16, 16), 16)
        total = None
        for k in range(0, members, pair):
            terms = [three_terms(control_ref[k + i, :, at, :].reshape(levels * 16, LANES)) for i in range(pair)]
            local = jnp.dot(matrix_ref[...], jnp.concatenate(terms, axis=1), preferred_element_type=f32)
            for i in range(pair):
                pert = pert_ref[k + i, :, at, :].astype(f32).reshape(levels * 16, LANES)
                part = pert * local[:, i * LANES : (i + 1) * LANES]
                total = part if total is None else total + part
        out_ref[:, at, :] = total.reshape(levels, 16, LANES)
        return carry

    lax.fori_loop(0, per_level // 16, chunk, 0)


def member_kernel(matrix_ref, adjoint_ref, control_ref, pert_ref, out_ref):
    pair, levels, per_level, _ = out_ref.shape
    first = pl.program_id(0) * pair

    def chunk(j, carry):
        at = pl.ds(pl.multiple_of(j * 16, 16), 16)
        adjoint = adjoint_ref[:, at, :].reshape(levels * 16, LANES)
        terms = [
            three_terms(pert_ref[first + i, :, at, :].astype(f32).reshape(levels * 16, LANES) * adjoint)
            for i in range(pair)
        ]
        change = jnp.dot(matrix_ref[...], jnp.concatenate(terms, axis=1), preferred_element_type=f32)
        for i in range(pair):
            out_ref[i, :, at, :] = control_ref[first + i, :, at, :] + change[:, i * LANES : (i + 1) * LANES].reshape(
                levels, 16, LANES
            )
        return carry

    lax.fori_loop(0, per_level // 16, chunk, 0)


def eastern(x):
    lane = lax.broadcasted_iota(jnp.int32, x.shape, 1)
    near = pltpu.roll(x, LANES - 1, 1)
    return jnp.where(lane == LANES - 1, pltpu.roll(near, x.shape[0] - 1, 0), near)


def western(x):
    lane = lax.broadcasted_iota(jnp.int32, x.shape, 1)
    near = pltpu.roll(x, 1, 1)
    return jnp.where(lane == 0, pltpu.roll(near, 1, 0), near)


def diffuse_rows(tiles, level, coef_ref, rows):
    blocks = tiles[0].shape[1] // rows
    field = [t[level, pl.ds(r, blocks, stride=rows), :] for t in tiles for r in range(rows)]
    for step in range(NDIFF):
        field = [
            coef_ref[0, i + step] * field[i]
            + coef_ref[1, i + step] * field[i - 1]
            + coef_ref[2, i + step] * field[i + 1]
            + coef_ref[3, i + step] * eastern(field[i])
            + coef_ref[4, i + step] * western(field[i])
            for i in range(1, len(field) - 1)
        ]
        field = list(field)
    return field


def tiles_of(before_ref, own_ref, after_ref, other_ref):
    odd = lax.axis_index("cols") % 2
    return [before_ref, other_ref.at[1 - odd], own_ref, other_ref.at[2 * odd], after_ref]


def first_diffusion_kernel(lev_share, rows, before_ref, own_ref, after_ref, other_ref, out_ref, coef_ref):
    tiles = tiles_of(before_ref, own_ref, after_ref, other_ref)
    blocks = own_ref.shape[1] // rows
    side = len(tiles) // 2
    north = [t[lev_share, pl.ds(r, blocks, stride=rows), :] for t in tiles for r in range(rows)]
    east = [t[lev_share + 1, pl.ds(r, blocks, stride=rows), :] for t in tiles for r in range(rows)]
    for i in range(1, len(north) - 1):
        south = north[i + 1]
        if (i + 1) % rows == 0 and i < side * rows:
            south = south * jnp.where(lax.axis_index("cols") == side - (i + 1) // rows, f32(0), f32(1))
        west = western(east[i])
        coef_ref[0, i] = 1.0 - north[i] - south - east[i] - west
        coef_ref[1, i] = north[i]
        coef_ref[2, i] = south
        coef_ref[3, i] = east[i]
        coef_ref[4, i] = west
    for i in (0, len(north) - 1):
        for c in range(5):
            coef_ref[c, i] = jnp.zeros_like(north[0])

    def body(level, carry):
        final = diffuse_rows(tiles, level, coef_ref, rows)
        for r in range(rows):
            out_ref[level, pl.ds(r, blocks, stride=rows), :] = final[r]
        return carry

    lax.fori_loop(0, lev_share, body, 0)


def second_diffusion_kernel(rows, coef_ref, before_ref, own_ref, after_ref, other_ref, out_ref):
    tiles = tiles_of(before_ref, own_ref, after_ref, other_ref)
    copies, lev_share = out_ref.shape[:2]
    blocks = own_ref.shape[1] // rows

    def body(level, carry):
        final = diffuse_rows(tiles, level, coef_ref, rows)
        for copy in range(copies):
            for r in range(rows):
                out_ref[copy, level, pl.ds(r, blocks, stride=rows), :] = final[r]
        return carry

    lax.fori_loop(0, lev_share, body, 0)


def lookup_kernel(part_ref, static_ref, row_ref, lane_ref, slots_ref, out_ref, terms_ref):
    copies = out_ref.shape[0]
    cells = part_ref.shape[0]
    own = static_ref.shape[0]
    n_lists, _, cap_rows, _ = slots_ref.shape
    at = pl.ds(pl.multiple_of(lax.axis_index("ens") * own, own), own)
    for here, field in ((slice(None), part_ref[...]), (at, part_ref[at, :] + static_ref[...])):
        high, low = halves(field)
        terms_ref[here, :LANES] = high
        terms_ref[here, LANES:] = low
    ids16 = lax.broadcasted_iota(jnp.int32, (LANES, cells), 1).astype(jnp.int16)
    ids = lax.broadcasted_iota(jnp.int32, (LANES, LANES), 1)
    diagonal = ids == lax.broadcasted_iota(jnp.int32, (LANES, LANES), 0)

    def look(q, carry):
        at = pl.ds(pl.multiple_of(q * cap_rows, cap_rows), cap_rows)
        rows = row_ref[at, :].astype(f32).T
        lanes = lane_ref[at, :].astype(f32).T
        picks = []
        for c in range(cap_rows):
            column = jnp.broadcast_to(rows[:, c : c + 1], (LANES, LANES)).astype(jnp.int32).astype(jnp.int16)
            column = jnp.concatenate([column] * (cells // LANES), axis=1)
            picks.append(jnp.where(ids16 == column, bf16(1), bf16(0)))
        got = jnp.dot(jnp.concatenate(picks, axis=0), terms_ref[...], preferred_element_type=f32)
        values = []
        for c in range(cap_rows):
            mask = ids == jnp.broadcast_to(lanes[:, c : c + 1], (LANES, LANES)).astype(jnp.int32)
            mine = got[c * LANES : (c + 1) * LANES]
            found = jnp.sum(jnp.where(mask, mine[:, :LANES] + mine[:, LANES:], f32(0)), axis=1, keepdims=True)
            values.append(jnp.sum(jnp.where(diagonal, found, f32(0)), axis=0, keepdims=True))
        values = jnp.concatenate(values, axis=0)
        for copy in range(copies):
            out_ref[copy, 0, at, :] = values
            out_ref[copy, 1, at, :] = slots_ref[q, 0]
            out_ref[copy, 2, at, :] = slots_ref[q, 1]
        return carry

    lax.fori_loop(0, n_lists, look, 0)


def put(acc_ref, rows, lanes, amounts):
    high, low = (h.astype(f32) for h in halves(amounts))
    left, right = [], []
    for c in range(rows.shape[0]):
        piece = slice(c, c + 1)
        left.append(placed_at(rows[piece, :], acc_ref.shape[0]))
        mask = matches(lanes[piece, :], LANES)
        right.append(
            jnp.concatenate(
                [
                    jnp.where(mask, spread(h[piece, :], bf16)[None], bf16(0)).reshape(LANES, LANES)
                    for h in (high, low)
                ],
                axis=0,
            )
        )
    acc_ref[...] += product_nt(jnp.concatenate(left, axis=1), jnp.concatenate(right, axis=1))


def amounts_of(shares_ref, at):
    value, weight, amount = (
        functools.reduce(jnp.add, [shares_ref[e, t, at, :] for e in range(shares_ref.shape[0])]) for t in range(3)
    )
    return value * weight - amount


def scatter_own_kernel(cap_rows, row_ref, lane_ref, shares_ref, out_ref, amount_ref, acc_ref):
    own = out_ref.shape[0]
    first = lax.axis_index("ens") * own
    acc_ref[...] = jnp.zeros_like(acc_ref)

    def step(q, carry):
        at = pl.ds(pl.multiple_of(q * cap_rows, cap_rows), cap_rows)
        amounts = amounts_of(shares_ref, at)
        amount_ref[at, :] = amounts
        put(acc_ref, row_ref[at, :] - first, lane_ref[at, :], amounts)
        return carry

    lax.fori_loop(0, row_ref.shape[0] // cap_rows, step, 0)
    out_ref[...] = acc_ref[:, :LANES] + acc_ref[:, LANES:]


def scatter_rest_kernel(cap_rows, row_ref, lane_ref, amount_ref, own_ref, out_ref, acc_ref):
    cells = out_ref.shape[0]
    own = own_ref.shape[0]
    n_ens = cells // own
    me = lax.axis_index("ens")
    first = (me + 1) * own
    acc_ref[...] = jnp.zeros_like(acc_ref)

    def step(q, carry):
        at = pl.ds(pl.multiple_of(q * cap_rows, cap_rows), cap_rows)
        row = row_ref[at, :]
        turned = row - first
        turned = jnp.where(row < 0, -1, jnp.where(turned < 0, turned + cells, turned))
        put(acc_ref, turned, lane_ref[at, :], amount_ref[at, :])
        return carry

    lax.fori_loop(0, row_ref.shape[0] // cap_rows, step, 0)
    out_ref[pl.ds(pl.multiple_of(me * own, own), own), :] = own_ref[...]
    for t in range(1, n_ens):
        to = pl.ds(pl.multiple_of((me + t) % n_ens * own, own), own)
        piece = acc_ref[(t - 1) * own : t * own, :]
        out_ref[to, :] = piece[:, :LANES] + piece[:, LANES:]


def static_kernel(matrix_ref, static_ref, smooth_ref, out_ref):
    levels, per_level, _ = static_ref.shape
    for j in range(0, per_level, 32):
        terms = [
            three_terms(smooth_ref[:, j + i : j + i + 16, :].reshape(levels * 16, LANES)) for i in (0, 16)
        ]
        change = jnp.dot(matrix_ref[...], jnp.concatenate(terms, axis=1), preferred_element_type=f32)
        for i, part in ((0, change[:, :LANES]), (16, change[:, LANES:])):
            at = slice(j + i, j + i + 16)
            out_ref[:, at, :] = static_ref[:, at, :] + part.reshape(levels, 16, LANES)


def shifted(x, by):
    count = lax.axis_size("cols")
    return lax.ppermute(x, "cols", [(i, i + by) for i in range(count) if 0 <= i + by < count])


def swapped(x):
    count = lax.axis_size("cols")
    return lax.ppermute(x, "cols", [(i, i ^ 1) for i in range(count)])


def local(
    static_control,
    ensemble_control,
    perturbations,
    vertical_root,
    vertical_local,
    face_north,
    face_east,
    innovation,
    obs_weight,
    obs_slot,
    send_index,
    send_count,
):
    n_ens = lax.axis_size("ens")
    n_cols = lax.axis_size("cols")
    members, levels, rows, lon = ensemble_control.shape
    per_level = rows * lon // LANES
    cells = levels * per_level
    lev_share = levels // n_ens
    own = lev_share * per_level
    lists, capacity = send_index.shape
    cap_rows = capacity // LANES
    entry_rows = lists * cap_rows
    member_scale = 1.0 / math.sqrt(members * n_ens - 1)

    static = in_hbm(tiled(static_control))
    control = in_hbm(tiled(ensemble_control))
    pert = in_hbm(tiled(perturbations))

    def whole(*shape):
        return pl.BlockSpec(shape, lambda i: (0,) * len(shape))

    packed, entry_row, entry_lane = pl.pallas_call(
        functools.partial(prepare_kernel, lev_share, rows),
        grid=(1,),
        in_specs=[
            SMEM,
            SMEM,
            whole(levels, per_level, LANES),
            whole(per_level, LANES),
            whole(per_level, LANES),
            whole(lists, capacity),
        ],
        out_specs=[VMEM] * 3,
        out_shape=[
            pltpu.VMEM((lev_share + 2, per_level, LANES), f32),
            pltpu.VMEM((entry_rows, LANES), jnp.int32),
            pltpu.VMEM((entry_rows, LANES), jnp.int32),
        ],
        compiler_params=params(8),
        name="prepare",
    )(
        in_hbm(vertical_root),
        in_hbm(send_count),
        static,
        in_hbm(tiled(face_north)),
        in_hbm(tiled(face_east)),
        in_hbm(send_index),
    )
    before, after = shifted(packed, 2), shifted(packed, -2)

    obs_rows = obs_slot.shape[0] // LANES
    share_rows = obs_rows // n_ens
    coarse = n_cols * capacity // FINE
    size = levels * 16
    obs_slot, packed = lax.optimization_barrier((obs_slot, packed))
    slots, static_here, control_here, pert_here, to_local, from_local, from_root = pl.pallas_call(
        functools.partial(slots_kernel, n_cols, cap_rows, member_scale),
        in_specs=[pl.BlockSpec(memory_space=pl.ANY)] * 8,
        out_specs=[VMEM] * 7,
        out_shape=[
            pltpu.VMEM((n_cols, 2, cap_rows, LANES), f32),
            pltpu.VMEM(static.shape, f32),
            pltpu.VMEM(control.shape, f32),
            pltpu.VMEM(pert.shape, bf16),
        ]
        + [pltpu.VMEM((size, 3 * size), bf16)] * 3,
        scratch_shapes=[
            pltpu.VMEM((coarse, LANES), f32),
            pltpu.VMEM((coarse, LANES), f32),
            pltpu.VMEM((share_rows, LANES), jnp.int32),
            pltpu.VMEM((share_rows, LANES), f32),
            pltpu.VMEM((share_rows, LANES), f32),
            pltpu.VMEM((levels, levels), f32),
            pltpu.VMEM((levels, levels), f32),
            pltpu.SemaphoreType.DMA((8,)),
        ],
        compiler_params=params(16),
        name="slot_sums",
    )(
        in_hbm(obs_slot.reshape(obs_rows, LANES)),
        in_hbm(obs_weight.reshape(obs_rows, LANES)),
        in_hbm(innovation.reshape(obs_rows, LANES)),
        in_hbm(vertical_local),
        in_hbm(vertical_root),
        static,
        control,
        pert,
    )
    before, after, slots = lax.optimization_barrier((before, after, slots))
    other = swapped(jnp.stack([packed, before, after]))
    slots = lax.all_to_all(slots, "cols", split_axis=0, concat_axis=0, tiled=True)

    part = pl.pallas_call(
        forward_kernel,
        in_specs=[VMEM] * 3,
        out_specs=VMEM,
        out_shape=pltpu.VMEM((levels, per_level, LANES), f32),
        compiler_params=params(8),
        name="members_forward",
    )(to_local, control_here, pert_here)

    increment, coefs = pl.pallas_call(
        functools.partial(first_diffusion_kernel, lev_share, rows),
        in_specs=[VMEM] * 4,
        out_specs=[VMEM] * 2,
        out_shape=[
            pltpu.VMEM((lev_share, per_level, LANES), f32),
            pltpu.VMEM((5, 5 * rows, per_level // rows, LANES), f32),
        ],
        compiler_params=params(8),
        name="diffuse_forward",
    )(before, packed, after, other)

    shares = pl.pallas_call(
        lookup_kernel,
        in_specs=[VMEM] * 5,
        out_specs=VMEM,
        out_shape=pltpu.VMEM((n_ens, 3, entry_rows, LANES), f32),
        scratch_shapes=[pltpu.VMEM((cells, 2 * LANES), bf16)],
        compiler_params=params(16),
        name="lookup",
    )(part.reshape(cells, LANES), increment.reshape(own, LANES), entry_row, entry_lane, slots)
    shares = lax.all_to_all(shares, "ens", split_axis=0, concat_axis=0, tiled=True)

    adjoint_own, amounts = pl.pallas_call(
        functools.partial(scatter_own_kernel, cap_rows),
        in_specs=[VMEM] * 3,
        out_specs=[VMEM] * 2,
        out_shape=[pltpu.VMEM((own, LANES), f32), pltpu.VMEM((entry_rows, LANES), f32)],
        scratch_shapes=[pltpu.VMEM((own, 2 * LANES), f32)],
        compiler_params=params(16),
        name="scatter_own",
    )(entry_row, entry_lane, shares)
    tile = adjoint_own.reshape(lev_share, per_level, LANES)
    tile_before, tile_after = shifted(tile, 2), shifted(tile, -2)

    adjoint = pl.pallas_call(
        functools.partial(scatter_rest_kernel, cap_rows),
        in_specs=[VMEM] * 4,
        out_specs=VMEM,
        out_shape=pltpu.VMEM((cells, LANES), f32),
        scratch_shapes=[pltpu.VMEM((cells - own, 2 * LANES), f32)],
        compiler_params=params(16),
        name="scatter_rest",
    )(entry_row, entry_lane, amounts, adjoint_own)
    tile_before, tile_after, adjoint = lax.optimization_barrier((tile_before, tile_after, adjoint))
    tile_other = swapped(jnp.stack([tile, tile_before, tile_after]))

    smooth = pl.pallas_call(
        functools.partial(second_diffusion_kernel, rows),
        in_specs=[VMEM] * 5,
        out_specs=VMEM,
        out_shape=pltpu.VMEM((n_ens, lev_share, per_level, LANES), f32),
        compiler_params=params(8),
        name="diffuse_adjoint",
    )(coefs, tile_before, tile, tile_after, tile_other)
    smooth, adjoint = lax.optimization_barrier((smooth, adjoint))
    smooth = lax.all_to_all(smooth, "ens", split_axis=0, concat_axis=0, tiled=True)

    pair = 2 - members % 2
    ensemble_grad = pl.pallas_call(
        member_kernel,
        grid=(members // pair,),
        in_specs=[VMEM] * 4,
        out_specs=pl.BlockSpec((pair, levels, per_level, LANES), lambda k: (k, 0, 0, 0)),
        out_shape=jax.ShapeDtypeStruct((members, levels, per_level, LANES), f32),
        compiler_params=params(16),
        name="members_gradient",
    )(from_local, adjoint.reshape(levels, per_level, LANES), control_here, pert_here)

    static_grad = pl.pallas_call(
        static_kernel,
        grid=(1,),
        in_specs=[VMEM] * 3,
        out_specs=whole(levels, per_level, LANES),
        out_shape=jax.ShapeDtypeStruct((levels, per_level, LANES), f32),
        compiler_params=params(8),
        name="static_gradient",
    )(from_root, static_here, smooth.reshape(levels, per_level, LANES))
    return (untiled(static_grad, rows), untiled(ensemble_grad, rows))


def solution(mesh):
    placed = (
        P(None, "cols", None),
        P("ens", None, "cols", None),
        P("ens", None, "cols", None),
        P(),
        P(),
        P("cols", None),
        P("cols", None),
        P("cols"),
        P("cols"),
        P("cols"),
        P("cols", None),
        P("cols"),
    )
    return jax.shard_map(
        local,
        mesh=mesh,
        in_specs=placed,
        out_specs=(P(None, "cols", None), P("ens", None, "cols", None)),
        check_vma=False,
    )
```

time: 101 us -> 89.7 us (0.89)
  Pallas kernels: 61.2 us -> 36.9 us
  local copies, waits for them, and re-layouts: 0 us -> 16 us
  starting transfers between devices: 33.8 us -> 20.7 us
  blocking collectives: 0 us -> 11.3 us
  waiting for transfers between devices: 3.86 us -> 2.29 us
    pallas_call x7 -> x8, Pallas kernels: 57.9 us -> 34.1 us  [the longest x1 8.46 us: local(): pl.pallas_call(lookup_kernel, in_specs=[VMEM] * 5, out_specs=VMEM, out_sh...]
    unnamed x0 -> x44, local copies, waits for them, and re-layouts: none -> 16 us
    all_to_all x0 -> x1, blocking collectives: none -> 11.3 us  [local(): lax.all_to_all(shares, 'ens', split_axis=0, concat_axis=0, tiled=True)]
    ppermute x8 -> x4, starting transfers between devices: 21.4 us -> 11.1 us  [shifted(): lax.ppermute(x, 'cols', [(i, i + by) for i in range(count) if 0 <= i + by...]
    ppermute x3 -> x2, starting transfers between devices: 4.45 us -> 0.07 us  [swapped(): return lax.ppermute(x, 'cols', [(i, i ^ 1) for i in range(count)])]
    ppermute x3 -> x2, waiting for transfers between devices: 3.83 us -> 1.71 us  [swapped(): return lax.ppermute(x, 'cols', [(i, i ^ 1) for i in range(count)])]
    all_to_all x1, starting transfers between devices: 4.56 us -> 6.06 us  [local(): lax.all_to_all(slots, 'cols', split_axis=0, concat_axis=0, tiled=True)]
  transfers between devices with their start and end apart: 13 -> 8, of which waited for: 3 -> 2; matrix products, arithmetic and copies ran while one was open for 0% -> 0% of each run, Pallas kernels for 27% -> 24%
where the time goes in v2:
time: 89.7 us; the launch traced here: 89 us
  Pallas kernels  36.9 us (41%)
  starting transfers between devices  20.7 us (23%)
  local copies, waits for them, and re-layouts  16 us (18%)
  blocking collectives  11.3 us (13%)
  waiting for transfers between devices  2.29 us (3%)
  other arithmetic  0.98 us (1%)
    unnamed x44, local copies, waits for them, and re-layouts  16 us
    all_to_all x1, blocking collectives, local(): lax.all_to_all(shares, 'ens', split_axis=0, concat_axis=0, tiled=True)  11.3 us
    ppermute x4, starting transfers between devices, shifted(): lax.ppermute(x, 'cols', [(i, i + by) for i in range(count) if 0 <= i + by...  11.1 us
    pallas_call x1, Pallas kernels, local(): pl.pallas_call(lookup_kernel, in_specs=[VMEM] * 5, out_specs=VMEM, out_sh...  8.46 us
    pallas_call x1, Pallas kernels, local(): pl.pallas_call(functools.partial(slots_kernel, n_cols, cap_rows, member_s...  7.3 us
    all_to_all x1, starting transfers between devices, local(): lax.all_to_all(slots, 'cols', split_axis=0, concat_axis=0, tiled=True)  6.06 us
    pallas_call x1, Pallas kernels, local(): pl.pallas_call(member_kernel, grid=(members // pair,), in_specs=[VMEM] *...  5.58 us
    pallas_call x1, Pallas kernels, local(): pl.pallas_call(functools.partial(scatter_rest_kernel, cap_rows), in_specs...  4.98 us
  transfers between devices with their start and end apart: 8, of which 2 were waited for; matrix products, arithmetic and copies ran while one was open for 0% of the time, Pallas kernels for 24%

profile of v2, /device:TPU:0, one launch (start us, length us, event | category | flops | bytes accessed | tf_op | source)
XLA Modules:
  0.0 89.0 jit_solution(10119403689502974360)
XLA Ops:
  0.6 1.3 %prepare.1 = (f32[6,64,128]{2,1,0:T(8,128)S(1)}, s32[64,128]{1,0:T(8,128)S(1)}, s32[64,128]{1,0:T(8,128)S(1)}) custom-call(f32[16,16]{1,0:T(8,128)} %refs_4_.1, s32[8]{0:T(128)} %count_ref.1, f32[16,64,128]{2,1,0:T(8,128)} %bitcast.65, f32[64,128]{1,0:T(8,128)} %bitcast.71, f32[64,128]{1,0:T(8,128)} %bitcast.72, s32[8,1024]{1,0:T(8,128)} %index_ref.1), custom_call_target="tpu_custom_call" | custom-call | tf_op jit(solution)/shard_map/prepare/pallas_call | solution.py:471
  2.0 4.9 %collective-permute-start = (f32[6,64,128]{2,1,0:T(8,128)S(1)}, f32[6,64,128]{2,1,0:T(8,128)S(1)}, u32[]{:S(2)}, u32[]{:S(2)}) collective-permute-start(f32[6,64,128]{2,1,0:T(8,128)S(1)} %get-tuple-element.32.own_ref), channel_id=1, source_target_pairs={{0,2},{1,3},{2,4},{3,5},{4,6},{5,7},{8,10},{9,11},{10,12},{11,13},... | collective-permute-start | bytes 589832 | tf_op jit(solution)/shard_map/ppermute | solution.py:430
  6.9 1.3 %collective-permute-start.1 = (f32[6,64,128]{2,1,0:T(8,128)S(1)}, f32[6,64,128]{2,1,0:T(8,128)S(1)}, u32[]{:S(2)}, u32[]{:S(2)}) collective-permute-start(f32[6,64,128]{2,1,0:T(8,128)S(1)} %get-tuple-element.32.own_ref), channel_id=1, source_target_pairs={{2,0},{3,1},{4,2},{5,3},{6,4},{7,5},{10,8},{11,9},{12,10},{13,11},... | collective-permute-start | bytes 589832 | tf_op jit(solution)/shard_map/ppermute | solution.py:430
  8.2 7.3 %slot_sums.1 = (f32[8,2,8,128]{3,2,1,0:T(8,128)}, f32[16,64,128]{2,1,0:T(8,128)S(1)}, f32[8,16,64,128]{3,2,1,0:T(8,128)S(1)}, bf16[8,16,64,128]{3,2,1,0:T(8,128)...) custom-call(s32[512,128]{1,0:T(8,128)} %bitcast.68, ...), custom_call_target="tpu_custom_call" | custom-call | tf_op jit(solution)/shard_map/slot_sums/pallas_call | solution.py:505
  15.5 2.0 %copy-done = f32[8,16,64,128]{3,2,1,0:T(8,128)} copy-done((f32[8,16,64,128]{3,2,1,0:T(8,128)}, f32[8,16,64,128]{3,2,1,0:T(8,128)S(1)}, u32[]{:S(2)}) %copy-start) | copy-done | bytes 4194328
  17.5 0.8 copy-done.16
  18.3 0.8 copy-done.18
  19.1 1.0 %pad_maximum_fusion = f32[3,6,64,128]{3,2,1,0:T(8,128)} fusion(f32[1,6,64,128]{3,2,1,0:T(8,128)S(1)} %bitcast.58, f32[1,6,64,128]{3,2,1,0:T(8,128)S(1)} %bitcast.57, f32[1,6,64,128]{3,2,1,0:T(8,128)S(1)} %bitcast.56), kind=kLoop, calls=%fused_computation | loop fusion | flops 294912 | bytes 1179648 | tf_op jit(solution)/shard_map/stack | solution.py:539
  20.2 0.7 copy-done.6
  20.9 6.1 %all-to-all-start = ((f32[8,2,8,128]{3,2,1,0:T(8,128)}), f32[8,2,8,128]{3,2,1,0:T(8,128)}, u32[]{:S(2)}, u32[]{:S(2)}) async-start(f32[8,2,8,128]{3,2,1,0:T(8,128)} %get-tuple-element.41), calls=%async_computation | async-start | bytes 131072 | tf_op jit(solution)/shard_map/all_to_all | solution.py:540
  27.0 2.2 %copy-done.1 = f32[8,16,64,128]{3,2,1,0:T(8,128)S(1)} copy-done((f32[8,16,64,128]{3,2,1,0:T(8,128)S(1)}, f32[8,16,64,128]{3,2,1,0:T(8,128)}, u32[]{:S(2)}) %copy-start.1) | copy-done | bytes 4194328
  29.2 1.0 %copy-done.17 = bf16[256,768]{1,0:T(8,128)(2,1)S(1)} copy-done((bf16[256,768]{1,0:T(8,128)(2,1)S(1)}, bf16[256,768]{1,0:T(8,128)(2,1)}, u32[]{:S(2)}) %copy-start.17) | copy-done | bytes 393240
  30.2 2.4 %members_forward.1 = f32[16,64,128]{2,1,0:T(8,128)S(1)} custom-call(bf16[256,768]{1,0:T(8,128)(2,1)S(1)} %copy-done.17, f32[8,16,64,128]{3,2,1,0:T(8,128)S(1)} %copy-done.1, bf16[8,16,64,128]{3,2,1,0:T(8,128)(2,1)S(1)} %get-tuple-element.39.pert_ref), custom_call_target="tpu_custom_call" | custom-call | tf_op jit(solution)/shard_map/members_forward/pallas_call | solution.py:542
  32.6 0.8 copy-done.10
  33.4 1.1 %copy-done.11 = f32[3,6,64,128]{3,2,1,0:T(8,128)S(1)} copy-done((f32[3,6,64,128]{3,2,1,0:T(8,128)S(1)}, f32[3,6,64,128]{3,2,1,0:T(8,128)}, u32[]{:S(2)}) %copy-start.11) | copy-done | bytes 589848
  34.5 1.5 %diffuse_forward.1 = (f32[4,64,128]{2,1,0:T(8,128)S(1)}, f32[5,10,32,128]{3,2,1,0:T(8,128)S(1)}) custom-call(f32[6,64,128]{2,1,0:T(8,128)S(1)} %copy-done.7, f32[6,64,128]{2,1,0:T(8,128)S(1)} %copy-done.5, f32[6,64,128]{2,1,0:T(8,128)S(1)} %copy-done.9, f32[3,6,64,128]{3,2,1,0:T(8,128)S(1)} %copy-done.11), custom_call_target="tpu_custom_call" | custom-call | tf_op jit(solution)/shard_map/diffuse_forward/pallas_call | solution.py:551
  36.6 0.9 %copy-done.21 = f32[4,64,128]{2,1,0:T(8,128)S(1)} copy-done((f32[4,64,128]{2,1,0:T(8,128)S(1)}, f32[4,64,128]{2,1,0:T(8,128)}, u32[]{:S(2)}) %copy-start.21) | copy-done | bytes 131096
  37.5 8.5 %lookup.1 = f32[4,3,64,128]{3,2,1,0:T(8,128)S(1)} custom-call(f32[1024,128]{1,0:T(8,128)S(1)} %bitcast.50, f32[256,128]{1,0:T(8,128)S(1)} %bitcast.61, s32[64,128]{1,0:T(8,128)S(1)} %get-tuple-element.35.row_ref, s32[64,128]{1,0:T(8,128)S(1)} %get-tuple-element.36.lane_ref, f32[8,2,8,128]{3,2,1,0:T(8,128)} %all-to-all-done.slots_ref), custom_call_target="tpu_custom_call" | custom-call | tf_op jit(solution)/shard_map/lookup/pallas_call | solution.py:563
  46.0 11.3 %all_to_all.15.shares_ref = f32[4,3,64,128]{3,2,1,0:T(8,128)S(1)} all-to-all(f32[4,3,64,128]{3,2,1,0:T(8,128)S(1)} %lookup.1), channel_id=1, replica_groups=mesh['ens'=4,'cols'=8] {'ens'}, dimensions={0} | all-to-all | bytes 786432 | tf_op jit(solution)/shard_map/all_to_all | solution.py:572
  57.3 2.8 %scatter_own.1 = (f32[256,128]{1,0:T(8,128)S(1)}, f32[64,128]{1,0:T(8,128)S(1)}) custom-call(s32[64,128]{1,0:T(8,128)S(1)} %get-tuple-element.35.row_ref, s32[64,128]{1,0:T(8,128)S(1)} %get-tuple-element.36.lane_ref, f32[4,3,64,128]{3,2,1,0:T(8,128)S(1)} %all_to_all.15.shares_ref), custom_call_target="tpu_custom_call" | custom-call | tf_op jit(solution)/shard_map/scatter_own/pallas_call | solution.py:574
  60.1 3.6 %collective-permute-start.3 = (f32[4,64,128]{2,1,0:T(8,128)S(1)}, f32[4,64,128]{2,1,0:T(8,128)S(1)}, u32[]{:S(2)}, u32[]{:S(2)}) collective-permute-start(f32[4,64,128]{2,1,0:T(8,128)S(1)} %bitcast.52), channel_id=1, source_target_pairs={{0,2},{1,3},{2,4},{3,5},{4,6},{5,7},{8,10},{9,11},{10,12},{11,13},... | collective-permute-start | bytes 393224 | tf_op jit(solution)/shard_map/ppermute | solution.py:430
  63.7 1.3 %collective-permute-start.4 = (f32[4,64,128]{2,1,0:T(8,128)S(1)}, f32[4,64,128]{2,1,0:T(8,128)S(1)}, u32[]{:S(2)}, u32[]{:S(2)}) collective-permute-start(f32[4,64,128]{2,1,0:T(8,128)S(1)} %bitcast.53), channel_id=1, source_target_pairs={{2,0},{3,1},{4,2},{5,3},{6,4},{7,5},{10,8},{11,9},{12,10},{13,11},... | collective-permute-start | bytes 393224 | tf_op jit(solution)/shard_map/ppermute | solution.py:430
  65.0 5.0 %scatter_rest.1 = f32[1024,128]{1,0:T(8,128)S(1)} custom-call(s32[64,128]{1,0:T(8,128)S(1)} %get-tuple-element.35.row_ref, s32[64,128]{1,0:T(8,128)S(1)} %get-tuple-element.36.lane_ref, f32[64,128]{1,0:T(8,128)S(1)} %get-tuple-element.43.amount_ref, f32[256,128]{1,0:T(8,128)S(1)} %get-tuple-element.42.own_ref), custom_call_target="tpu_custom_call" | custom-call | tf_op jit(solution)/shard_map/scatter_rest/pallas_call | solution.py:586
  70.7 1.7 %collective-permute-done.5.other_ref = f32[3,4,64,128]{3,2,1,0:T(8,128)S(1)} collective-permute-done((f32[3,4,64,128]{3,2,1,0:T(8,128)S(1)}, f32[3,4,64,128]{3,2,1,0:T(8,128)S(1)}, u32[]{:S(2)}, u32[]{:S(2)}) %collective-permute-start.5) | collective-permute-done | bytes 393248 | tf_op jit(solution)/shard_map/ppermute | solution.py:435
  72.4 1.4 %diffuse_adjoint.1 = f32[4,4,64,128]{3,2,1,0:T(8,128)S(1)} custom-call(f32[5,10,32,128]{3,2,1,0:T(8,128)S(1)} %get-tuple-element.34.coef_ref, f32[4,64,128]{2,1,0:T(8,128)S(1)} %collective-permute-done.3.before_ref, f32[4,64,128]{2,1,0:T(8,128)S(1)} %bitcast.55, f32[4,64,128]{2,1,0:T(8,128)S(1)} %collective-permute-done.4.after_ref, ...), custom_call_target="tpu_custom_call" | custom-call | tf_op jit(solution)/shard_map/diffuse_adjoint/pallas_call | solution.py:598
  73.8 0.8 copy-done.3
  74.6 3.5 %all-to-all-start.2 = ((f32[4,4,64,128]{3,2,1,0:T(8,128)}), f32[4,4,64,128]{3,2,1,0:T(8,128)S(1)}, u32[]{:S(2)}, u32[]{:S(2)}) async-start(f32[4,4,64,128]{3,2,1,0:T(8,128)} %copy-done.3), calls=%async_computation.2 | async-start | bytes 1048576 | tf_op jit(solution)/shard_map/all_to_all | solution.py:607
  78.1 2.2 %copy-done.2 = f32[8,16,64,128]{3,2,1,0:T(8,128)S(1)} copy-done((f32[8,16,64,128]{3,2,1,0:T(8,128)S(1)}, f32[8,16,64,128]{3,2,1,0:T(8,128)}, u32[]{:S(2)}) %copy-start.2) | copy-done | bytes 4194328
  80.2 1.0 %copy-done.15 = bf16[256,768]{1,0:T(8,128)(2,1)S(1)} copy-done((bf16[256,768]{1,0:T(8,128)(2,1)S(1)}, bf16[256,768]{1,0:T(8,128)(2,1)}, u32[]{:S(2)}) %copy-start.15) | copy-done | bytes 393240
  81.2 5.6 %members_gradient.1 = f32[8,16,64,128]{3,2,1,0:T(8,128)} custom-call(bf16[256,768]{1,0:T(8,128)(2,1)S(1)} %copy-done.15, f32[16,64,128]{2,1,0:T(8,128)S(1)} %bitcast.49, f32[8,16,64,128]{3,2,1,0:T(8,128)S(1)} %copy-done.2, bf16[8,16,64,128]{3,2,1,0:T(8,128)(2,1)S(1)} %get-tuple-element.39.pert_ref), custom_call_target="tpu_custom_call" | custom-call | tf_op jit(solution)/shard_map/members_gradient/pallas_call | solution.py:610
  86.8 1.0 %copy-done.13 = f32[16,64,128]{2,1,0:T(8,128)S(1)} copy-done((f32[16,64,128]{2,1,0:T(8,128)S(1)}, f32[16,64,128]{2,1,0:T(8,128)}, u32[]{:S(2)}) %copy-start.13) | copy-done | bytes 524312
  87.9 1.2 %static_gradient.1 = f32[16,64,128]{2,1,0:T(8,128)} custom-call(bf16[256,768]{1,0:T(8,128)(2,1)S(1)} %copy-done.19, f32[16,64,128]{2,1,0:T(8,128)S(1)} %copy-done.13, f32[16,64,128]{2,1,0:T(8,128)S(1)} %bitcast.51), custom_call_target="tpu_custom_call" | custom-call | tf_op jit(solution)/shard_map/static_gradient/pallas_call | solution.py:620
  (41 shorter events, 1.5 us)
Async XLA Ops:
  1.9 18.1 %copy-start.4 = (f32[6,64,128]{2,1,0:T(8,128)}, f32[6,64,128]{2,1,0:T(8,128)S(1)}, u32[]{:S(2)}) copy-start(f32[6,64,128]{2,1,0:T(8,128)S(1)} %get-tuple-element.32.own_ref) | copy-start | bytes 589828
  2.0 17.1 %collective-permute-start = (f32[6,64,128]{2,1,0:T(8,128)S(1)}, f32[6,64,128]{2,1,0:T(8,128)S(1)}, u32[]{:S(2)}, u32[]{:S(2)}) collective-permute-start(f32[6,64,128]{2,1,0:T(8,128)S(1)} %get-tuple-element.32.own_ref), channel_id=1, source_target_pairs={{0,2},{1,3},{2,4},{3,5},{4,6},{5,7},{8,10},{9,11},{10,12},{11,13},... | collective-permute-start | bytes 589832 | tf_op jit(solution)/shard_map/ppermute | solution.py:430
  6.9 12.2 %collective-permute-start.1 = (f32[6,64,128]{2,1,0:T(8,128)S(1)}, f32[6,64,128]{2,1,0:T(8,128)S(1)}, u32[]{:S(2)}, u32[]{:S(2)}) collective-permute-start(f32[6,64,128]{2,1,0:T(8,128)S(1)} %get-tuple-element.32.own_ref), channel_id=1, source_target_pairs={{2,0},{3,1},{4,2},{5,3},{6,4},{7,5},{10,8},{11,9},{12,10},{13,11},... | collective-permute-start | bytes 589832 | tf_op jit(solution)/shard_map/ppermute | solution.py:430
  15.5 2.0 %copy-start = (f32[8,16,64,128]{3,2,1,0:T(8,128)}, f32[8,16,64,128]{3,2,1,0:T(8,128)S(1)}, u32[]{:S(2)}) copy-start(f32[8,16,64,128]{3,2,1,0:T(8,128)S(1)} %get-tuple-element.38.control_ref) | copy-start | bytes 12582916
  17.5 0.8 copy-start.16
  18.3 0.8 copy-start.18
  19.1 1.0 %copy-start.12 = (f32[16,64,128]{2,1,0:T(8,128)}, f32[16,64,128]{2,1,0:T(8,128)S(1)}, u32[]{:S(2)}) copy-start(f32[16,64,128]{2,1,0:T(8,128)S(1)} %get-tuple-element.29.static_ref) | copy-start | bytes 1572868
  19.1 1.1 %copy-start.14 = (bf16[256,768]{1,0:T(8,128)(2,1)}, bf16[256,768]{1,0:T(8,128)(2,1)S(1)}, u32[]{:S(2)}) copy-start(bf16[256,768]{1,0:T(8,128)(2,1)S(1)} %get-tuple-element.48.matrix_ref) | copy-start | bytes 1179652
  19.1 1.2 %copy-start.8 = (f32[6,64,128]{2,1,0:T(8,128)}, f32[6,64,128]{2,1,0:T(8,128)S(1)}, u32[]{:S(2)}) copy-start(f32[6,64,128]{2,1,0:T(8,128)S(1)} %collective-permute-done.1.after_ref) | copy-start | bytes 589828
  20.2 0.7 copy-start.6
  20.9 11.7 %collective-permute-start.2 = (f32[3,6,64,128]{3,2,1,0:T(8,128)}, f32[3,6,64,128]{3,2,1,0:T(8,128)S(1)}, u32[]{:S(2)}, u32[]{:S(2)}) collective-permute-start(f32[3,6,64,128]{3,2,1,0:T(8,128)} %pad_maximum_fusion), channel_id=1, source_target_pairs={{0,1},{1,0},{2,3},{3,2},{4,5},{5,4},{6,7},{7,6},{8,9},{9,8},{10,11... | collective-permute-start | bytes 1769480 | tf_op jit(solution)/shard_map/ppermute | solution.py:435
  20.9 15.7 %all-to-all-start = ((f32[8,2,8,128]{3,2,1,0:T(8,128)}), f32[8,2,8,128]{3,2,1,0:T(8,128)}, u32[]{:S(2)}, u32[]{:S(2)}) async-start(f32[8,2,8,128]{3,2,1,0:T(8,128)} %get-tuple-element.41), calls=%async_computation | async-start | bytes 131072 | tf_op jit(solution)/shard_map/all_to_all | solution.py:540
  27.0 2.2 %copy-start.1 = (f32[8,16,64,128]{3,2,1,0:T(8,128)S(1)}, f32[8,16,64,128]{3,2,1,0:T(8,128)}, u32[]{:S(2)}) copy-start(f32[8,16,64,128]{3,2,1,0:T(8,128)} %copy-done) | copy-start | bytes 12582916
  29.2 1.0 %copy-start.17 = (bf16[256,768]{1,0:T(8,128)(2,1)S(1)}, bf16[256,768]{1,0:T(8,128)(2,1)}, u32[]{:S(2)}) copy-start(bf16[256,768]{1,0:T(8,128)(2,1)} %copy-done.16) | copy-start | bytes 1179652
  30.2 3.2 %copy-start.5 = (f32[6,64,128]{2,1,0:T(8,128)S(1)}, f32[6,64,128]{2,1,0:T(8,128)}, u32[]{:S(2)}) copy-start(f32[6,64,128]{2,1,0:T(8,128)} %copy-done.4) | copy-start | bytes 589828
  30.2 3.2 %copy-start.7 = (f32[6,64,128]{2,1,0:T(8,128)S(1)}, f32[6,64,128]{2,1,0:T(8,128)}, u32[]{:S(2)}) copy-start(f32[6,64,128]{2,1,0:T(8,128)} %copy-done.6) | copy-start | bytes 589828
  30.2 3.2 %copy-start.9 = (f32[6,64,128]{2,1,0:T(8,128)S(1)}, f32[6,64,128]{2,1,0:T(8,128)}, u32[]{:S(2)}) copy-start(f32[6,64,128]{2,1,0:T(8,128)} %copy-done.8) | copy-start | bytes 589828
  32.6 0.8 copy-start.10
  33.4 1.1 %copy-start.11 = (f32[3,6,64,128]{3,2,1,0:T(8,128)S(1)}, f32[3,6,64,128]{3,2,1,0:T(8,128)}, u32[]{:S(2)}) copy-start(f32[3,6,64,128]{3,2,1,0:T(8,128)} %copy-done.10) | copy-start | bytes 1769476
  36.0 0.6 copy-start.20
  36.6 0.9 %copy-start.21 = (f32[4,64,128]{2,1,0:T(8,128)S(1)}, f32[4,64,128]{2,1,0:T(8,128)}, u32[]{:S(2)}) copy-start(f32[4,64,128]{2,1,0:T(8,128)} %copy-done.20) | copy-start | bytes 393220
  60.1 9.9 %collective-permute-start.3 = (f32[4,64,128]{2,1,0:T(8,128)S(1)}, f32[4,64,128]{2,1,0:T(8,128)S(1)}, u32[]{:S(2)}, u32[]{:S(2)}) collective-permute-start(f32[4,64,128]{2,1,0:T(8,128)S(1)} %bitcast.52), channel_id=1, source_target_pairs={{0,2},{1,3},{2,4},{3,5},{4,6},{5,7},{8,10},{9,11},{10,12},{11,13},... | collective-permute-start | bytes 393224 | tf_op jit(solution)/shard_map/ppermute | solution.py:430
  63.7 6.9 %collective-permute-start.4 = (f32[4,64,128]{2,1,0:T(8,128)S(1)}, f32[4,64,128]{2,1,0:T(8,128)S(1)}, u32[]{:S(2)}, u32[]{:S(2)}) collective-permute-start(f32[4,64,128]{2,1,0:T(8,128)S(1)} %bitcast.53), channel_id=1, source_target_pairs={{2,0},{3,1},{4,2},{5,3},{6,4},{7,5},{10,8},{11,9},{12,10},{13,11},... | collective-permute-start | bytes 393224 | tf_op jit(solution)/shard_map/ppermute | solution.py:430
  70.6 1.8 %collective-permute-start.5 = (f32[3,4,64,128]{3,2,1,0:T(8,128)S(1)}, f32[3,4,64,128]{3,2,1,0:T(8,128)S(1)}, u32[]{:S(2)}, u32[]{:S(2)}) collective-permute-start(f32[3,4,64,128]{3,2,1,0:T(8,128)S(1)} %pad_maximum_fusion.1), channel_id=1, source_target_pairs={{0,1},{1,0},{2,3},{3,2},{4,5},{5,4},{6,7},{7,6},{8,9},{9,8},{10,11... | collective-permute-start | bytes 1179656 | tf_op jit(solution)/shard_map/ppermute | solution.py:435
  73.8 0.8 copy-start.3
  74.6 12.2 %all-to-all-start.2 = ((f32[4,4,64,128]{3,2,1,0:T(8,128)}), f32[4,4,64,128]{3,2,1,0:T(8,128)S(1)}, u32[]{:S(2)}, u32[]{:S(2)}) async-start(f32[4,4,64,128]{3,2,1,0:T(8,128)} %copy-done.3), calls=%async_computation.2 | async-start | bytes 1048576 | tf_op jit(solution)/shard_map/all_to_all | solution.py:607
  78.0 2.2 %copy-start.2 = (f32[8,16,64,128]{3,2,1,0:T(8,128)S(1)}, f32[8,16,64,128]{3,2,1,0:T(8,128)}, u32[]{:S(2)}) copy-start(f32[8,16,64,128]{3,2,1,0:T(8,128)} %copy-done) | copy-start | bytes 12582916
  80.2 1.0 %copy-start.15 = (bf16[256,768]{1,0:T(8,128)(2,1)S(1)}, bf16[256,768]{1,0:T(8,128)(2,1)}, u32[]{:S(2)}) copy-start(bf16[256,768]{1,0:T(8,128)(2,1)} %copy-done.14) | copy-start | bytes 1179652
  81.2 5.6 %copy-start.19 = (bf16[256,768]{1,0:T(8,128)(2,1)S(1)}, bf16[256,768]{1,0:T(8,128)(2,1)}, u32[]{:S(2)}) copy-start(bf16[256,768]{1,0:T(8,128)(2,1)} %copy-done.18) | copy-start | bytes 1179652
  86.8 1.0 %copy-start.13 = (f32[16,64,128]{2,1,0:T(8,128)S(1)}, f32[16,64,128]{2,1,0:T(8,128)}, u32[]{:S(2)}) copy-start(f32[16,64,128]{2,1,0:T(8,128)} %copy-done.12) | copy-start | bytes 1572868

commit v3 on v2

--- a/solution.py
+++ b/solution.py
@@ -119,14 +119,8 @@
     return jnp.concatenate([high, low, high], axis=0)
 
 
-def slots_kernel(n_cols, cap_rows, scale, *refs):
-    sources, (out_ref, *kept), matrices, (acc_ref, fold_ref, *landed), sems = (
-        refs[:8],
-        refs[8:12],
-        refs[12:15],
-        refs[15:22],
-        refs[22],
-    )
+def slots_kernel(n_cols, cap_rows, *refs):
+    sources, out_ref, (acc_ref, fold_ref), landed, sems = refs[:3], refs[3], refs[4:6], refs[6:9], refs[9]
     coarse = acc_ref.shape[0]
     obs_rows = landed[0].shape[0]
     group = min(8, obs_rows)
@@ -134,14 +128,12 @@
     copies = [
         pltpu.make_async_copy(sources[i].at[pl.ds(first, obs_rows), :], landed[i], sems.at[i]) for i in range(3)
     ]
-    copies += [pltpu.make_async_copy(sources[3 + i], landed[3 + i], sems.at[3 + i]) for i in range(2)]
-    copies += [pltpu.make_async_copy(sources[5 + i], kept[i], sems.at[5 + i]) for i in range(3)]
     for copy in copies:
         copy.start()
     acc_ref[...] = jnp.zeros_like(acc_ref)
-    for copy in copies[:5]:
+    for copy in copies:
         copy.wait()
-    slot_ref, weight_ref, innov_ref, local_ref, root_ref = landed
+    slot_ref, weight_ref, innov_ref = landed
 
     def step(i, carry):
         at = pl.ds(pl.multiple_of(i * group, group), group)
@@ -182,49 +174,48 @@
     for p in range(n_cols):
         out_ref[p, 0] = weights[p * cap_rows : (p + 1) * cap_rows]
         out_ref[p, 1] = amounts[p * cap_rows : (p + 1) * cap_rows]
-    matrices[0][...] = level_product(local_ref[...] * f32(scale), False)
-    matrices[1][...] = level_product(local_ref[...] * f32(scale), True)
-    matrices[2][...] = level_product(root_ref[...], True)
-    for copy in copies[5:]:
-        copy.wait()
-
-
-def forward_kernel(matrix_ref, control_ref, pert_ref, out_ref):
-    members, levels, per_level, _ = control_ref.shape
-    pair = 2 - members % 2
+
+
+def forward_kernel(scale, local_ref, control_ref, pert_ref, out_ref, matrix_ref):
+    group, levels, per_level, _ = control_ref.shape
+
+    @pl.when(pl.program_id(0) == 0)
+    def _():
+        matrix_ref[...] = level_product(local_ref[...] * f32(scale), False)
+        out_ref[...] = jnp.zeros_like(out_ref)
 
     def chunk(j, carry):
         at = pl.ds(pl.multiple_of(j * 16, 16), 16)
-        total = None
-        for k in range(0, members, pair):
-            terms = [three_terms(control_ref[k + i, :, at, :].reshape(levels * 16, LANES)) for i in range(pair)]
-            local = jnp.dot(matrix_ref[...], jnp.concatenate(terms, axis=1), preferred_element_type=f32)
-            for i in range(pair):
-                pert = pert_ref[k + i, :, at, :].astype(f32).reshape(levels * 16, LANES)
-                part = pert * local[:, i * LANES : (i + 1) * LANES]
-                total = part if total is None else total + part
-        out_ref[:, at, :] = total.reshape(levels, 16, LANES)
+        terms = [three_terms(control_ref[i, :, at, :].reshape(levels * 16, LANES)) for i in range(group)]
+        local = jnp.dot(matrix_ref[...], jnp.concatenate(terms, axis=1), preferred_element_type=f32)
+        total = out_ref[:, at, :]
+        for i in range(group):
+            part = local[:, i * LANES : (i + 1) * LANES].reshape(levels, 16, LANES)
+            total = total + pert_ref[i, :, at, :].astype(f32) * part
+        out_ref[:, at, :] = total
         return carry
 
     lax.fori_loop(0, per_level // 16, chunk, 0)
 
 
-def member_kernel(matrix_ref, adjoint_ref, control_ref, pert_ref, out_ref):
-    pair, levels, per_level, _ = out_ref.shape
-    first = pl.program_id(0) * pair
+def member_kernel(scale, local_ref, adjoint_ref, control_ref, pert_ref, out_ref, matrix_ref):
+    group, levels, per_level, _ = out_ref.shape
+
+    @pl.when(pl.program_id(0) == 0)
+    def _():
+        matrix_ref[...] = level_product(local_ref[...] * f32(scale), True)
 
     def chunk(j, carry):
         at = pl.ds(pl.multiple_of(j * 16, 16), 16)
-        adjoint = adjoint_ref[:, at, :].reshape(levels * 16, LANES)
+        adjoint = adjoint_ref[:, at, :]
         terms = [
-            three_terms(pert_ref[first + i, :, at, :].astype(f32).reshape(levels * 16, LANES) * adjoint)
-            for i in range(pair)
+            three_terms((pert_ref[i, :, at, :].astype(f32) * adjoint).reshape(levels * 16, LANES))
+            for i in range(group)
         ]
         change = jnp.dot(matrix_ref[...], jnp.concatenate(terms, axis=1), preferred_element_type=f32)
-        for i in range(pair):
-            out_ref[i, :, at, :] = control_ref[first + i, :, at, :] + change[:, i * LANES : (i + 1) * LANES].reshape(
-                levels, 16, LANES
-            )
+        for i in range(group):
+            part = change[:, i * LANES : (i + 1) * LANES].reshape(levels, 16, LANES)
+            out_ref[i, :, at, :] = control_ref[i, :, at, :] + part
         return carry
 
     lax.fori_loop(0, per_level // 16, chunk, 0)
@@ -260,7 +251,7 @@
 
 def tiles_of(before_ref, own_ref, after_ref, other_ref):
     odd = lax.axis_index("cols") % 2
-    return [before_ref, other_ref.at[1 - odd], own_ref, other_ref.at[2 * odd], after_ref]
+    return [before_ref, other_ref.at[1 - odd], own_ref, other_ref.at[odd], after_ref]
 
 
 def first_diffusion_kernel(lev_share, rows, before_ref, own_ref, after_ref, other_ref, out_ref, coef_ref):
@@ -308,7 +299,6 @@
 
 
 def lookup_kernel(part_ref, static_ref, row_ref, lane_ref, slots_ref, out_ref, terms_ref):
-    copies = out_ref.shape[0]
     cells = part_ref.shape[0]
     own = static_ref.shape[0]
     n_lists, _, cap_rows, _ = slots_ref.shape
@@ -337,11 +327,9 @@
             mine = got[c * LANES : (c + 1) * LANES]
             found = jnp.sum(jnp.where(mask, mine[:, :LANES] + mine[:, LANES:], f32(0)), axis=1, keepdims=True)
             values.append(jnp.sum(jnp.where(diagonal, found, f32(0)), axis=0, keepdims=True))
-        values = jnp.concatenate(values, axis=0)
-        for copy in range(copies):
-            out_ref[copy, 0, at, :] = values
-            out_ref[copy, 1, at, :] = slots_ref[q, 0]
-            out_ref[copy, 2, at, :] = slots_ref[q, 1]
+        out_ref[0, at, :] = jnp.concatenate(values, axis=0)
+        out_ref[1, at, :] = slots_ref[q, 0]
+        out_ref[2, at, :] = slots_ref[q, 1]
         return carry
 
     lax.fori_loop(0, n_lists, look, 0)
@@ -366,21 +354,16 @@
     acc_ref[...] += product_nt(jnp.concatenate(left, axis=1), jnp.concatenate(right, axis=1))
 
 
-def amounts_of(shares_ref, at):
-    value, weight, amount = (
-        functools.reduce(jnp.add, [shares_ref[e, t, at, :] for e in range(shares_ref.shape[0])]) for t in range(3)
-    )
-    return value * weight - amount
-
-
-def scatter_own_kernel(cap_rows, row_ref, lane_ref, shares_ref, out_ref, amount_ref, acc_ref):
+def scatter_own_kernel(cap_rows, row_ref, lane_ref, *refs):
+    shares, (out_ref, amount_ref, acc_ref) = refs[:-3], refs[-3:]
     own = out_ref.shape[0]
     first = lax.axis_index("ens") * own
     acc_ref[...] = jnp.zeros_like(acc_ref)
 
     def step(q, carry):
         at = pl.ds(pl.multiple_of(q * cap_rows, cap_rows), cap_rows)
-        amounts = amounts_of(shares_ref, at)
+        value, weight, amount = (functools.reduce(jnp.add, [s[t, at, :] for s in shares]) for t in range(3))
+        amounts = value * weight - amount
         amount_ref[at, :] = amounts
         put(acc_ref, row_ref[at, :] - first, lane_ref[at, :], amounts)
         return carry
@@ -413,13 +396,14 @@
         out_ref[to, :] = piece[:, :LANES] + piece[:, LANES:]
 
 
-def static_kernel(matrix_ref, static_ref, smooth_ref, out_ref):
+def static_kernel(root_ref, static_ref, smooth_ref, out_ref):
     levels, per_level, _ = static_ref.shape
+    matrix = level_product(root_ref[...], True)
     for j in range(0, per_level, 32):
         terms = [
             three_terms(smooth_ref[:, j + i : j + i + 16, :].reshape(levels * 16, LANES)) for i in (0, 16)
         ]
-        change = jnp.dot(matrix_ref[...], jnp.concatenate(terms, axis=1), preferred_element_type=f32)
+        change = jnp.dot(matrix, jnp.concatenate(terms, axis=1), preferred_element_type=f32)
         for i, part in ((0, change[:, :LANES]), (16, change[:, LANES:])):
             at = slice(j + i, j + i + 16)
             out_ref[:, at, :] = static_ref[:, at, :] + part.reshape(levels, 16, LANES)
@@ -430,9 +414,11 @@
     return lax.ppermute(x, "cols", [(i, i + by) for i in range(count) if 0 <= i + by < count])
 
 
-def swapped(x):
+def swapped(own, before, after):
+    odd = lax.axis_index("cols") % 2
     count = lax.axis_size("cols")
-    return lax.ppermute(x, "cols", [(i, i ^ 1) for i in range(count)])
+    pack = jnp.stack([own, jnp.where(odd == 1, before, after)])
+    return lax.ppermute(pack, "cols", [(i, i ^ 1) for i in range(count)])
 
 
 def local(
@@ -502,26 +488,18 @@
     coarse = n_cols * capacity // FINE
     size = levels * 16
     obs_slot, packed = lax.optimization_barrier((obs_slot, packed))
-    slots, static_here, control_here, pert_here, to_local, from_local, from_root = pl.pallas_call(
-        functools.partial(slots_kernel, n_cols, cap_rows, member_scale),
-        in_specs=[pl.BlockSpec(memory_space=pl.ANY)] * 8,
-        out_specs=[VMEM] * 7,
-        out_shape=[
-            pltpu.VMEM((n_cols, 2, cap_rows, LANES), f32),
-            pltpu.VMEM(static.shape, f32),
-            pltpu.VMEM(control.shape, f32),
-            pltpu.VMEM(pert.shape, bf16),
-        ]
-        + [pltpu.VMEM((size, 3 * size), bf16)] * 3,
+    slots = pl.pallas_call(
+        functools.partial(slots_kernel, n_cols, cap_rows),
+        in_specs=[pl.BlockSpec(memory_space=pl.ANY)] * 3,
+        out_specs=VMEM,
+        out_shape=pltpu.VMEM((n_cols, 2, cap_rows, LANES), f32),
         scratch_shapes=[
             pltpu.VMEM((coarse, LANES), f32),
             pltpu.VMEM((coarse, LANES), f32),
             pltpu.VMEM((share_rows, LANES), jnp.int32),
             pltpu.VMEM((share_rows, LANES), f32),
             pltpu.VMEM((share_rows, LANES), f32),
-            pltpu.VMEM((levels, levels), f32),
-            pltpu.VMEM((levels, levels), f32),
-            pltpu.SemaphoreType.DMA((8,)),
+            pltpu.SemaphoreType.DMA((3,)),
         ],
         compiler_params=params(16),
         name="slot_sums",
@@ -529,24 +507,24 @@
         in_hbm(obs_slot.reshape(obs_rows, LANES)),
         in_hbm(obs_weight.reshape(obs_rows, LANES)),
         in_hbm(innovation.reshape(obs_rows, LANES)),
-        in_hbm(vertical_local),
-        in_hbm(vertical_root),
-        static,
-        control,
-        pert,
     )
     before, after, slots = lax.optimization_barrier((before, after, slots))
-    other = swapped(jnp.stack([packed, before, after]))
+    other = swapped(packed, before, after)
     slots = lax.all_to_all(slots, "cols", split_axis=0, concat_axis=0, tiled=True)
 
+    group = 2 - members % 2
+    member_spec = pl.BlockSpec((group, levels, per_level, LANES), lambda k: (k, 0, 0, 0))
+    matrix_scratch = [pltpu.VMEM((size, 3 * size), bf16)]
     part = pl.pallas_call(
-        forward_kernel,
-        in_specs=[VMEM] * 3,
+        functools.partial(forward_kernel, member_scale),
+        grid=(members // group,),
+        in_specs=[whole(levels, levels), member_spec, member_spec],
         out_specs=VMEM,
         out_shape=pltpu.VMEM((levels, per_level, LANES), f32),
-        compiler_params=params(8),
+        scratch_shapes=matrix_scratch,
+        compiler_params=params(16),
         name="members_forward",
-    )(to_local, control_here, pert_here)
+    )(in_hbm(vertical_local), control, pert)
 
     increment, coefs = pl.pallas_call(
         functools.partial(first_diffusion_kernel, lev_share, rows),
@@ -560,26 +538,28 @@
         name="diffuse_forward",
     )(before, packed, after, other)
 
-    shares = pl.pallas_call(
+    share = pl.pallas_call(
         lookup_kernel,
         in_specs=[VMEM] * 5,
         out_specs=VMEM,
-        out_shape=pltpu.VMEM((n_ens, 3, entry_rows, LANES), f32),
+        out_shape=pltpu.VMEM((3, entry_rows, LANES), f32),
         scratch_shapes=[pltpu.VMEM((cells, 2 * LANES), bf16)],
         compiler_params=params(16),
         name="lookup",
     )(part.reshape(cells, LANES), increment.reshape(own, LANES), entry_row, entry_lane, slots)
-    shares = lax.all_to_all(shares, "ens", split_axis=0, concat_axis=0, tiled=True)
+    shares = [share] + [
+        lax.ppermute(share, "ens", [((i + d) % n_ens, i) for i in range(n_ens)]) for d in range(1, n_ens)
+    ]
 
     adjoint_own, amounts = pl.pallas_call(
         functools.partial(scatter_own_kernel, cap_rows),
-        in_specs=[VMEM] * 3,
+        in_specs=[VMEM] * (2 + n_ens),
         out_specs=[VMEM] * 2,
         out_shape=[pltpu.VMEM((own, LANES), f32), pltpu.VMEM((entry_rows, LANES), f32)],
         scratch_shapes=[pltpu.VMEM((own, 2 * LANES), f32)],
         compiler_params=params(16),
         name="scatter_own",
-    )(entry_row, entry_lane, shares)
+    )(entry_row, entry_lane, *shares)
     tile = adjoint_own.reshape(lev_share, per_level, LANES)
     tile_before, tile_after = shifted(tile, 2), shifted(tile, -2)
 
@@ -593,39 +573,39 @@
         name="scatter_rest",
     )(entry_row, entry_lane, amounts, adjoint_own)
     tile_before, tile_after, adjoint = lax.optimization_barrier((tile_before, tile_after, adjoint))
-    tile_other = swapped(jnp.stack([tile, tile_before, tile_after]))
+    tile_other = swapped(tile, tile_before, tile_after)
 
     smooth = pl.pallas_call(
         functools.partial(second_diffusion_kernel, rows),
         in_specs=[VMEM] * 5,
         out_specs=VMEM,
-        out_shape=pltpu.VMEM((n_ens, lev_share, per_level, LANES), f32),
+        out_shape=jax.ShapeDtypeStruct((n_ens, lev_share, per_level, LANES), f32),
         compiler_params=params(8),
         name="diffuse_adjoint",
     )(coefs, tile_before, tile, tile_after, tile_other)
     smooth, adjoint = lax.optimization_barrier((smooth, adjoint))
     smooth = lax.all_to_all(smooth, "ens", split_axis=0, concat_axis=0, tiled=True)
 
-    pair = 2 - members % 2
     ensemble_grad = pl.pallas_call(
-        member_kernel,
-        grid=(members // pair,),
-        in_specs=[VMEM] * 4,
-        out_specs=pl.BlockSpec((pair, levels, per_level, LANES), lambda k: (k, 0, 0, 0)),
+        functools.partial(member_kernel, member_scale),
+        grid=(members // group,),
+        in_specs=[whole(levels, levels), VMEM, member_spec, member_spec],
+        out_specs=member_spec,
         out_shape=jax.ShapeDtypeStruct((members, levels, per_level, LANES), f32),
+        scratch_shapes=matrix_scratch,
         compiler_params=params(16),
         name="members_gradient",
-    )(from_local, adjoint.reshape(levels, per_level, LANES), control_here, pert_here)
+    )(in_hbm(vertical_local), adjoint.reshape(levels, per_level, LANES), control, pert)
 
     static_grad = pl.pallas_call(
         static_kernel,
         grid=(1,),
-        in_specs=[VMEM] * 3,
+        in_specs=[whole(levels, levels), whole(levels, per_level, LANES), VMEM],
         out_specs=whole(levels, per_level, LANES),
         out_shape=jax.ShapeDtypeStruct((levels, per_level, LANES), f32),
         compiler_params=params(8),
         name="static_gradient",
-    )(from_root, static_here, smooth.reshape(levels, per_level, LANES))
+    )(in_hbm(vertical_root), static, smooth.reshape(levels, per_level, LANES))
     return (untiled(static_grad, rows), untiled(ensemble_grad, rows))
 
 

time: 89.7 us -> 76.8 us (0.86)
  local copies, waits for them, and re-layouts: 16 us -> 0 us
  blocking collectives: 11.3 us -> 0 us
  Pallas kernels: 36.9 us -> 44.3 us
  starting transfers between devices: 20.7 us -> 25.2 us
  waiting for transfers between devices: 2.29 us -> 5.79 us
    unnamed x44 -> x0, local copies, waits for them, and re-layouts: 16 us -> none
    all_to_all x1 -> x0, blocking collectives: 11.3 us -> none  [local(): lax.all_to_all(shares, 'ens', split_axis=0, concat_axis=0, tiled=True)]
    pallas_call x4, Pallas kernels: 16.5 us -> 23.9 us  [the longest x1 8.15 us: local(): pl.pallas_call(functools.partial(member_kernel, member_scale), grid=(memb...]
    ppermute x2 -> x5, starting transfers between devices: 0.07 us -> 4.64 us  [the longest x3 4.5 us: local(): lax.ppermute(share, 'ens', [((i + d) % n_ens, i) for i in range(n_ens)])]
    ppermute x2 -> x5, waiting for transfers between devices: 1.71 us -> 5.35 us  [the longest x3 3.83 us: local(): lax.ppermute(share, 'ens', [((i + d) % n_ens, i) for i in range(n_ens)])]
    all_to_all x1, starting transfers between devices: 6.06 us -> 4.4 us  [local(): lax.all_to_all(slots, 'cols', split_axis=0, concat_axis=0, tiled=True)]
    ppermute x4, starting transfers between devices: 11.1 us -> 12.7 us  [shifted(): lax.ppermute(x, 'cols', [(i, i + by) for i in range(count) if 0 <= i + by...]
  transfers between devices with their start and end apart: 8 -> 11, of which waited for: 2 -> 5; matrix products, arithmetic and copies ran while one was open for 0% -> 0% of each run, Pallas kernels for 24% -> 37%
where the time goes in v3:
time: 76.8 us; the launch traced here: 76.2 us
  Pallas kernels  44.3 us (58%)
  starting transfers between devices  25.2 us (33%)
  waiting for transfers between devices  5.79 us (8%)
  between operations  0.83 us (1%)
    ppermute x4, starting transfers between devices, shifted(): lax.ppermute(x, 'cols', [(i, i + by) for i in range(count) if 0 <= i + by...  12.7 us
    pallas_call x1, Pallas kernels, local(): pl.pallas_call(functools.partial(member_kernel, member_scale), grid=(memb...  8.15 us
    pallas_call x1, Pallas kernels, local(): pl.pallas_call(lookup_kernel, in_specs=[VMEM] * 5, out_specs=VMEM, out_sh...  7.62 us
    pallas_call x1, Pallas kernels, local(): pl.pallas_call(functools.partial(slots_kernel, n_cols, cap_rows), in_spec...  6.71 us
    pallas_call x1, Pallas kernels, local(): pl.pallas_call(functools.partial(forward_kernel, member_scale), grid=(mem...  6.6 us
    pallas_call x1, Pallas kernels, local(): pl.pallas_call(functools.partial(scatter_rest_kernel, cap_rows), in_specs...  4.98 us
    ppermute x3, starting transfers between devices, local(): lax.ppermute(share, 'ens', [((i + d) % n_ens, i) for i in range(n_ens)])  4.5 us
    all_to_all x1, starting transfers between devices, local(): lax.all_to_all(slots, 'cols', split_axis=0, concat_axis=0, tiled=True)  4.4 us
  transfers between devices with their start and end apart: 11, of which 5 were waited for; matrix products, arithmetic and copies ran while one was open for 0% of the time, Pallas kernels for 37%

profile of v3, /device:TPU:0, one launch (start us, length us, event | category | flops | bytes accessed | tf_op | source)
XLA Modules:
  0.0 76.2 jit_solution(5790500322821564749)
XLA Ops:
  0.6 1.3 %prepare.1 = (f32[6,64,128]{2,1,0:T(8,128)S(1)}, s32[64,128]{1,0:T(8,128)S(1)}, s32[64,128]{1,0:T(8,128)S(1)}) custom-call(f32[16,16]{1,0:T(8,128)} %root_ref.3, s32[8]{0:T(128)} %count_ref.1, f32[16,64,128]{2,1,0:T(8,128)} %bitcast.63, f32[64,128]{1,0:T(8,128)} %bitcast.69, f32[64,128]{1,0:T(8,128)} %bitcast.70, s32[8,1024]{1,0:T(8,128)} %index_ref.1), custom_call_target="tpu_custom_call" | custom-call | tf_op jit(solution)/shard_map/prepare/pallas_call | solution.py:457
  1.9 1.3 %collective-permute-start.1 = (f32[6,64,128]{2,1,0:T(8,128)S(1)}, f32[6,64,128]{2,1,0:T(8,128)S(1)}, u32[]{:S(2)}, u32[]{:S(2)}) collective-permute-start(f32[6,64,128]{2,1,0:T(8,128)S(1)} %get-tuple-element.22.own_ref), channel_id=1, source_target_pairs={{2,0},{3,1},{4,2},{5,3},{6,4},{7,5},{10,8},{11,9},{12,10},{13,11},... | collective-permute-start | bytes 589832 | tf_op jit(solution)/shard_map/ppermute | solution.py:414
  3.2 5.6 %collective-permute-start = (f32[6,64,128]{2,1,0:T(8,128)S(1)}, f32[6,64,128]{2,1,0:T(8,128)S(1)}, u32[]{:S(2)}, u32[]{:S(2)}) collective-permute-start(f32[6,64,128]{2,1,0:T(8,128)S(1)} %get-tuple-element.22.own_ref), channel_id=1, source_target_pairs={{0,2},{1,3},{2,4},{3,5},{4,6},{5,7},{8,10},{9,11},{10,12},{11,13},... | collective-permute-start | bytes 589832 | tf_op jit(solution)/shard_map/ppermute | solution.py:414
  8.8 6.7 %slot_sums.1 = f32[8,2,8,128]{3,2,1,0:T(8,128)} custom-call(s32[512,128]{1,0:T(8,128)} %bitcast.66, f32[512,128]{1,0:T(8,128)} %bitcast.67, f32[512,128]{1,0:T(8,128)} %bitcast.68), custom_call_target="tpu_custom_call" | custom-call | tf_op jit(solution)/shard_map/slot_sums/pallas_call | solution.py:491
  15.6 0.0 collective-permute-done.1.after_ref
  15.6 0.0 collective-permute-done.before_ref
  15.6 0.1 collective-permute-start.2
  15.7 4.4 %all-to-all-start = ((f32[8,2,8,128]{3,2,1,0:T(8,128)}), f32[8,2,8,128]{3,2,1,0:T(8,128)S(1)}, u32[]{:S(2)}, u32[]{:S(2)}) async-start(f32[8,2,8,128]{3,2,1,0:T(8,128)} %slot_sums.1), calls=%async_computation | async-start | bytes 131072 | tf_op jit(solution)/shard_map/all_to_all | solution.py:513
  20.1 6.6 %members_forward.1 = f32[16,64,128]{2,1,0:T(8,128)S(1)} custom-call(f32[16,16]{1,0:T(8,128)} %local_ref.3, f32[8,16,64,128]{3,2,1,0:T(8,128)} %bitcast.58, bf16[8,16,64,128]{3,2,1,0:T(8,128)(2,1)} %bitcast.60), custom_call_target="tpu_custom_call" | custom-call | tf_op jit(solution)/shard_map/members_forward/pallas_call | solution.py:518
  26.7 0.0 collective-permute-done.2.other_ref
  26.7 1.5 %diffuse_forward.1 = (f32[4,64,128]{2,1,0:T(8,128)S(1)}, f32[5,10,32,128]{3,2,1,0:T(8,128)S(1)}) custom-call(f32[6,64,128]{2,1,0:T(8,128)S(1)} %collective-permute-done.before_ref, f32[6,64,128]{2,1,0:T(8,128)S(1)} %get-tuple-element.22.own_ref, f32[6,64,128]{2,1,0:T(8,128)S(1)} %collective-permute-done.1.after_ref, ...), custom_call_target="tpu_custom_call" | custom-call | tf_op jit(solution)/shard_map/diffuse_forward/pallas_call | solution.py:529
  28.2 0.0 all-to-all-done.slots_ref
  28.2 7.6 %lookup.1.refs_0_ = f32[3,64,128]{2,1,0:T(8,128)S(1)} custom-call(f32[1024,128]{1,0:T(8,128)S(1)} %bitcast.51, f32[256,128]{1,0:T(8,128)S(1)} %bitcast.57, s32[64,128]{1,0:T(8,128)S(1)} %get-tuple-element.25.row_ref, s32[64,128]{1,0:T(8,128)S(1)} %get-tuple-element.26.lane_ref, f32[8,2,8,128]{3,2,1,0:T(8,128)S(1)} %all-to-all-done.slots_ref), custom_call_target="tpu_custom_call" | custom-call | tf_op jit(solution)/shard_map/lookup/pallas_call | solution.py:541
  35.9 1.5 %collective-permute-start.5 = (f32[3,64,128]{2,1,0:T(8,128)S(1)}, f32[3,64,128]{2,1,0:T(8,128)S(1)}, u32[]{:S(2)}, u32[]{:S(2)}) collective-permute-start(f32[3,64,128]{2,1,0:T(8,128)S(1)} %lookup.1.refs_0_), channel_id=1, source_target_pairs={{24,0},{0,8},{8,16},{16,24},{25,1},{1,9},{9,17},{17,25},{26,2},{2,... | collective-permute-start | bytes 294920 | tf_op jit(solution)/shard_map/ppermute | solution.py:551
  37.4 1.5 %collective-permute-start.4 = (f32[3,64,128]{2,1,0:T(8,128)S(1)}, f32[3,64,128]{2,1,0:T(8,128)S(1)}, u32[]{:S(2)}, u32[]{:S(2)}) collective-permute-start(f32[3,64,128]{2,1,0:T(8,128)S(1)} %lookup.1.refs_0_), channel_id=1, source_target_pairs={{16,0},{24,8},{0,16},{8,24},{17,1},{25,9},{1,17},{9,25},{18,2},{26... | collective-permute-start | bytes 294920 | tf_op jit(solution)/shard_map/ppermute | solution.py:551
  38.9 1.4 %collective-permute-start.3 = (f32[3,64,128]{2,1,0:T(8,128)S(1)}, f32[3,64,128]{2,1,0:T(8,128)S(1)}, u32[]{:S(2)}, u32[]{:S(2)}) collective-permute-start(f32[3,64,128]{2,1,0:T(8,128)S(1)} %lookup.1.refs_0_), channel_id=1, source_target_pairs={{8,0},{16,8},{24,16},{0,24},{9,1},{17,9},{25,17},{1,25},{10,2},{18... | collective-permute-start | bytes 294920 | tf_op jit(solution)/shard_map/ppermute | solution.py:551
  40.4 2.0 %collective-permute-done.5.refs_3_ = f32[3,64,128]{2,1,0:T(8,128)S(1)} collective-permute-done((f32[3,64,128]{2,1,0:T(8,128)S(1)}, f32[3,64,128]{2,1,0:T(8,128)S(1)}, u32[]{:S(2)}, u32[]{:S(2)}) %collective-permute-start.5) | collective-permute-done | bytes 98336 | tf_op jit(solution)/shard_map/ppermute | solution.py:551
  42.4 1.7 %collective-permute-done.4.refs_2_ = f32[3,64,128]{2,1,0:T(8,128)S(1)} collective-permute-done((f32[3,64,128]{2,1,0:T(8,128)S(1)}, f32[3,64,128]{2,1,0:T(8,128)S(1)}, u32[]{:S(2)}, u32[]{:S(2)}) %collective-permute-start.4) | collective-permute-done | bytes 98336 | tf_op jit(solution)/shard_map/ppermute | solution.py:551
  44.1 0.1 collective-permute-done.3.refs_1_
  44.2 2.8 %scatter_own.1 = (f32[256,128]{1,0:T(8,128)S(1)}, f32[64,128]{1,0:T(8,128)S(1)}) custom-call(s32[64,128]{1,0:T(8,128)S(1)} %get-tuple-element.25.row_ref, s32[64,128]{1,0:T(8,128)S(1)} %get-tuple-element.26.lane_ref, f32[3,64,128]{2,1,0:T(8,128)S(1)} %lookup.1.refs_0_, f32[3,64,128]{2,1,0:T(8,128)S(1)} %collective-permute-done.3.refs_1_, ...), custom_call_target="tpu_custom_call" | custom-call | tf_op jit(solution)/shard_map/scatter_own/pallas_call | solution.py:554
  47.0 1.3 %collective-permute-start.7 = (f32[4,64,128]{2,1,0:T(8,128)S(1)}, f32[4,64,128]{2,1,0:T(8,128)S(1)}, u32[]{:S(2)}, u32[]{:S(2)}) collective-permute-start(f32[4,64,128]{2,1,0:T(8,128)S(1)} %bitcast.52), channel_id=1, source_target_pairs={{2,0},{3,1},{4,2},{5,3},{6,4},{7,5},{10,8},{11,9},{12,10},{13,11},... | collective-permute-start | bytes 393224 | tf_op jit(solution)/shard_map/ppermute | solution.py:414
  48.3 4.6 %collective-permute-start.6 = (f32[4,64,128]{2,1,0:T(8,128)S(1)}, f32[4,64,128]{2,1,0:T(8,128)S(1)}, u32[]{:S(2)}, u32[]{:S(2)}) collective-permute-start(f32[4,64,128]{2,1,0:T(8,128)S(1)} %bitcast.53), channel_id=1, source_target_pairs={{0,2},{1,3},{2,4},{3,5},{4,6},{5,7},{8,10},{9,11},{10,12},{11,13},... | collective-permute-start | bytes 393224 | tf_op jit(solution)/shard_map/ppermute | solution.py:414
  52.9 5.0 %scatter_rest.1 = f32[1024,128]{1,0:T(8,128)S(1)} custom-call(s32[64,128]{1,0:T(8,128)S(1)} %get-tuple-element.25.row_ref, s32[64,128]{1,0:T(8,128)S(1)} %get-tuple-element.26.lane_ref, f32[64,128]{1,0:T(8,128)S(1)} %get-tuple-element.30.amount_ref, f32[256,128]{1,0:T(8,128)S(1)} %get-tuple-element.29.own_ref), custom_call_target="tpu_custom_call" | custom-call | tf_op jit(solution)/shard_map/scatter_rest/pallas_call | solution.py:566
  57.9 0.0 collective-permute-done.7.after_ref
  57.9 0.0 collective-permute-done.6.before_ref
  57.9 0.1 collective-permute-start.8
  58.0 1.5 %collective-permute-done.8.other_ref = f32[2,4,64,128]{3,2,1,0:T(8,128)S(1)} collective-permute-done((f32[2,4,64,128]{3,2,1,0:T(8,128)S(1)}, f32[2,4,64,128]{3,2,1,0:T(8,128)S(1)}, u32[]{:S(2)}, u32[]{:S(2)}) %collective-permute-start.8) | collective-permute-done | bytes 262176 | tf_op jit(solution)/shard_map/ppermute | solution.py:421
  59.5 2.2 %diffuse_adjoint.1 = f32[4,4,64,128]{3,2,1,0:T(8,128)} custom-call(f32[5,10,32,128]{3,2,1,0:T(8,128)S(1)} %get-tuple-element.24.coef_ref, f32[4,64,128]{2,1,0:T(8,128)S(1)} %collective-permute-done.6.before_ref, f32[4,64,128]{2,1,0:T(8,128)S(1)} %bitcast.55, f32[4,64,128]{2,1,0:T(8,128)S(1)} %collective-permute-done.7.after_ref, ...), custom_call_target="tpu_custom_call" | custom-call | tf_op jit(solution)/shard_map/diffuse_adjoint/pallas_call | solution.py:578
  61.7 3.5 %all-to-all-start.1 = ((f32[4,4,64,128]{3,2,1,0:T(8,128)}), f32[4,4,64,128]{3,2,1,0:T(8,128)S(1)}, u32[]{:S(2)}, u32[]{:S(2)}) async-start(f32[4,4,64,128]{3,2,1,0:T(8,128)} %diffuse_adjoint.1), calls=%async_computation.1 | async-start | bytes 1048576 | tf_op jit(solution)/shard_map/all_to_all | solution.py:587
  65.2 8.1 %members_gradient.1 = f32[8,16,64,128]{3,2,1,0:T(8,128)} custom-call(f32[16,16]{1,0:T(8,128)} %local_ref.3, f32[16,64,128]{2,1,0:T(8,128)S(1)} %bitcast.49, f32[8,16,64,128]{3,2,1,0:T(8,128)} %bitcast.59, bf16[8,16,64,128]{3,2,1,0:T(8,128)(2,1)} %bitcast.61), custom_call_target="tpu_custom_call" | custom-call | tf_op jit(solution)/shard_map/members_gradient/pallas_call | solution.py:589
  73.4 0.4 all-to-all-done.1
  73.8 2.4 %static_gradient.1 = f32[16,64,128]{2,1,0:T(8,128)} custom-call(f32[16,16]{1,0:T(8,128)} %root_ref.3, f32[16,64,128]{2,1,0:T(8,128)} %bitcast.64, f32[16,64,128]{2,1,0:T(8,128)S(1)} %bitcast.50), custom_call_target="tpu_custom_call" | custom-call | tf_op jit(solution)/shard_map/static_gradient/pallas_call | solution.py:600
  (4 shorter events, 0.1 us)
Async XLA Ops:
  1.9 13.6 %collective-permute-start.1 = (f32[6,64,128]{2,1,0:T(8,128)S(1)}, f32[6,64,128]{2,1,0:T(8,128)S(1)}, u32[]{:S(2)}, u32[]{:S(2)}) collective-permute-start(f32[6,64,128]{2,1,0:T(8,128)S(1)} %get-tuple-element.22.own_ref), channel_id=1, source_target_pairs={{2,0},{3,1},{4,2},{5,3},{6,4},{7,5},{10,8},{11,9},{12,10},{13,11},... | collective-permute-start | bytes 589832 | tf_op jit(solution)/shard_map/ppermute | solution.py:414
  3.2 12.3 %collective-permute-start = (f32[6,64,128]{2,1,0:T(8,128)S(1)}, f32[6,64,128]{2,1,0:T(8,128)S(1)}, u32[]{:S(2)}, u32[]{:S(2)}) collective-permute-start(f32[6,64,128]{2,1,0:T(8,128)S(1)} %get-tuple-element.22.own_ref), channel_id=1, source_target_pairs={{0,2},{1,3},{2,4},{3,5},{4,6},{5,7},{8,10},{9,11},{10,12},{11,13},... | collective-permute-start | bytes 589832 | tf_op jit(solution)/shard_map/ppermute | solution.py:414
  15.6 11.1 %collective-permute-start.2 = (f32[2,6,64,128]{3,2,1,0:T(8,128)S(1)}, f32[2,6,64,128]{3,2,1,0:T(8,128)S(1)}, u32[]{:S(2)}, u32[]{:S(2)}) collective-permute-start(f32[2,6,64,128]{3,2,1,0:T(8,128)S(1)} %pad_maximum_fusion), channel_id=1, source_target_pairs={{0,1},{1,0},{2,3},{3,2},{4,5},{5,4},{6,7},{7,6},{8,9},{9,8},{10,11... | collective-permute-start | bytes 1179656 | tf_op jit(solution)/shard_map/ppermute | solution.py:421
  15.7 12.5 %all-to-all-start = ((f32[8,2,8,128]{3,2,1,0:T(8,128)}), f32[8,2,8,128]{3,2,1,0:T(8,128)S(1)}, u32[]{:S(2)}, u32[]{:S(2)}) async-start(f32[8,2,8,128]{3,2,1,0:T(8,128)} %slot_sums.1), calls=%async_computation | async-start | bytes 131072 | tf_op jit(solution)/shard_map/all_to_all | solution.py:513
  35.9 6.5 %collective-permute-start.5 = (f32[3,64,128]{2,1,0:T(8,128)S(1)}, f32[3,64,128]{2,1,0:T(8,128)S(1)}, u32[]{:S(2)}, u32[]{:S(2)}) collective-permute-start(f32[3,64,128]{2,1,0:T(8,128)S(1)} %lookup.1.refs_0_), channel_id=1, source_target_pairs={{24,0},{0,8},{8,16},{16,24},{25,1},{1,9},{9,17},{17,25},{26,2},{2,... | collective-permute-start | bytes 294920 | tf_op jit(solution)/shard_map/ppermute | solution.py:551
  37.4 6.7 %collective-permute-start.4 = (f32[3,64,128]{2,1,0:T(8,128)S(1)}, f32[3,64,128]{2,1,0:T(8,128)S(1)}, u32[]{:S(2)}, u32[]{:S(2)}) collective-permute-start(f32[3,64,128]{2,1,0:T(8,128)S(1)} %lookup.1.refs_0_), channel_id=1, source_target_pairs={{16,0},{24,8},{0,16},{8,24},{17,1},{25,9},{1,17},{9,25},{18,2},{26... | collective-permute-start | bytes 294920 | tf_op jit(solution)/shard_map/ppermute | solution.py:551
  38.9 5.3 %collective-permute-start.3 = (f32[3,64,128]{2,1,0:T(8,128)S(1)}, f32[3,64,128]{2,1,0:T(8,128)S(1)}, u32[]{:S(2)}, u32[]{:S(2)}) collective-permute-start(f32[3,64,128]{2,1,0:T(8,128)S(1)} %lookup.1.refs_0_), channel_id=1, source_target_pairs={{8,0},{16,8},{24,16},{0,24},{9,1},{17,9},{25,17},{1,25},{10,2},{18... | collective-permute-start | bytes 294920 | tf_op jit(solution)/shard_map/ppermute | solution.py:551
  47.0 10.9 %collective-permute-start.7 = (f32[4,64,128]{2,1,0:T(8,128)S(1)}, f32[4,64,128]{2,1,0:T(8,128)S(1)}, u32[]{:S(2)}, u32[]{:S(2)}) collective-permute-start(f32[4,64,128]{2,1,0:T(8,128)S(1)} %bitcast.52), channel_id=1, source_target_pairs={{2,0},{3,1},{4,2},{5,3},{6,4},{7,5},{10,8},{11,9},{12,10},{13,11},... | collective-permute-start | bytes 393224 | tf_op jit(solution)/shard_map/ppermute | solution.py:414
  48.3 9.6 %collective-permute-start.6 = (f32[4,64,128]{2,1,0:T(8,128)S(1)}, f32[4,64,128]{2,1,0:T(8,128)S(1)}, u32[]{:S(2)}, u32[]{:S(2)}) collective-permute-start(f32[4,64,128]{2,1,0:T(8,128)S(1)} %bitcast.53), channel_id=1, source_target_pairs={{0,2},{1,3},{2,4},{3,5},{4,6},{5,7},{8,10},{9,11},{10,12},{11,13},... | collective-permute-start | bytes 393224 | tf_op jit(solution)/shard_map/ppermute | solution.py:414
  57.9 1.6 %collective-permute-start.8 = (f32[2,4,64,128]{3,2,1,0:T(8,128)S(1)}, f32[2,4,64,128]{3,2,1,0:T(8,128)S(1)}, u32[]{:S(2)}, u32[]{:S(2)}) collective-permute-start(f32[2,4,64,128]{3,2,1,0:T(8,128)S(1)} %pad_maximum_fusion.1), channel_id=1, source_target_pairs={{0,1},{1,0},{2,3},{3,2},{4,5},{5,4},{6,7},{7,6},{8,9},{9,8},{10,11... | collective-permute-start | bytes 786440 | tf_op jit(solution)/shard_map/ppermute | solution.py:421
  61.7 12.1 %all-to-all-start.1 = ((f32[4,4,64,128]{3,2,1,0:T(8,128)}), f32[4,4,64,128]{3,2,1,0:T(8,128)S(1)}, u32[]{:S(2)}, u32[]{:S(2)}) async-start(f32[4,4,64,128]{3,2,1,0:T(8,128)} %diffuse_adjoint.1), calls=%async_computation.1 | async-start | bytes 1048576 | tf_op jit(solution)/shard_map/all_to_all | solution.py:587

commit v4 on v3

--- a/solution.py
+++ b/solution.py
@@ -119,8 +119,14 @@
     return jnp.concatenate([high, low, high], axis=0)
 
 
-def slots_kernel(n_cols, cap_rows, *refs):
-    sources, out_ref, (acc_ref, fold_ref), landed, sems = refs[:3], refs[3], refs[4:6], refs[6:9], refs[9]
+def observe_kernel(n_cols, cap_rows, scale, *refs):
+    sources, (out_ref, part_ref), (acc_ref, fold_ref, matrix_ref), landed, sems = (
+        refs[:6],
+        refs[6:8],
+        refs[8:11],
+        refs[11:17],
+        refs[17],
+    )
     coarse = acc_ref.shape[0]
     obs_rows = landed[0].shape[0]
     group = min(8, obs_rows)
@@ -128,12 +134,13 @@
     copies = [
         pltpu.make_async_copy(sources[i].at[pl.ds(first, obs_rows), :], landed[i], sems.at[i]) for i in range(3)
     ]
+    copies += [pltpu.make_async_copy(sources[i], landed[i], sems.at[i]) for i in range(3, 6)]
     for copy in copies:
         copy.start()
     acc_ref[...] = jnp.zeros_like(acc_ref)
-    for copy in copies:
+    for copy in copies[:3]:
         copy.wait()
-    slot_ref, weight_ref, innov_ref = landed
+    slot_ref, weight_ref, innov_ref, local_ref, control_ref, pert_ref = landed
 
     def step(i, carry):
         at = pl.ds(pl.multiple_of(i * group, group), group)
@@ -174,48 +181,46 @@
     for p in range(n_cols):
         out_ref[p, 0] = weights[p * cap_rows : (p + 1) * cap_rows]
         out_ref[p, 1] = amounts[p * cap_rows : (p + 1) * cap_rows]
-
-
-def forward_kernel(scale, local_ref, control_ref, pert_ref, out_ref, matrix_ref):
-    group, levels, per_level, _ = control_ref.shape
-
-    @pl.when(pl.program_id(0) == 0)
-    def _():
-        matrix_ref[...] = level_product(local_ref[...] * f32(scale), False)
-        out_ref[...] = jnp.zeros_like(out_ref)
+    for copy in copies[3:]:
+        copy.wait()
+    matrix_ref[...] = level_product(local_ref[...] * f32(scale), False)
+    sum_members(matrix_ref, control_ref, pert_ref, part_ref)
+
+
+def sum_members(matrix_ref, control_ref, pert_ref, out_ref):
+    members, levels, per_level, _ = control_ref.shape
+    group = 2 - members % 2
 
     def chunk(j, carry):
         at = pl.ds(pl.multiple_of(j * 16, 16), 16)
-        terms = [three_terms(control_ref[i, :, at, :].reshape(levels * 16, LANES)) for i in range(group)]
-        local = jnp.dot(matrix_ref[...], jnp.concatenate(terms, axis=1), preferred_element_type=f32)
-        total = out_ref[:, at, :]
-        for i in range(group):
-            part = local[:, i * LANES : (i + 1) * LANES].reshape(levels, 16, LANES)
-            total = total + pert_ref[i, :, at, :].astype(f32) * part
-        out_ref[:, at, :] = total
+        total = jnp.zeros((levels * 16, LANES), f32)
+        for k in range(0, members, group):
+            terms = [three_terms(control_ref[k + i, :, at, :].reshape(levels * 16, LANES)) for i in range(group)]
+            local = jnp.dot(matrix_ref[...], jnp.concatenate(terms, axis=1), preferred_element_type=f32)
+            for i in range(group):
+                pert = pert_ref[k + i, :, at, :].astype(f32).reshape(levels * 16, LANES)
+                total = total + pert * local[:, i * LANES : (i + 1) * LANES]
+        out_ref[:, at, :] = total.reshape(levels, 16, LANES)
         return carry
 
     lax.fori_loop(0, per_level // 16, chunk, 0)
 
 
-def member_kernel(scale, local_ref, adjoint_ref, control_ref, pert_ref, out_ref, matrix_ref):
+def member_kernel(matrix_ref, adjoint_ref, control_ref, pert_ref, out_ref):
     group, levels, per_level, _ = out_ref.shape
-
-    @pl.when(pl.program_id(0) == 0)
-    def _():
-        matrix_ref[...] = level_product(local_ref[...] * f32(scale), True)
+    first = pl.program_id(0) * group
 
     def chunk(j, carry):
         at = pl.ds(pl.multiple_of(j * 16, 16), 16)
         adjoint = adjoint_ref[:, at, :]
         terms = [
-            three_terms((pert_ref[i, :, at, :].astype(f32) * adjoint).reshape(levels * 16, LANES))
+            three_terms((pert_ref[first + i, :, at, :].astype(f32) * adjoint).reshape(levels * 16, LANES))
             for i in range(group)
         ]
         change = jnp.dot(matrix_ref[...], jnp.concatenate(terms, axis=1), preferred_element_type=f32)
         for i in range(group):
             part = change[:, i * LANES : (i + 1) * LANES].reshape(levels, 16, LANES)
-            out_ref[i, :, at, :] = control_ref[i, :, at, :] + part
+            out_ref[i, :, at, :] = control_ref[first + i, :, at, :] + part
         return carry
 
     lax.fori_loop(0, per_level // 16, chunk, 0)
@@ -285,23 +290,22 @@
 
 def second_diffusion_kernel(rows, coef_ref, before_ref, own_ref, after_ref, other_ref, out_ref):
     tiles = tiles_of(before_ref, own_ref, after_ref, other_ref)
-    copies, lev_share = out_ref.shape[:2]
+    lev_share = out_ref.shape[0]
     blocks = own_ref.shape[1] // rows
 
     def body(level, carry):
         final = diffuse_rows(tiles, level, coef_ref, rows)
-        for copy in range(copies):
-            for r in range(rows):
-                out_ref[copy, level, pl.ds(r, blocks, stride=rows), :] = final[r]
+        for r in range(rows):
+            out_ref[level, pl.ds(r, blocks, stride=rows), :] = final[r]
         return carry
 
     lax.fori_loop(0, lev_share, body, 0)
 
 
-def lookup_kernel(part_ref, static_ref, row_ref, lane_ref, slots_ref, out_ref, terms_ref):
+def lookup_kernel(cap_rows, part_ref, static_ref, row_ref, lane_ref, out_ref, terms_ref):
     cells = part_ref.shape[0]
     own = static_ref.shape[0]
-    n_lists, _, cap_rows, _ = slots_ref.shape
+    n_lists = row_ref.shape[0] // cap_rows
     at = pl.ds(pl.multiple_of(lax.axis_index("ens") * own, own), own)
     for here, field in ((slice(None), part_ref[...]), (at, part_ref[at, :] + static_ref[...])):
         high, low = halves(field)
@@ -327,9 +331,7 @@
             mine = got[c * LANES : (c + 1) * LANES]
             found = jnp.sum(jnp.where(mask, mine[:, :LANES] + mine[:, LANES:], f32(0)), axis=1, keepdims=True)
             values.append(jnp.sum(jnp.where(diagonal, found, f32(0)), axis=0, keepdims=True))
-        out_ref[0, at, :] = jnp.concatenate(values, axis=0)
-        out_ref[1, at, :] = slots_ref[q, 0]
-        out_ref[2, at, :] = slots_ref[q, 1]
+        out_ref[at, :] = jnp.concatenate(values, axis=0)
         return carry
 
     lax.fori_loop(0, n_lists, look, 0)
@@ -372,7 +374,19 @@
     out_ref[...] = acc_ref[:, :LANES] + acc_ref[:, LANES:]
 
 
-def scatter_rest_kernel(cap_rows, row_ref, lane_ref, amount_ref, own_ref, out_ref, acc_ref):
+def scatter_rest_kernel(cap_rows, scale, row_ref, lane_ref, amount_ref, own_ref, *refs):
+    sources, out_ref, kept, matrices, acc_ref, landed, sems = (
+        refs[:5],
+        refs[5],
+        refs[6:9],
+        refs[9:11],
+        refs[11],
+        refs[12:14],
+        refs[14],
+    )
+    copies = [pltpu.make_async_copy(s, t, sems.at[i]) for i, (s, t) in enumerate(zip(sources, (*landed, *kept)))]
+    for copy in copies:
+        copy.start()
     cells = out_ref.shape[0]
     own = own_ref.shape[0]
     n_ens = cells // own
@@ -394,16 +408,22 @@
         to = pl.ds(pl.multiple_of((me + t) % n_ens * own, own), own)
         piece = acc_ref[(t - 1) * own : t * own, :]
         out_ref[to, :] = piece[:, :LANES] + piece[:, LANES:]
-
-
-def static_kernel(root_ref, static_ref, smooth_ref, out_ref):
+    for copy in copies:
+        copy.wait()
+    matrices[0][...] = level_product(landed[0][...] * f32(scale), True)
+    matrices[1][...] = level_product(landed[1][...], True)
+
+
+def static_kernel(matrix_ref, static_ref, *refs):
+    parts, (out_ref, smooth_ref) = refs[:-2], refs[-2:]
     levels, per_level, _ = static_ref.shape
-    matrix = level_product(root_ref[...], True)
+    share = levels // len(parts)
+    me = lax.axis_index("ens")
+    for d, part in enumerate(parts):
+        smooth_ref[pl.ds((me + d) % len(parts) * share, share)] = part[...]
     for j in range(0, per_level, 32):
-        terms = [
-            three_terms(smooth_ref[:, j + i : j + i + 16, :].reshape(levels * 16, LANES)) for i in (0, 16)
-        ]
-        change = jnp.dot(matrix, jnp.concatenate(terms, axis=1), preferred_element_type=f32)
+        terms = [three_terms(smooth_ref[:, j + i : j + i + 16, :].reshape(levels * 16, LANES)) for i in (0, 16)]
+        change = jnp.dot(matrix_ref[...], jnp.concatenate(terms, axis=1), preferred_element_type=f32)
         for i, part in ((0, change[:, :LANES]), (16, change[:, LANES:])):
             at = slice(j + i, j + i + 16)
             out_ref[:, at, :] = static_ref[:, at, :] + part.reshape(levels, 16, LANES)
@@ -412,6 +432,11 @@
 def shifted(x, by):
     count = lax.axis_size("cols")
     return lax.ppermute(x, "cols", [(i, i + by) for i in range(count) if 0 <= i + by < count])
+
+
+def from_peers(x):
+    count = lax.axis_size("ens")
+    return [lax.ppermute(x, "ens", [((i + d) % count, i) for i in range(count)]) for d in range(1, count)]
 
 
 def swapped(own, before, after):
@@ -488,43 +513,39 @@
     coarse = n_cols * capacity // FINE
     size = levels * 16
     obs_slot, packed = lax.optimization_barrier((obs_slot, packed))
-    slots = pl.pallas_call(
-        functools.partial(slots_kernel, n_cols, cap_rows),
-        in_specs=[pl.BlockSpec(memory_space=pl.ANY)] * 3,
-        out_specs=VMEM,
-        out_shape=pltpu.VMEM((n_cols, 2, cap_rows, LANES), f32),
+    slots, part = pl.pallas_call(
+        functools.partial(observe_kernel, n_cols, cap_rows, member_scale),
+        in_specs=[pl.BlockSpec(memory_space=pl.ANY)] * 6,
+        out_specs=[VMEM] * 2,
+        out_shape=[
+            pltpu.VMEM((n_cols, 2, cap_rows, LANES), f32),
+            pltpu.VMEM((levels, per_level, LANES), f32),
+        ],
         scratch_shapes=[
             pltpu.VMEM((coarse, LANES), f32),
             pltpu.VMEM((coarse, LANES), f32),
+            pltpu.VMEM((size, 3 * size), bf16),
             pltpu.VMEM((share_rows, LANES), jnp.int32),
             pltpu.VMEM((share_rows, LANES), f32),
             pltpu.VMEM((share_rows, LANES), f32),
-            pltpu.SemaphoreType.DMA((3,)),
+            pltpu.VMEM((levels, levels), f32),
+            pltpu.VMEM(control.shape, f32),
+            pltpu.VMEM(pert.shape, bf16),
+            pltpu.SemaphoreType.DMA((6,)),
         ],
-        compiler_params=params(16),
-        name="slot_sums",
+        compiler_params=params(24),
+        name="slot_sums_and_members",
     )(
         in_hbm(obs_slot.reshape(obs_rows, LANES)),
         in_hbm(obs_weight.reshape(obs_rows, LANES)),
         in_hbm(innovation.reshape(obs_rows, LANES)),
+        in_hbm(vertical_local),
+        control,
+        pert,
     )
     before, after, slots = lax.optimization_barrier((before, after, slots))
     other = swapped(packed, before, after)
     slots = lax.all_to_all(slots, "cols", split_axis=0, concat_axis=0, tiled=True)
-
-    group = 2 - members % 2
-    member_spec = pl.BlockSpec((group, levels, per_level, LANES), lambda k: (k, 0, 0, 0))
-    matrix_scratch = [pltpu.VMEM((size, 3 * size), bf16)]
-    part = pl.pallas_call(
-        functools.partial(forward_kernel, member_scale),
-        grid=(members // group,),
-        in_specs=[whole(levels, levels), member_spec, member_spec],
-        out_specs=VMEM,
-        out_shape=pltpu.VMEM((levels, per_level, LANES), f32),
-        scratch_shapes=matrix_scratch,
-        compiler_params=params(16),
-        name="members_forward",
-    )(in_hbm(vertical_local), control, pert)
 
     increment, coefs = pl.pallas_call(
         functools.partial(first_diffusion_kernel, lev_share, rows),
@@ -538,18 +559,18 @@
         name="diffuse_forward",
     )(before, packed, after, other)
 
-    share = pl.pallas_call(
-        lookup_kernel,
-        in_specs=[VMEM] * 5,
+    values = pl.pallas_call(
+        functools.partial(lookup_kernel, cap_rows),
+        in_specs=[VMEM] * 4,
         out_specs=VMEM,
-        out_shape=pltpu.VMEM((3, entry_rows, LANES), f32),
+        out_shape=pltpu.VMEM((entry_rows, LANES), f32),
         scratch_shapes=[pltpu.VMEM((cells, 2 * LANES), bf16)],
         compiler_params=params(16),
         name="lookup",
-    )(part.reshape(cells, LANES), increment.reshape(own, LANES), entry_row, entry_lane, slots)
-    shares = [share] + [
-        lax.ppermute(share, "ens", [((i + d) % n_ens, i) for i in range(n_ens)]) for d in range(1, n_ens)
-    ]
+    )(part.reshape(cells, LANES), increment.reshape(own, LANES), entry_row, entry_lane)
+    slots = jnp.swapaxes(slots, 0, 1).reshape(2, entry_rows, LANES)
+    share = jnp.concatenate([values[None], slots])
+    shares = [share] + from_peers(share)
 
     adjoint_own, amounts = pl.pallas_call(
         functools.partial(scatter_own_kernel, cap_rows),
@@ -563,15 +584,37 @@
     tile = adjoint_own.reshape(lev_share, per_level, LANES)
     tile_before, tile_after = shifted(tile, 2), shifted(tile, -2)
 
-    adjoint = pl.pallas_call(
-        functools.partial(scatter_rest_kernel, cap_rows),
-        in_specs=[VMEM] * 4,
-        out_specs=VMEM,
-        out_shape=pltpu.VMEM((cells, LANES), f32),
-        scratch_shapes=[pltpu.VMEM((cells - own, 2 * LANES), f32)],
+    adjoint, static_here, control_here, pert_here, from_local, from_root = pl.pallas_call(
+        functools.partial(scatter_rest_kernel, cap_rows, member_scale),
+        in_specs=[VMEM] * 4 + [pl.BlockSpec(memory_space=pl.ANY)] * 5,
+        out_specs=[VMEM] * 6,
+        out_shape=[
+            pltpu.VMEM((cells, LANES), f32),
+            pltpu.VMEM(static.shape, f32),
+            pltpu.VMEM(control.shape, f32),
+            pltpu.VMEM(pert.shape, bf16),
+            pltpu.VMEM((size, 3 * size), bf16),
+            pltpu.VMEM((size, 3 * size), bf16),
+        ],
+        scratch_shapes=[
+            pltpu.VMEM((cells - own, 2 * LANES), f32),
+            pltpu.VMEM((levels, levels), f32),
+            pltpu.VMEM((levels, levels), f32),
+            pltpu.SemaphoreType.DMA((5,)),
+        ],
         compiler_params=params(16),
         name="scatter_rest",
-    )(entry_row, entry_lane, amounts, adjoint_own)
+    )(
+        entry_row,
+        entry_lane,
+        amounts,
+        adjoint_own,
+        in_hbm(vertical_local),
+        in_hbm(vertical_root),
+        static,
+        control,
+        pert,
+    )
     tile_before, tile_after, adjoint = lax.optimization_barrier((tile_before, tile_after, adjoint))
     tile_other = swapped(tile, tile_before, tile_after)
 
@@ -579,33 +622,34 @@
         functools.partial(second_diffusion_kernel, rows),
         in_specs=[VMEM] * 5,
         out_specs=VMEM,
-        out_shape=jax.ShapeDtypeStruct((n_ens, lev_share, per_level, LANES), f32),
+        out_shape=pltpu.VMEM((lev_share, per_level, LANES), f32),
         compiler_params=params(8),
         name="diffuse_adjoint",
     )(coefs, tile_before, tile, tile_after, tile_other)
     smooth, adjoint = lax.optimization_barrier((smooth, adjoint))
-    smooth = lax.all_to_all(smooth, "ens", split_axis=0, concat_axis=0, tiled=True)
-
+    smooths = [smooth] + from_peers(smooth)
+
+    group = 2 - members % 2
     ensemble_grad = pl.pallas_call(
-        functools.partial(member_kernel, member_scale),
+        member_kernel,
         grid=(members // group,),
-        in_specs=[whole(levels, levels), VMEM, member_spec, member_spec],
-        out_specs=member_spec,
+        in_specs=[VMEM] * 4,
+        out_specs=pl.BlockSpec((group, levels, per_level, LANES), lambda k: (k, 0, 0, 0)),
         out_shape=jax.ShapeDtypeStruct((members, levels, per_level, LANES), f32),
-        scratch_shapes=matrix_scratch,
         compiler_params=params(16),
         name="members_gradient",
-    )(in_hbm(vertical_local), adjoint.reshape(levels, per_level, LANES), control, pert)
+    )(from_local, adjoint.reshape(levels, per_level, LANES), control_here, pert_here)
 
     static_grad = pl.pallas_call(
         static_kernel,
         grid=(1,),
-        in_specs=[whole(levels, levels), whole(levels, per_level, LANES), VMEM],
+        in_specs=[VMEM] * (2 + n_ens),
         out_specs=whole(levels, per_level, LANES),
         out_shape=jax.ShapeDtypeStruct((levels, per_level, LANES), f32),
+        scratch_shapes=[pltpu.VMEM((levels, per_level, LANES), f32)],
         compiler_params=params(8),
         name="static_gradient",
-    )(in_hbm(vertical_root), static, smooth.reshape(levels, per_level, LANES))
+    )(from_root, static_here, *smooths)
     return (untiled(static_grad, rows), untiled(ensemble_grad, rows))
 
 

time: 76.8 us -> 73 us (0.951)
  blocking collectives: 0 us -> 11.8 us
  Pallas kernels: 44.3 us -> 35.9 us
  starting transfers between devices: 25.2 us -> 17.2 us
  waiting for transfers between devices: 5.79 us -> 6.9 us
    all_to_all x0 -> x1, blocking collectives: none -> 11.8 us  [local(): lax.all_to_all(slots, 'cols', split_axis=0, concat_axis=0, tiled=True)]
    all_to_all x2 -> x0, starting transfers between devices: 7.87 us -> none  [the longest x1 4.4 us: local(): lax.all_to_all(slots, 'cols', split_axis=0, concat_axis=0, tiled=True)]
    pallas_call x6 -> x5, Pallas kernels: 36.5 us -> 28.9 us  [the longest x1 8.93 us: local(): pl.pallas_call(functools.partial(observe_kernel, n_cols, cap_rows, member...]
    ppermute x4, starting transfers between devices: 12.7 us -> 10.2 us  [shifted(): lax.ppermute(x, 'cols', [(i, i + by) for i in range(count) if 0 <= i + by...]
    ppermute x3 -> x6, starting transfers between devices: 4.5 us -> 6.86 us  [from_peers(): lax.ppermute(x, 'ens', [((i + d) % count, i) for i in range(count)])]
    ppermute x3 -> x6, waiting for transfers between devices: 3.83 us -> 5.36 us  [from_peers(): lax.ppermute(x, 'ens', [((i + d) % count, i) for i in range(count)])]
    pallas_call x1, Pallas kernels: 2.18 us -> 1.38 us  [local(): pl.pallas_call(functools.partial(second_diffusion_kernel, rows), in_specs...]
  transfers between devices with their start and end apart: 11 -> 12, of which waited for: 5 -> 4; matrix products, arithmetic and copies ran while one was open for 0% -> 0% of each run, Pallas kernels for 37% -> 28%
where the time goes in v4:
time: 73 us; the launch traced here: 72.8 us
  Pallas kernels  35.9 us (49%)
  starting transfers between devices  17.2 us (24%)
  blocking collectives  11.8 us (16%)
  waiting for transfers between devices  6.9 us (9%)
  between operations  0.82 us (1%)
    all_to_all x1, blocking collectives, local(): lax.all_to_all(slots, 'cols', split_axis=0, concat_axis=0, tiled=True)  11.8 us
    ppermute x4, starting transfers between devices, shifted(): lax.ppermute(x, 'cols', [(i, i + by) for i in range(count) if 0 <= i + by...  10.2 us
    pallas_call x1, Pallas kernels, local(): pl.pallas_call(functools.partial(observe_kernel, n_cols, cap_rows, member...  8.93 us
    pallas_call x1, Pallas kernels, local(): pl.pallas_call(functools.partial(lookup_kernel, cap_rows), in_specs=[VMEM...  7.62 us
    ppermute x6, starting transfers between devices, from_peers(): lax.ppermute(x, 'ens', [((i + d) % count, i) for i in range(count)])  6.86 us
    pallas_call x1, Pallas kernels, local(): pl.pallas_call(functools.partial(scatter_rest_kernel, cap_rows, member_sc...  5.6 us
    pallas_call x1, Pallas kernels, local(): pl.pallas_call(member_kernel, grid=(members // group,), in_specs=[VMEM] *...  5.58 us
    ppermute x6, waiting for transfers between devices, from_peers(): lax.ppermute(x, 'ens', [((i + d) % count, i) for i in range(count)])  5.36 us
  transfers between devices with their start and end apart: 12, of which 4 were waited for; matrix products, arithmetic and copies ran while one was open for 0% of the time, Pallas kernels for 28%

profile of v4, /device:TPU:0, one launch (start us, length us, event | category | flops | bytes accessed | tf_op | source)
XLA Modules:
  0.0 72.8 jit_solution(11039748670792028558)
XLA Ops:
  0.6 1.3 %prepare.1 = (f32[6,64,128]{2,1,0:T(8,128)S(1)}, s32[64,128]{1,0:T(8,128)S(1)}, s32[64,128]{1,0:T(8,128)S(1)}) custom-call(f32[16,16]{1,0:T(8,128)} %refs_1_.1, s32[8]{0:T(128)} %count_ref.1, f32[16,64,128]{2,1,0:T(8,128)} %bitcast.68, f32[64,128]{1,0:T(8,128)} %bitcast.74, f32[64,128]{1,0:T(8,128)} %bitcast.75, s32[8,1024]{1,0:T(8,128)} %index_ref.1), custom_call_target="tpu_custom_call" | custom-call | tf_op jit(solution)/shard_map/prepare/pallas_call | solution.py:482
  1.9 4.9 %collective-permute-start = (f32[6,64,128]{2,1,0:T(8,128)S(1)}, f32[6,64,128]{2,1,0:T(8,128)S(1)}, u32[]{:S(2)}, u32[]{:S(2)}) collective-permute-start(f32[6,64,128]{2,1,0:T(8,128)S(1)} %get-tuple-element.34.own_ref), channel_id=1, source_target_pairs={{0,2},{1,3},{2,4},{3,5},{4,6},{5,7},{8,10},{9,11},{10,12},{11,13},... | collective-permute-start | bytes 589832 | tf_op jit(solution)/shard_map/ppermute | solution.py:434
  6.9 1.3 %collective-permute-start.1 = (f32[6,64,128]{2,1,0:T(8,128)S(1)}, f32[6,64,128]{2,1,0:T(8,128)S(1)}, u32[]{:S(2)}, u32[]{:S(2)}) collective-permute-start(f32[6,64,128]{2,1,0:T(8,128)S(1)} %get-tuple-element.34.own_ref), channel_id=1, source_target_pairs={{2,0},{3,1},{4,2},{5,3},{6,4},{7,5},{10,8},{11,9},{12,10},{13,11},... | collective-permute-start | bytes 589832 | tf_op jit(solution)/shard_map/ppermute | solution.py:434
  8.2 8.9 %slot_sums_and_members.1 = (f32[8,2,8,128]{3,2,1,0:T(8,128)S(1)}, f32[16,64,128]{2,1,0:T(8,128)S(1)}) custom-call(s32[512,128]{1,0:T(8,128)} %bitcast.71, f32[512,128]{1,0:T(8,128)} %bitcast.72, f32[512,128]{1,0:T(8,128)} %bitcast.73, f32[16,16]{1,0:T(8,128)} %refs_0_.1, f32[8,16,64,128]{3,2,1,0:T(8,128)} %bitcast.63, bf16[8,16,64,128]{3,2,1,0:T(8,128)(2,1)} %bitcast.65), custom_call_target="tpu_custom_call" | custom-call | tf_op jit(solution)/shard_map/slot_sums_and_members/pallas_call | solution.py:516
  17.1 0.0 collective-permute-done.before_ref
  17.2 0.0 collective-permute-done.1.after_ref
  17.2 0.1 collective-permute-start.2
  17.3 11.8 %all_to_all.5 = f32[8,2,8,128]{3,2,1,0:T(8,128)S(1)} all-to-all(f32[8,2,8,128]{3,2,1,0:T(8,128)S(1)} %get-tuple-element.37), channel_id=1, replica_groups=mesh['ens'=4,'cols'=8] {'cols'}, dimensions={0} | all-to-all | bytes 131072 | tf_op jit(solution)/shard_map/all_to_all | solution.py:548
  29.1 1.5 %diffuse_forward.1 = (f32[4,64,128]{2,1,0:T(8,128)S(1)}, f32[5,10,32,128]{3,2,1,0:T(8,128)S(1)}) custom-call(f32[6,64,128]{2,1,0:T(8,128)S(1)} %collective-permute-done.before_ref, f32[6,64,128]{2,1,0:T(8,128)S(1)} %get-tuple-element.34.own_ref, f32[6,64,128]{2,1,0:T(8,128)S(1)} %collective-permute-done.1.after_ref, ...), custom_call_target="tpu_custom_call" | custom-call | tf_op jit(solution)/shard_map/diffuse_forward/pallas_call | solution.py:550
  30.6 7.6 %lookup.1 = f32[64,128]{1,0:T(8,128)S(1)} custom-call(f32[1024,128]{1,0:T(8,128)S(1)} %bitcast.60, f32[256,128]{1,0:T(8,128)S(1)} %bitcast.62, s32[64,128]{1,0:T(8,128)S(1)} %get-tuple-element.27.row_ref, s32[64,128]{1,0:T(8,128)S(1)} %get-tuple-element.28.lane_ref), custom_call_target="tpu_custom_call" | custom-call | tf_op jit(solution)/shard_map/lookup/pallas_call | solution.py:562
  38.2 2.5 %collective-permute-start.3 = (f32[3,64,128]{2,1,0:T(8,128)S(1)}, f32[3,64,128]{2,1,0:T(8,128)S(1)}, u32[]{:S(2)}, u32[]{:S(2)}) collective-permute-start(f32[3,64,128]{2,1,0:T(8,128)S(1)} %pad_maximum_fusion.2.refs_0_), channel_id=1, source_target_pairs={{8,0},{16,8},{24,16},{0,24},{9,1},{17,9},{25,17},{1,25},{10,2},{18... | collective-permute-start | bytes 294920 | tf_op jit(solution)/shard_map/ppermute | solution.py:439
  40.7 0.5 collective-permute-start.4
  41.2 0.6 collective-permute-start.5
  41.8 1.9 %collective-permute-done.3.refs_1_ = f32[3,64,128]{2,1,0:T(8,128)S(1)} collective-permute-done((f32[3,64,128]{2,1,0:T(8,128)S(1)}, f32[3,64,128]{2,1,0:T(8,128)S(1)}, u32[]{:S(2)}, u32[]{:S(2)}) %collective-permute-start.3) | collective-permute-done | bytes 98336 | tf_op jit(solution)/shard_map/ppermute | solution.py:439
  43.7 3.3 %collective-permute-done.4.refs_2_ = f32[3,64,128]{2,1,0:T(8,128)S(1)} collective-permute-done((f32[3,64,128]{2,1,0:T(8,128)S(1)}, f32[3,64,128]{2,1,0:T(8,128)S(1)}, u32[]{:S(2)}, u32[]{:S(2)}) %collective-permute-start.4) | collective-permute-done | bytes 98336 | tf_op jit(solution)/shard_map/ppermute | solution.py:439
  47.0 0.0 collective-permute-done.5.refs_3_
  47.0 2.8 %scatter_own.1 = (f32[256,128]{1,0:T(8,128)S(1)}, f32[64,128]{1,0:T(8,128)S(1)}) custom-call(s32[64,128]{1,0:T(8,128)S(1)} %get-tuple-element.27.row_ref, s32[64,128]{1,0:T(8,128)S(1)} %get-tuple-element.28.lane_ref, f32[3,64,128]{2,1,0:T(8,128)S(1)} %pad_maximum_fusion.2.refs_0_, f32[3,64,128]{2,1,0:T(8,128)S(1)} %collective-permute-done.3.refs_1_, ...), custom_call_target="tpu_custom_call" | custom-call | tf_op jit(solution)/shard_map/scatter_own/pallas_call | solution.py:575
  49.8 2.7 %collective-permute-start.6 = (f32[4,64,128]{2,1,0:T(8,128)S(1)}, f32[4,64,128]{2,1,0:T(8,128)S(1)}, u32[]{:S(2)}, u32[]{:S(2)}) collective-permute-start(f32[4,64,128]{2,1,0:T(8,128)S(1)} %bitcast.54), channel_id=1, source_target_pairs={{0,2},{1,3},{2,4},{3,5},{4,6},{5,7},{8,10},{9,11},{10,12},{11,13},... | collective-permute-start | bytes 393224 | tf_op jit(solution)/shard_map/ppermute | solution.py:434
  52.5 1.3 %collective-permute-start.7 = (f32[4,64,128]{2,1,0:T(8,128)S(1)}, f32[4,64,128]{2,1,0:T(8,128)S(1)}, u32[]{:S(2)}, u32[]{:S(2)}) collective-permute-start(f32[4,64,128]{2,1,0:T(8,128)S(1)} %bitcast.55), channel_id=1, source_target_pairs={{2,0},{3,1},{4,2},{5,3},{6,4},{7,5},{10,8},{11,9},{12,10},{13,11},... | collective-permute-start | bytes 393224 | tf_op jit(solution)/shard_map/ppermute | solution.py:434
  53.8 5.6 %scatter_rest.1 = (f32[1024,128]{1,0:T(8,128)S(1)}, f32[16,64,128]{2,1,0:T(8,128)S(1)}, f32[8,16,64,128]{3,2,1,0:T(8,128)S(1)}, bf16[8,16,64,128]{3,2,1,0:T(8,12...) custom-call(s32[64,128]{1,0:T(8,128)S(1)} %get-tuple-element.27.row_ref, ...), custom_call_target="tpu_custom_call" | custom-call | tf_op jit(solution)/shard_map/scatter_rest/pallas_call | solution.py:587
  59.4 0.0 collective-permute-done.6.before_ref
  59.4 0.0 collective-permute-done.7.after_ref
  59.5 0.1 collective-permute-start.8
  59.6 1.5 %collective-permute-done.8.other_ref = f32[2,4,64,128]{3,2,1,0:T(8,128)S(1)} collective-permute-done((f32[2,4,64,128]{3,2,1,0:T(8,128)S(1)}, f32[2,4,64,128]{3,2,1,0:T(8,128)S(1)}, u32[]{:S(2)}, u32[]{:S(2)}) %collective-permute-start.8) | collective-permute-done | bytes 262176 | tf_op jit(solution)/shard_map/ppermute | solution.py:446
  61.1 1.4 %diffuse_adjoint.1.refs_0_ = f32[4,64,128]{2,1,0:T(8,128)S(1)} custom-call(f32[5,10,32,128]{3,2,1,0:T(8,128)S(1)} %get-tuple-element.42.coef_ref, f32[4,64,128]{2,1,0:T(8,128)S(1)} %collective-permute-done.6.before_ref, f32[4,64,128]{2,1,0:T(8,128)S(1)} %bitcast.57, f32[4,64,128]{2,1,0:T(8,128)S(1)} %collective-permute-done.7.after_ref, ...), custom_call_target="tpu_custom_call" | custom-call | tf_op jit(solution)/shard_map/diffuse_adjoint/pallas_call | solution.py:621
  62.5 0.5 collective-permute-start.9
  63.0 1.3 %collective-permute-start.10 = (f32[4,64,128]{2,1,0:T(8,128)S(1)}, f32[4,64,128]{2,1,0:T(8,128)S(1)}, u32[]{:S(2)}, u32[]{:S(2)}) collective-permute-start(f32[4,64,128]{2,1,0:T(8,128)S(1)} %diffuse_adjoint.1.refs_0_), channel_id=1, source_target_pairs={{16,0},{24,8},{0,16},{8,24},{17,1},{25,9},{1,17},{9,25},{18,2},{26... | collective-permute-start | bytes 393224 | tf_op jit(solution)/shard_map/ppermute | solution.py:439
  64.3 1.5 %collective-permute-start.11 = (f32[4,64,128]{2,1,0:T(8,128)S(1)}, f32[4,64,128]{2,1,0:T(8,128)S(1)}, u32[]{:S(2)}, u32[]{:S(2)}) collective-permute-start(f32[4,64,128]{2,1,0:T(8,128)S(1)} %diffuse_adjoint.1.refs_0_), channel_id=1, source_target_pairs={{24,0},{0,8},{8,16},{16,24},{25,1},{1,9},{9,17},{17,25},{26,2},{2,... | collective-permute-start | bytes 393224 | tf_op jit(solution)/shard_map/ppermute | solution.py:439
  65.8 5.6 %members_gradient.1 = f32[8,16,64,128]{3,2,1,0:T(8,128)} custom-call(bf16[256,768]{1,0:T(8,128)(2,1)S(1)} %get-tuple-element.48.matrix_ref, f32[16,64,128]{2,1,0:T(8,128)S(1)} %bitcast.59, f32[8,16,64,128]{3,2,1,0:T(8,128)S(1)} %get-tuple-element.50.control_ref, bf16[8,16,64,128]{3,2,1,0:T(8,128)(2,1)S(1)} %get-tuple-element.51.pert_ref), custom_call_target="tpu_custom_call" | custom-call | tf_op jit(solution)/shard_map/members_gradient/pallas_call | solution.py:633
  71.4 0.0 collective-permute-done.9.refs_1_
  71.4 0.2 collective-permute-done.11.refs_3_
  71.5 1.2 %static_gradient.1 = f32[16,64,128]{2,1,0:T(8,128)} custom-call(bf16[256,768]{1,0:T(8,128)(2,1)S(1)} %get-tuple-element.40.matrix_ref, f32[16,64,128]{2,1,0:T(8,128)S(1)} %get-tuple-element.41.static_ref, f32[4,64,128]{2,1,0:T(8,128)S(1)} %diffuse_adjoint.1.refs_0_, f32[4,64,128]{2,1,0:T(8,128)S(1)} %collective-permute-done.9.refs_1_, ...), custom_call_target="tpu_custom_call" | custom-call | tf_op jit(solution)/shard_map/static_gradient/pallas_call | solution.py:643
  (8 shorter events, 0.1 us)
Async XLA Ops:
  1.9 15.2 %collective-permute-start = (f32[6,64,128]{2,1,0:T(8,128)S(1)}, f32[6,64,128]{2,1,0:T(8,128)S(1)}, u32[]{:S(2)}, u32[]{:S(2)}) collective-permute-start(f32[6,64,128]{2,1,0:T(8,128)S(1)} %get-tuple-element.34.own_ref), channel_id=1, source_target_pairs={{0,2},{1,3},{2,4},{3,5},{4,6},{5,7},{8,10},{9,11},{10,12},{11,13},... | collective-permute-start | bytes 589832 | tf_op jit(solution)/shard_map/ppermute | solution.py:434
  6.9 10.3 %collective-permute-start.1 = (f32[6,64,128]{2,1,0:T(8,128)S(1)}, f32[6,64,128]{2,1,0:T(8,128)S(1)}, u32[]{:S(2)}, u32[]{:S(2)}) collective-permute-start(f32[6,64,128]{2,1,0:T(8,128)S(1)} %get-tuple-element.34.own_ref), channel_id=1, source_target_pairs={{2,0},{3,1},{4,2},{5,3},{6,4},{7,5},{10,8},{11,9},{12,10},{13,11},... | collective-permute-start | bytes 589832 | tf_op jit(solution)/shard_map/ppermute | solution.py:434
  17.2 11.8 %collective-permute-start.2 = (f32[2,6,64,128]{3,2,1,0:T(8,128)S(1)}, f32[2,6,64,128]{3,2,1,0:T(8,128)S(1)}, u32[]{:S(2)}, u32[]{:S(2)}) collective-permute-start(f32[2,6,64,128]{3,2,1,0:T(8,128)S(1)} %pad_maximum_fusion), channel_id=1, source_target_pairs={{0,1},{1,0},{2,3},{3,2},{4,5},{5,4},{6,7},{7,6},{8,9},{9,8},{10,11... | collective-permute-start | bytes 1179656 | tf_op jit(solution)/shard_map/ppermute | solution.py:446
  38.2 5.5 %collective-permute-start.3 = (f32[3,64,128]{2,1,0:T(8,128)S(1)}, f32[3,64,128]{2,1,0:T(8,128)S(1)}, u32[]{:S(2)}, u32[]{:S(2)}) collective-permute-start(f32[3,64,128]{2,1,0:T(8,128)S(1)} %pad_maximum_fusion.2.refs_0_), channel_id=1, source_target_pairs={{8,0},{16,8},{24,16},{0,24},{9,1},{17,9},{25,17},{1,25},{10,2},{18... | collective-permute-start | bytes 294920 | tf_op jit(solution)/shard_map/ppermute | solution.py:439
  40.7 6.3 %collective-permute-start.4 = (f32[3,64,128]{2,1,0:T(8,128)S(1)}, f32[3,64,128]{2,1,0:T(8,128)S(1)}, u32[]{:S(2)}, u32[]{:S(2)}) collective-permute-start(f32[3,64,128]{2,1,0:T(8,128)S(1)} %pad_maximum_fusion.2.refs_0_), channel_id=1, source_target_pairs={{16,0},{24,8},{0,16},{8,24},{17,1},{25,9},{1,17},{9,25},{18,2},{26... | collective-permute-start | bytes 294920 | tf_op jit(solution)/shard_map/ppermute | solution.py:439
  41.2 5.8 %collective-permute-start.5 = (f32[3,64,128]{2,1,0:T(8,128)S(1)}, f32[3,64,128]{2,1,0:T(8,128)S(1)}, u32[]{:S(2)}, u32[]{:S(2)}) collective-permute-start(f32[3,64,128]{2,1,0:T(8,128)S(1)} %pad_maximum_fusion.2.refs_0_), channel_id=1, source_target_pairs={{24,0},{0,8},{8,16},{16,24},{25,1},{1,9},{9,17},{17,25},{26,2},{2,... | collective-permute-start | bytes 294920 | tf_op jit(solution)/shard_map/ppermute | solution.py:439
  49.8 9.6 %collective-permute-start.6 = (f32[4,64,128]{2,1,0:T(8,128)S(1)}, f32[4,64,128]{2,1,0:T(8,128)S(1)}, u32[]{:S(2)}, u32[]{:S(2)}) collective-permute-start(f32[4,64,128]{2,1,0:T(8,128)S(1)} %bitcast.54), channel_id=1, source_target_pairs={{0,2},{1,3},{2,4},{3,5},{4,6},{5,7},{8,10},{9,11},{10,12},{11,13},... | collective-permute-start | bytes 393224 | tf_op jit(solution)/shard_map/ppermute | solution.py:434
  52.5 6.9 %collective-permute-start.7 = (f32[4,64,128]{2,1,0:T(8,128)S(1)}, f32[4,64,128]{2,1,0:T(8,128)S(1)}, u32[]{:S(2)}, u32[]{:S(2)}) collective-permute-start(f32[4,64,128]{2,1,0:T(8,128)S(1)} %bitcast.55), channel_id=1, source_target_pairs={{2,0},{3,1},{4,2},{5,3},{6,4},{7,5},{10,8},{11,9},{12,10},{13,11},... | collective-permute-start | bytes 393224 | tf_op jit(solution)/shard_map/ppermute | solution.py:434
  59.5 1.6 %collective-permute-start.8 = (f32[2,4,64,128]{3,2,1,0:T(8,128)S(1)}, f32[2,4,64,128]{3,2,1,0:T(8,128)S(1)}, u32[]{:S(2)}, u32[]{:S(2)}) collective-permute-start(f32[2,4,64,128]{3,2,1,0:T(8,128)S(1)} %pad_maximum_fusion.1), channel_id=1, source_target_pairs={{0,1},{1,0},{2,3},{3,2},{4,5},{5,4},{6,7},{7,6},{8,9},{9,8},{10,11... | collective-permute-start | bytes 786440 | tf_op jit(solution)/shard_map/ppermute | solution.py:446
  62.5 8.9 %collective-permute-start.9 = (f32[4,64,128]{2,1,0:T(8,128)S(1)}, f32[4,64,128]{2,1,0:T(8,128)S(1)}, u32[]{:S(2)}, u32[]{:S(2)}) collective-permute-start(f32[4,64,128]{2,1,0:T(8,128)S(1)} %diffuse_adjoint.1.refs_0_), channel_id=1, source_target_pairs={{8,0},{16,8},{24,16},{0,24},{9,1},{17,9},{25,17},{1,25},{10,2},{18... | collective-permute-start | bytes 393224 | tf_op jit(solution)/shard_map/ppermute | solution.py:439
  63.0 8.4 %collective-permute-start.10 = (f32[4,64,128]{2,1,0:T(8,128)S(1)}, f32[4,64,128]{2,1,0:T(8,128)S(1)}, u32[]{:S(2)}, u32[]{:S(2)}) collective-permute-start(f32[4,64,128]{2,1,0:T(8,128)S(1)} %diffuse_adjoint.1.refs_0_), channel_id=1, source_target_pairs={{16,0},{24,8},{0,16},{8,24},{17,1},{25,9},{1,17},{9,25},{18,2},{26... | collective-permute-start | bytes 393224 | tf_op jit(solution)/shard_map/ppermute | solution.py:439
  64.3 7.3 %collective-permute-start.11 = (f32[4,64,128]{2,1,0:T(8,128)S(1)}, f32[4,64,128]{2,1,0:T(8,128)S(1)}, u32[]{:S(2)}, u32[]{:S(2)}) collective-permute-start(f32[4,64,128]{2,1,0:T(8,128)S(1)} %diffuse_adjoint.1.refs_0_), channel_id=1, source_target_pairs={{24,0},{0,8},{8,16},{16,24},{25,1},{1,9},{9,17},{17,25},{26,2},{2,... | collective-permute-start | bytes 393224 | tf_op jit(solution)/shard_map/ppermute | solution.py:439

commit v5 on v4

--- a/solution.py
+++ b/solution.py
@@ -10,7 +10,7 @@
 
 NDIFF = 4
 LANES = 128
-FINE = 32
+FINE = 64
 MIB = 1 << 20
 
 f32 = jnp.float32
@@ -166,18 +166,19 @@
         return carry
 
     lax.fori_loop(0, obs_rows // group, step, 0)
-    acc = acc_ref[...]
-    fold_ref[...] = acc + pltpu.roll(acc, LANES - FINE, 1)
+    for t in range(2):
+        terms = acc_ref[:, t * LANES : (t + 1) * LANES]
+        fold_ref[t] = terms + pltpu.roll(terms, FINE, 1)
     per_row = LANES // FINE
     lane = lax.broadcasted_iota(jnp.int32, (coarse // per_row, LANES), 1)
-    weights = jnp.zeros((coarse // per_row, LANES), f32)
-    amounts = jnp.zeros((coarse // per_row, LANES), f32)
-    for c in range(per_row):
-        piece = fold_ref[pl.ds(c, coarse // per_row, stride=per_row), :]
-        here = lane // FINE == c
-        weights = jnp.where(here, pltpu.roll(piece, c * FINE, 1) if c else piece, weights)
-        shift = (c * FINE - 2 * FINE) % LANES
-        amounts = jnp.where(here, pltpu.roll(piece, shift, 1) if shift else piece, amounts)
+    weights, amounts = (
+        jnp.where(
+            lane < FINE,
+            fold_ref[t, pl.ds(0, coarse // per_row, stride=per_row), :],
+            fold_ref[t, pl.ds(1, coarse // per_row, stride=per_row), :],
+        )
+        for t in range(2)
+    )
     for p in range(n_cols):
         out_ref[p, 0] = weights[p * cap_rows : (p + 1) * cap_rows]
         out_ref[p, 1] = amounts[p * cap_rows : (p + 1) * cap_rows]
@@ -238,9 +239,22 @@
     return jnp.where(lane == 0, pltpu.roll(near, 1, 0), near)
 
 
+def rows_of(tiles, plane, rows):
+    at = lax.axis_index("cols")
+    side = len(tiles) // 2
+    out = []
+    for i, tile in enumerate(tiles):
+        for r in range(rows):
+            row = tile[plane, pl.ds(r, tile.shape[1] // rows, stride=rows), :]
+            if i != side:
+                there = at + (i - side)
+                row = jnp.where(jnp.logical_and(there >= 0, there < lax.axis_size("cols")), row, f32(0))
+            out.append(row)
+    return out
+
+
 def diffuse_rows(tiles, level, coef_ref, rows):
-    blocks = tiles[0].shape[1] // rows
-    field = [t[level, pl.ds(r, blocks, stride=rows), :] for t in tiles for r in range(rows)]
+    field = rows_of(tiles, level, rows)
     for step in range(NDIFF):
         field = [
             coef_ref[0, i + step] * field[i]
@@ -263,8 +277,8 @@
     tiles = tiles_of(before_ref, own_ref, after_ref, other_ref)
     blocks = own_ref.shape[1] // rows
     side = len(tiles) // 2
-    north = [t[lev_share, pl.ds(r, blocks, stride=rows), :] for t in tiles for r in range(rows)]
-    east = [t[lev_share + 1, pl.ds(r, blocks, stride=rows), :] for t in tiles for r in range(rows)]
+    north = rows_of(tiles, lev_share, rows)
+    east = rows_of(tiles, lev_share + 1, rows)
     for i in range(1, len(north) - 1):
         south = north[i + 1]
         if (i + 1) % rows == 0 and i < side * rows:
@@ -374,17 +388,14 @@
     out_ref[...] = acc_ref[:, :LANES] + acc_ref[:, LANES:]
 
 
-def scatter_rest_kernel(cap_rows, scale, row_ref, lane_ref, amount_ref, own_ref, *refs):
-    sources, out_ref, kept, matrices, acc_ref, landed, sems = (
-        refs[:5],
-        refs[5],
-        refs[6:9],
-        refs[9:11],
-        refs[11],
-        refs[12:14],
-        refs[14],
-    )
-    copies = [pltpu.make_async_copy(s, t, sems.at[i]) for i, (s, t) in enumerate(zip(sources, (*landed, *kept)))]
+def matrices_kernel(scale, local_ref, root_ref, to_members_ref, to_static_ref):
+    to_members_ref[...] = level_product(local_ref[...] * f32(scale), True)
+    to_static_ref[...] = level_product(root_ref[...], True)
+
+
+def scatter_rest_kernel(cap_rows, row_ref, lane_ref, amount_ref, own_ref, *refs):
+    sources, out_ref, kept, acc_ref, sems = refs[:3], refs[3], refs[4:7], refs[7], refs[8]
+    copies = [pltpu.make_async_copy(s, t, sems.at[i]) for i, (s, t) in enumerate(zip(sources, kept))]
     for copy in copies:
         copy.start()
     cells = out_ref.shape[0]
@@ -410,8 +421,6 @@
         out_ref[to, :] = piece[:, :LANES] + piece[:, LANES:]
     for copy in copies:
         copy.wait()
-    matrices[0][...] = level_product(landed[0][...] * f32(scale), True)
-    matrices[1][...] = level_product(landed[1][...], True)
 
 
 def static_kernel(matrix_ref, static_ref, *refs):
@@ -431,7 +440,7 @@
 
 def shifted(x, by):
     count = lax.axis_size("cols")
-    return lax.ppermute(x, "cols", [(i, i + by) for i in range(count) if 0 <= i + by < count])
+    return lax.ppermute(x, "cols", [(i, (i + by) % count) for i in range(count)])
 
 
 def from_peers(x):
@@ -522,8 +531,8 @@
             pltpu.VMEM((levels, per_level, LANES), f32),
         ],
         scratch_shapes=[
-            pltpu.VMEM((coarse, LANES), f32),
-            pltpu.VMEM((coarse, LANES), f32),
+            pltpu.VMEM((coarse, 4 * FINE), f32),
+            pltpu.VMEM((2, coarse, LANES), f32),
             pltpu.VMEM((size, 3 * size), bf16),
             pltpu.VMEM((share_rows, LANES), jnp.int32),
             pltpu.VMEM((share_rows, LANES), f32),
@@ -556,6 +565,7 @@
             pltpu.VMEM((5, 5 * rows, per_level // rows, LANES), f32),
         ],
         compiler_params=params(8),
+        cost_estimate=pl.CostEstimate(flops=1 << 26, bytes_accessed=1 << 22, transcendentals=0),
         name="diffuse_forward",
     )(before, packed, after, other)
 
@@ -566,6 +576,9 @@
         out_shape=pltpu.VMEM((entry_rows, LANES), f32),
         scratch_shapes=[pltpu.VMEM((cells, 2 * LANES), bf16)],
         compiler_params=params(16),
+        cost_estimate=pl.CostEstimate(
+            flops=4 * cells * LANES * lists * capacity, bytes_accessed=8 * cells * lists * capacity // 4, transcendentals=0
+        ),
         name="lookup",
     )(part.reshape(cells, LANES), increment.reshape(own, LANES), entry_row, entry_lane)
     slots = jnp.swapaxes(slots, 0, 1).reshape(2, entry_rows, LANES)
@@ -584,39 +597,34 @@
     tile = adjoint_own.reshape(lev_share, per_level, LANES)
     tile_before, tile_after = shifted(tile, 2), shifted(tile, -2)
 
-    adjoint, static_here, control_here, pert_here, from_local, from_root = pl.pallas_call(
-        functools.partial(scatter_rest_kernel, cap_rows, member_scale),
-        in_specs=[VMEM] * 4 + [pl.BlockSpec(memory_space=pl.ANY)] * 5,
-        out_specs=[VMEM] * 6,
+    adjoint, static_here, control_here, pert_here = pl.pallas_call(
+        functools.partial(scatter_rest_kernel, cap_rows),
+        in_specs=[VMEM] * 4 + [pl.BlockSpec(memory_space=pl.ANY)] * 3,
+        out_specs=[VMEM] * 4,
         out_shape=[
             pltpu.VMEM((cells, LANES), f32),
             pltpu.VMEM(static.shape, f32),
             pltpu.VMEM(control.shape, f32),
             pltpu.VMEM(pert.shape, bf16),
-            pltpu.VMEM((size, 3 * size), bf16),
-            pltpu.VMEM((size, 3 * size), bf16),
         ],
-        scratch_shapes=[
-            pltpu.VMEM((cells - own, 2 * LANES), f32),
-            pltpu.VMEM((levels, levels), f32),
-            pltpu.VMEM((levels, levels), f32),
-            pltpu.SemaphoreType.DMA((5,)),
-        ],
+        scratch_shapes=[pltpu.VMEM((cells - own, 2 * LANES), f32), pltpu.SemaphoreType.DMA((3,))],
         compiler_params=params(16),
         name="scatter_rest",
-    )(
-        entry_row,
-        entry_lane,
-        amounts,
-        adjoint_own,
-        in_hbm(vertical_local),
-        in_hbm(vertical_root),
-        static,
-        control,
-        pert,
-    )
-    tile_before, tile_after, adjoint = lax.optimization_barrier((tile_before, tile_after, adjoint))
+    )(entry_row, entry_lane, amounts, adjoint_own, static, control, pert)
+    tile_before, tile_after, adjoint, vertical_local, vertical_root = lax.optimization_barrier(
+        (tile_before, tile_after, adjoint, vertical_local, vertical_root)
+    )
     tile_other = swapped(tile, tile_before, tile_after)
+    from_local, from_root = pl.pallas_call(
+        functools.partial(matrices_kernel, member_scale),
+        grid=(1,),
+        in_specs=[whole(levels, levels)] * 2,
+        out_specs=[VMEM] * 2,
+        out_shape=[pltpu.VMEM((size, 3 * size), bf16)] * 2,
+        compiler_params=params(8),
+        name="level_matrices",
+    )(in_hbm(vertical_local), in_hbm(vertical_root))
+    coefs, from_local, from_root = lax.optimization_barrier((coefs, from_local, from_root))
 
     smooth = pl.pallas_call(
         functools.partial(second_diffusion_kernel, rows),

time: 73 us -> 68.6 us (0.940)
  blocking collectives: 11.8 us -> 9.03 us
  waiting for transfers between devices: 6.9 us -> 5.76 us
  starting transfers between devices: 17.2 us -> 16.1 us
    all_to_all x1, blocking collectives: 11.8 us -> 9.03 us  [local(): lax.all_to_all(slots, 'cols', split_axis=0, concat_axis=0, tiled=True)]
    ppermute x2, waiting for transfers between devices: 1.52 us -> 0.27 us  [swapped(): return lax.ppermute(pack, 'cols', [(i, i ^ 1) for i in range(count)])]
    ppermute x4, starting transfers between devices: 10.2 us -> 9.04 us  [shifted(): lax.ppermute(x, 'cols', [(i, (i + by) % count) for i in range(count)])]
    pallas_call x1 -> x2, Pallas kernels: 5.6 us -> 6.25 us  [the longest x1 5 us: local(): pl.pallas_call(functools.partial(scatter_rest_kernel, cap_rows), in_specs...]
  transfers between devices with their start and end apart: 12 -> 12, of which waited for: 4 -> 4; matrix products, arithmetic and copies ran while one was open for 0% -> 0% of each run, Pallas kernels for 28% -> 30%
where the time goes in v5:
time: 68.6 us; the launch traced here: 68.3 us
  Pallas kernels  36.5 us (53%)
  starting transfers between devices  16.1 us (23%)
  blocking collectives  9.03 us (13%)
  waiting for transfers between devices  5.76 us (8%)
  between operations  0.78 us (1%)
    ppermute x4, starting transfers between devices, shifted(): lax.ppermute(x, 'cols', [(i, (i + by) % count) for i in range(count)])  9.04 us
    all_to_all x1, blocking collectives, local(): lax.all_to_all(slots, 'cols', split_axis=0, concat_axis=0, tiled=True)  9.03 us
    pallas_call x1, Pallas kernels, local(): pl.pallas_call(functools.partial(observe_kernel, n_cols, cap_rows, member...  8.86 us
    pallas_call x1, Pallas kernels, local(): pl.pallas_call(functools.partial(lookup_kernel, cap_rows), in_specs=[VMEM...  7.62 us
    ppermute x6, starting transfers between devices, from_peers(): lax.ppermute(x, 'ens', [((i + d) % count, i) for i in range(count)])  6.94 us
    pallas_call x1, Pallas kernels, local(): pl.pallas_call(member_kernel, grid=(members // group,), in_specs=[VMEM] *...  5.57 us
    ppermute x6, waiting for transfers between devices, from_peers(): lax.ppermute(x, 'ens', [((i + d) % count, i) for i in range(count)])  5.48 us
    pallas_call x1, Pallas kernels, local(): pl.pallas_call(functools.partial(scatter_rest_kernel, cap_rows), in_specs...  5 us
  transfers between devices with their start and end apart: 12, of which 4 were waited for; matrix products, arithmetic and copies ran while one was open for 0% of the time, Pallas kernels for 30%

profile of v5, /device:TPU:0, one launch (start us, length us, event | category | flops | bytes accessed | tf_op | source)
XLA Modules:
  0.0 68.3 jit_solution(7172166535315022215)
XLA Ops:
  0.6 1.3 %prepare.1 = (f32[6,64,128]{2,1,0:T(8,128)S(1)}, s32[64,128]{1,0:T(8,128)S(1)}, s32[64,128]{1,0:T(8,128)S(1)}) custom-call(f32[16,16]{1,0:T(8,128)} %root_ref.2, s32[8]{0:T(128)} %count_ref.1, f32[16,64,128]{2,1,0:T(8,128)} %bitcast.68, f32[64,128]{1,0:T(8,128)} %bitcast.74, f32[64,128]{1,0:T(8,128)} %bitcast.75, s32[8,1024]{1,0:T(8,128)} %index_ref.1), custom_call_target="tpu_custom_call" | custom-call | tf_op jit(solution)/shard_map/prepare/pallas_call | solution.py:491
  1.9 3.1 %collective-permute-start = (f32[6,64,128]{2,1,0:T(8,128)S(1)}, f32[6,64,128]{2,1,0:T(8,128)S(1)}, u32[]{:S(2)}, u32[]{:S(2)}) collective-permute-start(f32[6,64,128]{2,1,0:T(8,128)S(1)} %get-tuple-element.36.own_ref), channel_id=1, source_target_pairs={{0,2},{1,3},{2,4},{3,5},{4,6},{5,7},{6,0},{7,1},{8,10},{9,11},{10,... | collective-permute-start | bytes 589832 | tf_op jit(solution)/shard_map/ppermute | solution.py:443
  5.0 2.1 %collective-permute-start.1 = (f32[6,64,128]{2,1,0:T(8,128)S(1)}, f32[6,64,128]{2,1,0:T(8,128)S(1)}, u32[]{:S(2)}, u32[]{:S(2)}) collective-permute-start(f32[6,64,128]{2,1,0:T(8,128)S(1)} %get-tuple-element.36.own_ref), channel_id=1, source_target_pairs={{0,6},{1,7},{2,0},{3,1},{4,2},{5,3},{6,4},{7,5},{8,14},{9,15},{10,... | collective-permute-start | bytes 589832 | tf_op jit(solution)/shard_map/ppermute | solution.py:443
  7.1 8.9 %slot_sums_and_members.1 = (f32[8,2,8,128]{3,2,1,0:T(8,128)S(1)}, f32[16,64,128]{2,1,0:T(8,128)S(1)}) custom-call(s32[512,128]{1,0:T(8,128)} %bitcast.71, f32[512,128]{1,0:T(8,128)} %bitcast.72, f32[512,128]{1,0:T(8,128)} %bitcast.73, f32[16,16]{1,0:T(8,128)} %local_ref, f32[8,16,64,128]{3,2,1,0:T(8,128)} %bitcast.63, bf16[8,16,64,128]{3,2,1,0:T(8,128)(2,1)} %bitcast.65), custom_call_target="tpu_custom_call" | custom-call | tf_op jit(solution)/shard_map/slot_sums_and_members/pallas_call | solution.py:525
  16.0 0.0 collective-permute-done.before_ref
  16.1 0.1 collective-permute-start.2
  16.1 9.0 %all_to_all.5 = f32[8,2,8,128]{3,2,1,0:T(8,128)S(1)} all-to-all(f32[8,2,8,128]{3,2,1,0:T(8,128)S(1)} %get-tuple-element.43), channel_id=1, replica_groups=mesh['ens'=4,'cols'=8] {'cols'}, dimensions={0} | all-to-all | bytes 131072 | tf_op jit(solution)/shard_map/all_to_all | solution.py:557
  25.2 1.5 %diffuse_forward.1 = (f32[4,64,128]{2,1,0:T(8,128)S(1)}, f32[5,10,32,128]{3,2,1,0:T(8,128)S(1)}) custom-call(f32[6,64,128]{2,1,0:T(8,128)S(1)} %collective-permute-done.before_ref, f32[6,64,128]{2,1,0:T(8,128)S(1)} %get-tuple-element.36.own_ref, f32[6,64,128]{2,1,0:T(8,128)S(1)} %collective-permute-done.1.after_ref, ...), custom_call_target="tpu_custom_call" | custom-call | flops 67108864 | bytes 4194304 | tf_op jit(solution)/shard_map/diffuse_forward/pallas_call | solution.py:559
  26.7 7.6 %lookup.1 = f32[64,128]{1,0:T(8,128)S(1)} custom-call(f32[1024,128]{1,0:T(8,128)S(1)} %bitcast.61, f32[256,128]{1,0:T(8,128)S(1)} %bitcast.62, s32[64,128]{1,0:T(8,128)S(1)} %get-tuple-element.39.row_ref, s32[64,128]{1,0:T(8,128)S(1)} %get-tuple-element.40.lane_ref), custom_call_target="tpu_custom_call" | custom-call | flops 4294967296 | bytes 16777216 | tf_op jit(solution)/shard_map/lookup/pallas_call | solution.py:572
  34.3 2.5 %collective-permute-start.3 = (f32[3,64,128]{2,1,0:T(8,128)S(1)}, f32[3,64,128]{2,1,0:T(8,128)S(1)}, u32[]{:S(2)}, u32[]{:S(2)}) collective-permute-start(f32[3,64,128]{2,1,0:T(8,128)S(1)} %pad_maximum_fusion.2.refs_0_), channel_id=1, source_target_pairs={{8,0},{16,8},{24,16},{0,24},{9,1},{17,9},{25,17},{1,25},{10,2},{18... | collective-permute-start | bytes 294920 | tf_op jit(solution)/shard_map/ppermute | solution.py:448
  36.8 0.5 collective-permute-start.4
  37.4 0.6 collective-permute-start.5
  37.9 1.9 %collective-permute-done.3.refs_1_ = f32[3,64,128]{2,1,0:T(8,128)S(1)} collective-permute-done((f32[3,64,128]{2,1,0:T(8,128)S(1)}, f32[3,64,128]{2,1,0:T(8,128)S(1)}, u32[]{:S(2)}, u32[]{:S(2)}) %collective-permute-start.3) | collective-permute-done | bytes 98336 | tf_op jit(solution)/shard_map/ppermute | solution.py:448
  39.8 3.3 %collective-permute-done.4.refs_2_ = f32[3,64,128]{2,1,0:T(8,128)S(1)} collective-permute-done((f32[3,64,128]{2,1,0:T(8,128)S(1)}, f32[3,64,128]{2,1,0:T(8,128)S(1)}, u32[]{:S(2)}, u32[]{:S(2)}) %collective-permute-start.4) | collective-permute-done | bytes 98336 | tf_op jit(solution)/shard_map/ppermute | solution.py:448
  43.1 0.0 collective-permute-done.5.refs_3_
  43.1 2.8 %scatter_own.1 = (f32[256,128]{1,0:T(8,128)S(1)}, f32[64,128]{1,0:T(8,128)S(1)}) custom-call(s32[64,128]{1,0:T(8,128)S(1)} %get-tuple-element.39.row_ref, s32[64,128]{1,0:T(8,128)S(1)} %get-tuple-element.40.lane_ref, f32[3,64,128]{2,1,0:T(8,128)S(1)} %pad_maximum_fusion.2.refs_0_, f32[3,64,128]{2,1,0:T(8,128)S(1)} %collective-permute-done.3.refs_1_, ...), custom_call_target="tpu_custom_call" | custom-call | tf_op jit(solution)/shard_map/scatter_own/pallas_call | solution.py:588
  46.0 0.8 %collective-permute-start.6 = (f32[4,64,128]{2,1,0:T(8,128)S(1)}, f32[4,64,128]{2,1,0:T(8,128)S(1)}, u32[]{:S(2)}, u32[]{:S(2)}) collective-permute-start(f32[4,64,128]{2,1,0:T(8,128)S(1)} %bitcast.54), channel_id=1, source_target_pairs={{0,2},{1,3},{2,4},{3,5},{4,6},{5,7},{6,0},{7,1},{8,10},{9,11},{10,... | collective-permute-start | bytes 393224 | tf_op jit(solution)/shard_map/ppermute | solution.py:443
  46.8 3.0 %collective-permute-start.7 = (f32[4,64,128]{2,1,0:T(8,128)S(1)}, f32[4,64,128]{2,1,0:T(8,128)S(1)}, u32[]{:S(2)}, u32[]{:S(2)}) collective-permute-start(f32[4,64,128]{2,1,0:T(8,128)S(1)} %bitcast.55), channel_id=1, source_target_pairs={{0,6},{1,7},{2,0},{3,1},{4,2},{5,3},{6,4},{7,5},{8,14},{9,15},{10,... | collective-permute-start | bytes 393224 | tf_op jit(solution)/shard_map/ppermute | solution.py:443
  49.8 5.0 %scatter_rest.1 = (f32[1024,128]{1,0:T(8,128)S(1)}, f32[16,64,128]{2,1,0:T(8,128)S(1)}, f32[8,16,64,128]{3,2,1,0:T(8,128)S(1)}, bf16[8,16,64,128]{3,2,1,0:T(8,128)(2,1)S(1)}) custom-call(s32[64,128]{1,0:T(8,128)S(1)} %get-tuple-element.39.row_ref, s32[64,128]{1,0:T(8,128)S(1)} %get-tuple-element.40.lane_ref, f32[64,128]{1,0:T(8,128)S(1)} %get-tuple-element.45.amount_ref, ...), custom_call_target="tpu_custom_call" | custom-call | tf_op jit(solution)/shard_map/scatter_rest/pallas_call | solution.py:600
  54.9 0.0 collective-permute-done.7.after_ref
  54.9 0.1 collective-permute-start.8
  55.0 1.3 %level_matrices.1 = (bf16[256,768]{1,0:T(8,128)(2,1)S(1)}, bf16[256,768]{1,0:T(8,128)(2,1)S(1)}) custom-call(f32[16,16]{1,0:T(8,128)} %local_ref, f32[16,16]{1,0:T(8,128)} %root_ref.2), custom_call_target="tpu_custom_call" | custom-call | tf_op jit(solution)/shard_map/level_matrices/pallas_call | solution.py:618
  56.3 0.3 collective-permute-done.8.other_ref
  56.5 1.4 %diffuse_adjoint.1.refs_0_ = f32[4,64,128]{2,1,0:T(8,128)S(1)} custom-call(f32[5,10,32,128]{3,2,1,0:T(8,128)S(1)} %get-tuple-element.53.coef_ref, f32[4,64,128]{2,1,0:T(8,128)S(1)} %collective-permute-done.6.before_ref, f32[4,64,128]{2,1,0:T(8,128)S(1)} %bitcast.57, f32[4,64,128]{2,1,0:T(8,128)S(1)} %collective-permute-done.7.after_ref, ...), custom_call_target="tpu_custom_call" | custom-call | tf_op jit(solution)/shard_map/diffuse_adjoint/pallas_call | solution.py:629
  57.9 0.5 collective-permute-start.9
  58.4 1.2 %collective-permute-start.10 = (f32[4,64,128]{2,1,0:T(8,128)S(1)}, f32[4,64,128]{2,1,0:T(8,128)S(1)}, u32[]{:S(2)}, u32[]{:S(2)}) collective-permute-start(f32[4,64,128]{2,1,0:T(8,128)S(1)} %diffuse_adjoint.1.refs_0_), channel_id=1, source_target_pairs={{16,0},{24,8},{0,16},{8,24},{17,1},{25,9},{1,17},{9,25},{18,2},{26... | collective-permute-start | bytes 393224 | tf_op jit(solution)/shard_map/ppermute | solution.py:448
  59.6 1.6 %collective-permute-start.11 = (f32[4,64,128]{2,1,0:T(8,128)S(1)}, f32[4,64,128]{2,1,0:T(8,128)S(1)}, u32[]{:S(2)}, u32[]{:S(2)}) collective-permute-start(f32[4,64,128]{2,1,0:T(8,128)S(1)} %diffuse_adjoint.1.refs_0_), channel_id=1, source_target_pairs={{24,0},{0,8},{8,16},{16,24},{25,1},{1,9},{9,17},{17,25},{26,2},{2,... | collective-permute-start | bytes 393224 | tf_op jit(solution)/shard_map/ppermute | solution.py:448
  61.2 5.6 %members_gradient.1 = f32[8,16,64,128]{3,2,1,0:T(8,128)} custom-call(bf16[256,768]{1,0:T(8,128)(2,1)S(1)} %get-tuple-element.58.matrix_ref, f32[16,64,128]{2,1,0:T(8,128)S(1)} %bitcast.59, f32[8,16,64,128]{3,2,1,0:T(8,128)S(1)} %get-tuple-element.60.control_ref, bf16[8,16,64,128]{3,2,1,0:T(8,128)(2,1)S(1)} %get-tuple-element.61.pert_ref), custom_call_target="tpu_custom_call" | custom-call | tf_op jit(solution)/shard_map/members_gradient/pallas_call | solution.py:641
  66.8 0.0 collective-permute-done.9.refs_1_
  66.8 0.0 collective-permute-done.10.refs_2_
  66.8 0.3 collective-permute-done.11.refs_3_
  67.1 1.2 %static_gradient.1 = f32[16,64,128]{2,1,0:T(8,128)} custom-call(bf16[256,768]{1,0:T(8,128)(2,1)S(1)} %get-tuple-element.51.matrix_ref, f32[16,64,128]{2,1,0:T(8,128)S(1)} %get-tuple-element.52.static_ref, f32[4,64,128]{2,1,0:T(8,128)S(1)} %diffuse_adjoint.1.refs_0_, f32[4,64,128]{2,1,0:T(8,128)S(1)} %collective-permute-done.9.refs_1_, ...), custom_call_target="tpu_custom_call" | custom-call | tf_op jit(solution)/shard_map/static_gradient/pallas_call | solution.py:651
  (9 shorter events, 0.1 us)
Async XLA Ops:
  1.9 14.0 %collective-permute-start = (f32[6,64,128]{2,1,0:T(8,128)S(1)}, f32[6,64,128]{2,1,0:T(8,128)S(1)}, u32[]{:S(2)}, u32[]{:S(2)}) collective-permute-start(f32[6,64,128]{2,1,0:T(8,128)S(1)} %get-tuple-element.36.own_ref), channel_id=1, source_target_pairs={{0,2},{1,3},{2,4},{3,5},{4,6},{5,7},{6,0},{7,1},{8,10},{9,11},{10,... | collective-permute-start | bytes 589832 | tf_op jit(solution)/shard_map/ppermute | solution.py:443
  5.0 11.0 %collective-permute-start.1 = (f32[6,64,128]{2,1,0:T(8,128)S(1)}, f32[6,64,128]{2,1,0:T(8,128)S(1)}, u32[]{:S(2)}, u32[]{:S(2)}) collective-permute-start(f32[6,64,128]{2,1,0:T(8,128)S(1)} %get-tuple-element.36.own_ref), channel_id=1, source_target_pairs={{0,6},{1,7},{2,0},{3,1},{4,2},{5,3},{6,4},{7,5},{8,14},{9,15},{10,... | collective-permute-start | bytes 589832 | tf_op jit(solution)/shard_map/ppermute | solution.py:443
  16.1 9.1 %collective-permute-start.2 = (f32[2,6,64,128]{3,2,1,0:T(8,128)S(1)}, f32[2,6,64,128]{3,2,1,0:T(8,128)S(1)}, u32[]{:S(2)}, u32[]{:S(2)}) collective-permute-start(f32[2,6,64,128]{3,2,1,0:T(8,128)S(1)} %pad_maximum_fusion), channel_id=1, source_target_pairs={{0,1},{1,0},{2,3},{3,2},{4,5},{5,4},{6,7},{7,6},{8,9},{9,8},{10,11... | collective-permute-start | bytes 1179656 | tf_op jit(solution)/shard_map/ppermute | solution.py:455
  34.3 5.5 %collective-permute-start.3 = (f32[3,64,128]{2,1,0:T(8,128)S(1)}, f32[3,64,128]{2,1,0:T(8,128)S(1)}, u32[]{:S(2)}, u32[]{:S(2)}) collective-permute-start(f32[3,64,128]{2,1,0:T(8,128)S(1)} %pad_maximum_fusion.2.refs_0_), channel_id=1, source_target_pairs={{8,0},{16,8},{24,16},{0,24},{9,1},{17,9},{25,17},{1,25},{10,2},{18... | collective-permute-start | bytes 294920 | tf_op jit(solution)/shard_map/ppermute | solution.py:448
  36.8 6.3 %collective-permute-start.4 = (f32[3,64,128]{2,1,0:T(8,128)S(1)}, f32[3,64,128]{2,1,0:T(8,128)S(1)}, u32[]{:S(2)}, u32[]{:S(2)}) collective-permute-start(f32[3,64,128]{2,1,0:T(8,128)S(1)} %pad_maximum_fusion.2.refs_0_), channel_id=1, source_target_pairs={{16,0},{24,8},{0,16},{8,24},{17,1},{25,9},{1,17},{9,25},{18,2},{26... | collective-permute-start | bytes 294920 | tf_op jit(solution)/shard_map/ppermute | solution.py:448
  37.4 5.8 %collective-permute-start.5 = (f32[3,64,128]{2,1,0:T(8,128)S(1)}, f32[3,64,128]{2,1,0:T(8,128)S(1)}, u32[]{:S(2)}, u32[]{:S(2)}) collective-permute-start(f32[3,64,128]{2,1,0:T(8,128)S(1)} %pad_maximum_fusion.2.refs_0_), channel_id=1, source_target_pairs={{24,0},{0,8},{8,16},{16,24},{25,1},{1,9},{9,17},{17,25},{26,2},{2,... | collective-permute-start | bytes 294920 | tf_op jit(solution)/shard_map/ppermute | solution.py:448
  46.0 8.9 %collective-permute-start.6 = (f32[4,64,128]{2,1,0:T(8,128)S(1)}, f32[4,64,128]{2,1,0:T(8,128)S(1)}, u32[]{:S(2)}, u32[]{:S(2)}) collective-permute-start(f32[4,64,128]{2,1,0:T(8,128)S(1)} %bitcast.54), channel_id=1, source_target_pairs={{0,2},{1,3},{2,4},{3,5},{4,6},{5,7},{6,0},{7,1},{8,10},{9,11},{10,... | collective-permute-start | bytes 393224 | tf_op jit(solution)/shard_map/ppermute | solution.py:443
  46.8 8.1 %collective-permute-start.7 = (f32[4,64,128]{2,1,0:T(8,128)S(1)}, f32[4,64,128]{2,1,0:T(8,128)S(1)}, u32[]{:S(2)}, u32[]{:S(2)}) collective-permute-start(f32[4,64,128]{2,1,0:T(8,128)S(1)} %bitcast.55), channel_id=1, source_target_pairs={{0,6},{1,7},{2,0},{3,1},{4,2},{5,3},{6,4},{7,5},{8,14},{9,15},{10,... | collective-permute-start | bytes 393224 | tf_op jit(solution)/shard_map/ppermute | solution.py:443
  54.9 1.6 %collective-permute-start.8 = (f32[2,4,64,128]{3,2,1,0:T(8,128)S(1)}, f32[2,4,64,128]{3,2,1,0:T(8,128)S(1)}, u32[]{:S(2)}, u32[]{:S(2)}) collective-permute-start(f32[2,4,64,128]{3,2,1,0:T(8,128)S(1)} %pad_maximum_fusion.1), channel_id=1, source_target_pairs={{0,1},{1,0},{2,3},{3,2},{4,5},{5,4},{6,7},{7,6},{8,9},{9,8},{10,11... | collective-permute-start | bytes 786440 | tf_op jit(solution)/shard_map/ppermute | solution.py:455
  57.9 8.9 %collective-permute-start.9 = (f32[4,64,128]{2,1,0:T(8,128)S(1)}, f32[4,64,128]{2,1,0:T(8,128)S(1)}, u32[]{:S(2)}, u32[]{:S(2)}) collective-permute-start(f32[4,64,128]{2,1,0:T(8,128)S(1)} %diffuse_adjoint.1.refs_0_), channel_id=1, source_target_pairs={{8,0},{16,8},{24,16},{0,24},{9,1},{17,9},{25,17},{1,25},{10,2},{18... | collective-permute-start | bytes 393224 | tf_op jit(solution)/shard_map/ppermute | solution.py:448
  58.4 8.4 %collective-permute-start.10 = (f32[4,64,128]{2,1,0:T(8,128)S(1)}, f32[4,64,128]{2,1,0:T(8,128)S(1)}, u32[]{:S(2)}, u32[]{:S(2)}) collective-permute-start(f32[4,64,128]{2,1,0:T(8,128)S(1)} %diffuse_adjoint.1.refs_0_), channel_id=1, source_target_pairs={{16,0},{24,8},{0,16},{8,24},{17,1},{25,9},{1,17},{9,25},{18,2},{26... | collective-permute-start | bytes 393224 | tf_op jit(solution)/shard_map/ppermute | solution.py:448
  59.6 7.5 %collective-permute-start.11 = (f32[4,64,128]{2,1,0:T(8,128)S(1)}, f32[4,64,128]{2,1,0:T(8,128)S(1)}, u32[]{:S(2)}, u32[]{:S(2)}) collective-permute-start(f32[4,64,128]{2,1,0:T(8,128)S(1)} %diffuse_adjoint.1.refs_0_), channel_id=1, source_target_pairs={{24,0},{0,8},{8,16},{16,24},{25,1},{1,9},{9,17},{17,25},{26,2},{2,... | collective-permute-start | bytes 393224 | tf_op jit(solution)/shard_map/ppermute | solution.py:448

commit v6 on v5

--- a/solution.py
+++ b/solution.py
@@ -57,6 +57,21 @@
     where = matches(index, count)
     amount = bf16(1) if amount is None else spread(amount, bf16)[None]
     return jnp.where(where, amount, bf16(0)).reshape(count, index.shape[1])
+
+
+def in_turns(count, build, use, slots):
+    build(0, slots[0])
+
+    def step(i, carry):
+        use(2 * i, slots[0])
+        build(2 * i + 1, slots[1])
+        use(2 * i + 1, slots[1])
+        build(jnp.minimum(2 * i + 2, count - 1), slots[0])
+        return carry
+
+    lax.fori_loop(0, count // 2, step, 0)
+    if count % 2:
+        use(count - 1, slots[0])
 
 
 def product_nt(left, right):
@@ -120,12 +135,13 @@
 
 
 def observe_kernel(n_cols, cap_rows, scale, *refs):
-    sources, (out_ref, part_ref), (acc_ref, fold_ref, matrix_ref), landed, sems = (
+    sources, (out_ref, part_ref), (acc_ref, fold_ref, matrix_ref), landed, sems, slots = (
         refs[:6],
         refs[6:8],
         refs[8:11],
         refs[11:17],
         refs[17],
+        (refs[18:20], refs[20:22]),
     )
     coarse = acc_ref.shape[0]
     obs_rows = landed[0].shape[0]
@@ -142,30 +158,24 @@
         copy.wait()
     slot_ref, weight_ref, innov_ref, local_ref, control_ref, pert_ref = landed
 
-    def step(i, carry):
+    def build(i, to):
         at = pl.ds(pl.multiple_of(i * group, group), group)
-        slot = slot_ref[at, :]
         weight = weight_ref[at, :]
         amount = weight * innov_ref[at, :]
-        upper, lower = over(slot, FINE)
+        upper, lower = over(slot_ref[at, :], FINE)
         terms = [t.astype(f32) for t in halves(weight) + halves(amount)]
-        left, right = [], []
         for r in range(group):
-            left.append(placed_at(upper[r : r + 1, :], coarse))
+            here = slice(r * LANES, (r + 1) * LANES)
+            to[0][:, here] = placed_at(upper[r : r + 1, :], coarse)
             mask = matches(lower[r : r + 1, :], FINE)
-            right.append(
-                jnp.concatenate(
-                    [
-                        jnp.where(mask, spread(t[r : r + 1, :], bf16)[None], bf16(0)).reshape(FINE, LANES)
-                        for t in terms
-                    ],
-                    axis=0,
-                )
-            )
-        acc_ref[...] += product_nt(jnp.concatenate(left, axis=1), jnp.concatenate(right, axis=1))
-        return carry
-
-    lax.fori_loop(0, obs_rows // group, step, 0)
+            for t, term in enumerate(terms):
+                term = spread(term[r : r + 1, :], bf16)[None]
+                to[1][t * FINE : (t + 1) * FINE, here] = jnp.where(mask, term, bf16(0)).reshape(FINE, LANES)
+
+    def use(i, of):
+        acc_ref[...] += product_nt(of[0][...], of[1][...])
+
+    in_turns(obs_rows // group, build, use, slots)
     for t in range(2):
         terms = acc_ref[:, t * LANES : (t + 1) * LANES]
         fold_ref[t] = terms + pltpu.roll(terms, FINE, 1)
@@ -179,9 +189,10 @@
         )
         for t in range(2)
     )
-    for p in range(n_cols):
-        out_ref[p, 0] = weights[p * cap_rows : (p + 1) * cap_rows]
-        out_ref[p, 1] = amounts[p * cap_rows : (p + 1) * cap_rows]
+    for e in range(out_ref.shape[0] // n_cols):
+        for p in range(n_cols):
+            out_ref[e * n_cols + p, 0] = weights[p * cap_rows : (p + 1) * cap_rows]
+            out_ref[e * n_cols + p, 1] = amounts[p * cap_rows : (p + 1) * cap_rows]
     for copy in copies[3:]:
         copy.wait()
     matrix_ref[...] = level_product(local_ref[...] * f32(scale), False)
@@ -316,10 +327,9 @@
     lax.fori_loop(0, lev_share, body, 0)
 
 
-def lookup_kernel(cap_rows, part_ref, static_ref, row_ref, lane_ref, out_ref, terms_ref):
+def lookup_kernel(cap_rows, part_ref, static_ref, row_ref, lane_ref, out_ref, terms_ref, *slots):
     cells = part_ref.shape[0]
     own = static_ref.shape[0]
-    n_lists = row_ref.shape[0] // cap_rows
     at = pl.ds(pl.multiple_of(lax.axis_index("ens") * own, own), own)
     for here, field in ((slice(None), part_ref[...]), (at, part_ref[at, :] + static_ref[...])):
         high, low = halves(field)
@@ -329,16 +339,18 @@
     ids = lax.broadcasted_iota(jnp.int32, (LANES, LANES), 1)
     diagonal = ids == lax.broadcasted_iota(jnp.int32, (LANES, LANES), 0)
 
-    def look(q, carry):
+    def build(q, to):
         at = pl.ds(pl.multiple_of(q * cap_rows, cap_rows), cap_rows)
         rows = row_ref[at, :].astype(f32).T
-        lanes = lane_ref[at, :].astype(f32).T
-        picks = []
         for c in range(cap_rows):
             column = jnp.broadcast_to(rows[:, c : c + 1], (LANES, LANES)).astype(jnp.int32).astype(jnp.int16)
             column = jnp.concatenate([column] * (cells // LANES), axis=1)
-            picks.append(jnp.where(ids16 == column, bf16(1), bf16(0)))
-        got = jnp.dot(jnp.concatenate(picks, axis=0), terms_ref[...], preferred_element_type=f32)
+            to[c * LANES : (c + 1) * LANES, :] = jnp.where(ids16 == column, bf16(1), bf16(0))
+
+    def use(q, of):
+        at = pl.ds(pl.multiple_of(q * cap_rows, cap_rows), cap_rows)
+        lanes = lane_ref[at, :].astype(f32).T
+        got = jnp.dot(of[...], terms_ref[...], preferred_element_type=f32)
         values = []
         for c in range(cap_rows):
             mask = ids == jnp.broadcast_to(lanes[:, c : c + 1], (LANES, LANES)).astype(jnp.int32)
@@ -346,45 +358,44 @@
             found = jnp.sum(jnp.where(mask, mine[:, :LANES] + mine[:, LANES:], f32(0)), axis=1, keepdims=True)
             values.append(jnp.sum(jnp.where(diagonal, found, f32(0)), axis=0, keepdims=True))
         out_ref[at, :] = jnp.concatenate(values, axis=0)
-        return carry
-
-    lax.fori_loop(0, n_lists, look, 0)
-
-
-def put(acc_ref, rows, lanes, amounts):
-    high, low = (h.astype(f32) for h in halves(amounts))
-    left, right = [], []
+
+    in_turns(row_ref.shape[0] // cap_rows, build, use, slots)
+
+
+def put(to, rows, lanes, amounts):
+    count = to[0].shape[0]
+    terms = [h.astype(f32) for h in halves(amounts)]
     for c in range(rows.shape[0]):
-        piece = slice(c, c + 1)
-        left.append(placed_at(rows[piece, :], acc_ref.shape[0]))
-        mask = matches(lanes[piece, :], LANES)
-        right.append(
-            jnp.concatenate(
-                [
-                    jnp.where(mask, spread(h[piece, :], bf16)[None], bf16(0)).reshape(LANES, LANES)
-                    for h in (high, low)
-                ],
-                axis=0,
-            )
-        )
-    acc_ref[...] += product_nt(jnp.concatenate(left, axis=1), jnp.concatenate(right, axis=1))
-
-
-def scatter_own_kernel(cap_rows, row_ref, lane_ref, *refs):
-    shares, (out_ref, amount_ref, acc_ref) = refs[:-3], refs[-3:]
+        here = slice(c * LANES, (c + 1) * LANES)
+        to[0][:, here] = placed_at(rows[c : c + 1, :], count)
+        mask = matches(lanes[c : c + 1, :], LANES)
+        for t, term in enumerate(terms):
+            term = spread(term[c : c + 1, :], bf16)[None]
+            to[1][t * LANES : (t + 1) * LANES, here] = jnp.where(mask, term, bf16(0)).reshape(LANES, LANES)
+
+
+def scatter_own_kernel(cap_rows, row_ref, lane_ref, slots_ref, *refs):
+    values, (out_ref, amount_ref, acc_ref), slots = refs[:-7], refs[-7:-4], (refs[-4:-2], refs[-2:])
+    n_ens = len(values)
     own = out_ref.shape[0]
+    lists = row_ref.shape[0] // cap_rows
     first = lax.axis_index("ens") * own
     acc_ref[...] = jnp.zeros_like(acc_ref)
 
-    def step(q, carry):
+    def build(q, to):
         at = pl.ds(pl.multiple_of(q * cap_rows, cap_rows), cap_rows)
-        value, weight, amount = (functools.reduce(jnp.add, [s[t, at, :] for s in shares]) for t in range(3))
+        value = functools.reduce(jnp.add, [v[at, :] for v in values])
+        weight, amount = (
+            functools.reduce(jnp.add, [slots_ref[e * lists + q, t] for e in range(n_ens)]) for t in range(2)
+        )
         amounts = value * weight - amount
         amount_ref[at, :] = amounts
-        put(acc_ref, row_ref[at, :] - first, lane_ref[at, :], amounts)
-        return carry
-
-    lax.fori_loop(0, row_ref.shape[0] // cap_rows, step, 0)
+        put(to, row_ref[at, :] - first, lane_ref[at, :], amounts)
+
+    def use(q, of):
+        acc_ref[...] += product_nt(of[0][...], of[1][...])
+
+    in_turns(lists, build, use, slots)
     out_ref[...] = acc_ref[:, :LANES] + acc_ref[:, LANES:]
 
 
@@ -394,7 +405,14 @@
 
 
 def scatter_rest_kernel(cap_rows, row_ref, lane_ref, amount_ref, own_ref, *refs):
-    sources, out_ref, kept, acc_ref, sems = refs[:3], refs[3], refs[4:7], refs[7], refs[8]
+    sources, out_ref, kept, acc_ref, sems, slots = (
+        refs[:3],
+        refs[3],
+        refs[4:7],
+        refs[7],
+        refs[8],
+        (refs[9:11], refs[11:13]),
+    )
     copies = [pltpu.make_async_copy(s, t, sems.at[i]) for i, (s, t) in enumerate(zip(sources, kept))]
     for copy in copies:
         copy.start()
@@ -405,15 +423,17 @@
     first = (me + 1) * own
     acc_ref[...] = jnp.zeros_like(acc_ref)
 
-    def step(q, carry):
+    def build(q, to):
         at = pl.ds(pl.multiple_of(q * cap_rows, cap_rows), cap_rows)
         row = row_ref[at, :]
         turned = row - first
         turned = jnp.where(row < 0, -1, jnp.where(turned < 0, turned + cells, turned))
-        put(acc_ref, turned, lane_ref[at, :], amount_ref[at, :])
-        return carry
-
-    lax.fori_loop(0, row_ref.shape[0] // cap_rows, step, 0)
+        put(to, turned, lane_ref[at, :], amount_ref[at, :])
+
+    def use(q, of):
+        acc_ref[...] += product_nt(of[0][...], of[1][...])
+
+    in_turns(row_ref.shape[0] // cap_rows, build, use, slots)
     out_ref[pl.ds(pl.multiple_of(me * own, own), own), :] = own_ref[...]
     for t in range(1, n_ens):
         to = pl.ds(pl.multiple_of((me + t) % n_ens * own, own), own)
@@ -524,10 +544,11 @@
     obs_slot, packed = lax.optimization_barrier((obs_slot, packed))
     slots, part = pl.pallas_call(
         functools.partial(observe_kernel, n_cols, cap_rows, member_scale),
+        grid=(1,),
         in_specs=[pl.BlockSpec(memory_space=pl.ANY)] * 6,
-        out_specs=[VMEM] * 2,
+        out_specs=[whole(n_ens * n_cols, 2, cap_rows, LANES), VMEM],
         out_shape=[
-            pltpu.VMEM((n_cols, 2, cap_rows, LANES), f32),
+            pltpu.HBM((n_ens * n_cols, 2, cap_rows, LANES), f32),
             pltpu.VMEM((levels, per_level, LANES), f32),
         ],
         scratch_shapes=[
@@ -541,7 +562,8 @@
             pltpu.VMEM(control.shape, f32),
             pltpu.VMEM(pert.shape, bf16),
             pltpu.SemaphoreType.DMA((6,)),
-        ],
+        ]
+        + [pltpu.VMEM((coarse, 8 * LANES), bf16), pltpu.VMEM((4 * FINE, 8 * LANES), bf16)] * 2,
         compiler_params=params(24),
         name="slot_sums_and_members",
     )(
@@ -554,7 +576,7 @@
     )
     before, after, slots = lax.optimization_barrier((before, after, slots))
     other = swapped(packed, before, after)
-    slots = lax.all_to_all(slots, "cols", split_axis=0, concat_axis=0, tiled=True)
+    slots = lax.all_to_all(slots, ("ens", "cols"), split_axis=0, concat_axis=0, tiled=True)
 
     increment, coefs = pl.pallas_call(
         functools.partial(first_diffusion_kernel, lev_share, rows),
@@ -574,26 +596,26 @@
         in_specs=[VMEM] * 4,
         out_specs=VMEM,
         out_shape=pltpu.VMEM((entry_rows, LANES), f32),
-        scratch_shapes=[pltpu.VMEM((cells, 2 * LANES), bf16)],
+        scratch_shapes=[pltpu.VMEM((cells, 2 * LANES), bf16)] + [pltpu.VMEM((capacity, cells), bf16)] * 2,
         compiler_params=params(16),
         cost_estimate=pl.CostEstimate(
             flops=4 * cells * LANES * lists * capacity, bytes_accessed=8 * cells * lists * capacity // 4, transcendentals=0
         ),
         name="lookup",
     )(part.reshape(cells, LANES), increment.reshape(own, LANES), entry_row, entry_lane)
-    slots = jnp.swapaxes(slots, 0, 1).reshape(2, entry_rows, LANES)
-    share = jnp.concatenate([values[None], slots])
-    shares = [share] + from_peers(share)
+    values, slots = lax.optimization_barrier((values, slots))
+    shares = [values] + from_peers(values)
 
     adjoint_own, amounts = pl.pallas_call(
         functools.partial(scatter_own_kernel, cap_rows),
-        in_specs=[VMEM] * (2 + n_ens),
+        in_specs=[VMEM] * (3 + n_ens),
         out_specs=[VMEM] * 2,
         out_shape=[pltpu.VMEM((own, LANES), f32), pltpu.VMEM((entry_rows, LANES), f32)],
-        scratch_shapes=[pltpu.VMEM((own, 2 * LANES), f32)],
+        scratch_shapes=[pltpu.VMEM((own, 2 * LANES), f32)]
+        + [pltpu.VMEM((own, capacity), bf16), pltpu.VMEM((2 * LANES, capacity), bf16)] * 2,
         compiler_params=params(16),
         name="scatter_own",
-    )(entry_row, entry_lane, *shares)
+    )(entry_row, entry_lane, slots, *shares)
     tile = adjoint_own.reshape(lev_share, per_level, LANES)
     tile_before, tile_after = shifted(tile, 2), shifted(tile, -2)
 
@@ -607,7 +629,8 @@
             pltpu.VMEM(control.shape, f32),
             pltpu.VMEM(pert.shape, bf16),
         ],
-        scratch_shapes=[pltpu.VMEM((cells - own, 2 * LANES), f32), pltpu.SemaphoreType.DMA((3,))],
+        scratch_shapes=[pltpu.VMEM((cells - own, 2 * LANES), f32), pltpu.SemaphoreType.DMA((3,))]
+        + [pltpu.VMEM((cells - own, capacity), bf16), pltpu.VMEM((2 * LANES, capacity), bf16)] * 2,
         compiler_params=params(16),
         name="scatter_rest",
     )(entry_row, entry_lane, amounts, adjoint_own, static, control, pert)

time: 68.6 us -> 64.2 us (0.936)
  blocking collectives: 9.03 us -> 0 us
  starting transfers between devices: 16.1 us -> 20.7 us
    all_to_all x1 -> x0, blocking collectives: 9.03 us -> none  [local(): lax.all_to_all(slots, 'cols', split_axis=0, concat_axis=0, tiled=True)]
    all_to_all x0 -> x1, starting transfers between devices: none -> 4.66 us  [local(): lax.all_to_all(slots, ('ens', 'cols'), split_axis=0, concat_axis=0, tiled...]
    ppermute x6, waiting for transfers between devices: 5.48 us -> 4.54 us  [from_peers(): lax.ppermute(x, 'ens', [((i + d) % count, i) for i in range(count)])]
    pallas_call x1, Pallas kernels: 7.62 us -> 8.35 us  [local(): pl.pallas_call(functools.partial(lookup_kernel, cap_rows), in_specs=[VMEM...]
  transfers between devices with their start and end apart: 12 -> 13, of which waited for: 4 -> 7; matrix products, arithmetic and copies ran while one was open for 0% -> 0% of each run, Pallas kernels for 30% -> 47%
where the time goes in v6:
time: 64.2 us; the launch traced here: 63.9 us
  Pallas kernels  36.9 us (57%)
  starting transfers between devices  20.7 us (32%)
  waiting for transfers between devices  5.4 us (8%)
  between operations  0.79 us (1%)
    ppermute x4, starting transfers between devices, shifted(): lax.ppermute(x, 'cols', [(i, (i + by) % count) for i in range(count)])  9.04 us
    pallas_call x1, Pallas kernels, local(): pl.pallas_call(functools.partial(observe_kernel, n_cols, cap_rows, member...  8.4 us
    pallas_call x1, Pallas kernels, local(): pl.pallas_call(functools.partial(lookup_kernel, cap_rows), in_specs=[VMEM...  8.35 us
    ppermute x6, starting transfers between devices, from_peers(): lax.ppermute(x, 'ens', [((i + d) % count, i) for i in range(count)])  6.86 us
    pallas_call x1, Pallas kernels, local(): pl.pallas_call(member_kernel, grid=(members // group,), in_specs=[VMEM] *...  5.57 us
    pallas_call x1, Pallas kernels, local(): pl.pallas_call(functools.partial(scatter_rest_kernel, cap_rows), in_specs...  5.09 us
    all_to_all x1, starting transfers between devices, local(): lax.all_to_all(slots, ('ens', 'cols'), split_axis=0, concat_axis=0, tiled...  4.66 us
    ppermute x6, waiting for transfers between devices, from_peers(): lax.ppermute(x, 'ens', [((i + d) % count, i) for i in range(count)])  4.54 us
  transfers between devices with their start and end apart: 13, of which 7 were waited for; matrix products, arithmetic and copies ran while one was open for 0% of the time, Pallas kernels for 47%

profile of v6, /device:TPU:0, one launch (start us, length us, event | category | flops | bytes accessed | tf_op | source)
XLA Modules:
  0.0 63.9 jit_solution(5841285999813881497)
XLA Ops:
  0.6 1.3 %prepare.1 = (f32[6,64,128]{2,1,0:T(8,128)S(1)}, s32[64,128]{1,0:T(8,128)S(1)}, s32[64,128]{1,0:T(8,128)S(1)}) custom-call(f32[16,16]{1,0:T(8,128)} %root_ref.2, s32[8]{0:T(128)} %count_ref.1, f32[16,64,128]{2,1,0:T(8,128)} %bitcast.61, f32[64,128]{1,0:T(8,128)} %bitcast.67, f32[64,128]{1,0:T(8,128)} %bitcast.68, s32[8,1024]{1,0:T(8,128)} %index_ref.1), custom_call_target="tpu_custom_call" | custom-call | tf_op jit(solution)/shard_map/prepare/pallas_call | solution.py:511
  1.9 3.1 %collective-permute-start = (f32[6,64,128]{2,1,0:T(8,128)S(1)}, f32[6,64,128]{2,1,0:T(8,128)S(1)}, u32[]{:S(2)}, u32[]{:S(2)}) collective-permute-start(f32[6,64,128]{2,1,0:T(8,128)S(1)} %get-tuple-element.38.own_ref), channel_id=1, source_target_pairs={{0,2},{1,3},{2,4},{3,5},{4,6},{5,7},{6,0},{7,1},{8,10},{9,11},{10,... | collective-permute-start | bytes 589832 | tf_op jit(solution)/shard_map/ppermute | solution.py:463
  5.0 2.1 %collective-permute-start.1 = (f32[6,64,128]{2,1,0:T(8,128)S(1)}, f32[6,64,128]{2,1,0:T(8,128)S(1)}, u32[]{:S(2)}, u32[]{:S(2)}) collective-permute-start(f32[6,64,128]{2,1,0:T(8,128)S(1)} %get-tuple-element.38.own_ref), channel_id=1, source_target_pairs={{0,6},{1,7},{2,0},{3,1},{4,2},{5,3},{6,4},{7,5},{8,14},{9,15},{10,... | collective-permute-start | bytes 589832 | tf_op jit(solution)/shard_map/ppermute | solution.py:463
  7.1 8.4 %slot_sums_and_members.1 = (f32[32,2,8,128]{3,2,1,0:T(8,128)}, f32[16,64,128]{2,1,0:T(8,128)S(1)}) custom-call(s32[512,128]{1,0:T(8,128)} %bitcast.64, f32[512,128]{1,0:T(8,128)} %bitcast.65, f32[512,128]{1,0:T(8,128)} %bitcast.66, f32[16,16]{1,0:T(8,128)} %local_ref, f32[8,16,64,128]{3,2,1,0:T(8,128)} %bitcast.56, bf16[8,16,64,128]{3,2,1,0:T(8,128)(2,1)} %bitcast.58), custom_call_target="tpu_custom_call" | custom-call | tf_op jit(solution)/shard_map/slot_sums_and_members/pallas_call | solution.py:545
  15.5 0.1 collective-permute-done.1.after_ref
  15.7 0.1 collective-permute-start.2
  15.7 4.7 %all-to-all-start = ((f32[32,2,8,128]{3,2,1,0:T(8,128)}), f32[32,2,8,128]{3,2,1,0:T(8,128)S(1)}, u32[]{:S(2)}, u32[]{:S(2)}) async-start(f32[32,2,8,128]{3,2,1,0:T(8,128)} %get-tuple-element.45), calls=%async_computation | async-start | bytes 524288 | tf_op jit(solution)/shard_map/all_to_all | solution.py:579
  20.4 0.0 collective-permute-done.2.other_ref
  20.4 1.5 %diffuse_forward.1 = (f32[4,64,128]{2,1,0:T(8,128)S(1)}, f32[5,10,32,128]{3,2,1,0:T(8,128)S(1)}) custom-call(f32[6,64,128]{2,1,0:T(8,128)S(1)} %collective-permute-done.before_ref, f32[6,64,128]{2,1,0:T(8,128)S(1)} %get-tuple-element.38.own_ref, f32[6,64,128]{2,1,0:T(8,128)S(1)} %collective-permute-done.1.after_ref, ...), custom_call_target="tpu_custom_call" | custom-call | flops 67108864 | bytes 4194304 | tf_op jit(solution)/shard_map/diffuse_forward/pallas_call | solution.py:581
  21.9 8.3 %lookup.1.refs_0_ = f32[64,128]{1,0:T(8,128)S(1)} custom-call(f32[1024,128]{1,0:T(8,128)S(1)} %bitcast.54, f32[256,128]{1,0:T(8,128)S(1)} %bitcast.55, s32[64,128]{1,0:T(8,128)S(1)} %get-tuple-element.41.row_ref, s32[64,128]{1,0:T(8,128)S(1)} %get-tuple-element.42.lane_ref), custom_call_target="tpu_custom_call" | custom-call | flops 4294967296 | bytes 16777216 | tf_op jit(solution)/shard_map/lookup/pallas_call | solution.py:594
  30.3 0.5 all-to-all-done.slots_ref
  30.8 2.2 %collective-permute-start.3 = (f32[64,128]{1,0:T(8,128)S(1)}, f32[64,128]{1,0:T(8,128)S(1)}, u32[]{:S(2)}, u32[]{:S(2)}) collective-permute-start(f32[64,128]{1,0:T(8,128)S(1)} %lookup.1.refs_0_), channel_id=1, source_target_pairs={{8,0},{16,8},{24,16},{0,24},{9,1},{17,9},{25,17},{1,25},{10,2},{18... | collective-permute-start | bytes 98312 | tf_op jit(solution)/shard_map/ppermute | solution.py:468
  33.0 0.6 collective-permute-start.4
  33.6 0.6 collective-permute-start.5
  34.1 0.6 collective-permute-done.3.refs_1_
  34.7 2.5 %collective-permute-done.4.refs_2_ = f32[64,128]{1,0:T(8,128)S(1)} collective-permute-done((f32[64,128]{1,0:T(8,128)S(1)}, f32[64,128]{1,0:T(8,128)S(1)}, u32[]{:S(2)}, u32[]{:S(2)}) %collective-permute-start.4) | collective-permute-done | bytes 32800 | tf_op jit(solution)/shard_map/ppermute | solution.py:468
  37.3 1.1 %collective-permute-done.5.refs_3_ = f32[64,128]{1,0:T(8,128)S(1)} collective-permute-done((f32[64,128]{1,0:T(8,128)S(1)}, f32[64,128]{1,0:T(8,128)S(1)}, u32[]{:S(2)}, u32[]{:S(2)}) %collective-permute-start.5) | collective-permute-done | bytes 32800 | tf_op jit(solution)/shard_map/ppermute | solution.py:468
  38.4 2.9 %scatter_own.1 = (f32[256,128]{1,0:T(8,128)S(1)}, f32[64,128]{1,0:T(8,128)S(1)}) custom-call(s32[64,128]{1,0:T(8,128)S(1)} %get-tuple-element.41.row_ref, s32[64,128]{1,0:T(8,128)S(1)} %get-tuple-element.42.lane_ref, f32[32,2,8,128]{3,2,1,0:T(8,128)S(1)} %all-to-all-done.slots_ref, f32[64,128]{1,0:T(8,128)S(1)} %lookup.1.refs_0_, ...), custom_call_target="tpu_custom_call" | custom-call | tf_op jit(solution)/shard_map/scatter_own/pallas_call | solution.py:609
  41.2 1.5 %collective-permute-start.6 = (f32[4,64,128]{2,1,0:T(8,128)S(1)}, f32[4,64,128]{2,1,0:T(8,128)S(1)}, u32[]{:S(2)}, u32[]{:S(2)}) collective-permute-start(f32[4,64,128]{2,1,0:T(8,128)S(1)} %bitcast.48), channel_id=1, source_target_pairs={{0,2},{1,3},{2,4},{3,5},{4,6},{5,7},{6,0},{7,1},{8,10},{9,11},{10,... | collective-permute-start | bytes 393224 | tf_op jit(solution)/shard_map/ppermute | solution.py:463
  42.8 2.3 %collective-permute-start.7 = (f32[4,64,128]{2,1,0:T(8,128)S(1)}, f32[4,64,128]{2,1,0:T(8,128)S(1)}, u32[]{:S(2)}, u32[]{:S(2)}) collective-permute-start(f32[4,64,128]{2,1,0:T(8,128)S(1)} %bitcast.49), channel_id=1, source_target_pairs={{0,6},{1,7},{2,0},{3,1},{4,2},{5,3},{6,4},{7,5},{8,14},{9,15},{10,... | collective-permute-start | bytes 393224 | tf_op jit(solution)/shard_map/ppermute | solution.py:463
  45.1 5.1 %scatter_rest.1 = (f32[1024,128]{1,0:T(8,128)S(1)}, f32[16,64,128]{2,1,0:T(8,128)S(1)}, f32[8,16,64,128]{3,2,1,0:T(8,128)S(1)}, bf16[8,16,64,128]{3,2,1,0:T(8,128)(2,1)S(1)}) custom-call(s32[64,128]{1,0:T(8,128)S(1)} %get-tuple-element.41.row_ref, s32[64,128]{1,0:T(8,128)S(1)} %get-tuple-element.42.lane_ref, f32[64,128]{1,0:T(8,128)S(1)} %get-tuple-element.49.amount_ref, ...), custom_call_target="tpu_custom_call" | custom-call | tf_op jit(solution)/shard_map/scatter_rest/pallas_call | solution.py:622
  50.2 0.0 collective-permute-done.6.before_ref
  50.3 0.1 collective-permute-start.8
  50.4 1.2 %level_matrices.1 = (bf16[256,768]{1,0:T(8,128)(2,1)S(1)}, bf16[256,768]{1,0:T(8,128)(2,1)S(1)}) custom-call(f32[16,16]{1,0:T(8,128)} %local_ref, f32[16,16]{1,0:T(8,128)} %root_ref.2), custom_call_target="tpu_custom_call" | custom-call | tf_op jit(solution)/shard_map/level_matrices/pallas_call | solution.py:641
  51.6 0.3 collective-permute-done.8.other_ref
  51.9 1.4 %diffuse_adjoint.1.refs_0_ = f32[4,64,128]{2,1,0:T(8,128)S(1)} custom-call(f32[5,10,32,128]{3,2,1,0:T(8,128)S(1)} %get-tuple-element.57.coef_ref, f32[4,64,128]{2,1,0:T(8,128)S(1)} %collective-permute-done.6.before_ref, f32[4,64,128]{2,1,0:T(8,128)S(1)} %bitcast.51, f32[4,64,128]{2,1,0:T(8,128)S(1)} %collective-permute-done.7.after_ref, ...), custom_call_target="tpu_custom_call" | custom-call | tf_op jit(solution)/shard_map/diffuse_adjoint/pallas_call | solution.py:652
  53.3 0.1 collective-permute-start.9
  53.3 1.5 %collective-permute-start.10 = (f32[4,64,128]{2,1,0:T(8,128)S(1)}, f32[4,64,128]{2,1,0:T(8,128)S(1)}, u32[]{:S(2)}, u32[]{:S(2)}) collective-permute-start(f32[4,64,128]{2,1,0:T(8,128)S(1)} %diffuse_adjoint.1.refs_0_), channel_id=1, source_target_pairs={{16,0},{24,8},{0,16},{8,24},{17,1},{25,9},{1,17},{9,25},{18,2},{26... | collective-permute-start | bytes 393224 | tf_op jit(solution)/shard_map/ppermute | solution.py:468
  54.9 1.9 %collective-permute-start.11 = (f32[4,64,128]{2,1,0:T(8,128)S(1)}, f32[4,64,128]{2,1,0:T(8,128)S(1)}, u32[]{:S(2)}, u32[]{:S(2)}) collective-permute-start(f32[4,64,128]{2,1,0:T(8,128)S(1)} %diffuse_adjoint.1.refs_0_), channel_id=1, source_target_pairs={{24,0},{0,8},{8,16},{16,24},{25,1},{1,9},{9,17},{17,25},{26,2},{2,... | collective-permute-start | bytes 393224 | tf_op jit(solution)/shard_map/ppermute | solution.py:468
  56.8 5.6 %members_gradient.1 = f32[8,16,64,128]{3,2,1,0:T(8,128)} custom-call(bf16[256,768]{1,0:T(8,128)(2,1)S(1)} %get-tuple-element.62.matrix_ref, f32[16,64,128]{2,1,0:T(8,128)S(1)} %bitcast.53, f32[8,16,64,128]{3,2,1,0:T(8,128)S(1)} %get-tuple-element.64.control_ref, bf16[8,16,64,128]{3,2,1,0:T(8,128)(2,1)S(1)} %get-tuple-element.65.pert_ref), custom_call_target="tpu_custom_call" | custom-call | tf_op jit(solution)/shard_map/members_gradient/pallas_call | solution.py:664
  62.4 0.3 collective-permute-done.11.refs_3_
  62.7 1.2 %static_gradient.1 = f32[16,64,128]{2,1,0:T(8,128)} custom-call(bf16[256,768]{1,0:T(8,128)(2,1)S(1)} %get-tuple-element.55.matrix_ref, f32[16,64,128]{2,1,0:T(8,128)S(1)} %get-tuple-element.56.static_ref, f32[4,64,128]{2,1,0:T(8,128)S(1)} %diffuse_adjoint.1.refs_0_, f32[4,64,128]{2,1,0:T(8,128)S(1)} %collective-permute-done.9.refs_1_, ...), custom_call_target="tpu_custom_call" | custom-call | tf_op jit(solution)/shard_map/static_gradient/pallas_call | solution.py:674
  (8 shorter events, 0.1 us)
Async XLA Ops:
  1.9 13.6 %collective-permute-start = (f32[6,64,128]{2,1,0:T(8,128)S(1)}, f32[6,64,128]{2,1,0:T(8,128)S(1)}, u32[]{:S(2)}, u32[]{:S(2)}) collective-permute-start(f32[6,64,128]{2,1,0:T(8,128)S(1)} %get-tuple-element.38.own_ref), channel_id=1, source_target_pairs={{0,2},{1,3},{2,4},{3,5},{4,6},{5,7},{6,0},{7,1},{8,10},{9,11},{10,... | collective-permute-start | bytes 589832 | tf_op jit(solution)/shard_map/ppermute | solution.py:463
  5.0 10.6 %collective-permute-start.1 = (f32[6,64,128]{2,1,0:T(8,128)S(1)}, f32[6,64,128]{2,1,0:T(8,128)S(1)}, u32[]{:S(2)}, u32[]{:S(2)}) collective-permute-start(f32[6,64,128]{2,1,0:T(8,128)S(1)} %get-tuple-element.38.own_ref), channel_id=1, source_target_pairs={{0,6},{1,7},{2,0},{3,1},{4,2},{5,3},{6,4},{7,5},{8,14},{9,15},{10,... | collective-permute-start | bytes 589832 | tf_op jit(solution)/shard_map/ppermute | solution.py:463
  15.7 4.7 %collective-permute-start.2 = (f32[2,6,64,128]{3,2,1,0:T(8,128)S(1)}, f32[2,6,64,128]{3,2,1,0:T(8,128)S(1)}, u32[]{:S(2)}, u32[]{:S(2)}) collective-permute-start(f32[2,6,64,128]{3,2,1,0:T(8,128)S(1)} %pad_maximum_fusion), channel_id=1, source_target_pairs={{0,1},{1,0},{2,3},{3,2},{4,5},{5,4},{6,7},{7,6},{8,9},{9,8},{10,11... | collective-permute-start | bytes 1179656 | tf_op jit(solution)/shard_map/ppermute | solution.py:475
  15.7 15.0 %all-to-all-start = ((f32[32,2,8,128]{3,2,1,0:T(8,128)}), f32[32,2,8,128]{3,2,1,0:T(8,128)S(1)}, u32[]{:S(2)}, u32[]{:S(2)}) async-start(f32[32,2,8,128]{3,2,1,0:T(8,128)} %get-tuple-element.45), calls=%async_computation | async-start | bytes 524288 | tf_op jit(solution)/shard_map/all_to_all | solution.py:579
  30.8 3.9 %collective-permute-start.3 = (f32[64,128]{1,0:T(8,128)S(1)}, f32[64,128]{1,0:T(8,128)S(1)}, u32[]{:S(2)}, u32[]{:S(2)}) collective-permute-start(f32[64,128]{1,0:T(8,128)S(1)} %lookup.1.refs_0_), channel_id=1, source_target_pairs={{8,0},{16,8},{24,16},{0,24},{9,1},{17,9},{25,17},{1,25},{10,2},{18... | collective-permute-start | bytes 98312 | tf_op jit(solution)/shard_map/ppermute | solution.py:468
  33.0 4.3 %collective-permute-start.4 = (f32[64,128]{1,0:T(8,128)S(1)}, f32[64,128]{1,0:T(8,128)S(1)}, u32[]{:S(2)}, u32[]{:S(2)}) collective-permute-start(f32[64,128]{1,0:T(8,128)S(1)} %lookup.1.refs_0_), channel_id=1, source_target_pairs={{16,0},{24,8},{0,16},{8,24},{17,1},{25,9},{1,17},{9,25},{18,2},{26... | collective-permute-start | bytes 98312 | tf_op jit(solution)/shard_map/ppermute | solution.py:468
  33.6 4.8 %collective-permute-start.5 = (f32[64,128]{1,0:T(8,128)S(1)}, f32[64,128]{1,0:T(8,128)S(1)}, u32[]{:S(2)}, u32[]{:S(2)}) collective-permute-start(f32[64,128]{1,0:T(8,128)S(1)} %lookup.1.refs_0_), channel_id=1, source_target_pairs={{24,0},{0,8},{8,16},{16,24},{25,1},{1,9},{9,17},{17,25},{26,2},{2,... | collective-permute-start | bytes 98312 | tf_op jit(solution)/shard_map/ppermute | solution.py:468
  41.2 9.0 %collective-permute-start.6 = (f32[4,64,128]{2,1,0:T(8,128)S(1)}, f32[4,64,128]{2,1,0:T(8,128)S(1)}, u32[]{:S(2)}, u32[]{:S(2)}) collective-permute-start(f32[4,64,128]{2,1,0:T(8,128)S(1)} %bitcast.48), channel_id=1, source_target_pairs={{0,2},{1,3},{2,4},{3,5},{4,6},{5,7},{6,0},{7,1},{8,10},{9,11},{10,... | collective-permute-start | bytes 393224 | tf_op jit(solution)/shard_map/ppermute | solution.py:463
  42.8 7.5 %collective-permute-start.7 = (f32[4,64,128]{2,1,0:T(8,128)S(1)}, f32[4,64,128]{2,1,0:T(8,128)S(1)}, u32[]{:S(2)}, u32[]{:S(2)}) collective-permute-start(f32[4,64,128]{2,1,0:T(8,128)S(1)} %bitcast.49), channel_id=1, source_target_pairs={{0,6},{1,7},{2,0},{3,1},{4,2},{5,3},{6,4},{7,5},{8,14},{9,15},{10,... | collective-permute-start | bytes 393224 | tf_op jit(solution)/shard_map/ppermute | solution.py:463
  50.3 1.6 %collective-permute-start.8 = (f32[2,4,64,128]{3,2,1,0:T(8,128)S(1)}, f32[2,4,64,128]{3,2,1,0:T(8,128)S(1)}, u32[]{:S(2)}, u32[]{:S(2)}) collective-permute-start(f32[2,4,64,128]{3,2,1,0:T(8,128)S(1)} %pad_maximum_fusion.1), channel_id=1, source_target_pairs={{0,1},{1,0},{2,3},{3,2},{4,5},{5,4},{6,7},{7,6},{8,9},{9,8},{10,11... | collective-permute-start | bytes 786440 | tf_op jit(solution)/shard_map/ppermute | solution.py:475
  53.3 9.1 %collective-permute-start.9 = (f32[4,64,128]{2,1,0:T(8,128)S(1)}, f32[4,64,128]{2,1,0:T(8,128)S(1)}, u32[]{:S(2)}, u32[]{:S(2)}) collective-permute-start(f32[4,64,128]{2,1,0:T(8,128)S(1)} %diffuse_adjoint.1.refs_0_), channel_id=1, source_target_pairs={{8,0},{16,8},{24,16},{0,24},{9,1},{17,9},{25,17},{1,25},{10,2},{18... | collective-permute-start | bytes 393224 | tf_op jit(solution)/shard_map/ppermute | solution.py:468
  53.3 9.1 %collective-permute-start.10 = (f32[4,64,128]{2,1,0:T(8,128)S(1)}, f32[4,64,128]{2,1,0:T(8,128)S(1)}, u32[]{:S(2)}, u32[]{:S(2)}) collective-permute-start(f32[4,64,128]{2,1,0:T(8,128)S(1)} %diffuse_adjoint.1.refs_0_), channel_id=1, source_target_pairs={{16,0},{24,8},{0,16},{8,24},{17,1},{25,9},{1,17},{9,25},{18,2},{26... | collective-permute-start | bytes 393224 | tf_op jit(solution)/shard_map/ppermute | solution.py:468
  54.9 7.8 %collective-permute-start.11 = (f32[4,64,128]{2,1,0:T(8,128)S(1)}, f32[4,64,128]{2,1,0:T(8,128)S(1)}, u32[]{:S(2)}, u32[]{:S(2)}) collective-permute-start(f32[4,64,128]{2,1,0:T(8,128)S(1)} %diffuse_adjoint.1.refs_0_), channel_id=1, source_target_pairs={{24,0},{0,8},{8,16},{16,24},{25,1},{1,9},{9,17},{17,25},{26,2},{2,... | collective-permute-start | bytes 393224 | tf_op jit(solution)/shard_map/ppermute | solution.py:468

commit v7 on v6

--- a/solution.py
+++ b/solution.py
@@ -327,75 +327,73 @@
     lax.fori_loop(0, lev_share, body, 0)
 
 
-def lookup_kernel(cap_rows, part_ref, static_ref, row_ref, lane_ref, out_ref, terms_ref, *slots):
+def lookup_kernel(cap_rows, part_ref, static_ref, row_ref, lane_ref, out_ref, field_ref, terms_ref):
     cells = part_ref.shape[0]
     own = static_ref.shape[0]
     at = pl.ds(pl.multiple_of(lax.axis_index("ens") * own, own), own)
-    for here, field in ((slice(None), part_ref[...]), (at, part_ref[at, :] + static_ref[...])):
-        high, low = halves(field)
-        terms_ref[here, :LANES] = high
-        terms_ref[here, LANES:] = low
-    ids16 = lax.broadcasted_iota(jnp.int32, (LANES, cells), 1).astype(jnp.int16)
-    ids = lax.broadcasted_iota(jnp.int32, (LANES, LANES), 1)
-    diagonal = ids == lax.broadcasted_iota(jnp.int32, (LANES, LANES), 0)
-
-    def build(q, to):
+    field_ref[...] = part_ref[...]
+    field_ref[at, :] += static_ref[...]
+    for c in range(0, cells, LANES):
+        high, low = halves(field_ref[c : c + LANES, :].T)
+        terms_ref[:LANES, c : c + LANES] = high
+        terms_ref[LANES:, c : c + LANES] = low
+    ids = lax.broadcasted_iota(jnp.int32, (LANES, LANES), 0)
+
+    def look(q, carry):
         at = pl.ds(pl.multiple_of(q * cap_rows, cap_rows), cap_rows)
-        rows = row_ref[at, :].astype(f32).T
-        for c in range(cap_rows):
-            column = jnp.broadcast_to(rows[:, c : c + 1], (LANES, LANES)).astype(jnp.int32).astype(jnp.int16)
-            column = jnp.concatenate([column] * (cells // LANES), axis=1)
-            to[c * LANES : (c + 1) * LANES, :] = jnp.where(ids16 == column, bf16(1), bf16(0))
-
-    def use(q, of):
-        at = pl.ds(pl.multiple_of(q * cap_rows, cap_rows), cap_rows)
-        lanes = lane_ref[at, :].astype(f32).T
-        got = jnp.dot(of[...], terms_ref[...], preferred_element_type=f32)
+        rows = row_ref[at, :]
+        lanes = lane_ref[at, :]
+        picks = [placed_at(rows[c : c + 1, :], cells) for c in range(cap_rows)]
+        got = jnp.dot(terms_ref[...], jnp.concatenate(picks, axis=1), preferred_element_type=f32)
         values = []
         for c in range(cap_rows):
-            mask = ids == jnp.broadcast_to(lanes[:, c : c + 1], (LANES, LANES)).astype(jnp.int32)
-            mine = got[c * LANES : (c + 1) * LANES]
-            found = jnp.sum(jnp.where(mask, mine[:, :LANES] + mine[:, LANES:], f32(0)), axis=1, keepdims=True)
-            values.append(jnp.sum(jnp.where(diagonal, found, f32(0)), axis=0, keepdims=True))
+            here = slice(c * LANES, (c + 1) * LANES)
+            mine = got[:LANES, here] + got[LANES:, here]
+            values.append(jnp.sum(jnp.where(ids == lanes[c : c + 1, :], mine, f32(0)), axis=0, keepdims=True))
         out_ref[at, :] = jnp.concatenate(values, axis=0)
-
-    in_turns(row_ref.shape[0] // cap_rows, build, use, slots)
-
-
-def put(to, rows, lanes, amounts):
-    count = to[0].shape[0]
+        return carry
+
+    lax.fori_loop(0, row_ref.shape[0] // cap_rows, look, 0)
+
+
+def put(acc_ref, rows, lanes, amounts):
     terms = [h.astype(f32) for h in halves(amounts)]
+    left, right = [], []
     for c in range(rows.shape[0]):
-        here = slice(c * LANES, (c + 1) * LANES)
-        to[0][:, here] = placed_at(rows[c : c + 1, :], count)
+        left.append(placed_at(rows[c : c + 1, :], acc_ref.shape[0]))
         mask = matches(lanes[c : c + 1, :], LANES)
-        for t, term in enumerate(terms):
-            term = spread(term[c : c + 1, :], bf16)[None]
-            to[1][t * LANES : (t + 1) * LANES, here] = jnp.where(mask, term, bf16(0)).reshape(LANES, LANES)
+        right.append(
+            jnp.concatenate(
+                [
+                    jnp.where(mask, spread(t[c : c + 1, :], bf16)[None], bf16(0)).reshape(LANES, LANES)
+                    for t in terms
+                ],
+                axis=0,
+            )
+        )
+    acc_ref[...] += product_nt(jnp.concatenate(left, axis=1), jnp.concatenate(right, axis=1))
 
 
 def scatter_own_kernel(cap_rows, row_ref, lane_ref, slots_ref, *refs):
-    values, (out_ref, amount_ref, acc_ref), slots = refs[:-7], refs[-7:-4], (refs[-4:-2], refs[-2:])
-    n_ens = len(values)
+    values, (out_ref, amount_ref, acc_ref) = refs[:-3], refs[-3:]
     own = out_ref.shape[0]
     lists = row_ref.shape[0] // cap_rows
     first = lax.axis_index("ens") * own
     acc_ref[...] = jnp.zeros_like(acc_ref)
 
-    def build(q, to):
+    def step(q, carry):
         at = pl.ds(pl.multiple_of(q * cap_rows, cap_rows), cap_rows)
         value = functools.reduce(jnp.add, [v[at, :] for v in values])
         weight, amount = (
-            functools.reduce(jnp.add, [slots_ref[e * lists + q, t] for e in range(n_ens)]) for t in range(2)
+            functools.reduce(jnp.add, [slots_ref[e * lists + q, t] for e in range(slots_ref.shape[0] // lists)])
+            for t in range(2)
         )
         amounts = value * weight - amount
         amount_ref[at, :] = amounts
-        put(to, row_ref[at, :] - first, lane_ref[at, :], amounts)
-
-    def use(q, of):
-        acc_ref[...] += product_nt(of[0][...], of[1][...])
-
-    in_turns(lists, build, use, slots)
+        put(acc_ref, row_ref[at, :] - first, lane_ref[at, :], amounts)
+        return carry
+
+    lax.fori_loop(0, lists, step, 0)
     out_ref[...] = acc_ref[:, :LANES] + acc_ref[:, LANES:]
 
 
@@ -405,14 +403,7 @@
 
 
 def scatter_rest_kernel(cap_rows, row_ref, lane_ref, amount_ref, own_ref, *refs):
-    sources, out_ref, kept, acc_ref, sems, slots = (
-        refs[:3],
-        refs[3],
-        refs[4:7],
-        refs[7],
-        refs[8],
-        (refs[9:11], refs[11:13]),
-    )
+    sources, out_ref, kept, acc_ref, sems = refs[:3], refs[3], refs[4:7], refs[7], refs[8]
     copies = [pltpu.make_async_copy(s, t, sems.at[i]) for i, (s, t) in enumerate(zip(sources, kept))]
     for copy in copies:
         copy.start()
@@ -423,17 +414,15 @@
     first = (me + 1) * own
     acc_ref[...] = jnp.zeros_like(acc_ref)
 
-    def build(q, to):
+    def step(q, carry):
         at = pl.ds(pl.multiple_of(q * cap_rows, cap_rows), cap_rows)
         row = row_ref[at, :]
         turned = row - first
         turned = jnp.where(row < 0, -1, jnp.where(turned < 0, turned + cells, turned))
-        put(to, turned, lane_ref[at, :], amount_ref[at, :])
-
-    def use(q, of):
-        acc_ref[...] += product_nt(of[0][...], of[1][...])
-
-    in_turns(row_ref.shape[0] // cap_rows, build, use, slots)
+        put(acc_ref, turned, lane_ref[at, :], amount_ref[at, :])
+        return carry
+
+    lax.fori_loop(0, row_ref.shape[0] // cap_rows, step, 0)
     out_ref[pl.ds(pl.multiple_of(me * own, own), own), :] = own_ref[...]
     for t in range(1, n_ens):
         to = pl.ds(pl.multiple_of((me + t) % n_ens * own, own), own)
@@ -466,6 +455,19 @@
 def from_peers(x):
     count = lax.axis_size("ens")
     return [lax.ppermute(x, "ens", [((i + d) % count, i) for i in range(count)]) for d in range(1, count)]
+
+
+def over_ens(x):
+    count = lax.axis_size("ens")
+    if count < 2 or count & (count - 1):
+        return [x] + from_peers(x)
+    by = 1
+    while True:
+        other = lax.ppermute(x, "ens", [(i, i ^ by) for i in range(count)])
+        by *= 2
+        if by == count:
+            return [x, other]
+        x = x + other
 
 
 def swapped(own, before, after):
@@ -596,7 +598,7 @@
         in_specs=[VMEM] * 4,
         out_specs=VMEM,
         out_shape=pltpu.VMEM((entry_rows, LANES), f32),
-        scratch_shapes=[pltpu.VMEM((cells, 2 * LANES), bf16)] + [pltpu.VMEM((capacity, cells), bf16)] * 2,
+        scratch_shapes=[pltpu.VMEM((cells, LANES), f32), pltpu.VMEM((2 * LANES, cells), bf16)],
         compiler_params=params(16),
         cost_estimate=pl.CostEstimate(
             flops=4 * cells * LANES * lists * capacity, bytes_accessed=8 * cells * lists * capacity // 4, transcendentals=0
@@ -604,15 +606,14 @@
         name="lookup",
     )(part.reshape(cells, LANES), increment.reshape(own, LANES), entry_row, entry_lane)
     values, slots = lax.optimization_barrier((values, slots))
-    shares = [values] + from_peers(values)
+    shares = over_ens(values)
 
     adjoint_own, amounts = pl.pallas_call(
         functools.partial(scatter_own_kernel, cap_rows),
-        in_specs=[VMEM] * (3 + n_ens),
+        in_specs=[VMEM] * (3 + len(shares)),
         out_specs=[VMEM] * 2,
         out_shape=[pltpu.VMEM((own, LANES), f32), pltpu.VMEM((entry_rows, LANES), f32)],
-        scratch_shapes=[pltpu.VMEM((own, 2 * LANES), f32)]
-        + [pltpu.VMEM((own, capacity), bf16), pltpu.VMEM((2 * LANES, capacity), bf16)] * 2,
+        scratch_shapes=[pltpu.VMEM((own, 2 * LANES), f32)],
         compiler_params=params(16),
         name="scatter_own",
     )(entry_row, entry_lane, slots, *shares)
@@ -629,8 +630,7 @@
             pltpu.VMEM(control.shape, f32),
             pltpu.VMEM(pert.shape, bf16),
         ],
-        scratch_shapes=[pltpu.VMEM((cells - own, 2 * LANES), f32), pltpu.SemaphoreType.DMA((3,))]
-        + [pltpu.VMEM((cells - own, capacity), bf16), pltpu.VMEM((2 * LANES, capacity), bf16)] * 2,
+        scratch_shapes=[pltpu.VMEM((cells - own, 2 * LANES), f32), pltpu.SemaphoreType.DMA((3,))],
         compiler_params=params(16),
         name="scatter_rest",
     )(entry_row, entry_lane, amounts, adjoint_own, static, control, pert)

time: 64.2 us -> 63.9 us (level)
  waiting for transfers between devices: 5.4 us -> 10.6 us
  starting transfers between devices: 20.7 us -> 17.6 us
  Pallas kernels: 36.9 us -> 34.6 us
    ppermute x0 -> x2, waiting for transfers between devices: none -> 6.78 us  [over_ens(): other = lax.ppermute(x, 'ens', [(i, i ^ by) for i in range(count)])]
    ppermute x6 -> x3, starting transfers between devices: 6.86 us -> 2.64 us  [from_peers(): lax.ppermute(x, 'ens', [((i + d) % count, i) for i in range(count)])]
    ppermute x6 -> x3, waiting for transfers between devices: 4.54 us -> 0.77 us  [from_peers(): lax.ppermute(x, 'ens', [((i + d) % count, i) for i in range(count)])]
    all_to_all x1, waiting for transfers between devices: 0.52 us -> 2.67 us  [local(): lax.all_to_all(slots, ('ens', 'cols'), split_axis=0, concat_axis=0, tiled...]
    pallas_call x1, Pallas kernels: 8.35 us -> 6.2 us  [local(): pl.pallas_call(functools.partial(lookup_kernel, cap_rows), in_specs=[VMEM...]
    ppermute x0 -> x2, starting transfers between devices: none -> 1.07 us  [over_ens(): other = lax.ppermute(x, 'ens', [(i, i ^ by) for i in range(count)])]
  transfers between devices with their start and end apart: 13 -> 12, of which waited for: 7 -> 6; matrix products, arithmetic and copies ran while one was open for 0% -> 0% of each run, Pallas kernels for 47% -> 44%
where the time goes in v7:
time: 63.9 us; the launch traced here: 63.6 us
  Pallas kernels  34.6 us (54%)
  starting transfers between devices  17.6 us (28%)
  waiting for transfers between devices  10.6 us (17%)
  between operations  0.78 us (1%)
    ppermute x4, starting transfers between devices, shifted(): lax.ppermute(x, 'cols', [(i, (i + by) % count) for i in range(count)])  9.04 us
    pallas_call x1, Pallas kernels, local(): pl.pallas_call(functools.partial(observe_kernel, n_cols, cap_rows, member...  8.4 us
    ppermute x2, waiting for transfers between devices, over_ens(): other = lax.ppermute(x, 'ens', [(i, i ^ by) for i in range(count)])  6.78 us
    pallas_call x1, Pallas kernels, local(): pl.pallas_call(functools.partial(lookup_kernel, cap_rows), in_specs=[VMEM...  6.2 us
    pallas_call x1, Pallas kernels, local(): pl.pallas_call(member_kernel, grid=(members // group,), in_specs=[VMEM] *...  5.57 us
    pallas_call x1, Pallas kernels, local(): pl.pallas_call(functools.partial(scatter_rest_kernel, cap_rows), in_specs...  5 us
    all_to_all x1, starting transfers between devices, local(): lax.all_to_all(slots, ('ens', 'cols'), split_axis=0, concat_axis=0, tiled...  4.66 us
    pallas_call x1, Pallas kernels, local(): pl.pallas_call(functools.partial(scatter_own_kernel, cap_rows), in_specs=...  2.8 us
  transfers between devices with their start and end apart: 12, of which 6 were waited for; matrix products, arithmetic and copies ran while one was open for 0% of the time, Pallas kernels for 44%

profile of v7, /device:TPU:0, one launch (start us, length us, event | category | flops | bytes accessed | tf_op | source)
XLA Modules:
  0.0 63.6 jit_solution(14169967938241207212)
XLA Ops:
  0.6 1.3 %prepare.1 = (f32[6,64,128]{2,1,0:T(8,128)S(1)}, s32[64,128]{1,0:T(8,128)S(1)}, s32[64,128]{1,0:T(8,128)S(1)}) custom-call(f32[16,16]{1,0:T(8,128)} %root_ref.2, s32[8]{0:T(128)} %count_ref.1, f32[16,64,128]{2,1,0:T(8,128)} %bitcast.61, f32[64,128]{1,0:T(8,128)} %bitcast.67, f32[64,128]{1,0:T(8,128)} %bitcast.68, s32[8,1024]{1,0:T(8,128)} %index_ref.1), custom_call_target="tpu_custom_call" | custom-call | tf_op jit(solution)/shard_map/prepare/pallas_call | solution.py:513
  1.9 3.1 %collective-permute-start = (f32[6,64,128]{2,1,0:T(8,128)S(1)}, f32[6,64,128]{2,1,0:T(8,128)S(1)}, u32[]{:S(2)}, u32[]{:S(2)}) collective-permute-start(f32[6,64,128]{2,1,0:T(8,128)S(1)} %get-tuple-element.38.own_ref), channel_id=1, source_target_pairs={{0,2},{1,3},{2,4},{3,5},{4,6},{5,7},{6,0},{7,1},{8,10},{9,11},{10,... | collective-permute-start | bytes 589832 | tf_op jit(solution)/shard_map/ppermute | solution.py:452
  5.0 2.1 %collective-permute-start.1 = (f32[6,64,128]{2,1,0:T(8,128)S(1)}, f32[6,64,128]{2,1,0:T(8,128)S(1)}, u32[]{:S(2)}, u32[]{:S(2)}) collective-permute-start(f32[6,64,128]{2,1,0:T(8,128)S(1)} %get-tuple-element.38.own_ref), channel_id=1, source_target_pairs={{0,6},{1,7},{2,0},{3,1},{4,2},{5,3},{6,4},{7,5},{8,14},{9,15},{10,... | collective-permute-start | bytes 589832 | tf_op jit(solution)/shard_map/ppermute | solution.py:452
  7.1 8.4 %slot_sums_and_members.1 = (f32[32,2,8,128]{3,2,1,0:T(8,128)}, f32[16,64,128]{2,1,0:T(8,128)S(1)}) custom-call(s32[512,128]{1,0:T(8,128)} %bitcast.64, f32[512,128]{1,0:T(8,128)} %bitcast.65, f32[512,128]{1,0:T(8,128)} %bitcast.66, f32[16,16]{1,0:T(8,128)} %local_ref, f32[8,16,64,128]{3,2,1,0:T(8,128)} %bitcast.56, bf16[8,16,64,128]{3,2,1,0:T(8,128)(2,1)} %bitcast.58), custom_call_target="tpu_custom_call" | custom-call | tf_op jit(solution)/shard_map/slot_sums_and_members/pallas_call | solution.py:547
  15.5 0.0 collective-permute-done.before_ref
  15.5 0.1 collective-permute-done.1.after_ref
  15.7 0.1 collective-permute-start.2
  15.7 4.7 %all-to-all-start = ((f32[32,2,8,128]{3,2,1,0:T(8,128)}), f32[32,2,8,128]{3,2,1,0:T(8,128)S(1)}, u32[]{:S(2)}, u32[]{:S(2)}) async-start(f32[32,2,8,128]{3,2,1,0:T(8,128)} %get-tuple-element.45), calls=%async_computation | async-start | bytes 524288 | tf_op jit(solution)/shard_map/all_to_all | solution.py:581
  20.4 0.0 collective-permute-done.2.other_ref
  20.4 1.5 %diffuse_forward.1 = (f32[4,64,128]{2,1,0:T(8,128)S(1)}, f32[5,10,32,128]{3,2,1,0:T(8,128)S(1)}) custom-call(f32[6,64,128]{2,1,0:T(8,128)S(1)} %collective-permute-done.before_ref, f32[6,64,128]{2,1,0:T(8,128)S(1)} %get-tuple-element.38.own_ref, f32[6,64,128]{2,1,0:T(8,128)S(1)} %collective-permute-done.1.after_ref, ...), custom_call_target="tpu_custom_call" | custom-call | flops 67108864 | bytes 4194304 | tf_op jit(solution)/shard_map/diffuse_forward/pallas_call | solution.py:583
  21.9 6.2 %lookup.1 = f32[64,128]{1,0:T(8,128)S(1)} custom-call(f32[1024,128]{1,0:T(8,128)S(1)} %bitcast.54, f32[256,128]{1,0:T(8,128)S(1)} %bitcast.55, s32[64,128]{1,0:T(8,128)S(1)} %get-tuple-element.41.row_ref, s32[64,128]{1,0:T(8,128)S(1)} %get-tuple-element.42.lane_ref), custom_call_target="tpu_custom_call" | custom-call | flops 4294967296 | bytes 16777216 | tf_op jit(solution)/shard_map/lookup/pallas_call | solution.py:596
  28.1 2.7 %all-to-all-done.slots_ref = f32[32,2,8,128]{3,2,1,0:T(8,128)S(1)} async-done(((f32[32,2,8,128]{3,2,1,0:T(8,128)}), f32[32,2,8,128]{3,2,1,0:T(8,128)S(1)}, u32[]{:S(2)}, u32[]{:S(2)}) %all-to-all-start) | async-done | bytes 262176 | tf_op jit(solution)/shard_map/all_to_all | solution.py:581
  30.8 0.5 collective-permute-start.3
  31.3 3.4 %collective-permute-done.3 = f32[64,128]{1,0:T(8,128)S(1)} collective-permute-done((f32[64,128]{1,0:T(8,128)S(1)}, f32[64,128]{1,0:T(8,128)S(1)}, u32[]{:S(2)}, u32[]{:S(2)}) %collective-permute-start.3) | collective-permute-done | bytes 32800 | tf_op jit(solution)/shard_map/ppermute | solution.py:466
  34.7 0.6 collective-permute-start.4
  35.3 3.3 %collective-permute-done.4.refs_1_ = f32[64,128]{1,0:T(8,128)S(1)} collective-permute-done((f32[64,128]{1,0:T(8,128)S(1)}, f32[64,128]{1,0:T(8,128)S(1)}, u32[]{:S(2)}, u32[]{:S(2)}) %collective-permute-start.4) | collective-permute-done | bytes 32800 | tf_op jit(solution)/shard_map/ppermute | solution.py:466
  38.6 2.8 %scatter_own.1 = (f32[256,128]{1,0:T(8,128)S(1)}, f32[64,128]{1,0:T(8,128)S(1)}) custom-call(s32[64,128]{1,0:T(8,128)S(1)} %get-tuple-element.41.row_ref, s32[64,128]{1,0:T(8,128)S(1)} %get-tuple-element.42.lane_ref, f32[32,2,8,128]{3,2,1,0:T(8,128)S(1)} %all-to-all-done.slots_ref, f32[64,128]{1,0:T(8,128)S(1)} %add.9.refs_0_, ...), custom_call_target="tpu_custom_call" | custom-call | tf_op jit(solution)/shard_map/scatter_own/pallas_call | solution.py:611
  41.4 0.5 collective-permute-start.5
  42.0 3.4 %collective-permute-start.6 = (f32[4,64,128]{2,1,0:T(8,128)S(1)}, f32[4,64,128]{2,1,0:T(8,128)S(1)}, u32[]{:S(2)}, u32[]{:S(2)}) collective-permute-start(f32[4,64,128]{2,1,0:T(8,128)S(1)} %bitcast.49), channel_id=1, source_target_pairs={{0,6},{1,7},{2,0},{3,1},{4,2},{5,3},{6,4},{7,5},{8,14},{9,15},{10,... | collective-permute-start | bytes 393224 | tf_op jit(solution)/shard_map/ppermute | solution.py:452
  45.3 5.0 %scatter_rest.1 = (f32[1024,128]{1,0:T(8,128)S(1)}, f32[16,64,128]{2,1,0:T(8,128)S(1)}, f32[8,16,64,128]{3,2,1,0:T(8,128)S(1)}, bf16[8,16,64,128]{3,2,1,0:T(8,128)(2,1)S(1)}) custom-call(s32[64,128]{1,0:T(8,128)S(1)} %get-tuple-element.41.row_ref, s32[64,128]{1,0:T(8,128)S(1)} %get-tuple-element.42.lane_ref, f32[64,128]{1,0:T(8,128)S(1)} %get-tuple-element.49.amount_ref, ...), custom_call_target="tpu_custom_call" | custom-call | tf_op jit(solution)/shard_map/scatter_rest/pallas_call | solution.py:623
  50.3 0.0 collective-permute-done.6.after_ref
  50.4 0.1 collective-permute-start.7
  50.5 1.2 %level_matrices.1 = (bf16[256,768]{1,0:T(8,128)(2,1)S(1)}, bf16[256,768]{1,0:T(8,128)(2,1)S(1)}) custom-call(f32[16,16]{1,0:T(8,128)} %local_ref, f32[16,16]{1,0:T(8,128)} %root_ref.2), custom_call_target="tpu_custom_call" | custom-call | tf_op jit(solution)/shard_map/level_matrices/pallas_call | solution.py:641
  51.7 0.3 collective-permute-done.7.other_ref
  52.0 1.4 %diffuse_adjoint.1.refs_0_ = f32[4,64,128]{2,1,0:T(8,128)S(1)} custom-call(f32[5,10,32,128]{3,2,1,0:T(8,128)S(1)} %get-tuple-element.57.coef_ref, f32[4,64,128]{2,1,0:T(8,128)S(1)} %collective-permute-done.5.before_ref, f32[4,64,128]{2,1,0:T(8,128)S(1)} %bitcast.51, f32[4,64,128]{2,1,0:T(8,128)S(1)} %collective-permute-done.6.after_ref, ...), custom_call_target="tpu_custom_call" | custom-call | tf_op jit(solution)/shard_map/diffuse_adjoint/pallas_call | solution.py:652
  53.4 0.8 %collective-permute-start.8 = (f32[4,64,128]{2,1,0:T(8,128)S(1)}, f32[4,64,128]{2,1,0:T(8,128)S(1)}, u32[]{:S(2)}, u32[]{:S(2)}) collective-permute-start(f32[4,64,128]{2,1,0:T(8,128)S(1)} %diffuse_adjoint.1.refs_0_), channel_id=1, source_target_pairs={{8,0},{16,8},{24,16},{0,24},{9,1},{17,9},{25,17},{1,25},{10,2},{18... | collective-permute-start | bytes 393224 | tf_op jit(solution)/shard_map/ppermute | solution.py:457
  54.2 1.3 %collective-permute-start.9 = (f32[4,64,128]{2,1,0:T(8,128)S(1)}, f32[4,64,128]{2,1,0:T(8,128)S(1)}, u32[]{:S(2)}, u32[]{:S(2)}) collective-permute-start(f32[4,64,128]{2,1,0:T(8,128)S(1)} %diffuse_adjoint.1.refs_0_), channel_id=1, source_target_pairs={{16,0},{24,8},{0,16},{8,24},{17,1},{25,9},{1,17},{9,25},{18,2},{26... | collective-permute-start | bytes 393224 | tf_op jit(solution)/shard_map/ppermute | solution.py:457
  55.5 0.6 collective-permute-start.10
  56.0 5.6 %members_gradient.1 = f32[8,16,64,128]{3,2,1,0:T(8,128)} custom-call(bf16[256,768]{1,0:T(8,128)(2,1)S(1)} %get-tuple-element.62.matrix_ref, f32[16,64,128]{2,1,0:T(8,128)S(1)} %bitcast.53, f32[8,16,64,128]{3,2,1,0:T(8,128)S(1)} %get-tuple-element.64.control_ref, bf16[8,16,64,128]{3,2,1,0:T(8,128)(2,1)S(1)} %get-tuple-element.65.pert_ref), custom_call_target="tpu_custom_call" | custom-call | tf_op jit(solution)/shard_map/members_gradient/pallas_call | solution.py:664
  61.6 0.8 %collective-permute-done.9.refs_2_ = f32[4,64,128]{2,1,0:T(8,128)S(1)} collective-permute-done((f32[4,64,128]{2,1,0:T(8,128)S(1)}, f32[4,64,128]{2,1,0:T(8,128)S(1)}, u32[]{:S(2)}, u32[]{:S(2)}) %collective-permute-start.9) | collective-permute-done | bytes 131104 | tf_op jit(solution)/shard_map/ppermute | solution.py:457
  62.4 0.0 collective-permute-done.10.refs_3_
  62.4 1.2 %static_gradient.1 = f32[16,64,128]{2,1,0:T(8,128)} custom-call(bf16[256,768]{1,0:T(8,128)(2,1)S(1)} %get-tuple-element.55.matrix_ref, f32[16,64,128]{2,1,0:T(8,128)S(1)} %get-tuple-element.56.static_ref, f32[4,64,128]{2,1,0:T(8,128)S(1)} %diffuse_adjoint.1.refs_0_, f32[4,64,128]{2,1,0:T(8,128)S(1)} %collective-permute-done.8.refs_1_, ...), custom_call_target="tpu_custom_call" | custom-call | tf_op jit(solution)/shard_map/static_gradient/pallas_call | solution.py:674
  (7 shorter events, 0.1 us)
Async XLA Ops:
  1.9 13.6 %collective-permute-start = (f32[6,64,128]{2,1,0:T(8,128)S(1)}, f32[6,64,128]{2,1,0:T(8,128)S(1)}, u32[]{:S(2)}, u32[]{:S(2)}) collective-permute-start(f32[6,64,128]{2,1,0:T(8,128)S(1)} %get-tuple-element.38.own_ref), channel_id=1, source_target_pairs={{0,2},{1,3},{2,4},{3,5},{4,6},{5,7},{6,0},{7,1},{8,10},{9,11},{10,... | collective-permute-start | bytes 589832 | tf_op jit(solution)/shard_map/ppermute | solution.py:452
  5.0 10.6 %collective-permute-start.1 = (f32[6,64,128]{2,1,0:T(8,128)S(1)}, f32[6,64,128]{2,1,0:T(8,128)S(1)}, u32[]{:S(2)}, u32[]{:S(2)}) collective-permute-start(f32[6,64,128]{2,1,0:T(8,128)S(1)} %get-tuple-element.38.own_ref), channel_id=1, source_target_pairs={{0,6},{1,7},{2,0},{3,1},{4,2},{5,3},{6,4},{7,5},{8,14},{9,15},{10,... | collective-permute-start | bytes 589832 | tf_op jit(solution)/shard_map/ppermute | solution.py:452
  15.7 4.7 %collective-permute-start.2 = (f32[2,6,64,128]{3,2,1,0:T(8,128)S(1)}, f32[2,6,64,128]{3,2,1,0:T(8,128)S(1)}, u32[]{:S(2)}, u32[]{:S(2)}) collective-permute-start(f32[2,6,64,128]{3,2,1,0:T(8,128)S(1)} %pad_maximum_fusion), channel_id=1, source_target_pairs={{0,1},{1,0},{2,3},{3,2},{4,5},{5,4},{6,7},{7,6},{8,9},{9,8},{10,11... | collective-permute-start | bytes 1179656 | tf_op jit(solution)/shard_map/ppermute | solution.py:477
  15.7 15.0 %all-to-all-start = ((f32[32,2,8,128]{3,2,1,0:T(8,128)}), f32[32,2,8,128]{3,2,1,0:T(8,128)S(1)}, u32[]{:S(2)}, u32[]{:S(2)}) async-start(f32[32,2,8,128]{3,2,1,0:T(8,128)} %get-tuple-element.45), calls=%async_computation | async-start | bytes 524288 | tf_op jit(solution)/shard_map/all_to_all | solution.py:581
  30.8 3.9 %collective-permute-start.3 = (f32[64,128]{1,0:T(8,128)S(1)}, f32[64,128]{1,0:T(8,128)S(1)}, u32[]{:S(2)}, u32[]{:S(2)}) collective-permute-start(f32[64,128]{1,0:T(8,128)S(1)} %lookup.1), channel_id=1, source_target_pairs={{0,8},{8,0},{16,24},{24,16},{1,9},{9,1},{17,25},{25,17},{2,10},{10... | collective-permute-start | bytes 98312 | tf_op jit(solution)/shard_map/ppermute | solution.py:466
  34.7 3.9 %collective-permute-start.4 = (f32[64,128]{1,0:T(8,128)S(1)}, f32[64,128]{1,0:T(8,128)S(1)}, u32[]{:S(2)}, u32[]{:S(2)}) collective-permute-start(f32[64,128]{1,0:T(8,128)S(1)} %add.9.refs_0_), channel_id=1, source_target_pairs={{0,16},{8,24},{16,0},{24,8},{1,17},{9,25},{17,1},{25,9},{2,18},{10... | collective-permute-start | bytes 98312 | tf_op jit(solution)/shard_map/ppermute | solution.py:466
  41.4 8.9 %collective-permute-start.5 = (f32[4,64,128]{2,1,0:T(8,128)S(1)}, f32[4,64,128]{2,1,0:T(8,128)S(1)}, u32[]{:S(2)}, u32[]{:S(2)}) collective-permute-start(f32[4,64,128]{2,1,0:T(8,128)S(1)} %bitcast.48), channel_id=1, source_target_pairs={{0,2},{1,3},{2,4},{3,5},{4,6},{5,7},{6,0},{7,1},{8,10},{9,11},{10,... | collective-permute-start | bytes 393224 | tf_op jit(solution)/shard_map/ppermute | solution.py:452
  42.0 8.4 %collective-permute-start.6 = (f32[4,64,128]{2,1,0:T(8,128)S(1)}, f32[4,64,128]{2,1,0:T(8,128)S(1)}, u32[]{:S(2)}, u32[]{:S(2)}) collective-permute-start(f32[4,64,128]{2,1,0:T(8,128)S(1)} %bitcast.49), channel_id=1, source_target_pairs={{0,6},{1,7},{2,0},{3,1},{4,2},{5,3},{6,4},{7,5},{8,14},{9,15},{10,... | collective-permute-start | bytes 393224 | tf_op jit(solution)/shard_map/ppermute | solution.py:452
  50.4 1.6 %collective-permute-start.7 = (f32[2,4,64,128]{3,2,1,0:T(8,128)S(1)}, f32[2,4,64,128]{3,2,1,0:T(8,128)S(1)}, u32[]{:S(2)}, u32[]{:S(2)}) collective-permute-start(f32[2,4,64,128]{3,2,1,0:T(8,128)S(1)} %pad_maximum_fusion.1), channel_id=1, source_target_pairs={{0,1},{1,0},{2,3},{3,2},{4,5},{5,4},{6,7},{7,6},{8,9},{9,8},{10,11... | collective-permute-start | bytes 786440 | tf_op jit(solution)/shard_map/ppermute | solution.py:477
  53.4 8.2 %collective-permute-start.8 = (f32[4,64,128]{2,1,0:T(8,128)S(1)}, f32[4,64,128]{2,1,0:T(8,128)S(1)}, u32[]{:S(2)}, u32[]{:S(2)}) collective-permute-start(f32[4,64,128]{2,1,0:T(8,128)S(1)} %diffuse_adjoint.1.refs_0_), channel_id=1, source_target_pairs={{8,0},{16,8},{24,16},{0,24},{9,1},{17,9},{25,17},{1,25},{10,2},{18... | collective-permute-start | bytes 393224 | tf_op jit(solution)/shard_map/ppermute | solution.py:457
  54.2 8.2 %collective-permute-start.9 = (f32[4,64,128]{2,1,0:T(8,128)S(1)}, f32[4,64,128]{2,1,0:T(8,128)S(1)}, u32[]{:S(2)}, u32[]{:S(2)}) collective-permute-start(f32[4,64,128]{2,1,0:T(8,128)S(1)} %diffuse_adjoint.1.refs_0_), channel_id=1, source_target_pairs={{16,0},{24,8},{0,16},{8,24},{17,1},{25,9},{1,17},{9,25},{18,2},{26... | collective-permute-start | bytes 393224 | tf_op jit(solution)/shard_map/ppermute | solution.py:457
  55.5 6.9 %collective-permute-start.10 = (f32[4,64,128]{2,1,0:T(8,128)S(1)}, f32[4,64,128]{2,1,0:T(8,128)S(1)}, u32[]{:S(2)}, u32[]{:S(2)}) collective-permute-start(f32[4,64,128]{2,1,0:T(8,128)S(1)} %diffuse_adjoint.1.refs_0_), channel_id=1, source_target_pairs={{24,0},{0,8},{8,16},{16,24},{25,1},{1,9},{9,17},{17,25},{26,2},{2,... | collective-permute-start | bytes 393224 | tf_op jit(solution)/shard_map/ppermute | solution.py:457

commit v8 on v7

--- a/solution.py
+++ b/solution.py
@@ -82,6 +82,10 @@
     if size & (size - 1):
         return lax.div(x, jnp.int32(size)), lax.rem(x, jnp.int32(size))
     return lax.shift_right_logical(x, jnp.int32(size.bit_length() - 1)), x & (size - 1)
+
+
+def peer(i, d, count):
+    return (i + d) % count if count & (count - 1) else i ^ d
 
 
 def prepare_kernel(lev_share, rows, root_ref, count_ref, static_ref, north_ref, east_ref, index_ref, out_ref, row_ref, lane_ref):
@@ -189,10 +193,9 @@
         )
         for t in range(2)
     )
-    for e in range(out_ref.shape[0] // n_cols):
-        for p in range(n_cols):
-            out_ref[e * n_cols + p, 0] = weights[p * cap_rows : (p + 1) * cap_rows]
-            out_ref[e * n_cols + p, 1] = amounts[p * cap_rows : (p + 1) * cap_rows]
+    for p in range(n_cols):
+        out_ref[p, 0] = weights[p * cap_rows : (p + 1) * cap_rows]
+        out_ref[p, 1] = amounts[p * cap_rows : (p + 1) * cap_rows]
     for copy in copies[3:]:
         copy.wait()
     matrix_ref[...] = level_product(local_ref[...] * f32(scale), False)
@@ -250,22 +253,24 @@
     return jnp.where(lane == 0, pltpu.roll(near, 1, 0), near)
 
 
-def rows_of(tiles, plane, rows):
+def rows_of(first_ref, second_ref, own_ref, other_ref, plane, rows):
     at = lax.axis_index("cols")
-    side = len(tiles) // 2
-    out = []
-    for i, tile in enumerate(tiles):
-        for r in range(rows):
-            row = tile[plane, pl.ds(r, tile.shape[1] // rows, stride=rows), :]
-            if i != side:
-                there = at + (i - side)
-                row = jnp.where(jnp.logical_and(there >= 0, there < lax.axis_size("cols")), row, f32(0))
-            out.append(row)
-    return out
+    count = lax.axis_size("cols")
+    core, chip = at % 2, at // 2 % 2
+    reads = [pl.ds(r, own_ref.shape[1] // rows, stride=rows) for r in range(rows)]
+    first = [first_ref[plane, r, :] for r in reads]
+    second = [second_ref[plane, r, :] for r in reads]
+    out = [jnp.where(jnp.logical_and(chip == 1, at >= 2), f, f32(0)) for f in first]
+    out = [jnp.where(jnp.logical_and(chip == 0, at >= 2), s, o) for s, o in zip(second, out)]
+    out += [jnp.where(at >= 1, other_ref[1 - core, plane, r, :], f32(0)) for r in reads]
+    out += [own_ref[plane, r, :] for r in reads]
+    out += [jnp.where(at < count - 1, other_ref[core, plane, r, :], f32(0)) for r in reads]
+    last = [jnp.where(jnp.logical_and(chip == 0, at < count - 2), f, f32(0)) for f in first]
+    return out + [jnp.where(jnp.logical_and(chip == 1, at < count - 2), s, o) for s, o in zip(second, last)]
 
 
 def diffuse_rows(tiles, level, coef_ref, rows):
-    field = rows_of(tiles, level, rows)
+    field = rows_of(*tiles, level, rows)
     for step in range(NDIFF):
         field = [
             coef_ref[0, i + step] * field[i]
@@ -279,17 +284,12 @@
     return field
 
 
-def tiles_of(before_ref, own_ref, after_ref, other_ref):
-    odd = lax.axis_index("cols") % 2
-    return [before_ref, other_ref.at[1 - odd], own_ref, other_ref.at[odd], after_ref]
-
-
-def first_diffusion_kernel(lev_share, rows, before_ref, own_ref, after_ref, other_ref, out_ref, coef_ref):
-    tiles = tiles_of(before_ref, own_ref, after_ref, other_ref)
+def first_diffusion_kernel(lev_share, rows, first_ref, second_ref, own_ref, other_ref, out_ref, coef_ref):
+    tiles = (first_ref, second_ref, own_ref, other_ref)
     blocks = own_ref.shape[1] // rows
-    side = len(tiles) // 2
-    north = rows_of(tiles, lev_share, rows)
-    east = rows_of(tiles, lev_share + 1, rows)
+    side = 2
+    north = rows_of(*tiles, lev_share, rows)
+    east = rows_of(*tiles, lev_share + 1, rows)
     for i in range(1, len(north) - 1):
         south = north[i + 1]
         if (i + 1) % rows == 0 and i < side * rows:
@@ -313,8 +313,8 @@
     lax.fori_loop(0, lev_share, body, 0)
 
 
-def second_diffusion_kernel(rows, coef_ref, before_ref, own_ref, after_ref, other_ref, out_ref):
-    tiles = tiles_of(before_ref, own_ref, after_ref, other_ref)
+def second_diffusion_kernel(rows, coef_ref, first_ref, second_ref, own_ref, other_ref, out_ref):
+    tiles = (first_ref, second_ref, own_ref, other_ref)
     lev_share = out_ref.shape[0]
     blocks = own_ref.shape[1] // rows
 
@@ -374,8 +374,8 @@
     acc_ref[...] += product_nt(jnp.concatenate(left, axis=1), jnp.concatenate(right, axis=1))
 
 
-def scatter_own_kernel(cap_rows, row_ref, lane_ref, slots_ref, *refs):
-    values, (out_ref, amount_ref, acc_ref) = refs[:-3], refs[-3:]
+def scatter_own_kernel(cap_rows, row_ref, lane_ref, *refs):
+    shares, (out_ref, amount_ref, acc_ref) = refs[:-3], refs[-3:]
     own = out_ref.shape[0]
     lists = row_ref.shape[0] // cap_rows
     first = lax.axis_index("ens") * own
@@ -383,11 +383,7 @@
 
     def step(q, carry):
         at = pl.ds(pl.multiple_of(q * cap_rows, cap_rows), cap_rows)
-        value = functools.reduce(jnp.add, [v[at, :] for v in values])
-        weight, amount = (
-            functools.reduce(jnp.add, [slots_ref[e * lists + q, t] for e in range(slots_ref.shape[0] // lists)])
-            for t in range(2)
-        )
+        value, weight, amount = (functools.reduce(jnp.add, [s[t, at, :] for s in shares]) for t in range(3))
         amounts = value * weight - amount
         amount_ref[at, :] = amounts
         put(acc_ref, row_ref[at, :] - first, lane_ref[at, :], amounts)
@@ -438,7 +434,7 @@
     share = levels // len(parts)
     me = lax.axis_index("ens")
     for d, part in enumerate(parts):
-        smooth_ref[pl.ds((me + d) % len(parts) * share, share)] = part[...]
+        smooth_ref[pl.ds(peer(me, d, len(parts)) * share, share)] = part[...]
     for j in range(0, per_level, 32):
         terms = [three_terms(smooth_ref[:, j + i : j + i + 16, :].reshape(levels * 16, LANES)) for i in (0, 16)]
         change = jnp.dot(matrix_ref[...], jnp.concatenate(terms, axis=1), preferred_element_type=f32)
@@ -447,34 +443,28 @@
             out_ref[:, at, :] = static_ref[:, at, :] + part.reshape(levels, 16, LANES)
 
 
-def shifted(x, by):
+def exchanged(x):
     count = lax.axis_size("cols")
-    return lax.ppermute(x, "cols", [(i, (i + by) % count) for i in range(count)])
+    out = []
+    for start in (0, 1):
+        pairs = []
+        for i in range(count):
+            chip, core = divmod(i, 2)
+            partner = (chip + start ^ 1) - start
+            pairs.append((i, 2 * partner + core if 0 <= 2 * partner + core < count else i))
+        out.append(lax.ppermute(x, "cols", pairs))
+    return out
 
 
 def from_peers(x):
     count = lax.axis_size("ens")
-    return [lax.ppermute(x, "ens", [((i + d) % count, i) for i in range(count)]) for d in range(1, count)]
-
-
-def over_ens(x):
-    count = lax.axis_size("ens")
-    if count < 2 or count & (count - 1):
-        return [x] + from_peers(x)
-    by = 1
-    while True:
-        other = lax.ppermute(x, "ens", [(i, i ^ by) for i in range(count)])
-        by *= 2
-        if by == count:
-            return [x, other]
-        x = x + other
-
-
-def swapped(own, before, after):
-    odd = lax.axis_index("cols") % 2
-    count = lax.axis_size("cols")
-    pack = jnp.stack([own, jnp.where(odd == 1, before, after)])
-    return lax.ppermute(pack, "cols", [(i, i ^ 1) for i in range(count)])
+    return [lax.ppermute(x, "ens", [(peer(i, d, count), i) for i in range(count)]) for d in range(1, count)]
+
+
+def swapped(own, first, second):
+    at = lax.axis_index("cols")
+    pack = jnp.stack([own, jnp.where(at % 2 == at // 2 % 2, first, second)])
+    return lax.ppermute(pack, "cols", [(i, i ^ 1) for i in range(lax.axis_size("cols"))])
 
 
 def local(
@@ -537,7 +527,7 @@
         in_hbm(tiled(face_east)),
         in_hbm(send_index),
     )
-    before, after = shifted(packed, 2), shifted(packed, -2)
+    first, second = exchanged(packed)
 
     obs_rows = obs_slot.shape[0] // LANES
     share_rows = obs_rows // n_ens
@@ -548,9 +538,9 @@
         functools.partial(observe_kernel, n_cols, cap_rows, member_scale),
         grid=(1,),
         in_specs=[pl.BlockSpec(memory_space=pl.ANY)] * 6,
-        out_specs=[whole(n_ens * n_cols, 2, cap_rows, LANES), VMEM],
+        out_specs=[whole(n_cols, 2, cap_rows, LANES), VMEM],
         out_shape=[
-            pltpu.HBM((n_ens * n_cols, 2, cap_rows, LANES), f32),
+            pltpu.HBM((n_cols, 2, cap_rows, LANES), f32),
             pltpu.VMEM((levels, per_level, LANES), f32),
         ],
         scratch_shapes=[
@@ -576,9 +566,9 @@
         control,
         pert,
     )
-    before, after, slots = lax.optimization_barrier((before, after, slots))
-    other = swapped(packed, before, after)
-    slots = lax.all_to_all(slots, ("ens", "cols"), split_axis=0, concat_axis=0, tiled=True)
+    first, second, slots = lax.optimization_barrier((first, second, slots))
+    other = swapped(packed, first, second)
+    slots = lax.all_to_all(slots, "cols", split_axis=0, concat_axis=0, tiled=True)
 
     increment, coefs = pl.pallas_call(
         functools.partial(first_diffusion_kernel, lev_share, rows),
@@ -591,7 +581,7 @@
         compiler_params=params(8),
         cost_estimate=pl.CostEstimate(flops=1 << 26, bytes_accessed=1 << 22, transcendentals=0),
         name="diffuse_forward",
-    )(before, packed, after, other)
+    )(first, second, packed, other)
 
     values = pl.pallas_call(
         functools.partial(lookup_kernel, cap_rows),
@@ -606,19 +596,21 @@
         name="lookup",
     )(part.reshape(cells, LANES), increment.reshape(own, LANES), entry_row, entry_lane)
     values, slots = lax.optimization_barrier((values, slots))
-    shares = over_ens(values)
+    slots = jnp.swapaxes(slots, 0, 1).reshape(2, entry_rows, LANES)
+    share = jnp.concatenate([values[None], slots])
+    shares = [share] + from_peers(share)
 
     adjoint_own, amounts = pl.pallas_call(
         functools.partial(scatter_own_kernel, cap_rows),
-        in_specs=[VMEM] * (3 + len(shares)),
+        in_specs=[VMEM] * (2 + n_ens),
         out_specs=[VMEM] * 2,
         out_shape=[pltpu.VMEM((own, LANES), f32), pltpu.VMEM((entry_rows, LANES), f32)],
         scratch_shapes=[pltpu.VMEM((own, 2 * LANES), f32)],
         compiler_params=params(16),
         name="scatter_own",
-    )(entry_row, entry_lane, slots, *shares)
+    )(entry_row, entry_lane, *shares)
     tile = adjoint_own.reshape(lev_share, per_level, LANES)
-    tile_before, tile_after = shifted(tile, 2), shifted(tile, -2)
+    tile_first, tile_second = exchanged(tile)
 
     adjoint, static_here, control_here, pert_here = pl.pallas_call(
         functools.partial(scatter_rest_kernel, cap_rows),
@@ -634,10 +626,10 @@
         compiler_params=params(16),
         name="scatter_rest",
     )(entry_row, entry_lane, amounts, adjoint_own, static, control, pert)
-    tile_before, tile_after, adjoint, vertical_local, vertical_root = lax.optimization_barrier(
-        (tile_before, tile_after, adjoint, vertical_local, vertical_root)
+    tile_first, tile_second, adjoint, vertical_local, vertical_root = lax.optimization_barrier(
+        (tile_first, tile_second, adjoint, vertical_local, vertical_root)
     )
-    tile_other = swapped(tile, tile_before, tile_after)
+    tile_other = swapped(tile, tile_first, tile_second)
     from_local, from_root = pl.pallas_call(
         functools.partial(matrices_kernel, member_scale),
         grid=(1,),
@@ -656,7 +648,7 @@
         out_shape=pltpu.VMEM((lev_share, per_level, LANES), f32),
         compiler_params=params(8),
         name="diffuse_adjoint",
-    )(coefs, tile_before, tile, tile_after, tile_other)
+    )(coefs, tile_first, tile_second, tile, tile_other)
     smooth, adjoint = lax.optimization_barrier((smooth, adjoint))
     smooths = [smooth] + from_peers(smooth)
 

time: 63.9 us -> 61.8 us (0.967); the launches traced: 63.6 us -> 60.7 us
  waiting for transfers between devices: 10.6 us -> 5.63 us
  starting transfers between devices: 17.6 us -> 19.5 us
    all_to_all x1, waiting for transfers between devices: 2.67 us -> 0.01 us  [local(): lax.all_to_all(slots, 'cols', split_axis=0, concat_axis=0, tiled=True)]
    ppermute x11 -> x12, waiting for transfers between devices: 7.89 us -> 5.63 us  [the longest x6 5.35 us: from_peers(): lax.ppermute(x, 'ens', [(peer(i, d, count), i) for i in range(count)])]
    all_to_all x1, starting transfers between devices: 4.66 us -> 5.76 us  [local(): lax.all_to_all(slots, 'cols', split_axis=0, concat_axis=0, tiled=True)]
    ppermute x11 -> x12, starting transfers between devices: 12.9 us -> 13.7 us  [the longest x6 7.11 us: from_peers(): lax.ppermute(x, 'ens', [(peer(i, d, count), i) for i in range(count)])]
  transfers between devices with their start and end apart: 12 -> 13, of which waited for: 6 -> 5; matrix products, arithmetic and copies ran while one was open for 0% -> 0% of each run, Pallas kernels for 44% -> 46%
where the time goes in v8:
time: 61.8 us; the launch traced here: 60.7 us
  Pallas kernels  34.6 us (56%)
  starting transfers between devices  19.5 us (32%)
  waiting for transfers between devices  5.63 us (9%)
  between operations  0.86 us (1%)
    pallas_call x1, Pallas kernels, local(): pl.pallas_call(functools.partial(observe_kernel, n_cols, cap_rows, member...  8.33 us
    ppermute x6, starting transfers between devices, from_peers(): lax.ppermute(x, 'ens', [(peer(i, d, count), i) for i in range(count)])  7.11 us
    ppermute x4, starting transfers between devices, exchanged(): out.append(lax.ppermute(x, 'cols', pairs))  6.45 us
    pallas_call x1, Pallas kernels, local(): pl.pallas_call(functools.partial(lookup_kernel, cap_rows), in_specs=[VMEM...  6.2 us
    all_to_all x1, starting transfers between devices, local(): lax.all_to_all(slots, 'cols', split_axis=0, concat_axis=0, tiled=True)  5.76 us
    pallas_call x1, Pallas kernels, local(): pl.pallas_call(member_kernel, grid=(members // group,), in_specs=[VMEM] *...  5.57 us
    ppermute x6, waiting for transfers between devices, from_peers(): lax.ppermute(x, 'ens', [(peer(i, d, count), i) for i in range(count)])  5.35 us
    pallas_call x1, Pallas kernels, local(): pl.pallas_call(functools.partial(scatter_rest_kernel, cap_rows), in_specs...  5.04 us
  transfers between devices with their start and end apart: 13, of which 5 were waited for; matrix products, arithmetic and copies ran while one was open for 0% of the time, Pallas kernels for 46%

profile of v8, /device:TPU:0, one launch (start us, length us, event | category | flops | bytes accessed | tf_op | source)
XLA Modules:
  0.0 60.7 jit_solution(481509934828144492)
XLA Ops:
  0.6 1.3 %prepare.1 = (f32[6,64,128]{2,1,0:T(8,128)S(1)}, s32[64,128]{1,0:T(8,128)S(1)}, s32[64,128]{1,0:T(8,128)S(1)}) custom-call(f32[16,16]{1,0:T(8,128)} %root_ref.2, s32[8]{0:T(128)} %count_ref.1, f32[16,64,128]{2,1,0:T(8,128)} %bitcast.68, f32[64,128]{1,0:T(8,128)} %bitcast.74, f32[64,128]{1,0:T(8,128)} %bitcast.75, s32[8,1024]{1,0:T(8,128)} %index_ref.1), custom_call_target="tpu_custom_call" | custom-call | tf_op jit(solution)/shard_map/prepare/pallas_call | solution.py:503
  1.9 3.1 %collective-permute-start = (f32[6,64,128]{2,1,0:T(8,128)S(1)}, f32[6,64,128]{2,1,0:T(8,128)S(1)}, u32[]{:S(2)}, u32[]{:S(2)}) collective-permute-start(f32[6,64,128]{2,1,0:T(8,128)S(1)} %get-tuple-element.39.own_ref), channel_id=1, source_target_pairs={{0,2},{1,3},{2,0},{3,1},{4,6},{5,7},{6,4},{7,5},{8,10},{9,11},{10,... | collective-permute-start | bytes 589832 | tf_op jit(solution)/shard_map/ppermute | solution.py:455
  5.0 0.7 %collective-permute-start.1 = (f32[6,64,128]{2,1,0:T(8,128)S(1)}, f32[6,64,128]{2,1,0:T(8,128)S(1)}, u32[]{:S(2)}, u32[]{:S(2)}) collective-permute-start(f32[6,64,128]{2,1,0:T(8,128)S(1)} %get-tuple-element.39.own_ref), channel_id=1, source_target_pairs={{0,0},{1,1},{2,4},{3,5},{4,2},{5,3},{6,6},{7,7},{8,8},{9,9},{10,12... | collective-permute-start | bytes 589832 | tf_op jit(solution)/shard_map/ppermute | solution.py:455
  5.7 8.3 %slot_sums_and_members.1 = (f32[8,2,8,128]{3,2,1,0:T(8,128)}, f32[16,64,128]{2,1,0:T(8,128)S(1)}) custom-call(s32[512,128]{1,0:T(8,128)} %bitcast.71, f32[512,128]{1,0:T(8,128)} %bitcast.72, f32[512,128]{1,0:T(8,128)} %bitcast.73, f32[16,16]{1,0:T(8,128)} %local_ref, f32[8,16,64,128]{3,2,1,0:T(8,128)} %bitcast.63, bf16[8,16,64,128]{3,2,1,0:T(8,128)(2,1)} %bitcast.65), custom_call_target="tpu_custom_call" | custom-call | tf_op jit(solution)/shard_map/slot_sums_and_members/pallas_call | solution.py:537
  14.1 0.0 collective-permute-done.first_ref
  14.1 0.0 collective-permute-done.1.second_ref
  14.2 0.1 collective-permute-start.2
  14.2 5.8 %all-to-all-start = ((f32[8,2,8,128]{3,2,1,0:T(8,128)}), f32[8,2,8,128]{3,2,1,0:T(8,128)S(1)}, u32[]{:S(2)}, u32[]{:S(2)}) async-start(f32[8,2,8,128]{3,2,1,0:T(8,128)} %get-tuple-element.45), calls=%async_computation | async-start | bytes 131072 | tf_op jit(solution)/shard_map/all_to_all | solution.py:571
  20.0 0.0 collective-permute-done.2.other_ref
  20.0 1.5 %diffuse_forward.1 = (f32[4,64,128]{2,1,0:T(8,128)S(1)}, f32[5,10,32,128]{3,2,1,0:T(8,128)S(1)}) custom-call(f32[6,64,128]{2,1,0:T(8,128)S(1)} %collective-permute-done.first_ref, f32[6,64,128]{2,1,0:T(8,128)S(1)} %collective-permute-done.1.second_ref, f32[6,64,128]{2,1,0:T(8,128)S(1)} %get-tuple-element.39.own_ref, ...), custom_call_target="tpu_custom_call" | custom-call | flops 67108864 | bytes 4194304 | tf_op jit(solution)/shard_map/diffuse_forward/pallas_call | solution.py:573
  21.5 6.2 %lookup.1 = f32[64,128]{1,0:T(8,128)S(1)} custom-call(f32[1024,128]{1,0:T(8,128)S(1)} %bitcast.61, f32[256,128]{1,0:T(8,128)S(1)} %bitcast.62, s32[64,128]{1,0:T(8,128)S(1)} %get-tuple-element.41.row_ref, s32[64,128]{1,0:T(8,128)S(1)} %get-tuple-element.42.lane_ref), custom_call_target="tpu_custom_call" | custom-call | flops 4294967296 | bytes 16777216 | tf_op jit(solution)/shard_map/lookup/pallas_call | solution.py:586
  27.7 0.0 all-to-all-done
  27.8 1.6 %collective-permute-start.3 = (f32[3,64,128]{2,1,0:T(8,128)S(1)}, f32[3,64,128]{2,1,0:T(8,128)S(1)}, u32[]{:S(2)}, u32[]{:S(2)}) collective-permute-start(f32[3,64,128]{2,1,0:T(8,128)S(1)} %pad_maximum_fusion.2.refs_0_), channel_id=1, source_target_pairs={{8,0},{0,8},{24,16},{16,24},{9,1},{1,9},{25,17},{17,25},{10,2},{2,... | collective-permute-start | bytes 294920 | tf_op jit(solution)/shard_map/ppermute | solution.py:461
  29.3 1.5 %collective-permute-start.4 = (f32[3,64,128]{2,1,0:T(8,128)S(1)}, f32[3,64,128]{2,1,0:T(8,128)S(1)}, u32[]{:S(2)}, u32[]{:S(2)}) collective-permute-start(f32[3,64,128]{2,1,0:T(8,128)S(1)} %pad_maximum_fusion.2.refs_0_), channel_id=1, source_target_pairs={{16,0},{24,8},{0,16},{8,24},{17,1},{25,9},{1,17},{9,25},{18,2},{26... | collective-permute-start | bytes 294920 | tf_op jit(solution)/shard_map/ppermute | solution.py:461
  30.8 0.5 collective-permute-start.5
  31.3 1.7 %collective-permute-done.3.refs_1_ = f32[3,64,128]{2,1,0:T(8,128)S(1)} collective-permute-done((f32[3,64,128]{2,1,0:T(8,128)S(1)}, f32[3,64,128]{2,1,0:T(8,128)S(1)}, u32[]{:S(2)}, u32[]{:S(2)}) %collective-permute-start.3) | collective-permute-done | bytes 98336 | tf_op jit(solution)/shard_map/ppermute | solution.py:461
  33.0 2.4 %collective-permute-done.4.refs_2_ = f32[3,64,128]{2,1,0:T(8,128)S(1)} collective-permute-done((f32[3,64,128]{2,1,0:T(8,128)S(1)}, f32[3,64,128]{2,1,0:T(8,128)S(1)}, u32[]{:S(2)}, u32[]{:S(2)}) %collective-permute-start.4) | collective-permute-done | bytes 98336 | tf_op jit(solution)/shard_map/ppermute | solution.py:461
  35.4 1.0 %collective-permute-done.5.refs_3_ = f32[3,64,128]{2,1,0:T(8,128)S(1)} collective-permute-done((f32[3,64,128]{2,1,0:T(8,128)S(1)}, f32[3,64,128]{2,1,0:T(8,128)S(1)}, u32[]{:S(2)}, u32[]{:S(2)}) %collective-permute-start.5) | collective-permute-done | bytes 98336 | tf_op jit(solution)/shard_map/ppermute | solution.py:461
  36.4 2.8 %scatter_own.1 = (f32[256,128]{1,0:T(8,128)S(1)}, f32[64,128]{1,0:T(8,128)S(1)}) custom-call(s32[64,128]{1,0:T(8,128)S(1)} %get-tuple-element.41.row_ref, s32[64,128]{1,0:T(8,128)S(1)} %get-tuple-element.42.lane_ref, f32[3,64,128]{2,1,0:T(8,128)S(1)} %pad_maximum_fusion.2.refs_0_, f32[3,64,128]{2,1,0:T(8,128)S(1)} %collective-permute-done.3.refs_1_, ...), custom_call_target="tpu_custom_call" | custom-call | tf_op jit(solution)/shard_map/scatter_own/pallas_call | solution.py:603
  39.2 2.0 %collective-permute-start.6 = (f32[4,64,128]{2,1,0:T(8,128)S(1)}, f32[4,64,128]{2,1,0:T(8,128)S(1)}, u32[]{:S(2)}, u32[]{:S(2)}) collective-permute-start(f32[4,64,128]{2,1,0:T(8,128)S(1)} %bitcast.54), channel_id=1, source_target_pairs={{0,2},{1,3},{2,0},{3,1},{4,6},{5,7},{6,4},{7,5},{8,10},{9,11},{10,... | collective-permute-start | bytes 393224 | tf_op jit(solution)/shard_map/ppermute | solution.py:455
  41.2 0.7 %collective-permute-start.7 = (f32[4,64,128]{2,1,0:T(8,128)S(1)}, f32[4,64,128]{2,1,0:T(8,128)S(1)}, u32[]{:S(2)}, u32[]{:S(2)}) collective-permute-start(f32[4,64,128]{2,1,0:T(8,128)S(1)} %bitcast.55), channel_id=1, source_target_pairs={{0,0},{1,1},{2,4},{3,5},{4,2},{5,3},{6,6},{7,7},{8,8},{9,9},{10,12... | collective-permute-start | bytes 393224 | tf_op jit(solution)/shard_map/ppermute | solution.py:455
  41.9 5.0 %scatter_rest.1 = (f32[1024,128]{1,0:T(8,128)S(1)}, f32[16,64,128]{2,1,0:T(8,128)S(1)}, f32[8,16,64,128]{3,2,1,0:T(8,128)S(1)}, bf16[8,16,64,128]{3,2,1,0:T(8,128)(2,1)S(1)}) custom-call(s32[64,128]{1,0:T(8,128)S(1)} %get-tuple-element.41.row_ref, s32[64,128]{1,0:T(8,128)S(1)} %get-tuple-element.42.lane_ref, f32[64,128]{1,0:T(8,128)S(1)} %get-tuple-element.49.amount_ref, ...), custom_call_target="tpu_custom_call" | custom-call | tf_op jit(solution)/shard_map/scatter_rest/pallas_call | solution.py:615
  47.0 0.1 collective-permute-start.8
  47.1 1.2 %level_matrices.1 = (bf16[256,768]{1,0:T(8,128)(2,1)S(1)}, bf16[256,768]{1,0:T(8,128)(2,1)S(1)}) custom-call(f32[16,16]{1,0:T(8,128)} %local_ref, f32[16,16]{1,0:T(8,128)} %root_ref.2), custom_call_target="tpu_custom_call" | custom-call | tf_op jit(solution)/shard_map/level_matrices/pallas_call | solution.py:633
  48.4 0.3 collective-permute-done.8.other_ref
  48.6 1.4 %diffuse_adjoint.1.refs_0_ = f32[4,64,128]{2,1,0:T(8,128)S(1)} custom-call(f32[5,10,32,128]{3,2,1,0:T(8,128)S(1)} %get-tuple-element.57.coef_ref, f32[4,64,128]{2,1,0:T(8,128)S(1)} %collective-permute-done.6.first_ref, f32[4,64,128]{2,1,0:T(8,128)S(1)} %collective-permute-done.7.second_ref, f32[4,64,128]{2,1,0:T(8,128)S(1)} %bitcast.57, ...), custom_call_target="tpu_custom_call" | custom-call | tf_op jit(solution)/shard_map/diffuse_adjoint/pallas_call | solution.py:644
  50.0 1.2 %collective-permute-start.9 = (f32[4,64,128]{2,1,0:T(8,128)S(1)}, f32[4,64,128]{2,1,0:T(8,128)S(1)}, u32[]{:S(2)}, u32[]{:S(2)}) collective-permute-start(f32[4,64,128]{2,1,0:T(8,128)S(1)} %diffuse_adjoint.1.refs_0_), channel_id=1, source_target_pairs={{8,0},{0,8},{24,16},{16,24},{9,1},{1,9},{25,17},{17,25},{10,2},{2,... | collective-permute-start | bytes 393224 | tf_op jit(solution)/shard_map/ppermute | solution.py:461
  51.3 0.8 %collective-permute-start.10 = (f32[4,64,128]{2,1,0:T(8,128)S(1)}, f32[4,64,128]{2,1,0:T(8,128)S(1)}, u32[]{:S(2)}, u32[]{:S(2)}) collective-permute-start(f32[4,64,128]{2,1,0:T(8,128)S(1)} %diffuse_adjoint.1.refs_0_), channel_id=1, source_target_pairs={{16,0},{24,8},{0,16},{8,24},{17,1},{25,9},{1,17},{9,25},{18,2},{26... | collective-permute-start | bytes 393224 | tf_op jit(solution)/shard_map/ppermute | solution.py:461
  52.1 1.5 %collective-permute-start.11 = (f32[4,64,128]{2,1,0:T(8,128)S(1)}, f32[4,64,128]{2,1,0:T(8,128)S(1)}, u32[]{:S(2)}, u32[]{:S(2)}) collective-permute-start(f32[4,64,128]{2,1,0:T(8,128)S(1)} %diffuse_adjoint.1.refs_0_), channel_id=1, source_target_pairs={{24,0},{16,8},{8,16},{0,24},{25,1},{17,9},{9,17},{1,25},{26,2},{18... | collective-permute-start | bytes 393224 | tf_op jit(solution)/shard_map/ppermute | solution.py:461
  53.6 5.6 %members_gradient.1 = f32[8,16,64,128]{3,2,1,0:T(8,128)} custom-call(bf16[256,768]{1,0:T(8,128)(2,1)S(1)} %get-tuple-element.62.matrix_ref, f32[16,64,128]{2,1,0:T(8,128)S(1)} %bitcast.59, f32[8,16,64,128]{3,2,1,0:T(8,128)S(1)} %get-tuple-element.64.control_ref, bf16[8,16,64,128]{3,2,1,0:T(8,128)(2,1)S(1)} %get-tuple-element.65.pert_ref), custom_call_target="tpu_custom_call" | custom-call | tf_op jit(solution)/shard_map/members_gradient/pallas_call | solution.py:656
  59.2 0.3 collective-permute-done.11.refs_3_
  59.4 1.2 %static_gradient.1 = f32[16,64,128]{2,1,0:T(8,128)} custom-call(bf16[256,768]{1,0:T(8,128)(2,1)S(1)} %get-tuple-element.55.matrix_ref, f32[16,64,128]{2,1,0:T(8,128)S(1)} %get-tuple-element.56.static_ref, f32[4,64,128]{2,1,0:T(8,128)S(1)} %diffuse_adjoint.1.refs_0_, f32[4,64,128]{2,1,0:T(8,128)S(1)} %collective-permute-done.9.refs_1_, ...), custom_call_target="tpu_custom_call" | custom-call | tf_op jit(solution)/shard_map/static_gradient/pallas_call | solution.py:666
  (10 shorter events, 0.1 us)
Async XLA Ops:
  1.9 12.1 %collective-permute-start = (f32[6,64,128]{2,1,0:T(8,128)S(1)}, f32[6,64,128]{2,1,0:T(8,128)S(1)}, u32[]{:S(2)}, u32[]{:S(2)}) collective-permute-start(f32[6,64,128]{2,1,0:T(8,128)S(1)} %get-tuple-element.39.own_ref), channel_id=1, source_target_pairs={{0,2},{1,3},{2,0},{3,1},{4,6},{5,7},{6,4},{7,5},{8,10},{9,11},{10,... | collective-permute-start | bytes 589832 | tf_op jit(solution)/shard_map/ppermute | solution.py:455
  5.0 9.1 %collective-permute-start.1 = (f32[6,64,128]{2,1,0:T(8,128)S(1)}, f32[6,64,128]{2,1,0:T(8,128)S(1)}, u32[]{:S(2)}, u32[]{:S(2)}) collective-permute-start(f32[6,64,128]{2,1,0:T(8,128)S(1)} %get-tuple-element.39.own_ref), channel_id=1, source_target_pairs={{0,0},{1,1},{2,4},{3,5},{4,2},{5,3},{6,6},{7,7},{8,8},{9,9},{10,12... | collective-permute-start | bytes 589832 | tf_op jit(solution)/shard_map/ppermute | solution.py:455
  14.2 5.8 %collective-permute-start.2 = (f32[2,6,64,128]{3,2,1,0:T(8,128)S(1)}, f32[2,6,64,128]{3,2,1,0:T(8,128)S(1)}, u32[]{:S(2)}, u32[]{:S(2)}) collective-permute-start(f32[2,6,64,128]{3,2,1,0:T(8,128)S(1)} %pad_maximum_fusion), channel_id=1, source_target_pairs={{0,1},{1,0},{2,3},{3,2},{4,5},{5,4},{6,7},{7,6},{8,9},{9,8},{10,11... | collective-permute-start | bytes 1179656 | tf_op jit(solution)/shard_map/ppermute | solution.py:467
  14.2 13.5 %all-to-all-start = ((f32[8,2,8,128]{3,2,1,0:T(8,128)}), f32[8,2,8,128]{3,2,1,0:T(8,128)S(1)}, u32[]{:S(2)}, u32[]{:S(2)}) async-start(f32[8,2,8,128]{3,2,1,0:T(8,128)} %get-tuple-element.45), calls=%async_computation | async-start | bytes 131072 | tf_op jit(solution)/shard_map/all_to_all | solution.py:571
  27.8 5.3 %collective-permute-start.3 = (f32[3,64,128]{2,1,0:T(8,128)S(1)}, f32[3,64,128]{2,1,0:T(8,128)S(1)}, u32[]{:S(2)}, u32[]{:S(2)}) collective-permute-start(f32[3,64,128]{2,1,0:T(8,128)S(1)} %pad_maximum_fusion.2.refs_0_), channel_id=1, source_target_pairs={{8,0},{0,8},{24,16},{16,24},{9,1},{1,9},{25,17},{17,25},{10,2},{2,... | collective-permute-start | bytes 294920 | tf_op jit(solution)/shard_map/ppermute | solution.py:461
  29.3 6.1 %collective-permute-start.4 = (f32[3,64,128]{2,1,0:T(8,128)S(1)}, f32[3,64,128]{2,1,0:T(8,128)S(1)}, u32[]{:S(2)}, u32[]{:S(2)}) collective-permute-start(f32[3,64,128]{2,1,0:T(8,128)S(1)} %pad_maximum_fusion.2.refs_0_), channel_id=1, source_target_pairs={{16,0},{24,8},{0,16},{8,24},{17,1},{25,9},{1,17},{9,25},{18,2},{26... | collective-permute-start | bytes 294920 | tf_op jit(solution)/shard_map/ppermute | solution.py:461
  30.8 5.5 %collective-permute-start.5 = (f32[3,64,128]{2,1,0:T(8,128)S(1)}, f32[3,64,128]{2,1,0:T(8,128)S(1)}, u32[]{:S(2)}, u32[]{:S(2)}) collective-permute-start(f32[3,64,128]{2,1,0:T(8,128)S(1)} %pad_maximum_fusion.2.refs_0_), channel_id=1, source_target_pairs={{24,0},{16,8},{8,16},{0,24},{25,1},{17,9},{9,17},{1,25},{26,2},{18... | collective-permute-start | bytes 294920 | tf_op jit(solution)/shard_map/ppermute | solution.py:461
  39.2 7.8 %collective-permute-start.6 = (f32[4,64,128]{2,1,0:T(8,128)S(1)}, f32[4,64,128]{2,1,0:T(8,128)S(1)}, u32[]{:S(2)}, u32[]{:S(2)}) collective-permute-start(f32[4,64,128]{2,1,0:T(8,128)S(1)} %bitcast.54), channel_id=1, source_target_pairs={{0,2},{1,3},{2,0},{3,1},{4,6},{5,7},{6,4},{7,5},{8,10},{9,11},{10,... | collective-permute-start | bytes 393224 | tf_op jit(solution)/shard_map/ppermute | solution.py:455
  41.2 5.7 %collective-permute-start.7 = (f32[4,64,128]{2,1,0:T(8,128)S(1)}, f32[4,64,128]{2,1,0:T(8,128)S(1)}, u32[]{:S(2)}, u32[]{:S(2)}) collective-permute-start(f32[4,64,128]{2,1,0:T(8,128)S(1)} %bitcast.55), channel_id=1, source_target_pairs={{0,0},{1,1},{2,4},{3,5},{4,2},{5,3},{6,6},{7,7},{8,8},{9,9},{10,12... | collective-permute-start | bytes 393224 | tf_op jit(solution)/shard_map/ppermute | solution.py:455
  47.0 1.6 %collective-permute-start.8 = (f32[2,4,64,128]{3,2,1,0:T(8,128)S(1)}, f32[2,4,64,128]{3,2,1,0:T(8,128)S(1)}, u32[]{:S(2)}, u32[]{:S(2)}) collective-permute-start(f32[2,4,64,128]{3,2,1,0:T(8,128)S(1)} %pad_maximum_fusion.1), channel_id=1, source_target_pairs={{0,1},{1,0},{2,3},{3,2},{4,5},{5,4},{6,7},{7,6},{8,9},{9,8},{10,11... | collective-permute-start | bytes 786440 | tf_op jit(solution)/shard_map/ppermute | solution.py:467
  50.0 9.1 %collective-permute-start.9 = (f32[4,64,128]{2,1,0:T(8,128)S(1)}, f32[4,64,128]{2,1,0:T(8,128)S(1)}, u32[]{:S(2)}, u32[]{:S(2)}) collective-permute-start(f32[4,64,128]{2,1,0:T(8,128)S(1)} %diffuse_adjoint.1.refs_0_), channel_id=1, source_target_pairs={{8,0},{0,8},{24,16},{16,24},{9,1},{1,9},{25,17},{17,25},{10,2},{2,... | collective-permute-start | bytes 393224 | tf_op jit(solution)/shard_map/ppermute | solution.py:461
  51.3 7.9 %collective-permute-start.10 = (f32[4,64,128]{2,1,0:T(8,128)S(1)}, f32[4,64,128]{2,1,0:T(8,128)S(1)}, u32[]{:S(2)}, u32[]{:S(2)}) collective-permute-start(f32[4,64,128]{2,1,0:T(8,128)S(1)} %diffuse_adjoint.1.refs_0_), channel_id=1, source_target_pairs={{16,0},{24,8},{0,16},{8,24},{17,1},{25,9},{1,17},{9,25},{18,2},{26... | collective-permute-start | bytes 393224 | tf_op jit(solution)/shard_map/ppermute | solution.py:461
  52.1 7.3 %collective-permute-start.11 = (f32[4,64,128]{2,1,0:T(8,128)S(1)}, f32[4,64,128]{2,1,0:T(8,128)S(1)}, u32[]{:S(2)}, u32[]{:S(2)}) collective-permute-start(f32[4,64,128]{2,1,0:T(8,128)S(1)} %diffuse_adjoint.1.refs_0_), channel_id=1, source_target_pairs={{24,0},{16,8},{8,16},{0,24},{25,1},{17,9},{9,17},{1,25},{26,2},{18... | collective-permute-start | bytes 393224 | tf_op jit(solution)/shard_map/ppermute | solution.py:461

commit v9 on v8

--- a/solution.py
+++ b/solution.py
@@ -88,7 +88,14 @@
     return (i + d) % count if count & (count - 1) else i ^ d
 
 
-def prepare_kernel(lev_share, rows, root_ref, count_ref, static_ref, north_ref, east_ref, index_ref, out_ref, row_ref, lane_ref):
+def prepare_kernel(lev_share, rows, *refs):
+    (root_ref, count_ref, static_ref, north_ref, east_ref, index_ref), sources = refs[:6], refs[6:9]
+    (out_ref, row_ref, lane_ref), landed, sems = refs[9:12], refs[12:15], refs[15]
+    obs_rows = landed[0].shape[0]
+    here = pl.ds(pl.multiple_of(lax.axis_index("ens") * obs_rows, obs_rows), obs_rows)
+    copies = [pltpu.make_async_copy(s.at[here, :], t, sems.at[i]) for i, (s, t) in enumerate(zip(sources, landed))]
+    for copy in copies:
+        copy.start()
     levels, per_level, _ = static_ref.shape
     first = lax.axis_index("ens") * lev_share
     for j in range(lev_share):
@@ -112,6 +119,8 @@
             at = q * pieces + c
             row_ref[at : at + 1, :] = grid_row[:, c * LANES : (c + 1) * LANES]
             lane_ref[at : at + 1, :] = lane[:, c * LANES : (c + 1) * LANES]
+    for copy in copies:
+        copy.wait()
 
 
 def level_product(matrix, transpose):
@@ -139,28 +148,21 @@
 
 
 def observe_kernel(n_cols, cap_rows, scale, *refs):
-    sources, (out_ref, part_ref), (acc_ref, fold_ref, matrix_ref), landed, sems, slots = (
-        refs[:6],
-        refs[6:8],
+    (slot_ref, weight_ref, innov_ref), sources, (out_ref, part_ref) = refs[:3], refs[3:6], refs[6:8]
+    (acc_ref, fold_ref, matrix_ref), landed, sems, slots = (
         refs[8:11],
-        refs[11:17],
-        refs[17],
-        (refs[18:20], refs[20:22]),
+        refs[11:14],
+        refs[14],
+        (refs[15:17], refs[17:19]),
     )
-    coarse = acc_ref.shape[0]
-    obs_rows = landed[0].shape[0]
+    coarse = acc_ref.shape[1]
+    obs_rows = slot_ref.shape[0]
     group = min(8, obs_rows)
-    first = pl.multiple_of(lax.axis_index("ens") * obs_rows, obs_rows)
-    copies = [
-        pltpu.make_async_copy(sources[i].at[pl.ds(first, obs_rows), :], landed[i], sems.at[i]) for i in range(3)
-    ]
-    copies += [pltpu.make_async_copy(sources[i], landed[i], sems.at[i]) for i in range(3, 6)]
+    copies = [pltpu.make_async_copy(s, t, sems.at[i]) for i, (s, t) in enumerate(zip(sources, landed))]
     for copy in copies:
         copy.start()
     acc_ref[...] = jnp.zeros_like(acc_ref)
-    for copy in copies[:3]:
-        copy.wait()
-    slot_ref, weight_ref, innov_ref, local_ref, control_ref, pert_ref = landed
+    local_ref, control_ref, pert_ref = landed
 
     def build(i, to):
         at = pl.ds(pl.multiple_of(i * group, group), group)
@@ -177,12 +179,13 @@
                 to[1][t * FINE : (t + 1) * FINE, here] = jnp.where(mask, term, bf16(0)).reshape(FINE, LANES)
 
     def use(i, of):
-        acc_ref[...] += product_nt(of[0][...], of[1][...])
+        acc_ref[...] += product_nt(of[1][...], of[0][...])
 
     in_turns(obs_rows // group, build, use, slots)
     for t in range(2):
-        terms = acc_ref[:, t * LANES : (t + 1) * LANES]
-        fold_ref[t] = terms + pltpu.roll(terms, FINE, 1)
+        at = 2 * t * FINE
+        terms = acc_ref[at : at + FINE, :] + acc_ref[at + FINE : at + 2 * FINE, :]
+        fold_ref[t] = jnp.concatenate([terms] * (LANES // FINE), axis=0).T
     per_row = LANES // FINE
     lane = lax.broadcasted_iota(jnp.int32, (coarse // per_row, LANES), 1)
     weights, amounts = (
@@ -196,7 +199,7 @@
     for p in range(n_cols):
         out_ref[p, 0] = weights[p * cap_rows : (p + 1) * cap_rows]
         out_ref[p, 1] = amounts[p * cap_rows : (p + 1) * cap_rows]
-    for copy in copies[3:]:
+    for copy in copies:
         copy.wait()
     matrix_ref[...] = level_product(local_ref[...] * f32(scale), False)
     sum_members(matrix_ref, control_ref, pert_ref, part_ref)
@@ -443,10 +446,10 @@
             out_ref[:, at, :] = static_ref[:, at, :] + part.reshape(levels, 16, LANES)
 
 
-def exchanged(x):
+def exchanged(x, starts):
     count = lax.axis_size("cols")
     out = []
-    for start in (0, 1):
+    for start in starts:
         pairs = []
         for i in range(count):
             chip, core = divmod(i, 2)
@@ -500,7 +503,9 @@
     def whole(*shape):
         return pl.BlockSpec(shape, lambda i: (0,) * len(shape))
 
-    packed, entry_row, entry_lane = pl.pallas_call(
+    obs_rows = obs_slot.shape[0] // LANES
+    share_rows = obs_rows // n_ens
+    packed, entry_row, entry_lane, *observed = pl.pallas_call(
         functools.partial(prepare_kernel, lev_share, rows),
         grid=(1,),
         in_specs=[
@@ -510,13 +515,20 @@
             whole(per_level, LANES),
             whole(per_level, LANES),
             whole(lists, capacity),
+            pl.BlockSpec(memory_space=pl.ANY),
+            pl.BlockSpec(memory_space=pl.ANY),
+            pl.BlockSpec(memory_space=pl.ANY),
         ],
-        out_specs=[VMEM] * 3,
+        out_specs=[VMEM] * 6,
         out_shape=[
             pltpu.VMEM((lev_share + 2, per_level, LANES), f32),
             pltpu.VMEM((entry_rows, LANES), jnp.int32),
             pltpu.VMEM((entry_rows, LANES), jnp.int32),
+            pltpu.VMEM((share_rows, LANES), jnp.int32),
+            pltpu.VMEM((share_rows, LANES), f32),
+            pltpu.VMEM((share_rows, LANES), f32),
         ],
+        scratch_shapes=[pltpu.SemaphoreType.DMA((3,))],
         compiler_params=params(8),
         name="prepare",
     )(
@@ -526,46 +538,36 @@
         in_hbm(tiled(face_north)),
         in_hbm(tiled(face_east)),
         in_hbm(send_index),
+        in_hbm(obs_slot.reshape(obs_rows, LANES)),
+        in_hbm(obs_weight.reshape(obs_rows, LANES)),
+        in_hbm(innovation.reshape(obs_rows, LANES)),
     )
-    first, second = exchanged(packed)
-
-    obs_rows = obs_slot.shape[0] // LANES
-    share_rows = obs_rows // n_ens
+    second, first = exchanged(packed, (1, 0))
+
     coarse = n_cols * capacity // FINE
     size = levels * 16
-    obs_slot, packed = lax.optimization_barrier((obs_slot, packed))
     slots, part = pl.pallas_call(
         functools.partial(observe_kernel, n_cols, cap_rows, member_scale),
         grid=(1,),
-        in_specs=[pl.BlockSpec(memory_space=pl.ANY)] * 6,
+        in_specs=[VMEM] * 3 + [pl.BlockSpec(memory_space=pl.ANY)] * 3,
         out_specs=[whole(n_cols, 2, cap_rows, LANES), VMEM],
         out_shape=[
             pltpu.HBM((n_cols, 2, cap_rows, LANES), f32),
             pltpu.VMEM((levels, per_level, LANES), f32),
         ],
         scratch_shapes=[
-            pltpu.VMEM((coarse, 4 * FINE), f32),
+            pltpu.VMEM((4 * FINE, coarse), f32),
             pltpu.VMEM((2, coarse, LANES), f32),
             pltpu.VMEM((size, 3 * size), bf16),
-            pltpu.VMEM((share_rows, LANES), jnp.int32),
-            pltpu.VMEM((share_rows, LANES), f32),
-            pltpu.VMEM((share_rows, LANES), f32),
             pltpu.VMEM((levels, levels), f32),
             pltpu.VMEM(control.shape, f32),
             pltpu.VMEM(pert.shape, bf16),
-            pltpu.SemaphoreType.DMA((6,)),
+            pltpu.SemaphoreType.DMA((3,)),
         ]
         + [pltpu.VMEM((coarse, 8 * LANES), bf16), pltpu.VMEM((4 * FINE, 8 * LANES), bf16)] * 2,
         compiler_params=params(24),
         name="slot_sums_and_members",
-    )(
-        in_hbm(obs_slot.reshape(obs_rows, LANES)),
-        in_hbm(obs_weight.reshape(obs_rows, LANES)),
-        in_hbm(innovation.reshape(obs_rows, LANES)),
-        in_hbm(vertical_local),
-        control,
-        pert,
-    )
+    )(*observed, in_hbm(vertical_local), control, pert)
     first, second, slots = lax.optimization_barrier((first, second, slots))
     other = swapped(packed, first, second)
     slots = lax.all_to_all(slots, "cols", split_axis=0, concat_axis=0, tiled=True)
@@ -610,7 +612,7 @@
         name="scatter_own",
     )(entry_row, entry_lane, *shares)
     tile = adjoint_own.reshape(lev_share, per_level, LANES)
-    tile_first, tile_second = exchanged(tile)
+    tile_first, tile_second = exchanged(tile, (0, 1))
 
     adjoint, static_here, control_here, pert_here = pl.pallas_call(
         functools.partial(scatter_rest_kernel, cap_rows),

time: 61.8 us -> 61.6 us (level)
    pallas_call x1, Pallas kernels: 8.33 us -> 7.31 us  [local(): pl.pallas_call(functools.partial(observe_kernel, n_cols, cap_rows, member...]
    pallas_call x1, Pallas kernels: 1.3 us -> 2.02 us  [local(): pl.pallas_call(functools.partial(prepare_kernel, lev_share, rows), grid=(...]
  transfers between devices with their start and end apart: 13 -> 13, of which waited for: 5 -> 5; matrix products, arithmetic and copies ran while one was open for 0% -> 0% of each run, Pallas kernels for 46% -> 44%
where the time goes in v9:
time: 61.6 us; the launch traced here: 60.4 us
  Pallas kernels  34.3 us (56%)
  starting transfers between devices  19.5 us (32%)
  waiting for transfers between devices  5.63 us (9%)
  between operations  0.86 us (1%)
    pallas_call x1, Pallas kernels, local(): pl.pallas_call(functools.partial(observe_kernel, n_cols, cap_rows, member...  7.31 us
    ppermute x6, starting transfers between devices, from_peers(): lax.ppermute(x, 'ens', [(peer(i, d, count), i) for i in range(count)])  7.11 us
    ppermute x4, starting transfers between devices, exchanged(): out.append(lax.ppermute(x, 'cols', pairs))  6.45 us
    pallas_call x1, Pallas kernels, local(): pl.pallas_call(functools.partial(lookup_kernel, cap_rows), in_specs=[VMEM...  6.19 us
    all_to_all x1, starting transfers between devices, local(): lax.all_to_all(slots, 'cols', split_axis=0, concat_axis=0, tiled=True)  5.76 us
    pallas_call x1, Pallas kernels, local(): pl.pallas_call(member_kernel, grid=(members // group,), in_specs=[VMEM] *...  5.57 us
    ppermute x6, waiting for transfers between devices, from_peers(): lax.ppermute(x, 'ens', [(peer(i, d, count), i) for i in range(count)])  5.35 us
    pallas_call x1, Pallas kernels, local(): pl.pallas_call(functools.partial(scatter_rest_kernel, cap_rows), in_specs...  5.04 us
  transfers between devices with their start and end apart: 13, of which 5 were waited for; matrix products, arithmetic and copies ran while one was open for 0% of the time, Pallas kernels for 44%

profile of v9, /device:TPU:0, one launch (start us, length us, event | category | flops | bytes accessed | tf_op | source)
XLA Modules:
  0.0 60.4 jit_solution(11389570294795453141)
XLA Ops:
  0.6 2.0 %prepare.1 = (f32[6,64,128]{2,1,0:T(8,128)S(1)}, s32[64,128]{1,0:T(8,128)S(1)}, s32[64,128]{1,0:T(8,128)S(1)}, s32[128,128]{1,0:T(8,128)S(1)}, f32[128,128]{1,0:T(8,128)S(1)}, /*index=5*/f32[128,128]{1,0:T(8,128)S(1)}) custom-call(f32[16,16]{1,0:T(8,128)} %root_ref, s32[8]{0:T(128)} %refs_1_.1, f32[16,64,128]{2,1,0:T(8,128)} %bitcast.68, ...), custom_call_target="tpu_custom_call" | custom-call | tf_op jit(solution)/shard_map/prepare/pallas_call | solution.py:508
  2.7 3.1 %collective-permute-start = (f32[6,64,128]{2,1,0:T(8,128)S(1)}, f32[6,64,128]{2,1,0:T(8,128)S(1)}, u32[]{:S(2)}, u32[]{:S(2)}) collective-permute-start(f32[6,64,128]{2,1,0:T(8,128)S(1)} %get-tuple-element.35.own_ref), channel_id=1, source_target_pairs={{0,2},{1,3},{2,0},{3,1},{4,6},{5,7},{6,4},{7,5},{8,10},{9,11},{10,... | collective-permute-start | bytes 589832 | tf_op jit(solution)/shard_map/ppermute | solution.py:458
  5.7 0.7 %collective-permute-start.1 = (f32[6,64,128]{2,1,0:T(8,128)S(1)}, f32[6,64,128]{2,1,0:T(8,128)S(1)}, u32[]{:S(2)}, u32[]{:S(2)}) collective-permute-start(f32[6,64,128]{2,1,0:T(8,128)S(1)} %get-tuple-element.35.own_ref), channel_id=1, source_target_pairs={{0,0},{1,1},{2,4},{3,5},{4,2},{5,3},{6,6},{7,7},{8,8},{9,9},{10,12... | collective-permute-start | bytes 589832 | tf_op jit(solution)/shard_map/ppermute | solution.py:458
  6.5 7.3 %slot_sums_and_members.1 = (f32[8,2,8,128]{3,2,1,0:T(8,128)}, f32[16,64,128]{2,1,0:T(8,128)S(1)}) custom-call(s32[128,128]{1,0:T(8,128)S(1)} %get-tuple-element.36.refs_0_, f32[128,128]{1,0:T(8,128)S(1)} %get-tuple-element.37.refs_1_, f32[128,128]{1,0:T(8,128)S(1)} %get-tuple-element.38.refs_2_, f32[16,16]{1,0:T(8,128)} %local_ref, ...), custom_call_target="tpu_custom_call" | custom-call | tf_op jit(solution)/shard_map/slot_sums_and_members/pallas_call | solution.py:549
  13.8 0.0 collective-permute-done.first_ref
  13.8 0.0 collective-permute-done.1.second_ref
  13.9 0.1 collective-permute-start.2
  13.9 5.8 %all-to-all-start = ((f32[8,2,8,128]{3,2,1,0:T(8,128)}), f32[8,2,8,128]{3,2,1,0:T(8,128)S(1)}, u32[]{:S(2)}, u32[]{:S(2)}) async-start(f32[8,2,8,128]{3,2,1,0:T(8,128)} %get-tuple-element.47), calls=%async_computation | async-start | bytes 131072 | tf_op jit(solution)/shard_map/all_to_all | solution.py:573
  19.7 1.5 %diffuse_forward.1 = (f32[4,64,128]{2,1,0:T(8,128)S(1)}, f32[5,10,32,128]{3,2,1,0:T(8,128)S(1)}) custom-call(f32[6,64,128]{2,1,0:T(8,128)S(1)} %collective-permute-done.first_ref, f32[6,64,128]{2,1,0:T(8,128)S(1)} %collective-permute-done.1.second_ref, f32[6,64,128]{2,1,0:T(8,128)S(1)} %get-tuple-element.35.own_ref, ...), custom_call_target="tpu_custom_call" | custom-call | flops 67108864 | bytes 4194304 | tf_op jit(solution)/shard_map/diffuse_forward/pallas_call | solution.py:575
  21.2 6.2 %lookup.1 = f32[64,128]{1,0:T(8,128)S(1)} custom-call(f32[1024,128]{1,0:T(8,128)S(1)} %bitcast.61, f32[256,128]{1,0:T(8,128)S(1)} %bitcast.62, s32[64,128]{1,0:T(8,128)S(1)} %get-tuple-element.43.row_ref, s32[64,128]{1,0:T(8,128)S(1)} %get-tuple-element.44.lane_ref), custom_call_target="tpu_custom_call" | custom-call | flops 4294967296 | bytes 16777216 | tf_op jit(solution)/shard_map/lookup/pallas_call | solution.py:588
  27.4 0.0 all-to-all-done
  27.4 1.6 %collective-permute-start.3 = (f32[3,64,128]{2,1,0:T(8,128)S(1)}, f32[3,64,128]{2,1,0:T(8,128)S(1)}, u32[]{:S(2)}, u32[]{:S(2)}) collective-permute-start(f32[3,64,128]{2,1,0:T(8,128)S(1)} %pad_maximum_fusion.2.refs_0_), channel_id=1, source_target_pairs={{8,0},{0,8},{24,16},{16,24},{9,1},{1,9},{25,17},{17,25},{10,2},{2,... | collective-permute-start | bytes 294920 | tf_op jit(solution)/shard_map/ppermute | solution.py:464
  29.0 1.5 %collective-permute-start.4 = (f32[3,64,128]{2,1,0:T(8,128)S(1)}, f32[3,64,128]{2,1,0:T(8,128)S(1)}, u32[]{:S(2)}, u32[]{:S(2)}) collective-permute-start(f32[3,64,128]{2,1,0:T(8,128)S(1)} %pad_maximum_fusion.2.refs_0_), channel_id=1, source_target_pairs={{16,0},{24,8},{0,16},{8,24},{17,1},{25,9},{1,17},{9,25},{18,2},{26... | collective-permute-start | bytes 294920 | tf_op jit(solution)/shard_map/ppermute | solution.py:464
  30.5 0.5 collective-permute-start.5
  31.0 1.7 %collective-permute-done.3.refs_1_ = f32[3,64,128]{2,1,0:T(8,128)S(1)} collective-permute-done((f32[3,64,128]{2,1,0:T(8,128)S(1)}, f32[3,64,128]{2,1,0:T(8,128)S(1)}, u32[]{:S(2)}, u32[]{:S(2)}) %collective-permute-start.3) | collective-permute-done | bytes 98336 | tf_op jit(solution)/shard_map/ppermute | solution.py:464
  32.7 2.4 %collective-permute-done.4.refs_2_ = f32[3,64,128]{2,1,0:T(8,128)S(1)} collective-permute-done((f32[3,64,128]{2,1,0:T(8,128)S(1)}, f32[3,64,128]{2,1,0:T(8,128)S(1)}, u32[]{:S(2)}, u32[]{:S(2)}) %collective-permute-start.4) | collective-permute-done | bytes 98336 | tf_op jit(solution)/shard_map/ppermute | solution.py:464
  35.1 1.0 %collective-permute-done.5.refs_3_ = f32[3,64,128]{2,1,0:T(8,128)S(1)} collective-permute-done((f32[3,64,128]{2,1,0:T(8,128)S(1)}, f32[3,64,128]{2,1,0:T(8,128)S(1)}, u32[]{:S(2)}, u32[]{:S(2)}) %collective-permute-start.5) | collective-permute-done | bytes 98336 | tf_op jit(solution)/shard_map/ppermute | solution.py:464
  36.1 2.8 %scatter_own.1 = (f32[256,128]{1,0:T(8,128)S(1)}, f32[64,128]{1,0:T(8,128)S(1)}) custom-call(s32[64,128]{1,0:T(8,128)S(1)} %get-tuple-element.43.row_ref, s32[64,128]{1,0:T(8,128)S(1)} %get-tuple-element.44.lane_ref, f32[3,64,128]{2,1,0:T(8,128)S(1)} %pad_maximum_fusion.2.refs_0_, f32[3,64,128]{2,1,0:T(8,128)S(1)} %collective-permute-done.3.refs_1_, ...), custom_call_target="tpu_custom_call" | custom-call | tf_op jit(solution)/shard_map/scatter_own/pallas_call | solution.py:605
  38.9 2.0 %collective-permute-start.6 = (f32[4,64,128]{2,1,0:T(8,128)S(1)}, f32[4,64,128]{2,1,0:T(8,128)S(1)}, u32[]{:S(2)}, u32[]{:S(2)}) collective-permute-start(f32[4,64,128]{2,1,0:T(8,128)S(1)} %bitcast.54), channel_id=1, source_target_pairs={{0,2},{1,3},{2,0},{3,1},{4,6},{5,7},{6,4},{7,5},{8,10},{9,11},{10,... | collective-permute-start | bytes 393224 | tf_op jit(solution)/shard_map/ppermute | solution.py:458
  40.9 0.7 %collective-permute-start.7 = (f32[4,64,128]{2,1,0:T(8,128)S(1)}, f32[4,64,128]{2,1,0:T(8,128)S(1)}, u32[]{:S(2)}, u32[]{:S(2)}) collective-permute-start(f32[4,64,128]{2,1,0:T(8,128)S(1)} %bitcast.55), channel_id=1, source_target_pairs={{0,0},{1,1},{2,4},{3,5},{4,2},{5,3},{6,6},{7,7},{8,8},{9,9},{10,12... | collective-permute-start | bytes 393224 | tf_op jit(solution)/shard_map/ppermute | solution.py:458
  41.6 5.0 %scatter_rest.1 = (f32[1024,128]{1,0:T(8,128)S(1)}, f32[16,64,128]{2,1,0:T(8,128)S(1)}, f32[8,16,64,128]{3,2,1,0:T(8,128)S(1)}, bf16[8,16,64,128]{3,2,1,0:T(8,128)(2,1)S(1)}) custom-call(s32[64,128]{1,0:T(8,128)S(1)} %get-tuple-element.43.row_ref, s32[64,128]{1,0:T(8,128)S(1)} %get-tuple-element.44.lane_ref, f32[64,128]{1,0:T(8,128)S(1)} %get-tuple-element.51.amount_ref, ...), custom_call_target="tpu_custom_call" | custom-call | tf_op jit(solution)/shard_map/scatter_rest/pallas_call | solution.py:617
  46.6 0.0 collective-permute-done.6.first_ref
  46.7 0.1 collective-permute-start.8
  46.8 1.2 %level_matrices.1 = (bf16[256,768]{1,0:T(8,128)(2,1)S(1)}, bf16[256,768]{1,0:T(8,128)(2,1)S(1)}) custom-call(f32[16,16]{1,0:T(8,128)} %local_ref, f32[16,16]{1,0:T(8,128)} %root_ref), custom_call_target="tpu_custom_call" | custom-call | tf_op jit(solution)/shard_map/level_matrices/pallas_call | solution.py:635
  48.0 0.3 collective-permute-done.8.other_ref
  48.3 1.4 %diffuse_adjoint.1.refs_0_ = f32[4,64,128]{2,1,0:T(8,128)S(1)} custom-call(f32[5,10,32,128]{3,2,1,0:T(8,128)S(1)} %get-tuple-element.59.coef_ref, f32[4,64,128]{2,1,0:T(8,128)S(1)} %collective-permute-done.6.first_ref, f32[4,64,128]{2,1,0:T(8,128)S(1)} %collective-permute-done.7.second_ref, f32[4,64,128]{2,1,0:T(8,128)S(1)} %bitcast.57, ...), custom_call_target="tpu_custom_call" | custom-call | tf_op jit(solution)/shard_map/diffuse_adjoint/pallas_call | solution.py:646
  49.7 1.2 %collective-permute-start.9 = (f32[4,64,128]{2,1,0:T(8,128)S(1)}, f32[4,64,128]{2,1,0:T(8,128)S(1)}, u32[]{:S(2)}, u32[]{:S(2)}) collective-permute-start(f32[4,64,128]{2,1,0:T(8,128)S(1)} %diffuse_adjoint.1.refs_0_), channel_id=1, source_target_pairs={{8,0},{0,8},{24,16},{16,24},{9,1},{1,9},{25,17},{17,25},{10,2},{2,... | collective-permute-start | bytes 393224 | tf_op jit(solution)/shard_map/ppermute | solution.py:464
  50.9 0.8 %collective-permute-start.10 = (f32[4,64,128]{2,1,0:T(8,128)S(1)}, f32[4,64,128]{2,1,0:T(8,128)S(1)}, u32[]{:S(2)}, u32[]{:S(2)}) collective-permute-start(f32[4,64,128]{2,1,0:T(8,128)S(1)} %diffuse_adjoint.1.refs_0_), channel_id=1, source_target_pairs={{16,0},{24,8},{0,16},{8,24},{17,1},{25,9},{1,17},{9,25},{18,2},{26... | collective-permute-start | bytes 393224 | tf_op jit(solution)/shard_map/ppermute | solution.py:464
  51.8 1.5 %collective-permute-start.11 = (f32[4,64,128]{2,1,0:T(8,128)S(1)}, f32[4,64,128]{2,1,0:T(8,128)S(1)}, u32[]{:S(2)}, u32[]{:S(2)}) collective-permute-start(f32[4,64,128]{2,1,0:T(8,128)S(1)} %diffuse_adjoint.1.refs_0_), channel_id=1, source_target_pairs={{24,0},{16,8},{8,16},{0,24},{25,1},{17,9},{9,17},{1,25},{26,2},{18... | collective-permute-start | bytes 393224 | tf_op jit(solution)/shard_map/ppermute | solution.py:464
  53.3 5.6 %members_gradient.1 = f32[8,16,64,128]{3,2,1,0:T(8,128)} custom-call(bf16[256,768]{1,0:T(8,128)(2,1)S(1)} %get-tuple-element.64.matrix_ref, f32[16,64,128]{2,1,0:T(8,128)S(1)} %bitcast.59, f32[8,16,64,128]{3,2,1,0:T(8,128)S(1)} %get-tuple-element.66.control_ref, bf16[8,16,64,128]{3,2,1,0:T(8,128)(2,1)S(1)} %get-tuple-element.67.pert_ref), custom_call_target="tpu_custom_call" | custom-call | tf_op jit(solution)/shard_map/members_gradient/pallas_call | solution.py:658
  58.9 0.3 collective-permute-done.11.refs_3_
  59.1 1.2 %static_gradient.1 = f32[16,64,128]{2,1,0:T(8,128)} custom-call(bf16[256,768]{1,0:T(8,128)(2,1)S(1)} %get-tuple-element.57.matrix_ref, f32[16,64,128]{2,1,0:T(8,128)S(1)} %get-tuple-element.58.static_ref, f32[4,64,128]{2,1,0:T(8,128)S(1)} %diffuse_adjoint.1.refs_0_, f32[4,64,128]{2,1,0:T(8,128)S(1)} %collective-permute-done.9.refs_1_, ...), custom_call_target="tpu_custom_call" | custom-call | tf_op jit(solution)/shard_map/static_gradient/pallas_call | solution.py:668
  (10 shorter events, 0.1 us)
Async XLA Ops:
  2.7 11.1 %collective-permute-start = (f32[6,64,128]{2,1,0:T(8,128)S(1)}, f32[6,64,128]{2,1,0:T(8,128)S(1)}, u32[]{:S(2)}, u32[]{:S(2)}) collective-permute-start(f32[6,64,128]{2,1,0:T(8,128)S(1)} %get-tuple-element.35.own_ref), channel_id=1, source_target_pairs={{0,2},{1,3},{2,0},{3,1},{4,6},{5,7},{6,4},{7,5},{8,10},{9,11},{10,... | collective-permute-start | bytes 589832 | tf_op jit(solution)/shard_map/ppermute | solution.py:458
  5.7 8.0 %collective-permute-start.1 = (f32[6,64,128]{2,1,0:T(8,128)S(1)}, f32[6,64,128]{2,1,0:T(8,128)S(1)}, u32[]{:S(2)}, u32[]{:S(2)}) collective-permute-start(f32[6,64,128]{2,1,0:T(8,128)S(1)} %get-tuple-element.35.own_ref), channel_id=1, source_target_pairs={{0,0},{1,1},{2,4},{3,5},{4,2},{5,3},{6,6},{7,7},{8,8},{9,9},{10,12... | collective-permute-start | bytes 589832 | tf_op jit(solution)/shard_map/ppermute | solution.py:458
  13.9 5.8 %collective-permute-start.2 = (f32[2,6,64,128]{3,2,1,0:T(8,128)S(1)}, f32[2,6,64,128]{3,2,1,0:T(8,128)S(1)}, u32[]{:S(2)}, u32[]{:S(2)}) collective-permute-start(f32[2,6,64,128]{3,2,1,0:T(8,128)S(1)} %pad_maximum_fusion), channel_id=1, source_target_pairs={{0,1},{1,0},{2,3},{3,2},{4,5},{5,4},{6,7},{7,6},{8,9},{9,8},{10,11... | collective-permute-start | bytes 1179656 | tf_op jit(solution)/shard_map/ppermute | solution.py:470
  13.9 13.5 %all-to-all-start = ((f32[8,2,8,128]{3,2,1,0:T(8,128)}), f32[8,2,8,128]{3,2,1,0:T(8,128)S(1)}, u32[]{:S(2)}, u32[]{:S(2)}) async-start(f32[8,2,8,128]{3,2,1,0:T(8,128)} %get-tuple-element.47), calls=%async_computation | async-start | bytes 131072 | tf_op jit(solution)/shard_map/all_to_all | solution.py:573
  27.4 5.3 %collective-permute-start.3 = (f32[3,64,128]{2,1,0:T(8,128)S(1)}, f32[3,64,128]{2,1,0:T(8,128)S(1)}, u32[]{:S(2)}, u32[]{:S(2)}) collective-permute-start(f32[3,64,128]{2,1,0:T(8,128)S(1)} %pad_maximum_fusion.2.refs_0_), channel_id=1, source_target_pairs={{8,0},{0,8},{24,16},{16,24},{9,1},{1,9},{25,17},{17,25},{10,2},{2,... | collective-permute-start | bytes 294920 | tf_op jit(solution)/shard_map/ppermute | solution.py:464
  29.0 6.1 %collective-permute-start.4 = (f32[3,64,128]{2,1,0:T(8,128)S(1)}, f32[3,64,128]{2,1,0:T(8,128)S(1)}, u32[]{:S(2)}, u32[]{:S(2)}) collective-permute-start(f32[3,64,128]{2,1,0:T(8,128)S(1)} %pad_maximum_fusion.2.refs_0_), channel_id=1, source_target_pairs={{16,0},{24,8},{0,16},{8,24},{17,1},{25,9},{1,17},{9,25},{18,2},{26... | collective-permute-start | bytes 294920 | tf_op jit(solution)/shard_map/ppermute | solution.py:464
  30.5 5.5 %collective-permute-start.5 = (f32[3,64,128]{2,1,0:T(8,128)S(1)}, f32[3,64,128]{2,1,0:T(8,128)S(1)}, u32[]{:S(2)}, u32[]{:S(2)}) collective-permute-start(f32[3,64,128]{2,1,0:T(8,128)S(1)} %pad_maximum_fusion.2.refs_0_), channel_id=1, source_target_pairs={{24,0},{16,8},{8,16},{0,24},{25,1},{17,9},{9,17},{1,25},{26,2},{18... | collective-permute-start | bytes 294920 | tf_op jit(solution)/shard_map/ppermute | solution.py:464
  38.9 7.8 %collective-permute-start.6 = (f32[4,64,128]{2,1,0:T(8,128)S(1)}, f32[4,64,128]{2,1,0:T(8,128)S(1)}, u32[]{:S(2)}, u32[]{:S(2)}) collective-permute-start(f32[4,64,128]{2,1,0:T(8,128)S(1)} %bitcast.54), channel_id=1, source_target_pairs={{0,2},{1,3},{2,0},{3,1},{4,6},{5,7},{6,4},{7,5},{8,10},{9,11},{10,... | collective-permute-start | bytes 393224 | tf_op jit(solution)/shard_map/ppermute | solution.py:458
  40.9 5.7 %collective-permute-start.7 = (f32[4,64,128]{2,1,0:T(8,128)S(1)}, f32[4,64,128]{2,1,0:T(8,128)S(1)}, u32[]{:S(2)}, u32[]{:S(2)}) collective-permute-start(f32[4,64,128]{2,1,0:T(8,128)S(1)} %bitcast.55), channel_id=1, source_target_pairs={{0,0},{1,1},{2,4},{3,5},{4,2},{5,3},{6,6},{7,7},{8,8},{9,9},{10,12... | collective-permute-start | bytes 393224 | tf_op jit(solution)/shard_map/ppermute | solution.py:458
  46.7 1.6 %collective-permute-start.8 = (f32[2,4,64,128]{3,2,1,0:T(8,128)S(1)}, f32[2,4,64,128]{3,2,1,0:T(8,128)S(1)}, u32[]{:S(2)}, u32[]{:S(2)}) collective-permute-start(f32[2,4,64,128]{3,2,1,0:T(8,128)S(1)} %pad_maximum_fusion.1), channel_id=1, source_target_pairs={{0,1},{1,0},{2,3},{3,2},{4,5},{5,4},{6,7},{7,6},{8,9},{9,8},{10,11... | collective-permute-start | bytes 786440 | tf_op jit(solution)/shard_map/ppermute | solution.py:470
  49.7 9.1 %collective-permute-start.9 = (f32[4,64,128]{2,1,0:T(8,128)S(1)}, f32[4,64,128]{2,1,0:T(8,128)S(1)}, u32[]{:S(2)}, u32[]{:S(2)}) collective-permute-start(f32[4,64,128]{2,1,0:T(8,128)S(1)} %diffuse_adjoint.1.refs_0_), channel_id=1, source_target_pairs={{8,0},{0,8},{24,16},{16,24},{9,1},{1,9},{25,17},{17,25},{10,2},{2,... | collective-permute-start | bytes 393224 | tf_op jit(solution)/shard_map/ppermute | solution.py:464
  50.9 7.9 %collective-permute-start.10 = (f32[4,64,128]{2,1,0:T(8,128)S(1)}, f32[4,64,128]{2,1,0:T(8,128)S(1)}, u32[]{:S(2)}, u32[]{:S(2)}) collective-permute-start(f32[4,64,128]{2,1,0:T(8,128)S(1)} %diffuse_adjoint.1.refs_0_), channel_id=1, source_target_pairs={{16,0},{24,8},{0,16},{8,24},{17,1},{25,9},{1,17},{9,25},{18,2},{26... | collective-permute-start | bytes 393224 | tf_op jit(solution)/shard_map/ppermute | solution.py:464
  51.8 7.3 %collective-permute-start.11 = (f32[4,64,128]{2,1,0:T(8,128)S(1)}, f32[4,64,128]{2,1,0:T(8,128)S(1)}, u32[]{:S(2)}, u32[]{:S(2)}) collective-permute-start(f32[4,64,128]{2,1,0:T(8,128)S(1)} %diffuse_adjoint.1.refs_0_), channel_id=1, source_target_pairs={{24,0},{16,8},{8,16},{0,24},{25,1},{17,9},{9,17},{1,25},{26,2},{18... | collective-permute-start | bytes 393224 | tf_op jit(solution)/shard_map/ppermute | solution.py:464

commit v10 on v9

--- a/solution.py
+++ b/solution.py
@@ -225,11 +225,13 @@
 
 
 def member_kernel(matrix_ref, adjoint_ref, control_ref, pert_ref, out_ref):
-    group, levels, per_level, _ = out_ref.shape
+    group, levels, height, _ = out_ref.shape
     first = pl.program_id(0) * group
+    top = pl.program_id(1) * height
 
     def chunk(j, carry):
-        at = pl.ds(pl.multiple_of(j * 16, 16), 16)
+        to = pl.ds(pl.multiple_of(j * 16, 16), 16)
+        at = pl.ds(pl.multiple_of(top + j * 16, 16), 16)
         adjoint = adjoint_ref[:, at, :]
         terms = [
             three_terms((pert_ref[first + i, :, at, :].astype(f32) * adjoint).reshape(levels * 16, LANES))
@@ -238,10 +240,10 @@
         change = jnp.dot(matrix_ref[...], jnp.concatenate(terms, axis=1), preferred_element_type=f32)
         for i in range(group):
             part = change[:, i * LANES : (i + 1) * LANES].reshape(levels, 16, LANES)
-            out_ref[i, :, at, :] = control_ref[first + i, :, at, :] + part
+            out_ref[i, :, to, :] = control_ref[first + i, :, at, :] + part
         return carry
 
-    lax.fori_loop(0, per_level // 16, chunk, 0)
+    lax.fori_loop(0, height // 16, chunk, 0)
 
 
 def eastern(x):
@@ -256,7 +258,7 @@
     return jnp.where(lane == 0, pltpu.roll(near, 1, 0), near)
 
 
-def rows_of(first_ref, second_ref, own_ref, other_ref, plane, rows):
+def rows_of(second_ref, first_ref, own_ref, other_ref, plane, rows):
     at = lax.axis_index("cols")
     count = lax.axis_size("cols")
     core, chip = at % 2, at // 2 % 2
@@ -287,8 +289,8 @@
     return field
 
 
-def first_diffusion_kernel(lev_share, rows, first_ref, second_ref, own_ref, other_ref, out_ref, coef_ref):
-    tiles = (first_ref, second_ref, own_ref, other_ref)
+def first_diffusion_kernel(lev_share, rows, second_ref, first_ref, own_ref, other_ref, out_ref, coef_ref):
+    tiles = (second_ref, first_ref, own_ref, other_ref)
     blocks = own_ref.shape[1] // rows
     side = 2
     north = rows_of(*tiles, lev_share, rows)
@@ -316,8 +318,8 @@
     lax.fori_loop(0, lev_share, body, 0)
 
 
-def second_diffusion_kernel(rows, coef_ref, first_ref, second_ref, own_ref, other_ref, out_ref):
-    tiles = (first_ref, second_ref, own_ref, other_ref)
+def second_diffusion_kernel(rows, coef_ref, second_ref, first_ref, own_ref, other_ref, out_ref):
+    tiles = (second_ref, first_ref, own_ref, other_ref)
     lev_share = out_ref.shape[0]
     blocks = own_ref.shape[1] // rows
 
@@ -436,8 +438,9 @@
     levels, per_level, _ = static_ref.shape
     share = levels // len(parts)
     me = lax.axis_index("ens")
-    for d, part in enumerate(parts):
-        smooth_ref[pl.ds(peer(me, d, len(parts)) * share, share)] = part[...]
+    for i, part in enumerate(parts):
+        at = peer(me, (len(parts) - i) % len(parts), len(parts))
+        smooth_ref[pl.ds(at * share, share)] = part[...]
     for j in range(0, per_level, 32):
         terms = [three_terms(smooth_ref[:, j + i : j + i + 16, :].reshape(levels * 16, LANES)) for i in (0, 16)]
         change = jnp.dot(matrix_ref[...], jnp.concatenate(terms, axis=1), preferred_element_type=f32)
@@ -461,7 +464,7 @@
 
 def from_peers(x):
     count = lax.axis_size("ens")
-    return [lax.ppermute(x, "ens", [(peer(i, d, count), i) for i in range(count)]) for d in range(1, count)]
+    return [lax.ppermute(x, "ens", [(peer(i, d, count), i) for i in range(count)]) for d in range(count - 1, 0, -1)]
 
 
 def swapped(own, first, second):
@@ -568,7 +571,7 @@
         compiler_params=params(24),
         name="slot_sums_and_members",
     )(*observed, in_hbm(vertical_local), control, pert)
-    first, second, slots = lax.optimization_barrier((first, second, slots))
+    second, first, slots = lax.optimization_barrier((second, first, slots))
     other = swapped(packed, first, second)
     slots = lax.all_to_all(slots, "cols", split_axis=0, concat_axis=0, tiled=True)
 
@@ -583,7 +586,7 @@
         compiler_params=params(8),
         cost_estimate=pl.CostEstimate(flops=1 << 26, bytes_accessed=1 << 22, transcendentals=0),
         name="diffuse_forward",
-    )(first, second, packed, other)
+    )(second, first, packed, other)
 
     values = pl.pallas_call(
         functools.partial(lookup_kernel, cap_rows),
@@ -650,16 +653,16 @@
         out_shape=pltpu.VMEM((lev_share, per_level, LANES), f32),
         compiler_params=params(8),
         name="diffuse_adjoint",
-    )(coefs, tile_first, tile_second, tile, tile_other)
+    )(coefs, tile_second, tile_first, tile, tile_other)
     smooth, adjoint = lax.optimization_barrier((smooth, adjoint))
     smooths = [smooth] + from_peers(smooth)
 
     group = 2 - members % 2
     ensemble_grad = pl.pallas_call(
         member_kernel,
-        grid=(members // group,),
+        grid=(members // group, 2),
         in_specs=[VMEM] * 4,
-        out_specs=pl.BlockSpec((group, levels, per_level, LANES), lambda k: (k, 0, 0, 0)),
+        out_specs=pl.BlockSpec((group, levels, per_level // 2, LANES), lambda k, h: (k, 0, h, 0)),
         out_shape=jax.ShapeDtypeStruct((members, levels, per_level, LANES), f32),
         compiler_params=params(16),
         name="members_gradient",

time: 61.6 us -> 61.7 us (level)
  the two profiles are of different devices: /device:TPU:0 before, /device:TPU:10 now
where the time goes in v10:
time: 61.7 us; the launch traced here: 61.4 us
  Pallas kernels  34.7 us (56%)
  starting transfers between devices  21 us (34%)
  waiting for transfers between devices  4.74 us (8%)
  between operations  0.87 us (1%)
    ppermute x4, starting transfers between devices, exchanged(): out.append(lax.ppermute(x, 'cols', pairs))  8.47 us
    pallas_call x1, Pallas kernels, local(): pl.pallas_call(functools.partial(observe_kernel, n_cols, cap_rows, member...  7.3 us
    ppermute x6, starting transfers between devices, from_peers(): lax.ppermute(x, 'ens', [(peer(i, d, count), i) for i in range(count)])  7.11 us
    pallas_call x1, Pallas kernels, local(): pl.pallas_call(functools.partial(lookup_kernel, cap_rows), in_specs=[VMEM...  6.2 us
    pallas_call x1, Pallas kernels, local(): pl.pallas_call(member_kernel, grid=(members // group, 2), in_specs=[VMEM]...  6.05 us
    all_to_all x1, starting transfers between devices, local(): lax.all_to_all(slots, 'cols', split_axis=0, concat_axis=0, tiled=True)  5.24 us
    pallas_call x1, Pallas kernels, local(): pl.pallas_call(functools.partial(scatter_rest_kernel, cap_rows), in_specs...  5.01 us
    ppermute x6, waiting for transfers between devices, from_peers(): lax.ppermute(x, 'ens', [(peer(i, d, count), i) for i in range(count)])  4.46 us
  transfers between devices with their start and end apart: 13, of which 4 were waited for; matrix products, arithmetic and copies ran while one was open for 0% of the time, Pallas kernels for 44%

profile of v10, /device:TPU:10, one launch (start us, length us, event | category | flops | bytes accessed | tf_op | source)
XLA Modules:
  0.0 61.4 jit_solution(13389485334367861798)
XLA Ops:
  0.6 2.0 %prepare.1 = (f32[6,64,128]{2,1,0:T(8,128)S(1)}, s32[64,128]{1,0:T(8,128)S(1)}, s32[64,128]{1,0:T(8,128)S(1)}, s32[128,128]{1,0:T(8,128)S(1)}, f32[128,128]{1,0:T(8,128)S(1)}, /*index=5*/f32[128,128]{1,0:T(8,128)S(1)}) custom-call(f32[16,16]{1,0:T(8,128)} %root_ref, s32[8]{0:T(128)} %refs_1_.1, f32[16,64,128]{2,1,0:T(8,128)} %bitcast.68, ...), custom_call_target="tpu_custom_call" | custom-call | tf_op jit(solution)/shard_map/prepare/pallas_call | solution.py:511
  2.7 3.5 %collective-permute-start = (f32[6,64,128]{2,1,0:T(8,128)S(1)}, f32[6,64,128]{2,1,0:T(8,128)S(1)}, u32[]{:S(2)}, u32[]{:S(2)}) collective-permute-start(f32[6,64,128]{2,1,0:T(8,128)S(1)} %get-tuple-element.35.own_ref), channel_id=1, source_target_pairs={{0,0},{1,1},{2,4},{3,5},{4,2},{5,3},{6,6},{7,7},{8,8},{9,9},{10,12... | collective-permute-start | bytes 589832 | tf_op jit(solution)/shard_map/ppermute | solution.py:461
  6.1 0.1 collective-permute-start.1
  6.3 7.3 %slot_sums_and_members.1 = (f32[8,2,8,128]{3,2,1,0:T(8,128)}, f32[16,64,128]{2,1,0:T(8,128)S(1)}) custom-call(s32[128,128]{1,0:T(8,128)S(1)} %get-tuple-element.36.refs_0_, f32[128,128]{1,0:T(8,128)S(1)} %get-tuple-element.37.refs_1_, f32[128,128]{1,0:T(8,128)S(1)} %get-tuple-element.38.refs_2_, f32[16,16]{1,0:T(8,128)} %local_ref, ...), custom_call_target="tpu_custom_call" | custom-call | tf_op jit(solution)/shard_map/slot_sums_and_members/pallas_call | solution.py:552
  13.6 0.0 collective-permute-done.second_ref
  13.6 0.0 collective-permute-done.1.first_ref
  13.7 0.1 collective-permute-start.2
  13.7 5.2 %all-to-all-start = ((f32[8,2,8,128]{3,2,1,0:T(8,128)}), f32[8,2,8,128]{3,2,1,0:T(8,128)S(1)}, u32[]{:S(2)}, u32[]{:S(2)}) async-start(f32[8,2,8,128]{3,2,1,0:T(8,128)} %get-tuple-element.47), calls=%async_computation | async-start | bytes 131072 | tf_op jit(solution)/shard_map/all_to_all | solution.py:576
  19.0 0.0 collective-permute-done.2.other_ref
  19.0 1.5 %diffuse_forward.1 = (f32[4,64,128]{2,1,0:T(8,128)S(1)}, f32[5,10,32,128]{3,2,1,0:T(8,128)S(1)}) custom-call(f32[6,64,128]{2,1,0:T(8,128)S(1)} %collective-permute-done.second_ref, f32[6,64,128]{2,1,0:T(8,128)S(1)} %collective-permute-done.1.first_ref, f32[6,64,128]{2,1,0:T(8,128)S(1)} %get-tuple-element.35.own_ref, ...), custom_call_target="tpu_custom_call" | custom-call | flops 67108864 | bytes 4194304 | tf_op jit(solution)/shard_map/diffuse_forward/pallas_call | solution.py:578
  20.5 6.2 %lookup.1 = f32[64,128]{1,0:T(8,128)S(1)} custom-call(f32[1024,128]{1,0:T(8,128)S(1)} %bitcast.61, f32[256,128]{1,0:T(8,128)S(1)} %bitcast.62, s32[64,128]{1,0:T(8,128)S(1)} %get-tuple-element.43.row_ref, s32[64,128]{1,0:T(8,128)S(1)} %get-tuple-element.44.lane_ref), custom_call_target="tpu_custom_call" | custom-call | flops 4294967296 | bytes 16777216 | tf_op jit(solution)/shard_map/lookup/pallas_call | solution.py:591
  26.7 1.6 %collective-permute-start.3 = (f32[3,64,128]{2,1,0:T(8,128)S(1)}, f32[3,64,128]{2,1,0:T(8,128)S(1)}, u32[]{:S(2)}, u32[]{:S(2)}) collective-permute-start(f32[3,64,128]{2,1,0:T(8,128)S(1)} %pad_maximum_fusion.2.refs_0_), channel_id=1, source_target_pairs={{24,0},{16,8},{8,16},{0,24},{25,1},{17,9},{9,17},{1,25},{26,2},{18... | collective-permute-start | bytes 294920 | tf_op jit(solution)/shard_map/ppermute | solution.py:467
  28.3 0.5 collective-permute-start.4
  28.8 1.5 %collective-permute-start.5 = (f32[3,64,128]{2,1,0:T(8,128)S(1)}, f32[3,64,128]{2,1,0:T(8,128)S(1)}, u32[]{:S(2)}, u32[]{:S(2)}) collective-permute-start(f32[3,64,128]{2,1,0:T(8,128)S(1)} %pad_maximum_fusion.2.refs_0_), channel_id=1, source_target_pairs={{8,0},{0,8},{24,16},{16,24},{9,1},{1,9},{25,17},{17,25},{10,2},{2,... | collective-permute-start | bytes 294920 | tf_op jit(solution)/shard_map/ppermute | solution.py:467
  30.3 2.9 %collective-permute-done.3.refs_1_ = f32[3,64,128]{2,1,0:T(8,128)S(1)} collective-permute-done((f32[3,64,128]{2,1,0:T(8,128)S(1)}, f32[3,64,128]{2,1,0:T(8,128)S(1)}, u32[]{:S(2)}, u32[]{:S(2)}) %collective-permute-start.3) | collective-permute-done | bytes 98336 | tf_op jit(solution)/shard_map/ppermute | solution.py:467
  33.2 1.4 %collective-permute-done.4.refs_2_ = f32[3,64,128]{2,1,0:T(8,128)S(1)} collective-permute-done((f32[3,64,128]{2,1,0:T(8,128)S(1)}, f32[3,64,128]{2,1,0:T(8,128)S(1)}, u32[]{:S(2)}, u32[]{:S(2)}) %collective-permute-start.4) | collective-permute-done | bytes 98336 | tf_op jit(solution)/shard_map/ppermute | solution.py:467
  34.7 0.1 collective-permute-done.5.refs_3_
  34.7 2.8 %scatter_own.1 = (f32[256,128]{1,0:T(8,128)S(1)}, f32[64,128]{1,0:T(8,128)S(1)}) custom-call(s32[64,128]{1,0:T(8,128)S(1)} %get-tuple-element.43.row_ref, s32[64,128]{1,0:T(8,128)S(1)} %get-tuple-element.44.lane_ref, f32[3,64,128]{2,1,0:T(8,128)S(1)} %pad_maximum_fusion.2.refs_0_, f32[3,64,128]{2,1,0:T(8,128)S(1)} %collective-permute-done.3.refs_1_, ...), custom_call_target="tpu_custom_call" | custom-call | tf_op jit(solution)/shard_map/scatter_own/pallas_call | solution.py:608
  37.6 0.5 collective-permute-start.6
  38.0 4.4 %collective-permute-start.7 = (f32[4,64,128]{2,1,0:T(8,128)S(1)}, f32[4,64,128]{2,1,0:T(8,128)S(1)}, u32[]{:S(2)}, u32[]{:S(2)}) collective-permute-start(f32[4,64,128]{2,1,0:T(8,128)S(1)} %bitcast.55), channel_id=1, source_target_pairs={{0,0},{1,1},{2,4},{3,5},{4,2},{5,3},{6,6},{7,7},{8,8},{9,9},{10,12... | collective-permute-start | bytes 393224 | tf_op jit(solution)/shard_map/ppermute | solution.py:461
  42.5 5.0 %scatter_rest.1 = (f32[1024,128]{1,0:T(8,128)S(1)}, f32[16,64,128]{2,1,0:T(8,128)S(1)}, f32[8,16,64,128]{3,2,1,0:T(8,128)S(1)}, bf16[8,16,64,128]{3,2,1,0:T(8,128)(2,1)S(1)}) custom-call(s32[64,128]{1,0:T(8,128)S(1)} %get-tuple-element.43.row_ref, s32[64,128]{1,0:T(8,128)S(1)} %get-tuple-element.44.lane_ref, f32[64,128]{1,0:T(8,128)S(1)} %get-tuple-element.51.amount_ref, ...), custom_call_target="tpu_custom_call" | custom-call | tf_op jit(solution)/shard_map/scatter_rest/pallas_call | solution.py:620
  47.5 0.0 collective-permute-done.6.first_ref
  47.5 0.0 collective-permute-done.7.second_ref
  47.6 0.1 collective-permute-start.8
  47.7 1.2 %level_matrices.1 = (bf16[256,768]{1,0:T(8,128)(2,1)S(1)}, bf16[256,768]{1,0:T(8,128)(2,1)S(1)}) custom-call(f32[16,16]{1,0:T(8,128)} %local_ref, f32[16,16]{1,0:T(8,128)} %root_ref), custom_call_target="tpu_custom_call" | custom-call | tf_op jit(solution)/shard_map/level_matrices/pallas_call | solution.py:638
  48.9 0.3 collective-permute-done.8.other_ref
  49.2 1.4 %diffuse_adjoint.1.refs_0_ = f32[4,64,128]{2,1,0:T(8,128)S(1)} custom-call(f32[5,10,32,128]{3,2,1,0:T(8,128)S(1)} %get-tuple-element.59.coef_ref, f32[4,64,128]{2,1,0:T(8,128)S(1)} %collective-permute-done.7.second_ref, f32[4,64,128]{2,1,0:T(8,128)S(1)} %collective-permute-done.6.first_ref, f32[4,64,128]{2,1,0:T(8,128)S(1)} %bitcast.57, ...), custom_call_target="tpu_custom_call" | custom-call | tf_op jit(solution)/shard_map/diffuse_adjoint/pallas_call | solution.py:649
  50.6 1.5 %collective-permute-start.9 = (f32[4,64,128]{2,1,0:T(8,128)S(1)}, f32[4,64,128]{2,1,0:T(8,128)S(1)}, u32[]{:S(2)}, u32[]{:S(2)}) collective-permute-start(f32[4,64,128]{2,1,0:T(8,128)S(1)} %diffuse_adjoint.1.refs_0_), channel_id=1, source_target_pairs={{24,0},{16,8},{8,16},{0,24},{25,1},{17,9},{9,17},{1,25},{26,2},{18... | collective-permute-start | bytes 393224 | tf_op jit(solution)/shard_map/ppermute | solution.py:467
  52.1 0.5 collective-permute-start.10
  52.6 1.5 %collective-permute-start.11 = (f32[4,64,128]{2,1,0:T(8,128)S(1)}, f32[4,64,128]{2,1,0:T(8,128)S(1)}, u32[]{:S(2)}, u32[]{:S(2)}) collective-permute-start(f32[4,64,128]{2,1,0:T(8,128)S(1)} %diffuse_adjoint.1.refs_0_), channel_id=1, source_target_pairs={{8,0},{0,8},{24,16},{16,24},{9,1},{1,9},{25,17},{17,25},{10,2},{2,... | collective-permute-start | bytes 393224 | tf_op jit(solution)/shard_map/ppermute | solution.py:467
  54.1 6.0 %members_gradient.1 = f32[8,16,64,128]{3,2,1,0:T(8,128)} custom-call(bf16[256,768]{1,0:T(8,128)(2,1)S(1)} %get-tuple-element.64.matrix_ref, f32[16,64,128]{2,1,0:T(8,128)S(1)} %bitcast.59, f32[8,16,64,128]{3,2,1,0:T(8,128)S(1)} %get-tuple-element.66.control_ref, bf16[8,16,64,128]{3,2,1,0:T(8,128)(2,1)S(1)} %get-tuple-element.67.pert_ref), custom_call_target="tpu_custom_call" | custom-call | tf_op jit(solution)/shard_map/members_gradient/pallas_call | solution.py:661
  60.2 1.2 %static_gradient.1 = f32[16,64,128]{2,1,0:T(8,128)} custom-call(bf16[256,768]{1,0:T(8,128)(2,1)S(1)} %get-tuple-element.57.matrix_ref, f32[16,64,128]{2,1,0:T(8,128)S(1)} %get-tuple-element.58.static_ref, f32[4,64,128]{2,1,0:T(8,128)S(1)} %diffuse_adjoint.1.refs_0_, f32[4,64,128]{2,1,0:T(8,128)S(1)} %collective-permute-done.9.refs_1_, ...), custom_call_target="tpu_custom_call" | custom-call | tf_op jit(solution)/shard_map/static_gradient/pallas_call | solution.py:671
  (10 shorter events, 0.1 us)
Async XLA Ops:
  2.7 10.9 %collective-permute-start = (f32[6,64,128]{2,1,0:T(8,128)S(1)}, f32[6,64,128]{2,1,0:T(8,128)S(1)}, u32[]{:S(2)}, u32[]{:S(2)}) collective-permute-start(f32[6,64,128]{2,1,0:T(8,128)S(1)} %get-tuple-element.35.own_ref), channel_id=1, source_target_pairs={{0,0},{1,1},{2,4},{3,5},{4,2},{5,3},{6,6},{7,7},{8,8},{9,9},{10,12... | collective-permute-start | bytes 589832 | tf_op jit(solution)/shard_map/ppermute | solution.py:461
  6.1 7.4 %collective-permute-start.1 = (f32[6,64,128]{2,1,0:T(8,128)S(1)}, f32[6,64,128]{2,1,0:T(8,128)S(1)}, u32[]{:S(2)}, u32[]{:S(2)}) collective-permute-start(f32[6,64,128]{2,1,0:T(8,128)S(1)} %get-tuple-element.35.own_ref), channel_id=1, source_target_pairs={{0,2},{1,3},{2,0},{3,1},{4,6},{5,7},{6,4},{7,5},{8,10},{9,11},{10,... | collective-permute-start | bytes 589832 | tf_op jit(solution)/shard_map/ppermute | solution.py:461
  13.7 5.3 %collective-permute-start.2 = (f32[2,6,64,128]{3,2,1,0:T(8,128)S(1)}, f32[2,6,64,128]{3,2,1,0:T(8,128)S(1)}, u32[]{:S(2)}, u32[]{:S(2)}) collective-permute-start(f32[2,6,64,128]{3,2,1,0:T(8,128)S(1)} %pad_maximum_fusion), channel_id=1, source_target_pairs={{0,1},{1,0},{2,3},{3,2},{4,5},{5,4},{6,7},{7,6},{8,9},{9,8},{10,11... | collective-permute-start | bytes 1179656 | tf_op jit(solution)/shard_map/ppermute | solution.py:473
  13.7 13.0 %all-to-all-start = ((f32[8,2,8,128]{3,2,1,0:T(8,128)}), f32[8,2,8,128]{3,2,1,0:T(8,128)S(1)}, u32[]{:S(2)}, u32[]{:S(2)}) async-start(f32[8,2,8,128]{3,2,1,0:T(8,128)} %get-tuple-element.47), calls=%async_computation | async-start | bytes 131072 | tf_op jit(solution)/shard_map/all_to_all | solution.py:576
  26.7 6.5 %collective-permute-start.3 = (f32[3,64,128]{2,1,0:T(8,128)S(1)}, f32[3,64,128]{2,1,0:T(8,128)S(1)}, u32[]{:S(2)}, u32[]{:S(2)}) collective-permute-start(f32[3,64,128]{2,1,0:T(8,128)S(1)} %pad_maximum_fusion.2.refs_0_), channel_id=1, source_target_pairs={{24,0},{16,8},{8,16},{0,24},{25,1},{17,9},{9,17},{1,25},{26,2},{18... | collective-permute-start | bytes 294920 | tf_op jit(solution)/shard_map/ppermute | solution.py:467
  28.3 6.4 %collective-permute-start.4 = (f32[3,64,128]{2,1,0:T(8,128)S(1)}, f32[3,64,128]{2,1,0:T(8,128)S(1)}, u32[]{:S(2)}, u32[]{:S(2)}) collective-permute-start(f32[3,64,128]{2,1,0:T(8,128)S(1)} %pad_maximum_fusion.2.refs_0_), channel_id=1, source_target_pairs={{16,0},{24,8},{0,16},{8,24},{17,1},{25,9},{1,17},{9,25},{18,2},{26... | collective-permute-start | bytes 294920 | tf_op jit(solution)/shard_map/ppermute | solution.py:467
  28.8 5.9 %collective-permute-start.5 = (f32[3,64,128]{2,1,0:T(8,128)S(1)}, f32[3,64,128]{2,1,0:T(8,128)S(1)}, u32[]{:S(2)}, u32[]{:S(2)}) collective-permute-start(f32[3,64,128]{2,1,0:T(8,128)S(1)} %pad_maximum_fusion.2.refs_0_), channel_id=1, source_target_pairs={{8,0},{0,8},{24,16},{16,24},{9,1},{1,9},{25,17},{17,25},{10,2},{2,... | collective-permute-start | bytes 294920 | tf_op jit(solution)/shard_map/ppermute | solution.py:467
  37.6 9.9 %collective-permute-start.6 = (f32[4,64,128]{2,1,0:T(8,128)S(1)}, f32[4,64,128]{2,1,0:T(8,128)S(1)}, u32[]{:S(2)}, u32[]{:S(2)}) collective-permute-start(f32[4,64,128]{2,1,0:T(8,128)S(1)} %bitcast.54), channel_id=1, source_target_pairs={{0,2},{1,3},{2,0},{3,1},{4,6},{5,7},{6,4},{7,5},{8,10},{9,11},{10,... | collective-permute-start | bytes 393224 | tf_op jit(solution)/shard_map/ppermute | solution.py:461
  38.0 9.5 %collective-permute-start.7 = (f32[4,64,128]{2,1,0:T(8,128)S(1)}, f32[4,64,128]{2,1,0:T(8,128)S(1)}, u32[]{:S(2)}, u32[]{:S(2)}) collective-permute-start(f32[4,64,128]{2,1,0:T(8,128)S(1)} %bitcast.55), channel_id=1, source_target_pairs={{0,0},{1,1},{2,4},{3,5},{4,2},{5,3},{6,6},{7,7},{8,8},{9,9},{10,12... | collective-permute-start | bytes 393224 | tf_op jit(solution)/shard_map/ppermute | solution.py:461
  47.6 1.6 %collective-permute-start.8 = (f32[2,4,64,128]{3,2,1,0:T(8,128)S(1)}, f32[2,4,64,128]{3,2,1,0:T(8,128)S(1)}, u32[]{:S(2)}, u32[]{:S(2)}) collective-permute-start(f32[2,4,64,128]{3,2,1,0:T(8,128)S(1)} %pad_maximum_fusion.1), channel_id=1, source_target_pairs={{0,1},{1,0},{2,3},{3,2},{4,5},{5,4},{6,7},{7,6},{8,9},{9,8},{10,11... | collective-permute-start | bytes 786440 | tf_op jit(solution)/shard_map/ppermute | solution.py:473
  50.6 9.6 %collective-permute-start.9 = (f32[4,64,128]{2,1,0:T(8,128)S(1)}, f32[4,64,128]{2,1,0:T(8,128)S(1)}, u32[]{:S(2)}, u32[]{:S(2)}) collective-permute-start(f32[4,64,128]{2,1,0:T(8,128)S(1)} %diffuse_adjoint.1.refs_0_), channel_id=1, source_target_pairs={{24,0},{16,8},{8,16},{0,24},{25,1},{17,9},{9,17},{1,25},{26,2},{18... | collective-permute-start | bytes 393224 | tf_op jit(solution)/shard_map/ppermute | solution.py:467
  52.1 8.1 %collective-permute-start.10 = (f32[4,64,128]{2,1,0:T(8,128)S(1)}, f32[4,64,128]{2,1,0:T(8,128)S(1)}, u32[]{:S(2)}, u32[]{:S(2)}) collective-permute-start(f32[4,64,128]{2,1,0:T(8,128)S(1)} %diffuse_adjoint.1.refs_0_), channel_id=1, source_target_pairs={{16,0},{24,8},{0,16},{8,24},{17,1},{25,9},{1,17},{9,25},{18,2},{26... | collective-permute-start | bytes 393224 | tf_op jit(solution)/shard_map/ppermute | solution.py:467
  52.6 7.6 %collective-permute-start.11 = (f32[4,64,128]{2,1,0:T(8,128)S(1)}, f32[4,64,128]{2,1,0:T(8,128)S(1)}, u32[]{:S(2)}, u32[]{:S(2)}) collective-permute-start(f32[4,64,128]{2,1,0:T(8,128)S(1)} %diffuse_adjoint.1.refs_0_), channel_id=1, source_target_pairs={{8,0},{0,8},{24,16},{16,24},{9,1},{1,9},{25,17},{17,25},{10,2},{2,... | collective-permute-start | bytes 393224 | tf_op jit(solution)/shard_map/ppermute | solution.py:467

commit v11 on v10

--- a/solution.py
+++ b/solution.py
@@ -86,6 +86,10 @@
 
 def peer(i, d, count):
     return (i + d) % count if count & (count - 1) else i ^ d
+
+
+def back(d, count):
+    return count - d if count & (count - 1) else d
 
 
 def prepare_kernel(lev_share, rows, *refs):
@@ -148,12 +152,14 @@
 
 
 def observe_kernel(n_cols, cap_rows, scale, *refs):
-    (slot_ref, weight_ref, innov_ref), sources, (out_ref, part_ref) = refs[:3], refs[3:6], refs[6:8]
-    (acc_ref, fold_ref, matrix_ref), landed, sems, slots = (
-        refs[8:11],
-        refs[11:14],
-        refs[14],
-        (refs[15:17], refs[17:19]),
+    n_ens = len(refs) - 19
+    (slot_ref, weight_ref, innov_ref), sources, out_ref, parts = refs[:3], refs[3:6], refs[6], refs[7 : 7 + n_ens]
+    refs = refs[7 + n_ens :]
+    (acc_ref, fold_ref, matrix_ref, part_ref), landed, sems, slots = (
+        refs[:4],
+        refs[4:7],
+        refs[7],
+        (refs[8:10], refs[10:12]),
     )
     coarse = acc_ref.shape[1]
     obs_rows = slot_ref.shape[0]
@@ -196,13 +202,18 @@
         )
         for t in range(2)
     )
-    for p in range(n_cols):
-        out_ref[p, 0] = weights[p * cap_rows : (p + 1) * cap_rows]
-        out_ref[p, 1] = amounts[p * cap_rows : (p + 1) * cap_rows]
+    for e in range(n_ens):
+        for p in range(n_cols):
+            out_ref[e * n_cols + p, 0] = weights[p * cap_rows : (p + 1) * cap_rows]
+            out_ref[e * n_cols + p, 1] = amounts[p * cap_rows : (p + 1) * cap_rows]
     for copy in copies:
         copy.wait()
     matrix_ref[...] = level_product(local_ref[...] * f32(scale), False)
     sum_members(matrix_ref, control_ref, pert_ref, part_ref)
+    share = part_ref.shape[0] // n_ens
+    for d, part in enumerate(parts):
+        at = peer(lax.axis_index("ens"), d, n_ens) * share
+        part[...] = part_ref[pl.ds(at, share)]
 
 
 def sum_members(matrix_ref, control_ref, pert_ref, out_ref):
@@ -224,14 +235,24 @@
     lax.fori_loop(0, per_level // 16, chunk, 0)
 
 
-def member_kernel(matrix_ref, adjoint_ref, control_ref, pert_ref, out_ref):
-    group, levels, height, _ = out_ref.shape
+def gather_levels(parts, to_ref):
+    share = to_ref.shape[0] // len(parts)
+    for i, part in enumerate(parts):
+        at = peer(lax.axis_index("ens"), (len(parts) - i) % len(parts), len(parts))
+        to_ref[pl.ds(at * share, share)] = part[...]
+
+
+def member_kernel(matrix_ref, control_ref, pert_ref, *refs):
+    parts, out_ref, adjoint_ref = refs[:-2], refs[-2], refs[-1]
+    group, levels, per_level, _ = out_ref.shape
     first = pl.program_id(0) * group
-    top = pl.program_id(1) * height
+
+    @pl.when(pl.program_id(0) == 0)
+    def _():
+        gather_levels(parts, adjoint_ref)
 
     def chunk(j, carry):
-        to = pl.ds(pl.multiple_of(j * 16, 16), 16)
-        at = pl.ds(pl.multiple_of(top + j * 16, 16), 16)
+        at = pl.ds(pl.multiple_of(j * 16, 16), 16)
         adjoint = adjoint_ref[:, at, :]
         terms = [
             three_terms((pert_ref[first + i, :, at, :].astype(f32) * adjoint).reshape(levels * 16, LANES))
@@ -240,10 +261,10 @@
         change = jnp.dot(matrix_ref[...], jnp.concatenate(terms, axis=1), preferred_element_type=f32)
         for i in range(group):
             part = change[:, i * LANES : (i + 1) * LANES].reshape(levels, 16, LANES)
-            out_ref[i, :, to, :] = control_ref[first + i, :, at, :] + part
+            out_ref[i, :, at, :] = control_ref[first + i, :, at, :] + part
         return carry
 
-    lax.fori_loop(0, height // 16, chunk, 0)
+    lax.fori_loop(0, per_level // 16, chunk, 0)
 
 
 def eastern(x):
@@ -280,12 +301,11 @@
         field = [
             coef_ref[0, i + step] * field[i]
             + coef_ref[1, i + step] * field[i - 1]
-            + coef_ref[2, i + step] * field[i + 1]
-            + coef_ref[3, i + step] * eastern(field[i])
-            + coef_ref[4, i + step] * western(field[i])
+            + coef_ref[1, i + step + 1] * field[i + 1]
+            + coef_ref[2, i + step] * eastern(field[i])
+            + western(coef_ref[2, i + step] * field[i])
             for i in range(1, len(field) - 1)
         ]
-        field = list(field)
     return field
 
 
@@ -295,19 +315,15 @@
     side = 2
     north = rows_of(*tiles, lev_share, rows)
     east = rows_of(*tiles, lev_share + 1, rows)
-    for i in range(1, len(north) - 1):
-        south = north[i + 1]
-        if (i + 1) % rows == 0 and i < side * rows:
-            south = south * jnp.where(lax.axis_index("cols") == side - (i + 1) // rows, f32(0), f32(1))
-        west = western(east[i])
-        coef_ref[0, i] = 1.0 - north[i] - south - east[i] - west
-        coef_ref[1, i] = north[i]
-        coef_ref[2, i] = south
-        coef_ref[3, i] = east[i]
-        coef_ref[4, i] = west
-    for i in (0, len(north) - 1):
-        for c in range(5):
-            coef_ref[c, i] = jnp.zeros_like(north[0])
+    faces = [
+        jnp.where(lax.axis_index("cols") == side - i // rows, f32(0), n) if i % rows == 0 and i <= side * rows else n
+        for i, n in enumerate(north)
+    ]
+    for i in range(len(north)):
+        inner = 0 < i < len(north) - 1
+        coef_ref[0, i] = 1.0 - north[i] - faces[i + 1] - east[i] - western(east[i]) if inner else jnp.zeros_like(east[i])
+        coef_ref[1, i] = faces[i]
+        coef_ref[2, i] = east[i]
 
     def body(level, carry):
         final = diffuse_rows(tiles, level, coef_ref, rows)
@@ -332,115 +348,59 @@
     lax.fori_loop(0, lev_share, body, 0)
 
 
-def lookup_kernel(cap_rows, part_ref, static_ref, row_ref, lane_ref, out_ref, field_ref, terms_ref):
-    cells = part_ref.shape[0]
-    own = static_ref.shape[0]
-    at = pl.ds(pl.multiple_of(lax.axis_index("ens") * own, own), own)
-    field_ref[...] = part_ref[...]
-    field_ref[at, :] += static_ref[...]
-    for c in range(0, cells, LANES):
-        high, low = halves(field_ref[c : c + LANES, :].T)
-        terms_ref[:LANES, c : c + LANES] = high
-        terms_ref[LANES:, c : c + LANES] = low
-    ids = lax.broadcasted_iota(jnp.int32, (LANES, LANES), 0)
-
-    def look(q, carry):
-        at = pl.ds(pl.multiple_of(q * cap_rows, cap_rows), cap_rows)
-        rows = row_ref[at, :]
-        lanes = lane_ref[at, :]
-        picks = [placed_at(rows[c : c + 1, :], cells) for c in range(cap_rows)]
-        got = jnp.dot(terms_ref[...], jnp.concatenate(picks, axis=1), preferred_element_type=f32)
-        values = []
-        for c in range(cap_rows):
-            here = slice(c * LANES, (c + 1) * LANES)
-            mine = got[:LANES, here] + got[LANES:, here]
-            values.append(jnp.sum(jnp.where(ids == lanes[c : c + 1, :], mine, f32(0)), axis=0, keepdims=True))
-        out_ref[at, :] = jnp.concatenate(values, axis=0)
-        return carry
-
-    lax.fori_loop(0, row_ref.shape[0] // cap_rows, look, 0)
-
-
-def put(acc_ref, rows, lanes, amounts):
-    terms = [h.astype(f32) for h in halves(amounts)]
-    left, right = [], []
-    for c in range(rows.shape[0]):
-        left.append(placed_at(rows[c : c + 1, :], acc_ref.shape[0]))
-        mask = matches(lanes[c : c + 1, :], LANES)
-        right.append(
-            jnp.concatenate(
-                [
-                    jnp.where(mask, spread(t[c : c + 1, :], bf16)[None], bf16(0)).reshape(LANES, LANES)
-                    for t in terms
-                ],
-                axis=0,
-            )
-        )
-    acc_ref[...] += product_nt(jnp.concatenate(left, axis=1), jnp.concatenate(right, axis=1))
-
-
-def scatter_own_kernel(cap_rows, row_ref, lane_ref, *refs):
-    shares, (out_ref, amount_ref, acc_ref) = refs[:-3], refs[-3:]
-    own = out_ref.shape[0]
-    lists = row_ref.shape[0] // cap_rows
-    first = lax.axis_index("ens") * own
-    acc_ref[...] = jnp.zeros_like(acc_ref)
-
-    def step(q, carry):
-        at = pl.ds(pl.multiple_of(q * cap_rows, cap_rows), cap_rows)
-        value, weight, amount = (functools.reduce(jnp.add, [s[t, at, :] for s in shares]) for t in range(3))
-        amounts = value * weight - amount
-        amount_ref[at, :] = amounts
-        put(acc_ref, row_ref[at, :] - first, lane_ref[at, :], amounts)
-        return carry
-
-    lax.fori_loop(0, lists, step, 0)
-    out_ref[...] = acc_ref[:, :LANES] + acc_ref[:, LANES:]
-
-
-def matrices_kernel(scale, local_ref, root_ref, to_members_ref, to_static_ref):
-    to_members_ref[...] = level_product(local_ref[...] * f32(scale), True)
-    to_static_ref[...] = level_product(root_ref[...], True)
-
-
-def scatter_rest_kernel(cap_rows, row_ref, lane_ref, amount_ref, own_ref, *refs):
+def scatter_kernel(cap_rows, row_ref, lane_ref, slots_ref, *refs):
     sources, out_ref, kept, acc_ref, sems = refs[:3], refs[3], refs[4:7], refs[7], refs[8]
     copies = [pltpu.make_async_copy(s, t, sems.at[i]) for i, (s, t) in enumerate(zip(sources, kept))]
     for copy in copies:
         copy.start()
-    cells = out_ref.shape[0]
-    own = own_ref.shape[0]
-    n_ens = cells // own
-    me = lax.axis_index("ens")
-    first = (me + 1) * own
+    own = out_ref.shape[1]
+    lists = row_ref.shape[0] // cap_rows
+    first = lax.axis_index("ens") * own
     acc_ref[...] = jnp.zeros_like(acc_ref)
 
     def step(q, carry):
         at = pl.ds(pl.multiple_of(q * cap_rows, cap_rows), cap_rows)
-        row = row_ref[at, :]
-        turned = row - first
-        turned = jnp.where(row < 0, -1, jnp.where(turned < 0, turned + cells, turned))
-        put(acc_ref, turned, lane_ref[at, :], amount_ref[at, :])
+        rows = row_ref[at, :] - first
+        lanes = lane_ref[at, :]
+        terms = []
+        for t in range(2):
+            total = functools.reduce(
+                jnp.add, [slots_ref[e * lists + q, t] for e in range(slots_ref.shape[0] // lists)]
+            )
+            terms += [h.astype(f32) for h in halves(total)]
+        left, right = [], []
+        for c in range(cap_rows):
+            left.append(placed_at(rows[c : c + 1, :], own))
+            mask = matches(lanes[c : c + 1, :], LANES)
+            right.append(
+                jnp.concatenate(
+                    [
+                        jnp.where(mask, spread(t[c : c + 1, :], bf16)[None], bf16(0)).reshape(LANES, LANES)
+                        for t in terms
+                    ],
+                    axis=0,
+                )
+            )
+        acc_ref[...] += product_nt(jnp.concatenate(right, axis=1), jnp.concatenate(left, axis=1))
         return carry
 
-    lax.fori_loop(0, row_ref.shape[0] // cap_rows, step, 0)
-    out_ref[pl.ds(pl.multiple_of(me * own, own), own), :] = own_ref[...]
-    for t in range(1, n_ens):
-        to = pl.ds(pl.multiple_of((me + t) % n_ens * own, own), own)
-        piece = acc_ref[(t - 1) * own : t * own, :]
-        out_ref[to, :] = piece[:, :LANES] + piece[:, LANES:]
+    lax.fori_loop(0, lists, step, 0)
+    for t in range(2):
+        at = 2 * t * LANES
+        out_ref[t] = (acc_ref[at : at + LANES, :] + acc_ref[at + LANES : at + 2 * LANES, :]).T
     for copy in copies:
         copy.wait()
+
+
+def matrices_kernel(scale, local_ref, root_ref, to_members_ref, to_static_ref):
+    to_members_ref[...] = level_product(local_ref[...] * f32(scale), True)
+    to_static_ref[...] = level_product(root_ref[...], True)
 
 
 def static_kernel(matrix_ref, static_ref, *refs):
     parts, (out_ref, smooth_ref) = refs[:-2], refs[-2:]
     levels, per_level, _ = static_ref.shape
-    share = levels // len(parts)
-    me = lax.axis_index("ens")
-    for i, part in enumerate(parts):
-        at = peer(me, (len(parts) - i) % len(parts), len(parts))
-        smooth_ref[pl.ds(at * share, share)] = part[...]
+    gather_levels(parts, smooth_ref)
     for j in range(0, per_level, 32):
         terms = [three_terms(smooth_ref[:, j + i : j + i + 16, :].reshape(levels * 16, LANES)) for i in (0, 16)]
         change = jnp.dot(matrix_ref[...], jnp.concatenate(terms, axis=1), preferred_element_type=f32)
@@ -545,23 +505,22 @@
         in_hbm(obs_weight.reshape(obs_rows, LANES)),
         in_hbm(innovation.reshape(obs_rows, LANES)),
     )
-    second, first = exchanged(packed, (1, 0))
-
     coarse = n_cols * capacity // FINE
     size = levels * 16
-    slots, part = pl.pallas_call(
+    slots, *parts = pl.pallas_call(
         functools.partial(observe_kernel, n_cols, cap_rows, member_scale),
         grid=(1,),
         in_specs=[VMEM] * 3 + [pl.BlockSpec(memory_space=pl.ANY)] * 3,
-        out_specs=[whole(n_cols, 2, cap_rows, LANES), VMEM],
+        out_specs=[whole(n_ens * n_cols, 2, cap_rows, LANES)] + [VMEM] * n_ens,
         out_shape=[
-            pltpu.HBM((n_cols, 2, cap_rows, LANES), f32),
-            pltpu.VMEM((levels, per_level, LANES), f32),
-        ],
+            pltpu.HBM((n_ens * n_cols, 2, cap_rows, LANES), f32),
+        ]
+        + [pltpu.VMEM((lev_share, per_level, LANES), f32)] * n_ens,
         scratch_shapes=[
             pltpu.VMEM((4 * FINE, coarse), f32),
             pltpu.VMEM((2, coarse, LANES), f32),
             pltpu.VMEM((size, 3 * size), bf16),
+            pltpu.VMEM((levels, per_level, LANES), f32),
             pltpu.VMEM((levels, levels), f32),
             pltpu.VMEM(control.shape, f32),
             pltpu.VMEM(pert.shape, bf16),
@@ -571,9 +530,14 @@
         compiler_params=params(24),
         name="slot_sums_and_members",
     )(*observed, in_hbm(vertical_local), control, pert)
-    second, first, slots = lax.optimization_barrier((second, first, slots))
+    slots, packed = lax.optimization_barrier((slots, packed))
+    slots = lax.all_to_all(slots, ("ens", "cols"), split_axis=0, concat_axis=0, tiled=True)
+    second, first = exchanged(packed, (1, 0))
+    sums = [parts[0]] + [
+        lax.ppermute(parts[back(d, n_ens)], "ens", [(peer(i, d, n_ens), i) for i in range(n_ens)])
+        for d in range(n_ens - 1, 0, -1)
+    ]
     other = swapped(packed, first, second)
-    slots = lax.all_to_all(slots, "cols", split_axis=0, concat_axis=0, tiled=True)
 
     increment, coefs = pl.pallas_call(
         functools.partial(first_diffusion_kernel, lev_share, rows),
@@ -581,58 +545,36 @@
         out_specs=[VMEM] * 2,
         out_shape=[
             pltpu.VMEM((lev_share, per_level, LANES), f32),
-            pltpu.VMEM((5, 5 * rows, per_level // rows, LANES), f32),
+            pltpu.VMEM((3, 5 * rows, per_level // rows, LANES), f32),
         ],
         compiler_params=params(8),
         cost_estimate=pl.CostEstimate(flops=1 << 26, bytes_accessed=1 << 22, transcendentals=0),
         name="diffuse_forward",
     )(second, first, packed, other)
 
-    values = pl.pallas_call(
-        functools.partial(lookup_kernel, cap_rows),
-        in_specs=[VMEM] * 4,
-        out_specs=VMEM,
-        out_shape=pltpu.VMEM((entry_rows, LANES), f32),
-        scratch_shapes=[pltpu.VMEM((cells, LANES), f32), pltpu.VMEM((2 * LANES, cells), bf16)],
-        compiler_params=params(16),
-        cost_estimate=pl.CostEstimate(
-            flops=4 * cells * LANES * lists * capacity, bytes_accessed=8 * cells * lists * capacity // 4, transcendentals=0
-        ),
-        name="lookup",
-    )(part.reshape(cells, LANES), increment.reshape(own, LANES), entry_row, entry_lane)
-    values, slots = lax.optimization_barrier((values, slots))
-    slots = jnp.swapaxes(slots, 0, 1).reshape(2, entry_rows, LANES)
-    share = jnp.concatenate([values[None], slots])
-    shares = [share] + from_peers(share)
-
-    adjoint_own, amounts = pl.pallas_call(
-        functools.partial(scatter_own_kernel, cap_rows),
-        in_specs=[VMEM] * (2 + n_ens),
-        out_specs=[VMEM] * 2,
-        out_shape=[pltpu.VMEM((own, LANES), f32), pltpu.VMEM((entry_rows, LANES), f32)],
-        scratch_shapes=[pltpu.VMEM((own, 2 * LANES), f32)],
-        compiler_params=params(16),
-        name="scatter_own",
-    )(entry_row, entry_lane, *shares)
-    tile = adjoint_own.reshape(lev_share, per_level, LANES)
-    tile_first, tile_second = exchanged(tile, (0, 1))
-
-    adjoint, static_here, control_here, pert_here = pl.pallas_call(
-        functools.partial(scatter_rest_kernel, cap_rows),
-        in_specs=[VMEM] * 4 + [pl.BlockSpec(memory_space=pl.ANY)] * 3,
+    slot_sums, static_here, control_here, pert_here = pl.pallas_call(
+        functools.partial(scatter_kernel, cap_rows),
+        in_specs=[VMEM] * 3 + [pl.BlockSpec(memory_space=pl.ANY)] * 3,
         out_specs=[VMEM] * 4,
         out_shape=[
-            pltpu.VMEM((cells, LANES), f32),
+            pltpu.VMEM((2, own, LANES), f32),
             pltpu.VMEM(static.shape, f32),
             pltpu.VMEM(control.shape, f32),
             pltpu.VMEM(pert.shape, bf16),
         ],
-        scratch_shapes=[pltpu.VMEM((cells - own, 2 * LANES), f32), pltpu.SemaphoreType.DMA((3,))],
+        scratch_shapes=[pltpu.VMEM((4 * LANES, own), f32), pltpu.SemaphoreType.DMA((3,))],
         compiler_params=params(16),
-        name="scatter_rest",
-    )(entry_row, entry_lane, amounts, adjoint_own, static, control, pert)
-    tile_first, tile_second, adjoint, vertical_local, vertical_root = lax.optimization_barrier(
-        (tile_first, tile_second, adjoint, vertical_local, vertical_root)
+        cost_estimate=pl.CostEstimate(flops=8 * own * LANES * lists * capacity, bytes_accessed=1 << 23, transcendentals=0),
+        name="scatter",
+    )(entry_row, entry_lane, slots, static, control, pert)
+
+    slot_sums = slot_sums.reshape(2, lev_share, per_level, LANES)
+    tile = functools.reduce(jnp.add, sums) + increment
+    tile = tile * slot_sums[0] - slot_sums[1]
+    tile_first, tile_second = exchanged(tile, (0, 1))
+    adjoints = [tile] + from_peers(tile)
+    tile_first, tile_second, vertical_local, vertical_root = lax.optimization_barrier(
+        (tile_first, tile_second, vertical_local, vertical_root)
     )
     tile_other = swapped(tile, tile_first, tile_second)
     from_local, from_root = pl.pallas_call(
@@ -654,19 +596,20 @@
         compiler_params=params(8),
         name="diffuse_adjoint",
     )(coefs, tile_second, tile_first, tile, tile_other)
-    smooth, adjoint = lax.optimization_barrier((smooth, adjoint))
+    smooth, from_local = lax.optimization_barrier((smooth, from_local))
     smooths = [smooth] + from_peers(smooth)
 
     group = 2 - members % 2
     ensemble_grad = pl.pallas_call(
         member_kernel,
-        grid=(members // group, 2),
-        in_specs=[VMEM] * 4,
-        out_specs=pl.BlockSpec((group, levels, per_level // 2, LANES), lambda k, h: (k, 0, h, 0)),
+        grid=(members // group,),
+        in_specs=[VMEM] * (3 + n_ens),
+        out_specs=pl.BlockSpec((group, levels, per_level, LANES), lambda k: (k, 0, 0, 0)),
         out_shape=jax.ShapeDtypeStruct((members, levels, per_level, LANES), f32),
+        scratch_shapes=[pltpu.VMEM((levels, per_level, LANES), f32)],
         compiler_params=params(16),
         name="members_gradient",
-    )(from_local, adjoint.reshape(levels, per_level, LANES), control_here, pert_here)
+    )(from_local, control_here, pert_here, *adjoints)
 
     static_grad = pl.pallas_call(
         static_kernel,

time: 61.7 us -> 59.8 us (0.969)
  the two profiles are of different devices: /device:TPU:10 before, /device:TPU:0 now
where the time goes in v11:
time: 59.8 us; the launch traced here: 58.9 us
  Pallas kernels  24.3 us (41%)
  starting transfers between devices  22.2 us (37%)
  waiting for transfers between devices  11.4 us (19%)
  between operations  0.81 us (1%)
    ppermute x4, starting transfers between devices, exchanged(): out.append(lax.ppermute(x, 'cols', pairs))  7.79 us
    pallas_call x1, Pallas kernels, local(): pl.pallas_call(functools.partial(observe_kernel, n_cols, cap_rows, member...  7.37 us
    ppermute x6, starting transfers between devices, from_peers(): lax.ppermute(x, 'ens', [(peer(i, d, count), i) for i in range(count)])  7.11 us
    all_to_all x1, waiting for transfers between devices, local(): lax.all_to_all(slots, ('ens', 'cols'), split_axis=0, concat_axis=0, tiled...  6.68 us
    pallas_call x1, Pallas kernels, local(): pl.pallas_call(member_kernel, grid=(members // group,), in_specs=[VMEM] *...  5.65 us
    ppermute x4, waiting for transfers between devices, exchanged(): out.append(lax.ppermute(x, 'cols', pairs))  4.65 us
    pallas_call x1, Pallas kernels, local(): pl.pallas_call(functools.partial(scatter_kernel, cap_rows), in_specs=[VME...  3.99 us
    all_to_all x1, starting transfers between devices, local(): lax.all_to_all(slots, ('ens', 'cols'), split_axis=0, concat_axis=0, tiled...  3.59 us
  transfers between devices with their start and end apart: 16, of which 2 were waited for; matrix products, arithmetic and copies ran while one was open for 0% of the time, Pallas kernels for 23%

profile of v11, /device:TPU:0, one launch (start us, length us, event | category | flops | bytes accessed | tf_op | source)
XLA Modules:
  0.0 58.9 jit_solution(3187413405652175257)
XLA Ops:
  0.6 2.0 %prepare.1 = (f32[6,64,128]{2,1,0:T(8,128)S(1)}, s32[64,128]{1,0:T(8,128)S(1)}, s32[64,128]{1,0:T(8,128)S(1)}, s32[128,128]{1,0:T(8,128)S(1)}, f32[128,128]{1,0:T(8,128)S(1)}, /*index=5*/f32[128,128]{1,0:T(8,128)S(1)}) custom-call(f32[16,16]{1,0:T(8,128)} %root_ref, s32[8]{0:T(128)} %refs_1_.1, f32[16,64,128]{2,1,0:T(8,128)} %bitcast.53, ...), custom_call_target="tpu_custom_call" | custom-call | tf_op jit(solution)/shard_map/prepare/pallas_call | solution.py:471
  2.7 7.4 %slot_sums_and_members.1 = (f32[32,2,8,128]{3,2,1,0:T(8,128)}, f32[4,64,128]{2,1,0:T(8,128)S(1)}, f32[4,64,128]{2,1,0:T(8,128)S(1)}, f32[4,64,128]{2,1,0:T(8,128)S(1)}, f32[4,64,128]{2,1,0:T(8,128)S(1)}) custom-call(s32[128,128]{1,0:T(8,128)S(1)} %get-tuple-element.32.refs_0_, f32[128,128]{1,0:T(8,128)S(1)} %get-tuple-element.33.refs_1_, ...), custom_call_target="tpu_custom_call" | custom-call | tf_op jit(solution)/shard_map/slot_sums_and_members/pallas_call | solution.py:510
  10.0 0.7 %collective-permute-start = (f32[6,64,128]{2,1,0:T(8,128)S(1)}, f32[6,64,128]{2,1,0:T(8,128)S(1)}, u32[]{:S(2)}, u32[]{:S(2)}) collective-permute-start(f32[6,64,128]{2,1,0:T(8,128)S(1)} %get-tuple-element.37.own_ref), channel_id=1, source_target_pairs={{0,0},{1,1},{2,4},{3,5},{4,2},{5,3},{6,6},{7,7},{8,8},{9,9},{10,12... | collective-permute-start | bytes 589832 | tf_op jit(solution)/shard_map/ppermute | solution.py:421
  10.7 5.9 %collective-permute-start.1 = (f32[6,64,128]{2,1,0:T(8,128)S(1)}, f32[6,64,128]{2,1,0:T(8,128)S(1)}, u32[]{:S(2)}, u32[]{:S(2)}) collective-permute-start(f32[6,64,128]{2,1,0:T(8,128)S(1)} %get-tuple-element.37.own_ref), channel_id=1, source_target_pairs={{0,2},{1,3},{2,0},{3,1},{4,6},{5,7},{6,4},{7,5},{8,10},{9,11},{10,... | collective-permute-start | bytes 589832 | tf_op jit(solution)/shard_map/ppermute | solution.py:421
  16.6 3.6 %all-to-all-start = ((f32[32,2,8,128]{3,2,1,0:T(8,128)}), f32[32,2,8,128]{3,2,1,0:T(8,128)S(1)}, u32[]{:S(2)}, u32[]{:S(2)}) async-start(f32[32,2,8,128]{3,2,1,0:T(8,128)} %get-tuple-element.46), calls=%async_computation | async-start | bytes 524288 | tf_op jit(solution)/shard_map/all_to_all | solution.py:534
  20.2 1.8 %collective-permute-start.5 = (f32[4,64,128]{2,1,0:T(8,128)S(1)}, f32[4,64,128]{2,1,0:T(8,128)S(1)}, u32[]{:S(2)}, u32[]{:S(2)}) collective-permute-start(f32[4,64,128]{2,1,0:T(8,128)S(1)} %get-tuple-element.42), channel_id=1, source_target_pairs={{8,0},{0,8},{24,16},{16,24},{9,1},{1,9},{25,17},{17,25},{10,2},{2,... | collective-permute-start | bytes 393224 | tf_op jit(solution)/shard_map/ppermute | solution.py:537
  22.1 1.5 %collective-permute-start.4 = (f32[4,64,128]{2,1,0:T(8,128)S(1)}, f32[4,64,128]{2,1,0:T(8,128)S(1)}, u32[]{:S(2)}, u32[]{:S(2)}) collective-permute-start(f32[4,64,128]{2,1,0:T(8,128)S(1)} %get-tuple-element.41), channel_id=1, source_target_pairs={{16,0},{24,8},{0,16},{8,24},{17,1},{25,9},{1,17},{9,25},{18,2},{26... | collective-permute-start | bytes 393224 | tf_op jit(solution)/shard_map/ppermute | solution.py:537
  23.5 0.3 collective-permute-start.3
  23.8 0.0 collective-permute-done.second_ref
  23.8 0.0 collective-permute-done.1.first_ref
  23.8 0.1 collective-permute-start.2
  23.9 6.7 %all-to-all-done.slots_ref = f32[32,2,8,128]{3,2,1,0:T(8,128)S(1)} async-done(((f32[32,2,8,128]{3,2,1,0:T(8,128)}), f32[32,2,8,128]{3,2,1,0:T(8,128)S(1)}, u32[]{:S(2)}, u32[]{:S(2)}) %all-to-all-start) | async-done | bytes 262176 | tf_op jit(solution)/shard_map/all_to_all | solution.py:534
  30.6 4.0 %scatter.1 = (f32[2,256,128]{2,1,0:T(8,128)S(1)}, f32[16,64,128]{2,1,0:T(8,128)S(1)}, f32[8,16,64,128]{3,2,1,0:T(8,128)S(1)}, bf16[8,16,64,128]{3,2,1,0:T(8,128)(2,1)S(1)}) custom-call(s32[64,128]{1,0:T(8,128)S(1)} %get-tuple-element.44.row_ref, s32[64,128]{1,0:T(8,128)S(1)} %get-tuple-element.45.lane_ref, f32[32,2,8,128]{3,2,1,0:T(8,128)S(1)} %all-to-all-done.slots_ref, ...), custom_call_target="tpu_custom_call" | custom-call | flops 2147483648 | bytes 8388608 | tf_op jit(solution)/shard_map/scatter/pallas_call | solution.py:555
  34.6 0.0 collective-permute-done.2.other_ref
  34.7 1.5 %diffuse_forward.1 = (f32[4,64,128]{2,1,0:T(8,128)S(1)}, f32[3,10,32,128]{3,2,1,0:T(8,128)S(1)}) custom-call(f32[6,64,128]{2,1,0:T(8,128)S(1)} %collective-permute-done.second_ref, f32[6,64,128]{2,1,0:T(8,128)S(1)} %collective-permute-done.1.first_ref, f32[6,64,128]{2,1,0:T(8,128)S(1)} %get-tuple-element.37.own_ref, ...), custom_call_target="tpu_custom_call" | custom-call | flops 67108864 | bytes 4194304 | tf_op jit(solution)/shard_map/diffuse_forward/pallas_call | solution.py:542
  36.2 0.0 collective-permute-done.5
  36.2 0.1 multiply_subtract_fusion.own_ref.refs_0_
  36.3 0.6 collective-permute-start.6
  36.8 0.7 %collective-permute-start.7 = (f32[4,64,128]{2,1,0:T(8,128)S(1)}, f32[4,64,128]{2,1,0:T(8,128)S(1)}, u32[]{:S(2)}, u32[]{:S(2)}) collective-permute-start(f32[4,64,128]{2,1,0:T(8,128)S(1)} %multiply_subtract_fusion.own_ref.refs_0_), channel_id=1, source_target_pairs={{0,0},{1,1},{2,4},{3,5},{4,2},{5,3},{6,6},{7,7},{8,8},{9,9},{10,12... | collective-permute-start | bytes 393224 | tf_op jit(solution)/shard_map/ppermute | solution.py:421
  37.5 4.6 %collective-permute-done.6.first_ref = f32[4,64,128]{2,1,0:T(8,128)S(1)} collective-permute-done((f32[4,64,128]{2,1,0:T(8,128)S(1)}, f32[4,64,128]{2,1,0:T(8,128)S(1)}, u32[]{:S(2)}, u32[]{:S(2)}) %collective-permute-start.6) | collective-permute-done | bytes 131104 | tf_op jit(solution)/shard_map/ppermute | solution.py:421
  42.2 0.1 collective-permute-start.8
  42.3 1.0 %collective-permute-start.12 = (f32[4,64,128]{2,1,0:T(8,128)S(1)}, f32[4,64,128]{2,1,0:T(8,128)S(1)}, u32[]{:S(2)}, u32[]{:S(2)}) collective-permute-start(f32[4,64,128]{2,1,0:T(8,128)S(1)} %multiply_subtract_fusion.own_ref.refs_0_), channel_id=1, source_target_pairs={{24,0},{16,8},{8,16},{0,24},{25,1},{17,9},{9,17},{1,25},{26,2},{18... | collective-permute-start | bytes 393224 | tf_op jit(solution)/shard_map/ppermute | solution.py:427
  43.2 1.5 %collective-permute-start.13 = (f32[4,64,128]{2,1,0:T(8,128)S(1)}, f32[4,64,128]{2,1,0:T(8,128)S(1)}, u32[]{:S(2)}, u32[]{:S(2)}) collective-permute-start(f32[4,64,128]{2,1,0:T(8,128)S(1)} %multiply_subtract_fusion.own_ref.refs_0_), channel_id=1, source_target_pairs={{16,0},{24,8},{0,16},{8,24},{17,1},{25,9},{1,17},{9,25},{18,2},{26... | collective-permute-start | bytes 393224 | tf_op jit(solution)/shard_map/ppermute | solution.py:427
  44.7 1.1 %collective-permute-start.14 = (f32[4,64,128]{2,1,0:T(8,128)S(1)}, f32[4,64,128]{2,1,0:T(8,128)S(1)}, u32[]{:S(2)}, u32[]{:S(2)}) collective-permute-start(f32[4,64,128]{2,1,0:T(8,128)S(1)} %multiply_subtract_fusion.own_ref.refs_0_), channel_id=1, source_target_pairs={{8,0},{0,8},{24,16},{16,24},{9,1},{1,9},{25,17},{17,25},{10,2},{2,... | collective-permute-start | bytes 393224 | tf_op jit(solution)/shard_map/ppermute | solution.py:427
  45.8 1.2 %level_matrices.1 = (bf16[256,768]{1,0:T(8,128)(2,1)S(1)}, bf16[256,768]{1,0:T(8,128)(2,1)S(1)}) custom-call(f32[16,16]{1,0:T(8,128)} %local_ref, f32[16,16]{1,0:T(8,128)} %root_ref), custom_call_target="tpu_custom_call" | custom-call | tf_op jit(solution)/shard_map/level_matrices/pallas_call | solution.py:580
  47.1 1.3 %diffuse_adjoint.1.refs_0_ = f32[4,64,128]{2,1,0:T(8,128)S(1)} custom-call(f32[3,10,32,128]{3,2,1,0:T(8,128)S(1)} %get-tuple-element.54.coef_ref, f32[4,64,128]{2,1,0:T(8,128)S(1)} %collective-permute-done.7.second_ref, f32[4,64,128]{2,1,0:T(8,128)S(1)} %collective-permute-done.6.first_ref, f32[4,64,128]{2,1,0:T(8,128)S(1)} %multiply_subtract_fusion.own_ref.refs_0_, ...), custom_call_target="tpu_custom_call" | custom-call | tf_op jit(solution)/shard_map/diffuse_adjoint/pallas_call | solution.py:591
  48.4 1.0 %collective-permute-start.9 = (f32[4,64,128]{2,1,0:T(8,128)S(1)}, f32[4,64,128]{2,1,0:T(8,128)S(1)}, u32[]{:S(2)}, u32[]{:S(2)}) collective-permute-start(f32[4,64,128]{2,1,0:T(8,128)S(1)} %diffuse_adjoint.1.refs_0_), channel_id=1, source_target_pairs={{24,0},{16,8},{8,16},{0,24},{25,1},{17,9},{9,17},{1,25},{26,2},{18... | collective-permute-start | bytes 393224 | tf_op jit(solution)/shard_map/ppermute | solution.py:427
  49.4 1.5 %collective-permute-start.10 = (f32[4,64,128]{2,1,0:T(8,128)S(1)}, f32[4,64,128]{2,1,0:T(8,128)S(1)}, u32[]{:S(2)}, u32[]{:S(2)}) collective-permute-start(f32[4,64,128]{2,1,0:T(8,128)S(1)} %diffuse_adjoint.1.refs_0_), channel_id=1, source_target_pairs={{16,0},{24,8},{0,16},{8,24},{17,1},{25,9},{1,17},{9,25},{18,2},{26... | collective-permute-start | bytes 393224 | tf_op jit(solution)/shard_map/ppermute | solution.py:427
  50.9 1.1 %collective-permute-start.11 = (f32[4,64,128]{2,1,0:T(8,128)S(1)}, f32[4,64,128]{2,1,0:T(8,128)S(1)}, u32[]{:S(2)}, u32[]{:S(2)}) collective-permute-start(f32[4,64,128]{2,1,0:T(8,128)S(1)} %diffuse_adjoint.1.refs_0_), channel_id=1, source_target_pairs={{8,0},{0,8},{24,16},{16,24},{9,1},{1,9},{25,17},{17,25},{10,2},{2,... | collective-permute-start | bytes 393224 | tf_op jit(solution)/shard_map/ppermute | solution.py:427
  52.0 0.0 collective-permute-done.13.refs_2_
  52.0 5.6 %members_gradient.1 = f32[8,16,64,128]{3,2,1,0:T(8,128)} custom-call(bf16[256,768]{1,0:T(8,128)(2,1)S(1)} %get-tuple-element.59.matrix_ref, f32[8,16,64,128]{3,2,1,0:T(8,128)S(1)} %get-tuple-element.60.control_ref, bf16[8,16,64,128]{3,2,1,0:T(8,128)(2,1)S(1)} %get-tuple-element.61.pert_ref, f32[4,64,128]{2,1,0:T(8,128)S(1)} %multiply_subtract_fusion.own_ref.refs_0_, ...), custom_call_target="tpu_custom_call" | custom-call | tf_op jit(solution)/shard_map/members_gradient/pallas_call | solution.py:603
  57.7 1.2 %static_gradient.1 = f32[16,64,128]{2,1,0:T(8,128)} custom-call(bf16[256,768]{1,0:T(8,128)(2,1)S(1)} %get-tuple-element.52.matrix_ref, f32[16,64,128]{2,1,0:T(8,128)S(1)} %get-tuple-element.53.static_ref, f32[4,64,128]{2,1,0:T(8,128)S(1)} %diffuse_adjoint.1.refs_0_, f32[4,64,128]{2,1,0:T(8,128)S(1)} %collective-permute-done.9.refs_1_, ...), custom_call_target="tpu_custom_call" | custom-call | tf_op jit(solution)/shard_map/static_gradient/pallas_call | solution.py:614
  (14 shorter events, 0.1 us)
Async XLA Ops:
  10.0 13.7 %collective-permute-start = (f32[6,64,128]{2,1,0:T(8,128)S(1)}, f32[6,64,128]{2,1,0:T(8,128)S(1)}, u32[]{:S(2)}, u32[]{:S(2)}) collective-permute-start(f32[6,64,128]{2,1,0:T(8,128)S(1)} %get-tuple-element.37.own_ref), channel_id=1, source_target_pairs={{0,0},{1,1},{2,4},{3,5},{4,2},{5,3},{6,6},{7,7},{8,8},{9,9},{10,12... | collective-permute-start | bytes 589832 | tf_op jit(solution)/shard_map/ppermute | solution.py:421
  10.7 13.1 %collective-permute-start.1 = (f32[6,64,128]{2,1,0:T(8,128)S(1)}, f32[6,64,128]{2,1,0:T(8,128)S(1)}, u32[]{:S(2)}, u32[]{:S(2)}) collective-permute-start(f32[6,64,128]{2,1,0:T(8,128)S(1)} %get-tuple-element.37.own_ref), channel_id=1, source_target_pairs={{0,2},{1,3},{2,0},{3,1},{4,6},{5,7},{6,4},{7,5},{8,10},{9,11},{10,... | collective-permute-start | bytes 589832 | tf_op jit(solution)/shard_map/ppermute | solution.py:421
  16.6 14.0 %all-to-all-start = ((f32[32,2,8,128]{3,2,1,0:T(8,128)}), f32[32,2,8,128]{3,2,1,0:T(8,128)S(1)}, u32[]{:S(2)}, u32[]{:S(2)}) async-start(f32[32,2,8,128]{3,2,1,0:T(8,128)} %get-tuple-element.46), calls=%async_computation | async-start | bytes 524288 | tf_op jit(solution)/shard_map/all_to_all | solution.py:534
  20.2 15.9 %collective-permute-start.5 = (f32[4,64,128]{2,1,0:T(8,128)S(1)}, f32[4,64,128]{2,1,0:T(8,128)S(1)}, u32[]{:S(2)}, u32[]{:S(2)}) collective-permute-start(f32[4,64,128]{2,1,0:T(8,128)S(1)} %get-tuple-element.42), channel_id=1, source_target_pairs={{8,0},{0,8},{24,16},{16,24},{9,1},{1,9},{25,17},{17,25},{10,2},{2,... | collective-permute-start | bytes 393224 | tf_op jit(solution)/shard_map/ppermute | solution.py:537
  22.1 14.1 %collective-permute-start.4 = (f32[4,64,128]{2,1,0:T(8,128)S(1)}, f32[4,64,128]{2,1,0:T(8,128)S(1)}, u32[]{:S(2)}, u32[]{:S(2)}) collective-permute-start(f32[4,64,128]{2,1,0:T(8,128)S(1)} %get-tuple-element.41), channel_id=1, source_target_pairs={{16,0},{24,8},{0,16},{8,24},{17,1},{25,9},{1,17},{9,25},{18,2},{26... | collective-permute-start | bytes 393224 | tf_op jit(solution)/shard_map/ppermute | solution.py:537
  23.5 12.7 %collective-permute-start.3 = (f32[4,64,128]{2,1,0:T(8,128)S(1)}, f32[4,64,128]{2,1,0:T(8,128)S(1)}, u32[]{:S(2)}, u32[]{:S(2)}) collective-permute-start(f32[4,64,128]{2,1,0:T(8,128)S(1)} %get-tuple-element.40), channel_id=1, source_target_pairs={{24,0},{16,8},{8,16},{0,24},{25,1},{17,9},{9,17},{1,25},{26,2},{18... | collective-permute-start | bytes 393224 | tf_op jit(solution)/shard_map/ppermute | solution.py:537
  23.8 10.8 %collective-permute-start.2 = (f32[2,6,64,128]{3,2,1,0:T(8,128)S(1)}, f32[2,6,64,128]{3,2,1,0:T(8,128)S(1)}, u32[]{:S(2)}, u32[]{:S(2)}) collective-permute-start(f32[2,6,64,128]{3,2,1,0:T(8,128)S(1)} %pad_maximum_fusion), channel_id=1, source_target_pairs={{0,1},{1,0},{2,3},{3,2},{4,5},{5,4},{6,7},{7,6},{8,9},{9,8},{10,11... | collective-permute-start | bytes 1179656 | tf_op jit(solution)/shard_map/ppermute | solution.py:433
  36.3 5.9 %collective-permute-start.6 = (f32[4,64,128]{2,1,0:T(8,128)S(1)}, f32[4,64,128]{2,1,0:T(8,128)S(1)}, u32[]{:S(2)}, u32[]{:S(2)}) collective-permute-start(f32[4,64,128]{2,1,0:T(8,128)S(1)} %multiply_subtract_fusion.own_ref.refs_0_), channel_id=1, source_target_pairs={{0,2},{1,3},{2,0},{3,1},{4,6},{5,7},{6,4},{7,5},{8,10},{9,11},{10,... | collective-permute-start | bytes 393224 | tf_op jit(solution)/shard_map/ppermute | solution.py:421
  36.8 5.3 %collective-permute-start.7 = (f32[4,64,128]{2,1,0:T(8,128)S(1)}, f32[4,64,128]{2,1,0:T(8,128)S(1)}, u32[]{:S(2)}, u32[]{:S(2)}) collective-permute-start(f32[4,64,128]{2,1,0:T(8,128)S(1)} %multiply_subtract_fusion.own_ref.refs_0_), channel_id=1, source_target_pairs={{0,0},{1,1},{2,4},{3,5},{4,2},{5,3},{6,6},{7,7},{8,8},{9,9},{10,12... | collective-permute-start | bytes 393224 | tf_op jit(solution)/shard_map/ppermute | solution.py:421
  42.2 4.9 %collective-permute-start.8 = (f32[2,4,64,128]{3,2,1,0:T(8,128)S(1)}, f32[2,4,64,128]{3,2,1,0:T(8,128)S(1)}, u32[]{:S(2)}, u32[]{:S(2)}) collective-permute-start(f32[2,4,64,128]{3,2,1,0:T(8,128)S(1)} %pad_maximum_fusion.1), channel_id=1, source_target_pairs={{0,1},{1,0},{2,3},{3,2},{4,5},{5,4},{6,7},{7,6},{8,9},{9,8},{10,11... | collective-permute-start | bytes 786440 | tf_op jit(solution)/shard_map/ppermute | solution.py:433
  42.3 8.6 %collective-permute-start.12 = (f32[4,64,128]{2,1,0:T(8,128)S(1)}, f32[4,64,128]{2,1,0:T(8,128)S(1)}, u32[]{:S(2)}, u32[]{:S(2)}) collective-permute-start(f32[4,64,128]{2,1,0:T(8,128)S(1)} %multiply_subtract_fusion.own_ref.refs_0_), channel_id=1, source_target_pairs={{24,0},{16,8},{8,16},{0,24},{25,1},{17,9},{9,17},{1,25},{26,2},{18... | collective-permute-start | bytes 393224 | tf_op jit(solution)/shard_map/ppermute | solution.py:427
  43.2 8.8 %collective-permute-start.13 = (f32[4,64,128]{2,1,0:T(8,128)S(1)}, f32[4,64,128]{2,1,0:T(8,128)S(1)}, u32[]{:S(2)}, u32[]{:S(2)}) collective-permute-start(f32[4,64,128]{2,1,0:T(8,128)S(1)} %multiply_subtract_fusion.own_ref.refs_0_), channel_id=1, source_target_pairs={{16,0},{24,8},{0,16},{8,24},{17,1},{25,9},{1,17},{9,25},{18,2},{26... | collective-permute-start | bytes 393224 | tf_op jit(solution)/shard_map/ppermute | solution.py:427
  44.7 7.3 %collective-permute-start.14 = (f32[4,64,128]{2,1,0:T(8,128)S(1)}, f32[4,64,128]{2,1,0:T(8,128)S(1)}, u32[]{:S(2)}, u32[]{:S(2)}) collective-permute-start(f32[4,64,128]{2,1,0:T(8,128)S(1)} %multiply_subtract_fusion.own_ref.refs_0_), channel_id=1, source_target_pairs={{8,0},{0,8},{24,16},{16,24},{9,1},{1,9},{25,17},{17,25},{10,2},{2,... | collective-permute-start | bytes 393224 | tf_op jit(solution)/shard_map/ppermute | solution.py:427
  48.4 9.2 %collective-permute-start.9 = (f32[4,64,128]{2,1,0:T(8,128)S(1)}, f32[4,64,128]{2,1,0:T(8,128)S(1)}, u32[]{:S(2)}, u32[]{:S(2)}) collective-permute-start(f32[4,64,128]{2,1,0:T(8,128)S(1)} %diffuse_adjoint.1.refs_0_), channel_id=1, source_target_pairs={{24,0},{16,8},{8,16},{0,24},{25,1},{17,9},{9,17},{1,25},{26,2},{18... | collective-permute-start | bytes 393224 | tf_op jit(solution)/shard_map/ppermute | solution.py:427
  49.4 8.3 %collective-permute-start.10 = (f32[4,64,128]{2,1,0:T(8,128)S(1)}, f32[4,64,128]{2,1,0:T(8,128)S(1)}, u32[]{:S(2)}, u32[]{:S(2)}) collective-permute-start(f32[4,64,128]{2,1,0:T(8,128)S(1)} %diffuse_adjoint.1.refs_0_), channel_id=1, source_target_pairs={{16,0},{24,8},{0,16},{8,24},{17,1},{25,9},{1,17},{9,25},{18,2},{26... | collective-permute-start | bytes 393224 | tf_op jit(solution)/shard_map/ppermute | solution.py:427
  50.9 6.8 %collective-permute-start.11 = (f32[4,64,128]{2,1,0:T(8,128)S(1)}, f32[4,64,128]{2,1,0:T(8,128)S(1)}, u32[]{:S(2)}, u32[]{:S(2)}) collective-permute-start(f32[4,64,128]{2,1,0:T(8,128)S(1)} %diffuse_adjoint.1.refs_0_), channel_id=1, source_target_pairs={{8,0},{0,8},{24,16},{16,24},{9,1},{1,9},{25,17},{17,25},{10,2},{2,... | collective-permute-start | bytes 393224 | tf_op jit(solution)/shard_map/ppermute | solution.py:427

commit v12 on v11

--- a/solution.py
+++ b/solution.py
@@ -151,24 +151,12 @@
     return jnp.concatenate([high, low, high], axis=0)
 
 
-def observe_kernel(n_cols, cap_rows, scale, *refs):
-    n_ens = len(refs) - 19
-    (slot_ref, weight_ref, innov_ref), sources, out_ref, parts = refs[:3], refs[3:6], refs[6], refs[7 : 7 + n_ens]
-    refs = refs[7 + n_ens :]
-    (acc_ref, fold_ref, matrix_ref, part_ref), landed, sems, slots = (
-        refs[:4],
-        refs[4:7],
-        refs[7],
-        (refs[8:10], refs[10:12]),
-    )
+def slots_kernel(n_cols, cap_rows, slot_ref, weight_ref, innov_ref, out_ref, acc_ref, fold_ref, *slots):
+    slots = (slots[:2], slots[2:])
     coarse = acc_ref.shape[1]
     obs_rows = slot_ref.shape[0]
     group = min(8, obs_rows)
-    copies = [pltpu.make_async_copy(s, t, sems.at[i]) for i, (s, t) in enumerate(zip(sources, landed))]
-    for copy in copies:
-        copy.start()
     acc_ref[...] = jnp.zeros_like(acc_ref)
-    local_ref, control_ref, pert_ref = landed
 
     def build(i, to):
         at = pl.ds(pl.multiple_of(i * group, group), group)
@@ -202,37 +190,48 @@
         )
         for t in range(2)
     )
-    for e in range(n_ens):
+    for e in range(out_ref.shape[0] // n_cols):
         for p in range(n_cols):
             out_ref[e * n_cols + p, 0] = weights[p * cap_rows : (p + 1) * cap_rows]
             out_ref[e * n_cols + p, 1] = amounts[p * cap_rows : (p + 1) * cap_rows]
-    for copy in copies:
-        copy.wait()
-    matrix_ref[...] = level_product(local_ref[...] * f32(scale), False)
-    sum_members(matrix_ref, control_ref, pert_ref, part_ref)
-    share = part_ref.shape[0] // n_ens
-    for d, part in enumerate(parts):
-        at = peer(lax.axis_index("ens"), d, n_ens) * share
-        part[...] = part_ref[pl.ds(at, share)]
-
-
-def sum_members(matrix_ref, control_ref, pert_ref, out_ref):
+
+
+def forward_kernel(scale, local_ref, *refs):
+    sources, parts = refs[:2], refs[2:-5]
+    matrix_ref, part_ref, control_ref, pert_ref, sems = refs[-5:]
     members, levels, per_level, _ = control_ref.shape
     group = 2 - members % 2
-
-    def chunk(j, carry):
-        at = pl.ds(pl.multiple_of(j * 16, 16), 16)
-        total = jnp.zeros((levels * 16, LANES), f32)
-        for k in range(0, members, group):
+    copies = [
+        [
+            pltpu.make_async_copy(s.at[pl.ds(k, group)], t.at[pl.ds(k, group)], sems.at[i, k // group])
+            for i, (s, t) in enumerate(zip(sources, (control_ref, pert_ref)))
+        ]
+        for k in range(0, members, group)
+    ]
+    for pair in copies:
+        for copy in pair:
+            copy.start()
+    matrix_ref[...] = level_product(local_ref[...] * f32(scale), False)
+    for k, pair in zip(range(0, members, group), copies):
+        for copy in pair:
+            copy.wait()
+
+        def chunk(j, carry):
+            at = pl.ds(pl.multiple_of(j * 16, 16), 16)
             terms = [three_terms(control_ref[k + i, :, at, :].reshape(levels * 16, LANES)) for i in range(group)]
             local = jnp.dot(matrix_ref[...], jnp.concatenate(terms, axis=1), preferred_element_type=f32)
+            total = part_ref[:, at, :] if k else jnp.zeros((levels, 16, LANES), f32)
             for i in range(group):
-                pert = pert_ref[k + i, :, at, :].astype(f32).reshape(levels * 16, LANES)
-                total = total + pert * local[:, i * LANES : (i + 1) * LANES]
-        out_ref[:, at, :] = total.reshape(levels, 16, LANES)
-        return carry
-
-    lax.fori_loop(0, per_level // 16, chunk, 0)
+                part = local[:, i * LANES : (i + 1) * LANES].reshape(levels, 16, LANES)
+                total = total + pert_ref[k + i, :, at, :].astype(f32) * part
+            part_ref[:, at, :] = total
+            return carry
+
+        lax.fori_loop(0, per_level // 16, chunk, 0)
+    share = levels // len(parts)
+    for d, part in enumerate(parts):
+        at = peer(lax.axis_index("ens"), d, len(parts)) * share
+        part[...] = part_ref[pl.ds(at, share)]
 
 
 def gather_levels(parts, to_ref):
@@ -507,30 +506,39 @@
     )
     coarse = n_cols * capacity // FINE
     size = levels * 16
-    slots, *parts = pl.pallas_call(
-        functools.partial(observe_kernel, n_cols, cap_rows, member_scale),
+    slots = pl.pallas_call(
+        functools.partial(slots_kernel, n_cols, cap_rows),
         grid=(1,),
-        in_specs=[VMEM] * 3 + [pl.BlockSpec(memory_space=pl.ANY)] * 3,
-        out_specs=[whole(n_ens * n_cols, 2, cap_rows, LANES)] + [VMEM] * n_ens,
-        out_shape=[
-            pltpu.HBM((n_ens * n_cols, 2, cap_rows, LANES), f32),
-        ]
-        + [pltpu.VMEM((lev_share, per_level, LANES), f32)] * n_ens,
+        in_specs=[VMEM] * 3,
+        out_specs=whole(n_ens * n_cols, 2, cap_rows, LANES),
+        out_shape=pltpu.HBM((n_ens * n_cols, 2, cap_rows, LANES), f32),
         scratch_shapes=[
             pltpu.VMEM((4 * FINE, coarse), f32),
             pltpu.VMEM((2, coarse, LANES), f32),
+        ]
+        + [pltpu.VMEM((coarse, 8 * LANES), bf16), pltpu.VMEM((4 * FINE, 8 * LANES), bf16)] * 2,
+        compiler_params=params(16),
+        name="slot_sums",
+    )(*observed)
+    slots, packed, vertical_local = lax.optimization_barrier((slots, packed, vertical_local))
+    groups = members // (2 - members % 2)
+    parts = pl.pallas_call(
+        functools.partial(forward_kernel, member_scale),
+        grid=(1,),
+        in_specs=[whole(levels, levels)] + [pl.BlockSpec(memory_space=pl.ANY)] * 2,
+        out_specs=[VMEM] * n_ens,
+        out_shape=[pltpu.VMEM((lev_share, per_level, LANES), f32)] * n_ens,
+        scratch_shapes=[
             pltpu.VMEM((size, 3 * size), bf16),
             pltpu.VMEM((levels, per_level, LANES), f32),
-            pltpu.VMEM((levels, levels), f32),
             pltpu.VMEM(control.shape, f32),
             pltpu.VMEM(pert.shape, bf16),
-            pltpu.SemaphoreType.DMA((3,)),
-        ]
-        + [pltpu.VMEM((coarse, 8 * LANES), bf16), pltpu.VMEM((4 * FINE, 8 * LANES), bf16)] * 2,
+            pltpu.SemaphoreType.DMA((2, groups)),
+        ],
         compiler_params=params(24),
-        name="slot_sums_and_members",
-    )(*observed, in_hbm(vertical_local), control, pert)
-    slots, packed = lax.optimization_barrier((slots, packed))
+        cost_estimate=pl.CostEstimate(flops=1 << 31, bytes_accessed=1 << 24, transcendentals=0),
+        name="members_forward",
+    )(in_hbm(vertical_local), control, pert)
     slots = lax.all_to_all(slots, ("ens", "cols"), split_axis=0, concat_axis=0, tiled=True)
     second, first = exchanged(packed, (1, 0))
     sums = [parts[0]] + [
@@ -552,6 +560,7 @@
         name="diffuse_forward",
     )(second, first, packed, other)
 
+    increment, coefs, slots = lax.optimization_barrier((increment, coefs, slots))
     slot_sums, static_here, control_here, pert_here = pl.pallas_call(
         functools.partial(scatter_kernel, cap_rows),
         in_specs=[VMEM] * 3 + [pl.BlockSpec(memory_space=pl.ANY)] * 3,
@@ -573,10 +582,7 @@
     tile = tile * slot_sums[0] - slot_sums[1]
     tile_first, tile_second = exchanged(tile, (0, 1))
     adjoints = [tile] + from_peers(tile)
-    tile_first, tile_second, vertical_local, vertical_root = lax.optimization_barrier(
-        (tile_first, tile_second, vertical_local, vertical_root)
-    )
-    tile_other = swapped(tile, tile_first, tile_second)
+    tile, vertical_local, vertical_root = lax.optimization_barrier((tile, vertical_local, vertical_root))
     from_local, from_root = pl.pallas_call(
         functools.partial(matrices_kernel, member_scale),
         grid=(1,),
@@ -586,7 +592,10 @@
         compiler_params=params(8),
         name="level_matrices",
     )(in_hbm(vertical_local), in_hbm(vertical_root))
-    coefs, from_local, from_root = lax.optimization_barrier((coefs, from_local, from_root))
+    tile_first, tile_second, from_local, from_root = lax.optimization_barrier(
+        (tile_first, tile_second, from_local, from_root)
+    )
+    tile_other = swapped(tile, tile_first, tile_second)
 
     smooth = pl.pallas_call(
         functools.partial(second_diffusion_kernel, rows),

time: 59.8 us -> 59.3 us (level)
  the two profiles are of different devices: /device:TPU:0 before, /device:TPU:17 now
where the time goes in v12:
time: 59.3 us; the launch traced here: 59 us
  Pallas kernels  28.6 us (48%)
  starting transfers between devices  24.1 us (41%)
  waiting for transfers between devices  5.27 us (9%)
  between operations  0.83 us (1%)
    all_to_all x1, starting transfers between devices, local(): lax.all_to_all(slots, ('ens', 'cols'), split_axis=0, concat_axis=0, tiled...  6.97 us
    pallas_call x1, Pallas kernels, local(): pl.pallas_call(functools.partial(forward_kernel, member_scale), grid=(1,)...  6.59 us
    pallas_call x1, Pallas kernels, local(): pl.pallas_call(member_kernel, grid=(members // group,), in_specs=[VMEM] *...  5.65 us
    ppermute x6, starting transfers between devices, from_peers(): lax.ppermute(x, 'ens', [(peer(i, d, count), i) for i in range(count)])  5.58 us
    ppermute x4, starting transfers between devices, exchanged(): out.append(lax.ppermute(x, 'cols', pairs))  5.49 us
    pallas_call x1, Pallas kernels, local(): pl.pallas_call(functools.partial(slots_kernel, n_cols, cap_rows), grid=(1...  5.1 us
    pallas_call x1, Pallas kernels, local(): pl.pallas_call(functools.partial(scatter_kernel, cap_rows), in_specs=[VME...  4 us
    ppermute x2, starting transfers between devices, swapped(): lax.ppermute(pack, 'cols', [(i, i ^ 1) for i in range(lax.axis_size('cols...  3.34 us
  transfers between devices with their start and end apart: 16, of which 3 were waited for; matrix products, arithmetic and copies ran while one was open for 0% of the time, Pallas kernels for 34%

profile of v12, /device:TPU:17, one launch (start us, length us, event | category | flops | bytes accessed | tf_op | source)
XLA Modules:
  0.0 59.0 jit_solution(12334600252909384430)
XLA Ops:
  0.6 2.0 %prepare.1 = (f32[6,64,128]{2,1,0:T(8,128)S(1)}, s32[64,128]{1,0:T(8,128)S(1)}, s32[64,128]{1,0:T(8,128)S(1)}, s32[128,128]{1,0:T(8,128)S(1)}, f32[128,128]{1,0:T(8,128)S(1)}, /*index=5*/f32[128,128]{1,0:T(8,128)S(1)}) custom-call(f32[16,16]{1,0:T(8,128)} %root_ref, s32[8]{0:T(128)} %refs_1_.1, f32[16,64,128]{2,1,0:T(8,128)} %bitcast.49, ...), custom_call_target="tpu_custom_call" | custom-call | tf_op jit(solution)/shard_map/prepare/pallas_call | solution.py:470
  2.7 5.1 %slot_sums.1 = f32[32,2,8,128]{3,2,1,0:T(8,128)} custom-call(s32[128,128]{1,0:T(8,128)S(1)} %get-tuple-element.35.slot_ref, f32[128,128]{1,0:T(8,128)S(1)} %get-tuple-element.36.weight_ref, f32[128,128]{1,0:T(8,128)S(1)} %get-tuple-element.37.innov_ref), custom_call_target="tpu_custom_call" | custom-call | tf_op jit(solution)/shard_map/slot_sums/pallas_call | solution.py:509
  7.8 2.1 %collective-permute-start.3 = (f32[6,64,128]{2,1,0:T(8,128)S(1)}, f32[6,64,128]{2,1,0:T(8,128)S(1)}, u32[]{:S(2)}, u32[]{:S(2)}) collective-permute-start(f32[6,64,128]{2,1,0:T(8,128)S(1)} %get-tuple-element.44.own_ref), channel_id=1, source_target_pairs={{0,0},{1,1},{2,4},{3,5},{4,2},{5,3},{6,6},{7,7},{8,8},{9,9},{10,12... | collective-permute-start | bytes 589832 | tf_op jit(solution)/shard_map/ppermute | solution.py:420
  9.8 0.1 collective-permute-start.4
  9.9 7.0 %all-to-all-start = ((f32[32,2,8,128]{3,2,1,0:T(8,128)}), f32[32,2,8,128]{3,2,1,0:T(8,128)S(1)}, u32[]{:S(2)}, u32[]{:S(2)}) async-start(f32[32,2,8,128]{3,2,1,0:T(8,128)} %slot_sums.1), calls=%async_computation | async-start | bytes 524288 | tf_op jit(solution)/shard_map/all_to_all | solution.py:542
  16.9 0.0 collective-permute-done.3.second_ref
  17.0 0.4 collective-permute-start.5
  17.4 6.6 %members_forward.1 = (f32[4,64,128]{2,1,0:T(8,128)S(1)}, f32[4,64,128]{2,1,0:T(8,128)S(1)}, f32[4,64,128]{2,1,0:T(8,128)S(1)}, f32[4,64,128]{2,1,0:T(8,128)S(1)}) custom-call(f32[16,16]{1,0:T(8,128)} %local_ref.1, f32[8,16,64,128]{3,2,1,0:T(8,128)} %bitcast.59, bf16[8,16,64,128]{3,2,1,0:T(8,128)(2,1)} %bitcast.61), custom_call_target="tpu_custom_call" | custom-call | flops 2147483648 | bytes 16777216 | tf_op jit(solution)/shard_map/members_forward/pallas_call | solution.py:525
  24.0 1.2 %collective-permute-start.2 = (f32[4,64,128]{2,1,0:T(8,128)S(1)}, f32[4,64,128]{2,1,0:T(8,128)S(1)}, u32[]{:S(2)}, u32[]{:S(2)}) collective-permute-start(f32[4,64,128]{2,1,0:T(8,128)S(1)} %get-tuple-element.43), channel_id=1, source_target_pairs={{8,0},{0,8},{24,16},{16,24},{9,1},{1,9},{25,17},{17,25},{10,2},{2,... | collective-permute-start | bytes 393224 | tf_op jit(solution)/shard_map/ppermute | solution.py:545
  25.3 1.2 %collective-permute-start.1 = (f32[4,64,128]{2,1,0:T(8,128)S(1)}, f32[4,64,128]{2,1,0:T(8,128)S(1)}, u32[]{:S(2)}, u32[]{:S(2)}) collective-permute-start(f32[4,64,128]{2,1,0:T(8,128)S(1)} %get-tuple-element.42), channel_id=1, source_target_pairs={{16,0},{24,8},{0,16},{8,24},{17,1},{25,9},{1,17},{9,25},{18,2},{26... | collective-permute-start | bytes 393224 | tf_op jit(solution)/shard_map/ppermute | solution.py:545
  26.5 0.3 collective-permute-start
  26.7 0.0 collective-permute-done.5.other_ref
  26.7 1.5 %diffuse_forward.1 = (f32[4,64,128]{2,1,0:T(8,128)S(1)}, f32[3,10,32,128]{3,2,1,0:T(8,128)S(1)}) custom-call(f32[6,64,128]{2,1,0:T(8,128)S(1)} %collective-permute-done.3.second_ref, f32[6,64,128]{2,1,0:T(8,128)S(1)} %collective-permute-done.4.first_ref, f32[6,64,128]{2,1,0:T(8,128)S(1)} %get-tuple-element.44.own_ref, ...), custom_call_target="tpu_custom_call" | custom-call | flops 67108864 | bytes 4194304 | tf_op jit(solution)/shard_map/diffuse_forward/pallas_call | solution.py:550
  28.2 4.0 %scatter.1 = (f32[2,256,128]{2,1,0:T(8,128)S(1)}, f32[16,64,128]{2,1,0:T(8,128)S(1)}, f32[8,16,64,128]{3,2,1,0:T(8,128)S(1)}, bf16[8,16,64,128]{3,2,1,0:T(8,128)(2,1)S(1)}) custom-call(s32[64,128]{1,0:T(8,128)S(1)} %get-tuple-element.49.row_ref, s32[64,128]{1,0:T(8,128)S(1)} %get-tuple-element.50.lane_ref, f32[32,2,8,128]{3,2,1,0:T(8,128)S(1)} %all-to-all-done.slots_ref, ...), custom_call_target="tpu_custom_call" | custom-call | flops 2147483648 | bytes 8388608 | tf_op jit(solution)/shard_map/scatter/pallas_call | solution.py:564
  32.3 0.0 collective-permute-done.1
  32.3 0.3 collective-permute-done
  32.6 1.3 %collective-permute-start.6 = (f32[4,64,128]{2,1,0:T(8,128)S(1)}, f32[4,64,128]{2,1,0:T(8,128)S(1)}, u32[]{:S(2)}, u32[]{:S(2)}) collective-permute-start(f32[4,64,128]{2,1,0:T(8,128)S(1)} %multiply_subtract_fusion.own_ref.refs_0_), channel_id=1, source_target_pairs={{0,2},{1,3},{2,0},{3,1},{4,6},{5,7},{6,4},{7,5},{8,10},{9,11},{10,... | collective-permute-start | bytes 393224 | tf_op jit(solution)/shard_map/ppermute | solution.py:420
  33.9 2.0 %collective-permute-start.7 = (f32[4,64,128]{2,1,0:T(8,128)S(1)}, f32[4,64,128]{2,1,0:T(8,128)S(1)}, u32[]{:S(2)}, u32[]{:S(2)}) collective-permute-start(f32[4,64,128]{2,1,0:T(8,128)S(1)} %multiply_subtract_fusion.own_ref.refs_0_), channel_id=1, source_target_pairs={{0,0},{1,1},{2,4},{3,5},{4,2},{5,3},{6,6},{7,7},{8,8},{9,9},{10,12... | collective-permute-start | bytes 393224 | tf_op jit(solution)/shard_map/ppermute | solution.py:420
  36.0 1.3 %level_matrices.1 = (bf16[256,768]{1,0:T(8,128)(2,1)S(1)}, bf16[256,768]{1,0:T(8,128)(2,1)S(1)}) custom-call(f32[16,16]{1,0:T(8,128)} %local_ref.1, f32[16,16]{1,0:T(8,128)} %root_ref), custom_call_target="tpu_custom_call" | custom-call | tf_op jit(solution)/shard_map/level_matrices/pallas_call | solution.py:586
  37.3 0.0 collective-permute-done.6.first_ref
  37.3 2.4 %collective-permute-done.7.second_ref = f32[4,64,128]{2,1,0:T(8,128)S(1)} collective-permute-done((f32[4,64,128]{2,1,0:T(8,128)S(1)}, f32[4,64,128]{2,1,0:T(8,128)S(1)}, u32[]{:S(2)}, u32[]{:S(2)}) %collective-permute-start.7) | collective-permute-done | bytes 131104 | tf_op jit(solution)/shard_map/ppermute | solution.py:420
  39.7 2.9 %collective-permute-start.8 = (f32[2,4,64,128]{3,2,1,0:T(8,128)S(1)}, f32[2,4,64,128]{3,2,1,0:T(8,128)S(1)}, u32[]{:S(2)}, u32[]{:S(2)}) collective-permute-start(f32[2,4,64,128]{3,2,1,0:T(8,128)S(1)} %pad_maximum_fusion.1), channel_id=1, source_target_pairs={{0,1},{1,0},{2,3},{3,2},{4,5},{5,4},{6,7},{7,6},{8,9},{9,8},{10,11... | collective-permute-start | bytes 786440 | tf_op jit(solution)/shard_map/ppermute | solution.py:432
  42.6 1.4 %collective-permute-start.12 = (f32[4,64,128]{2,1,0:T(8,128)S(1)}, f32[4,64,128]{2,1,0:T(8,128)S(1)}, u32[]{:S(2)}, u32[]{:S(2)}) collective-permute-start(f32[4,64,128]{2,1,0:T(8,128)S(1)} %multiply_subtract_fusion.own_ref.refs_0_), channel_id=1, source_target_pairs={{24,0},{16,8},{8,16},{0,24},{25,1},{17,9},{9,17},{1,25},{26,2},{18... | collective-permute-start | bytes 393224 | tf_op jit(solution)/shard_map/ppermute | solution.py:426
  44.0 0.7 %collective-permute-start.13 = (f32[4,64,128]{2,1,0:T(8,128)S(1)}, f32[4,64,128]{2,1,0:T(8,128)S(1)}, u32[]{:S(2)}, u32[]{:S(2)}) collective-permute-start(f32[4,64,128]{2,1,0:T(8,128)S(1)} %multiply_subtract_fusion.own_ref.refs_0_), channel_id=1, source_target_pairs={{16,0},{24,8},{0,16},{8,24},{17,1},{25,9},{1,17},{9,25},{18,2},{26... | collective-permute-start | bytes 393224 | tf_op jit(solution)/shard_map/ppermute | solution.py:426
  44.7 0.5 collective-permute-start.14
  45.3 1.3 %diffuse_adjoint.1.refs_0_ = f32[4,64,128]{2,1,0:T(8,128)S(1)} custom-call(f32[3,10,32,128]{3,2,1,0:T(8,128)S(1)} %get-tuple-element.59.coef_ref, f32[4,64,128]{2,1,0:T(8,128)S(1)} %collective-permute-done.7.second_ref, f32[4,64,128]{2,1,0:T(8,128)S(1)} %collective-permute-done.6.first_ref, f32[4,64,128]{2,1,0:T(8,128)S(1)} %multiply_subtract_fusion.own_ref.refs_0_, ...), custom_call_target="tpu_custom_call" | custom-call | tf_op jit(solution)/shard_map/diffuse_adjoint/pallas_call | solution.py:600
  46.6 1.5 %collective-permute-start.9 = (f32[4,64,128]{2,1,0:T(8,128)S(1)}, f32[4,64,128]{2,1,0:T(8,128)S(1)}, u32[]{:S(2)}, u32[]{:S(2)}) collective-permute-start(f32[4,64,128]{2,1,0:T(8,128)S(1)} %diffuse_adjoint.1.refs_0_), channel_id=1, source_target_pairs={{24,0},{16,8},{8,16},{0,24},{25,1},{17,9},{9,17},{1,25},{26,2},{18... | collective-permute-start | bytes 393224 | tf_op jit(solution)/shard_map/ppermute | solution.py:426
  48.1 0.7 %collective-permute-start.10 = (f32[4,64,128]{2,1,0:T(8,128)S(1)}, f32[4,64,128]{2,1,0:T(8,128)S(1)}, u32[]{:S(2)}, u32[]{:S(2)}) collective-permute-start(f32[4,64,128]{2,1,0:T(8,128)S(1)} %diffuse_adjoint.1.refs_0_), channel_id=1, source_target_pairs={{16,0},{24,8},{0,16},{8,24},{17,1},{25,9},{1,17},{9,25},{18,2},{26... | collective-permute-start | bytes 393224 | tf_op jit(solution)/shard_map/ppermute | solution.py:426
  48.8 0.8 %collective-permute-start.11 = (f32[4,64,128]{2,1,0:T(8,128)S(1)}, f32[4,64,128]{2,1,0:T(8,128)S(1)}, u32[]{:S(2)}, u32[]{:S(2)}) collective-permute-start(f32[4,64,128]{2,1,0:T(8,128)S(1)} %diffuse_adjoint.1.refs_0_), channel_id=1, source_target_pairs={{8,0},{0,8},{24,16},{16,24},{9,1},{1,9},{25,17},{17,25},{10,2},{2,... | collective-permute-start | bytes 393224 | tf_op jit(solution)/shard_map/ppermute | solution.py:426
  49.5 2.6 %collective-permute-done.13.refs_2_ = f32[4,64,128]{2,1,0:T(8,128)S(1)} collective-permute-done((f32[4,64,128]{2,1,0:T(8,128)S(1)}, f32[4,64,128]{2,1,0:T(8,128)S(1)}, u32[]{:S(2)}, u32[]{:S(2)}) %collective-permute-start.13) | collective-permute-done | bytes 131104 | tf_op jit(solution)/shard_map/ppermute | solution.py:426
  52.1 5.6 %members_gradient.1 = f32[8,16,64,128]{3,2,1,0:T(8,128)} custom-call(bf16[256,768]{1,0:T(8,128)(2,1)S(1)} %get-tuple-element.65.matrix_ref, f32[8,16,64,128]{3,2,1,0:T(8,128)S(1)} %get-tuple-element.66.control_ref, bf16[8,16,64,128]{3,2,1,0:T(8,128)(2,1)S(1)} %get-tuple-element.67.pert_ref, f32[4,64,128]{2,1,0:T(8,128)S(1)} %multiply_subtract_fusion.own_ref.refs_0_, ...), custom_call_target="tpu_custom_call" | custom-call | tf_op jit(solution)/shard_map/members_gradient/pallas_call | solution.py:612
  57.8 1.2 %static_gradient.1 = f32[16,64,128]{2,1,0:T(8,128)} custom-call(bf16[256,768]{1,0:T(8,128)(2,1)S(1)} %get-tuple-element.57.matrix_ref, f32[16,64,128]{2,1,0:T(8,128)S(1)} %get-tuple-element.58.static_ref, f32[4,64,128]{2,1,0:T(8,128)S(1)} %diffuse_adjoint.1.refs_0_, f32[4,64,128]{2,1,0:T(8,128)S(1)} %collective-permute-done.9.refs_1_, ...), custom_call_target="tpu_custom_call" | custom-call | tf_op jit(solution)/shard_map/static_gradient/pallas_call | solution.py:623
  (15 shorter events, 0.2 us)
Async XLA Ops:
  7.8 9.2 %collective-permute-start.3 = (f32[6,64,128]{2,1,0:T(8,128)S(1)}, f32[6,64,128]{2,1,0:T(8,128)S(1)}, u32[]{:S(2)}, u32[]{:S(2)}) collective-permute-start(f32[6,64,128]{2,1,0:T(8,128)S(1)} %get-tuple-element.44.own_ref), channel_id=1, source_target_pairs={{0,0},{1,1},{2,4},{3,5},{4,2},{5,3},{6,6},{7,7},{8,8},{9,9},{10,12... | collective-permute-start | bytes 589832 | tf_op jit(solution)/shard_map/ppermute | solution.py:420
  9.8 7.1 %collective-permute-start.4 = (f32[6,64,128]{2,1,0:T(8,128)S(1)}, f32[6,64,128]{2,1,0:T(8,128)S(1)}, u32[]{:S(2)}, u32[]{:S(2)}) collective-permute-start(f32[6,64,128]{2,1,0:T(8,128)S(1)} %get-tuple-element.44.own_ref), channel_id=1, source_target_pairs={{0,2},{1,3},{2,0},{3,1},{4,6},{5,7},{6,4},{7,5},{8,10},{9,11},{10,... | collective-permute-start | bytes 589832 | tf_op jit(solution)/shard_map/ppermute | solution.py:420
  9.9 18.3 %all-to-all-start = ((f32[32,2,8,128]{3,2,1,0:T(8,128)}), f32[32,2,8,128]{3,2,1,0:T(8,128)S(1)}, u32[]{:S(2)}, u32[]{:S(2)}) async-start(f32[32,2,8,128]{3,2,1,0:T(8,128)} %slot_sums.1), calls=%async_computation | async-start | bytes 524288 | tf_op jit(solution)/shard_map/all_to_all | solution.py:542
  17.0 9.7 %collective-permute-start.5 = (f32[2,6,64,128]{3,2,1,0:T(8,128)S(1)}, f32[2,6,64,128]{3,2,1,0:T(8,128)S(1)}, u32[]{:S(2)}, u32[]{:S(2)}) collective-permute-start(f32[2,6,64,128]{3,2,1,0:T(8,128)S(1)} %pad_maximum_fusion), channel_id=1, source_target_pairs={{0,1},{1,0},{2,3},{3,2},{4,5},{5,4},{6,7},{7,6},{8,9},{9,8},{10,11... | collective-permute-start | bytes 1179656 | tf_op jit(solution)/shard_map/ppermute | solution.py:432
  24.0 8.2 %collective-permute-start.2 = (f32[4,64,128]{2,1,0:T(8,128)S(1)}, f32[4,64,128]{2,1,0:T(8,128)S(1)}, u32[]{:S(2)}, u32[]{:S(2)}) collective-permute-start(f32[4,64,128]{2,1,0:T(8,128)S(1)} %get-tuple-element.43), channel_id=1, source_target_pairs={{8,0},{0,8},{24,16},{16,24},{9,1},{1,9},{25,17},{17,25},{10,2},{2,... | collective-permute-start | bytes 393224 | tf_op jit(solution)/shard_map/ppermute | solution.py:545
  25.3 7.0 %collective-permute-start.1 = (f32[4,64,128]{2,1,0:T(8,128)S(1)}, f32[4,64,128]{2,1,0:T(8,128)S(1)}, u32[]{:S(2)}, u32[]{:S(2)}) collective-permute-start(f32[4,64,128]{2,1,0:T(8,128)S(1)} %get-tuple-element.42), channel_id=1, source_target_pairs={{16,0},{24,8},{0,16},{8,24},{17,1},{25,9},{1,17},{9,25},{18,2},{26... | collective-permute-start | bytes 393224 | tf_op jit(solution)/shard_map/ppermute | solution.py:545
  26.5 6.1 %collective-permute-start = (f32[4,64,128]{2,1,0:T(8,128)S(1)}, f32[4,64,128]{2,1,0:T(8,128)S(1)}, u32[]{:S(2)}, u32[]{:S(2)}) collective-permute-start(f32[4,64,128]{2,1,0:T(8,128)S(1)} %get-tuple-element.41), channel_id=1, source_target_pairs={{24,0},{16,8},{8,16},{0,24},{25,1},{17,9},{9,17},{1,25},{26,2},{18... | collective-permute-start | bytes 393224 | tf_op jit(solution)/shard_map/ppermute | solution.py:545
  32.6 4.6 %collective-permute-start.6 = (f32[4,64,128]{2,1,0:T(8,128)S(1)}, f32[4,64,128]{2,1,0:T(8,128)S(1)}, u32[]{:S(2)}, u32[]{:S(2)}) collective-permute-start(f32[4,64,128]{2,1,0:T(8,128)S(1)} %multiply_subtract_fusion.own_ref.refs_0_), channel_id=1, source_target_pairs={{0,2},{1,3},{2,0},{3,1},{4,6},{5,7},{6,4},{7,5},{8,10},{9,11},{10,... | collective-permute-start | bytes 393224 | tf_op jit(solution)/shard_map/ppermute | solution.py:420
  33.9 5.7 %collective-permute-start.7 = (f32[4,64,128]{2,1,0:T(8,128)S(1)}, f32[4,64,128]{2,1,0:T(8,128)S(1)}, u32[]{:S(2)}, u32[]{:S(2)}) collective-permute-start(f32[4,64,128]{2,1,0:T(8,128)S(1)} %multiply_subtract_fusion.own_ref.refs_0_), channel_id=1, source_target_pairs={{0,0},{1,1},{2,4},{3,5},{4,2},{5,3},{6,6},{7,7},{8,8},{9,9},{10,12... | collective-permute-start | bytes 393224 | tf_op jit(solution)/shard_map/ppermute | solution.py:420
  39.7 5.6 %collective-permute-start.8 = (f32[2,4,64,128]{3,2,1,0:T(8,128)S(1)}, f32[2,4,64,128]{3,2,1,0:T(8,128)S(1)}, u32[]{:S(2)}, u32[]{:S(2)}) collective-permute-start(f32[2,4,64,128]{3,2,1,0:T(8,128)S(1)} %pad_maximum_fusion.1), channel_id=1, source_target_pairs={{0,1},{1,0},{2,3},{3,2},{4,5},{5,4},{6,7},{7,6},{8,9},{9,8},{10,11... | collective-permute-start | bytes 786440 | tf_op jit(solution)/shard_map/ppermute | solution.py:432
  42.6 6.2 %collective-permute-start.12 = (f32[4,64,128]{2,1,0:T(8,128)S(1)}, f32[4,64,128]{2,1,0:T(8,128)S(1)}, u32[]{:S(2)}, u32[]{:S(2)}) collective-permute-start(f32[4,64,128]{2,1,0:T(8,128)S(1)} %multiply_subtract_fusion.own_ref.refs_0_), channel_id=1, source_target_pairs={{24,0},{16,8},{8,16},{0,24},{25,1},{17,9},{9,17},{1,25},{26,2},{18... | collective-permute-start | bytes 393224 | tf_op jit(solution)/shard_map/ppermute | solution.py:426
  44.0 8.1 %collective-permute-start.13 = (f32[4,64,128]{2,1,0:T(8,128)S(1)}, f32[4,64,128]{2,1,0:T(8,128)S(1)}, u32[]{:S(2)}, u32[]{:S(2)}) collective-permute-start(f32[4,64,128]{2,1,0:T(8,128)S(1)} %multiply_subtract_fusion.own_ref.refs_0_), channel_id=1, source_target_pairs={{16,0},{24,8},{0,16},{8,24},{17,1},{25,9},{1,17},{9,25},{18,2},{26... | collective-permute-start | bytes 393224 | tf_op jit(solution)/shard_map/ppermute | solution.py:426
  44.7 7.4 %collective-permute-start.14 = (f32[4,64,128]{2,1,0:T(8,128)S(1)}, f32[4,64,128]{2,1,0:T(8,128)S(1)}, u32[]{:S(2)}, u32[]{:S(2)}) collective-permute-start(f32[4,64,128]{2,1,0:T(8,128)S(1)} %multiply_subtract_fusion.own_ref.refs_0_), channel_id=1, source_target_pairs={{8,0},{0,8},{24,16},{16,24},{9,1},{1,9},{25,17},{17,25},{10,2},{2,... | collective-permute-start | bytes 393224 | tf_op jit(solution)/shard_map/ppermute | solution.py:426
  46.6 11.2 %collective-permute-start.9 = (f32[4,64,128]{2,1,0:T(8,128)S(1)}, f32[4,64,128]{2,1,0:T(8,128)S(1)}, u32[]{:S(2)}, u32[]{:S(2)}) collective-permute-start(f32[4,64,128]{2,1,0:T(8,128)S(1)} %diffuse_adjoint.1.refs_0_), channel_id=1, source_target_pairs={{24,0},{16,8},{8,16},{0,24},{25,1},{17,9},{9,17},{1,25},{26,2},{18... | collective-permute-start | bytes 393224 | tf_op jit(solution)/shard_map/ppermute | solution.py:426
  48.1 9.7 %collective-permute-start.10 = (f32[4,64,128]{2,1,0:T(8,128)S(1)}, f32[4,64,128]{2,1,0:T(8,128)S(1)}, u32[]{:S(2)}, u32[]{:S(2)}) collective-permute-start(f32[4,64,128]{2,1,0:T(8,128)S(1)} %diffuse_adjoint.1.refs_0_), channel_id=1, source_target_pairs={{16,0},{24,8},{0,16},{8,24},{17,1},{25,9},{1,17},{9,25},{18,2},{26... | collective-permute-start | bytes 393224 | tf_op jit(solution)/shard_map/ppermute | solution.py:426
  48.8 9.0 %collective-permute-start.11 = (f32[4,64,128]{2,1,0:T(8,128)S(1)}, f32[4,64,128]{2,1,0:T(8,128)S(1)}, u32[]{:S(2)}, u32[]{:S(2)}) collective-permute-start(f32[4,64,128]{2,1,0:T(8,128)S(1)} %diffuse_adjoint.1.refs_0_), channel_id=1, source_target_pairs={{8,0},{0,8},{24,16},{16,24},{9,1},{1,9},{25,17},{17,25},{10,2},{2,... | collective-permute-start | bytes 393224 | tf_op jit(solution)/shard_map/ppermute | solution.py:426

commit v13 on v11

--- a/solution.py
+++ b/solution.py
@@ -92,15 +92,8 @@
     return count - d if count & (count - 1) else d
 
 
-def prepare_kernel(lev_share, rows, *refs):
-    (root_ref, count_ref, static_ref, north_ref, east_ref, index_ref), sources = refs[:6], refs[6:9]
-    (out_ref, row_ref, lane_ref), landed, sems = refs[9:12], refs[12:15], refs[15]
-    obs_rows = landed[0].shape[0]
-    here = pl.ds(pl.multiple_of(lax.axis_index("ens") * obs_rows, obs_rows), obs_rows)
-    copies = [pltpu.make_async_copy(s.at[here, :], t, sems.at[i]) for i, (s, t) in enumerate(zip(sources, landed))]
-    for copy in copies:
-        copy.start()
-    levels, per_level, _ = static_ref.shape
+def prepare_kernel(lev_share, root_ref, static_ref, north_ref, east_ref, out_ref):
+    levels = static_ref.shape[0]
     first = lax.axis_index("ens") * lev_share
     for j in range(lev_share):
         total = root_ref[first + j, 0] * static_ref[0]
@@ -109,22 +102,22 @@
         out_ref[j] = total
     out_ref[lev_share] = north_ref[...]
     out_ref[lev_share + 1] = east_ref[...]
+
+
+def list_cells(rows, lon, index_ref, count_ref, row_ref, lane_ref):
     lists, capacity = index_ref.shape
-    lon = per_level // rows * LANES
     pieces = capacity // LANES
     slot = lax.broadcasted_iota(jnp.int32, (1, capacity), 1)
     for q in range(lists):
-        cell = index_ref[q : q + 1, :]
-        rest, lane = over(cell, LANES)
+        rest, lane = over(index_ref[q : q + 1, :], LANES)
         rest, block = over(rest, lon // LANES)
         level, row = over(rest, rows)
-        grid_row = jnp.where(slot < count_ref[q], level * per_level + block * rows + row, -1)
+        grid_row = (level * (lon // LANES) + block) * rows + row
+        grid_row = jnp.where(slot < count_ref[q], grid_row, -1)
         for c in range(pieces):
             at = q * pieces + c
             row_ref[at : at + 1, :] = grid_row[:, c * LANES : (c + 1) * LANES]
             lane_ref[at : at + 1, :] = lane[:, c * LANES : (c + 1) * LANES]
-    for copy in copies:
-        copy.wait()
 
 
 def level_product(matrix, transpose):
@@ -151,24 +144,30 @@
     return jnp.concatenate([high, low, high], axis=0)
 
 
-def observe_kernel(n_cols, cap_rows, scale, *refs):
-    n_ens = len(refs) - 19
-    (slot_ref, weight_ref, innov_ref), sources, out_ref, parts = refs[:3], refs[3:6], refs[6], refs[7 : 7 + n_ens]
-    refs = refs[7 + n_ens :]
+def observe_kernel(n_cols, cap_rows, rows, lon, scale, *refs):
+    n_ens = len(refs) - 28
+    sources, (out_ref, row_ref, lane_ref), parts = refs[:8], refs[8:11], refs[11 : 11 + n_ens]
+    refs = refs[11 + n_ens :]
     (acc_ref, fold_ref, matrix_ref, part_ref), landed, sems, slots = (
         refs[:4],
-        refs[4:7],
-        refs[7],
-        (refs[8:10], refs[10:12]),
+        refs[4:12],
+        refs[12],
+        (refs[13:15], refs[15:17]),
     )
+    slot_ref, weight_ref, innov_ref, index_ref, count_ref, local_ref, control_ref, pert_ref = landed
     coarse = acc_ref.shape[1]
     obs_rows = slot_ref.shape[0]
     group = min(8, obs_rows)
-    copies = [pltpu.make_async_copy(s, t, sems.at[i]) for i, (s, t) in enumerate(zip(sources, landed))]
+    here = pl.ds(pl.multiple_of(lax.axis_index("ens") * obs_rows, obs_rows), obs_rows)
+    copies = [
+        pltpu.make_async_copy(s.at[here, :] if i < 3 else s, t, sems.at[i])
+        for i, (s, t) in enumerate(zip(sources, landed))
+    ]
     for copy in copies:
         copy.start()
     acc_ref[...] = jnp.zeros_like(acc_ref)
-    local_ref, control_ref, pert_ref = landed
+    for copy in copies[:3]:
+        copy.wait()
 
     def build(i, to):
         at = pl.ds(pl.multiple_of(i * group, group), group)
@@ -206,8 +205,9 @@
         for p in range(n_cols):
             out_ref[e * n_cols + p, 0] = weights[p * cap_rows : (p + 1) * cap_rows]
             out_ref[e * n_cols + p, 1] = amounts[p * cap_rows : (p + 1) * cap_rows]
-    for copy in copies:
+    for copy in copies[3:]:
         copy.wait()
+    list_cells(rows, lon, index_ref, count_ref, row_ref, lane_ref)
     matrix_ref[...] = level_product(local_ref[...] * f32(scale), False)
     sum_members(matrix_ref, control_ref, pert_ref, part_ref)
     share = part_ref.shape[0] // n_ens
@@ -468,52 +468,17 @@
 
     obs_rows = obs_slot.shape[0] // LANES
     share_rows = obs_rows // n_ens
-    packed, entry_row, entry_lane, *observed = pl.pallas_call(
-        functools.partial(prepare_kernel, lev_share, rows),
+    coarse = n_cols * capacity // FINE
+    size = levels * 16
+    slots, entry_row, entry_lane, *parts = pl.pallas_call(
+        functools.partial(observe_kernel, n_cols, cap_rows, rows, lon, member_scale),
         grid=(1,),
-        in_specs=[
-            SMEM,
-            SMEM,
-            whole(levels, per_level, LANES),
-            whole(per_level, LANES),
-            whole(per_level, LANES),
-            whole(lists, capacity),
-            pl.BlockSpec(memory_space=pl.ANY),
-            pl.BlockSpec(memory_space=pl.ANY),
-            pl.BlockSpec(memory_space=pl.ANY),
-        ],
-        out_specs=[VMEM] * 6,
+        in_specs=[pl.BlockSpec(memory_space=pl.ANY)] * 8,
+        out_specs=[whole(n_ens * n_cols, 2, cap_rows, LANES)] + [VMEM] * (2 + n_ens),
         out_shape=[
-            pltpu.VMEM((lev_share + 2, per_level, LANES), f32),
+            pltpu.HBM((n_ens * n_cols, 2, cap_rows, LANES), f32),
             pltpu.VMEM((entry_rows, LANES), jnp.int32),
             pltpu.VMEM((entry_rows, LANES), jnp.int32),
-            pltpu.VMEM((share_rows, LANES), jnp.int32),
-            pltpu.VMEM((share_rows, LANES), f32),
-            pltpu.VMEM((share_rows, LANES), f32),
-        ],
-        scratch_shapes=[pltpu.SemaphoreType.DMA((3,))],
-        compiler_params=params(8),
-        name="prepare",
-    )(
-        in_hbm(vertical_root),
-        in_hbm(send_count),
-        static,
-        in_hbm(tiled(face_north)),
-        in_hbm(tiled(face_east)),
-        in_hbm(send_index),
-        in_hbm(obs_slot.reshape(obs_rows, LANES)),
-        in_hbm(obs_weight.reshape(obs_rows, LANES)),
-        in_hbm(innovation.reshape(obs_rows, LANES)),
-    )
-    coarse = n_cols * capacity // FINE
-    size = levels * 16
-    slots, *parts = pl.pallas_call(
-        functools.partial(observe_kernel, n_cols, cap_rows, member_scale),
-        grid=(1,),
-        in_specs=[VMEM] * 3 + [pl.BlockSpec(memory_space=pl.ANY)] * 3,
-        out_specs=[whole(n_ens * n_cols, 2, cap_rows, LANES)] + [VMEM] * n_ens,
-        out_shape=[
-            pltpu.HBM((n_ens * n_cols, 2, cap_rows, LANES), f32),
         ]
         + [pltpu.VMEM((lev_share, per_level, LANES), f32)] * n_ens,
         scratch_shapes=[
@@ -521,16 +486,40 @@
             pltpu.VMEM((2, coarse, LANES), f32),
             pltpu.VMEM((size, 3 * size), bf16),
             pltpu.VMEM((levels, per_level, LANES), f32),
+            pltpu.VMEM((share_rows, LANES), jnp.int32),
+            pltpu.VMEM((share_rows, LANES), f32),
+            pltpu.VMEM((share_rows, LANES), f32),
+            pltpu.VMEM((lists, capacity), jnp.int32),
+            pltpu.SMEM((lists,), jnp.int32),
             pltpu.VMEM((levels, levels), f32),
             pltpu.VMEM(control.shape, f32),
             pltpu.VMEM(pert.shape, bf16),
-            pltpu.SemaphoreType.DMA((3,)),
+            pltpu.SemaphoreType.DMA((8,)),
         ]
         + [pltpu.VMEM((coarse, 8 * LANES), bf16), pltpu.VMEM((4 * FINE, 8 * LANES), bf16)] * 2,
         compiler_params=params(24),
         name="slot_sums_and_members",
-    )(*observed, in_hbm(vertical_local), control, pert)
-    slots, packed = lax.optimization_barrier((slots, packed))
+    )(
+        in_hbm(obs_slot.reshape(obs_rows, LANES)),
+        in_hbm(obs_weight.reshape(obs_rows, LANES)),
+        in_hbm(innovation.reshape(obs_rows, LANES)),
+        in_hbm(send_index),
+        in_hbm(send_count),
+        in_hbm(vertical_local),
+        control,
+        pert,
+    )
+    slots, face_north, face_east = lax.optimization_barrier((slots, face_north, face_east))
+    packed = pl.pallas_call(
+        functools.partial(prepare_kernel, lev_share),
+        grid=(1,),
+        in_specs=[SMEM, whole(levels, per_level, LANES), whole(per_level, LANES), whole(per_level, LANES)],
+        out_specs=VMEM,
+        out_shape=pltpu.VMEM((lev_share + 2, per_level, LANES), f32),
+        compiler_params=params(8),
+        cost_estimate=pl.CostEstimate(flops=1 << 31, bytes_accessed=1 << 25, transcendentals=0),
+        name="prepare",
+    )(in_hbm(vertical_root), static, in_hbm(tiled(face_north)), in_hbm(tiled(face_east)))
     slots = lax.all_to_all(slots, ("ens", "cols"), split_axis=0, concat_axis=0, tiled=True)
     second, first = exchanged(packed, (1, 0))
     sums = [parts[0]] + [
@@ -552,6 +541,7 @@
         name="diffuse_forward",
     )(second, first, packed, other)
 
+    increment, coefs, slots = lax.optimization_barrier((increment, coefs, slots))
     slot_sums, static_here, control_here, pert_here = pl.pallas_call(
         functools.partial(scatter_kernel, cap_rows),
         in_specs=[VMEM] * 3 + [pl.BlockSpec(memory_space=pl.ANY)] * 3,
@@ -573,10 +563,7 @@
     tile = tile * slot_sums[0] - slot_sums[1]
     tile_first, tile_second = exchanged(tile, (0, 1))
     adjoints = [tile] + from_peers(tile)
-    tile_first, tile_second, vertical_local, vertical_root = lax.optimization_barrier(
-        (tile_first, tile_second, vertical_local, vertical_root)
-    )
-    tile_other = swapped(tile, tile_first, tile_second)
+    tile, vertical_local, vertical_root = lax.optimization_barrier((tile, vertical_local, vertical_root))
     from_local, from_root = pl.pallas_call(
         functools.partial(matrices_kernel, member_scale),
         grid=(1,),
@@ -586,7 +573,10 @@
         compiler_params=params(8),
         name="level_matrices",
     )(in_hbm(vertical_local), in_hbm(vertical_root))
-    coefs, from_local, from_root = lax.optimization_barrier((coefs, from_local, from_root))
+    tile_first, tile_second, from_local, from_root = lax.optimization_barrier(
+        (tile_first, tile_second, from_local, from_root)
+    )
+    tile_other = swapped(tile, tile_first, tile_second)
 
     smooth = pl.pallas_call(
         functools.partial(second_diffusion_kernel, rows),

time: 59.8 us -> 59.5 us (level)
  waiting for transfers between devices: 11.4 us -> 10.3 us
  Pallas kernels: 24.3 us -> 25.1 us
    all_to_all x1, waiting for transfers between devices: 6.68 us -> 4.19 us  [local(): lax.all_to_all(slots, ('ens', 'cols'), split_axis=0, concat_axis=0, tiled...]
    ppermute x6, waiting for transfers between devices: 0.04 us -> 1.72 us  [from_peers(): lax.ppermute(x, 'ens', [(peer(i, d, count), i) for i in range(count)])]
    pallas_call x2, Pallas kernels: 9.39 us -> 10.2 us  [the longest x1 8.98 us: local(): pl.pallas_call(functools.partial(observe_kernel, n_cols, cap_rows, rows,...]
  transfers between devices with their start and end apart: 16 -> 16, of which waited for: 2 -> 4; matrix products, arithmetic and copies ran while one was open for 0% -> 0% of each run, Pallas kernels for 23% -> 23%
where the time goes in v13:
time: 59.5 us; the launch traced here: 58.6 us
  Pallas kernels  25.1 us (42%)
  starting transfers between devices  22.2 us (37%)
  waiting for transfers between devices  10.3 us (17%)
  between operations  0.84 us (1%)
    pallas_call x1, Pallas kernels, local(): pl.pallas_call(functools.partial(observe_kernel, n_cols, cap_rows, rows,...  8.98 us
    ppermute x4, starting transfers between devices, exchanged(): out.append(lax.ppermute(x, 'cols', pairs))  7.77 us
    ppermute x6, starting transfers between devices, from_peers(): lax.ppermute(x, 'ens', [(peer(i, d, count), i) for i in range(count)])  7.11 us
    pallas_call x1, Pallas kernels, local(): pl.pallas_call(member_kernel, grid=(members // group,), in_specs=[VMEM] *...  5.65 us
    ppermute x4, waiting for transfers between devices, exchanged(): out.append(lax.ppermute(x, 'cols', pairs))  4.36 us
    all_to_all x1, waiting for transfers between devices, local(): lax.all_to_all(slots, ('ens', 'cols'), split_axis=0, concat_axis=0, tiled...  4.19 us
    pallas_call x1, Pallas kernels, local(): pl.pallas_call(functools.partial(scatter_kernel, cap_rows), in_specs=[VME...  4 us
    all_to_all x1, starting transfers between devices, local(): lax.all_to_all(slots, ('ens', 'cols'), split_axis=0, concat_axis=0, tiled...  3.59 us
  transfers between devices with their start and end apart: 16, of which 4 were waited for; matrix products, arithmetic and copies ran while one was open for 0% of the time, Pallas kernels for 23%

profile of v13, /device:TPU:0, one launch (start us, length us, event | category | flops | bytes accessed | tf_op | source)
XLA Modules:
  0.0 58.6 jit_solution(4327187333899204510)
XLA Ops:
  0.6 9.0 %slot_sums_and_members.1 = (f32[32,2,8,128]{3,2,1,0:T(8,128)}, s32[64,128]{1,0:T(8,128)S(1)}, s32[64,128]{1,0:T(8,128)S(1)}, f32[4,64,128]{2,1,0:T(8,128)S(1)}, ...) custom-call(s32[512,128]{1,0:T(8,128)} %bitcast.56, f32[512,128]{1,0:T(8,128)} %bitcast.57, ...), custom_call_target="tpu_custom_call" | custom-call | tf_op jit(solution)/shard_map/slot_sums_and_members/pallas_call | solution.py:473
  9.6 1.2 %prepare.1.own_ref = f32[6,64,128]{2,1,0:T(8,128)S(1)} custom-call(f32[16,16]{1,0:T(8,128)} %root_ref.2, f32[16,64,128]{2,1,0:T(8,128)} %bitcast.59, f32[64,128]{1,0:T(8,128)} %bitcast.61, f32[64,128]{1,0:T(8,128)} %bitcast.62), custom_call_target="tpu_custom_call" | custom-call | flops 2147483648 | bytes 33554432 | tf_op jit(solution)/shard_map/prepare/pallas_call | solution.py:513
  10.9 0.7 %collective-permute-start.3 = (f32[6,64,128]{2,1,0:T(8,128)S(1)}, f32[6,64,128]{2,1,0:T(8,128)S(1)}, u32[]{:S(2)}, u32[]{:S(2)}) collective-permute-start(f32[6,64,128]{2,1,0:T(8,128)S(1)} %prepare.1.own_ref), channel_id=1, source_target_pairs={{0,0},{1,1},{2,4},{3,5},{4,2},{5,3},{6,6},{7,7},{8,8},{9,9},{10,12... | collective-permute-start | bytes 589832 | tf_op jit(solution)/shard_map/ppermute | solution.py:421
  11.5 5.9 %collective-permute-start.4 = (f32[6,64,128]{2,1,0:T(8,128)S(1)}, f32[6,64,128]{2,1,0:T(8,128)S(1)}, u32[]{:S(2)}, u32[]{:S(2)}) collective-permute-start(f32[6,64,128]{2,1,0:T(8,128)S(1)} %prepare.1.own_ref), channel_id=1, source_target_pairs={{0,2},{1,3},{2,0},{3,1},{4,6},{5,7},{6,4},{7,5},{8,10},{9,11},{10,... | collective-permute-start | bytes 589832 | tf_op jit(solution)/shard_map/ppermute | solution.py:421
  17.5 3.6 %all-to-all-start = ((f32[32,2,8,128]{3,2,1,0:T(8,128)}), f32[32,2,8,128]{3,2,1,0:T(8,128)S(1)}, u32[]{:S(2)}, u32[]{:S(2)}) async-start(f32[32,2,8,128]{3,2,1,0:T(8,128)} %get-tuple-element.41), calls=%async_computation | async-start | bytes 524288 | tf_op jit(solution)/shard_map/all_to_all | solution.py:523
  21.1 0.0 collective-permute-done.3.second_ref
  21.1 1.0 %collective-permute-done.4.first_ref = f32[6,64,128]{2,1,0:T(8,128)S(1)} collective-permute-done((f32[6,64,128]{2,1,0:T(8,128)S(1)}, f32[6,64,128]{2,1,0:T(8,128)S(1)}, u32[]{:S(2)}, u32[]{:S(2)}) %collective-permute-start.4) | collective-permute-done | bytes 196640 | tf_op jit(solution)/shard_map/ppermute | solution.py:421
  22.1 0.1 collective-permute-start.5
  22.2 1.6 %collective-permute-start.2 = (f32[4,64,128]{2,1,0:T(8,128)S(1)}, f32[4,64,128]{2,1,0:T(8,128)S(1)}, u32[]{:S(2)}, u32[]{:S(2)}) collective-permute-start(f32[4,64,128]{2,1,0:T(8,128)S(1)} %get-tuple-element.35), channel_id=1, source_target_pairs={{8,0},{0,8},{24,16},{16,24},{9,1},{1,9},{25,17},{17,25},{10,2},{2,... | collective-permute-start | bytes 393224 | tf_op jit(solution)/shard_map/ppermute | solution.py:526
  23.8 1.5 %collective-permute-start.1 = (f32[4,64,128]{2,1,0:T(8,128)S(1)}, f32[4,64,128]{2,1,0:T(8,128)S(1)}, u32[]{:S(2)}, u32[]{:S(2)}) collective-permute-start(f32[4,64,128]{2,1,0:T(8,128)S(1)} %get-tuple-element.34), channel_id=1, source_target_pairs={{16,0},{24,8},{0,16},{8,24},{17,1},{25,9},{1,17},{9,25},{18,2},{26... | collective-permute-start | bytes 393224 | tf_op jit(solution)/shard_map/ppermute | solution.py:526
  25.3 0.5 collective-permute-start
  25.8 0.0 collective-permute-done.5.other_ref
  25.8 1.5 %diffuse_forward.1 = (f32[4,64,128]{2,1,0:T(8,128)S(1)}, f32[3,10,32,128]{3,2,1,0:T(8,128)S(1)}) custom-call(f32[6,64,128]{2,1,0:T(8,128)S(1)} %collective-permute-done.3.second_ref, f32[6,64,128]{2,1,0:T(8,128)S(1)} %collective-permute-done.4.first_ref, f32[6,64,128]{2,1,0:T(8,128)S(1)} %prepare.1.own_ref, ...), custom_call_target="tpu_custom_call" | custom-call | flops 67108864 | bytes 4194304 | tf_op jit(solution)/shard_map/diffuse_forward/pallas_call | solution.py:531
  27.2 4.2 %all-to-all-done.slots_ref = f32[32,2,8,128]{3,2,1,0:T(8,128)S(1)} async-done(((f32[32,2,8,128]{3,2,1,0:T(8,128)}), f32[32,2,8,128]{3,2,1,0:T(8,128)S(1)}, u32[]{:S(2)}, u32[]{:S(2)}) %all-to-all-start) | async-done | bytes 262176 | tf_op jit(solution)/shard_map/all_to_all | solution.py:523
  31.4 4.0 %scatter.1 = (f32[2,256,128]{2,1,0:T(8,128)S(1)}, f32[16,64,128]{2,1,0:T(8,128)S(1)}, f32[8,16,64,128]{3,2,1,0:T(8,128)S(1)}, bf16[8,16,64,128]{3,2,1,0:T(8,128)(2,1)S(1)}) custom-call(s32[64,128]{1,0:T(8,128)S(1)} %get-tuple-element.43.row_ref, s32[64,128]{1,0:T(8,128)S(1)} %get-tuple-element.44.lane_ref, f32[32,2,8,128]{3,2,1,0:T(8,128)S(1)} %all-to-all-done.slots_ref, ...), custom_call_target="tpu_custom_call" | custom-call | flops 2147483648 | bytes 8388608 | tf_op jit(solution)/shard_map/scatter/pallas_call | solution.py:545
  35.5 0.0 collective-permute-done.2
  35.5 0.1 multiply_subtract_fusion.own_ref.refs_0_
  35.6 0.5 collective-permute-start.6
  36.1 0.7 %collective-permute-start.7 = (f32[4,64,128]{2,1,0:T(8,128)S(1)}, f32[4,64,128]{2,1,0:T(8,128)S(1)}, u32[]{:S(2)}, u32[]{:S(2)}) collective-permute-start(f32[4,64,128]{2,1,0:T(8,128)S(1)} %multiply_subtract_fusion.own_ref.refs_0_), channel_id=1, source_target_pairs={{0,0},{1,1},{2,4},{3,5},{4,2},{5,3},{6,6},{7,7},{8,8},{9,9},{10,12... | collective-permute-start | bytes 393224 | tf_op jit(solution)/shard_map/ppermute | solution.py:421
  36.8 1.2 %level_matrices.1 = (bf16[256,768]{1,0:T(8,128)(2,1)S(1)}, bf16[256,768]{1,0:T(8,128)(2,1)S(1)}) custom-call(f32[16,16]{1,0:T(8,128)} %local_ref, f32[16,16]{1,0:T(8,128)} %root_ref.2), custom_call_target="tpu_custom_call" | custom-call | tf_op jit(solution)/shard_map/level_matrices/pallas_call | solution.py:567
  38.0 3.4 %collective-permute-done.6.first_ref = f32[4,64,128]{2,1,0:T(8,128)S(1)} collective-permute-done((f32[4,64,128]{2,1,0:T(8,128)S(1)}, f32[4,64,128]{2,1,0:T(8,128)S(1)}, u32[]{:S(2)}, u32[]{:S(2)}) %collective-permute-start.6) | collective-permute-done | bytes 131104 | tf_op jit(solution)/shard_map/ppermute | solution.py:421
  41.5 0.1 collective-permute-start.8
  41.5 1.0 %collective-permute-start.12 = (f32[4,64,128]{2,1,0:T(8,128)S(1)}, f32[4,64,128]{2,1,0:T(8,128)S(1)}, u32[]{:S(2)}, u32[]{:S(2)}) collective-permute-start(f32[4,64,128]{2,1,0:T(8,128)S(1)} %multiply_subtract_fusion.own_ref.refs_0_), channel_id=1, source_target_pairs={{24,0},{16,8},{8,16},{0,24},{25,1},{17,9},{9,17},{1,25},{26,2},{18... | collective-permute-start | bytes 393224 | tf_op jit(solution)/shard_map/ppermute | solution.py:427
  42.5 1.5 %collective-permute-start.13 = (f32[4,64,128]{2,1,0:T(8,128)S(1)}, f32[4,64,128]{2,1,0:T(8,128)S(1)}, u32[]{:S(2)}, u32[]{:S(2)}) collective-permute-start(f32[4,64,128]{2,1,0:T(8,128)S(1)} %multiply_subtract_fusion.own_ref.refs_0_), channel_id=1, source_target_pairs={{16,0},{24,8},{0,16},{8,24},{17,1},{25,9},{1,17},{9,25},{18,2},{26... | collective-permute-start | bytes 393224 | tf_op jit(solution)/shard_map/ppermute | solution.py:427
  44.0 1.1 %collective-permute-start.14 = (f32[4,64,128]{2,1,0:T(8,128)S(1)}, f32[4,64,128]{2,1,0:T(8,128)S(1)}, u32[]{:S(2)}, u32[]{:S(2)}) collective-permute-start(f32[4,64,128]{2,1,0:T(8,128)S(1)} %multiply_subtract_fusion.own_ref.refs_0_), channel_id=1, source_target_pairs={{8,0},{0,8},{24,16},{16,24},{9,1},{1,9},{25,17},{17,25},{10,2},{2,... | collective-permute-start | bytes 393224 | tf_op jit(solution)/shard_map/ppermute | solution.py:427
  45.1 1.3 %diffuse_adjoint.1.refs_0_ = f32[4,64,128]{2,1,0:T(8,128)S(1)} custom-call(f32[3,10,32,128]{3,2,1,0:T(8,128)S(1)} %get-tuple-element.53.coef_ref, f32[4,64,128]{2,1,0:T(8,128)S(1)} %collective-permute-done.7.second_ref, f32[4,64,128]{2,1,0:T(8,128)S(1)} %collective-permute-done.6.first_ref, f32[4,64,128]{2,1,0:T(8,128)S(1)} %multiply_subtract_fusion.own_ref.refs_0_, ...), custom_call_target="tpu_custom_call" | custom-call | tf_op jit(solution)/shard_map/diffuse_adjoint/pallas_call | solution.py:581
  46.4 1.0 %collective-permute-start.9 = (f32[4,64,128]{2,1,0:T(8,128)S(1)}, f32[4,64,128]{2,1,0:T(8,128)S(1)}, u32[]{:S(2)}, u32[]{:S(2)}) collective-permute-start(f32[4,64,128]{2,1,0:T(8,128)S(1)} %diffuse_adjoint.1.refs_0_), channel_id=1, source_target_pairs={{24,0},{16,8},{8,16},{0,24},{25,1},{17,9},{9,17},{1,25},{26,2},{18... | collective-permute-start | bytes 393224 | tf_op jit(solution)/shard_map/ppermute | solution.py:427
  47.4 1.5 %collective-permute-start.10 = (f32[4,64,128]{2,1,0:T(8,128)S(1)}, f32[4,64,128]{2,1,0:T(8,128)S(1)}, u32[]{:S(2)}, u32[]{:S(2)}) collective-permute-start(f32[4,64,128]{2,1,0:T(8,128)S(1)} %diffuse_adjoint.1.refs_0_), channel_id=1, source_target_pairs={{16,0},{24,8},{0,16},{8,24},{17,1},{25,9},{1,17},{9,25},{18,2},{26... | collective-permute-start | bytes 393224 | tf_op jit(solution)/shard_map/ppermute | solution.py:427
  48.9 1.1 %collective-permute-start.11 = (f32[4,64,128]{2,1,0:T(8,128)S(1)}, f32[4,64,128]{2,1,0:T(8,128)S(1)}, u32[]{:S(2)}, u32[]{:S(2)}) collective-permute-start(f32[4,64,128]{2,1,0:T(8,128)S(1)} %diffuse_adjoint.1.refs_0_), channel_id=1, source_target_pairs={{8,0},{0,8},{24,16},{16,24},{9,1},{1,9},{25,17},{17,25},{10,2},{2,... | collective-permute-start | bytes 393224 | tf_op jit(solution)/shard_map/ppermute | solution.py:427
  50.0 1.7 %collective-permute-done.13.refs_2_ = f32[4,64,128]{2,1,0:T(8,128)S(1)} collective-permute-done((f32[4,64,128]{2,1,0:T(8,128)S(1)}, f32[4,64,128]{2,1,0:T(8,128)S(1)}, u32[]{:S(2)}, u32[]{:S(2)}) %collective-permute-start.13) | collective-permute-done | bytes 131104 | tf_op jit(solution)/shard_map/ppermute | solution.py:427
  51.7 5.6 %members_gradient.1 = f32[8,16,64,128]{3,2,1,0:T(8,128)} custom-call(bf16[256,768]{1,0:T(8,128)(2,1)S(1)} %get-tuple-element.59.matrix_ref, f32[8,16,64,128]{3,2,1,0:T(8,128)S(1)} %get-tuple-element.60.control_ref, bf16[8,16,64,128]{3,2,1,0:T(8,128)(2,1)S(1)} %get-tuple-element.61.pert_ref, f32[4,64,128]{2,1,0:T(8,128)S(1)} %multiply_subtract_fusion.own_ref.refs_0_, ...), custom_call_target="tpu_custom_call" | custom-call | tf_op jit(solution)/shard_map/members_gradient/pallas_call | solution.py:593
  57.4 1.2 %static_gradient.1 = f32[16,64,128]{2,1,0:T(8,128)} custom-call(bf16[256,768]{1,0:T(8,128)(2,1)S(1)} %get-tuple-element.51.matrix_ref, f32[16,64,128]{2,1,0:T(8,128)S(1)} %get-tuple-element.52.static_ref, f32[4,64,128]{2,1,0:T(8,128)S(1)} %diffuse_adjoint.1.refs_0_, f32[4,64,128]{2,1,0:T(8,128)S(1)} %collective-permute-done.9.refs_1_, ...), custom_call_target="tpu_custom_call" | custom-call | tf_op jit(solution)/shard_map/static_gradient/pallas_call | solution.py:604
  (14 shorter events, 0.1 us)
Async XLA Ops:
  10.9 10.2 %collective-permute-start.3 = (f32[6,64,128]{2,1,0:T(8,128)S(1)}, f32[6,64,128]{2,1,0:T(8,128)S(1)}, u32[]{:S(2)}, u32[]{:S(2)}) collective-permute-start(f32[6,64,128]{2,1,0:T(8,128)S(1)} %prepare.1.own_ref), channel_id=1, source_target_pairs={{0,0},{1,1},{2,4},{3,5},{4,2},{5,3},{6,6},{7,7},{8,8},{9,9},{10,12... | collective-permute-start | bytes 589832 | tf_op jit(solution)/shard_map/ppermute | solution.py:421
  11.5 10.5 %collective-permute-start.4 = (f32[6,64,128]{2,1,0:T(8,128)S(1)}, f32[6,64,128]{2,1,0:T(8,128)S(1)}, u32[]{:S(2)}, u32[]{:S(2)}) collective-permute-start(f32[6,64,128]{2,1,0:T(8,128)S(1)} %prepare.1.own_ref), channel_id=1, source_target_pairs={{0,2},{1,3},{2,0},{3,1},{4,6},{5,7},{6,4},{7,5},{8,10},{9,11},{10,... | collective-permute-start | bytes 589832 | tf_op jit(solution)/shard_map/ppermute | solution.py:421
  17.5 14.0 %all-to-all-start = ((f32[32,2,8,128]{3,2,1,0:T(8,128)}), f32[32,2,8,128]{3,2,1,0:T(8,128)S(1)}, u32[]{:S(2)}, u32[]{:S(2)}) async-start(f32[32,2,8,128]{3,2,1,0:T(8,128)} %get-tuple-element.41), calls=%async_computation | async-start | bytes 524288 | tf_op jit(solution)/shard_map/all_to_all | solution.py:523
  22.1 3.6 %collective-permute-start.5 = (f32[2,6,64,128]{3,2,1,0:T(8,128)S(1)}, f32[2,6,64,128]{3,2,1,0:T(8,128)S(1)}, u32[]{:S(2)}, u32[]{:S(2)}) collective-permute-start(f32[2,6,64,128]{3,2,1,0:T(8,128)S(1)} %pad_maximum_fusion), channel_id=1, source_target_pairs={{0,1},{1,0},{2,3},{3,2},{4,5},{5,4},{6,7},{7,6},{8,9},{9,8},{10,11... | collective-permute-start | bytes 1179656 | tf_op jit(solution)/shard_map/ppermute | solution.py:433
  22.2 13.3 %collective-permute-start.2 = (f32[4,64,128]{2,1,0:T(8,128)S(1)}, f32[4,64,128]{2,1,0:T(8,128)S(1)}, u32[]{:S(2)}, u32[]{:S(2)}) collective-permute-start(f32[4,64,128]{2,1,0:T(8,128)S(1)} %get-tuple-element.35), channel_id=1, source_target_pairs={{8,0},{0,8},{24,16},{16,24},{9,1},{1,9},{25,17},{17,25},{10,2},{2,... | collective-permute-start | bytes 393224 | tf_op jit(solution)/shard_map/ppermute | solution.py:526
  23.8 11.7 %collective-permute-start.1 = (f32[4,64,128]{2,1,0:T(8,128)S(1)}, f32[4,64,128]{2,1,0:T(8,128)S(1)}, u32[]{:S(2)}, u32[]{:S(2)}) collective-permute-start(f32[4,64,128]{2,1,0:T(8,128)S(1)} %get-tuple-element.34), channel_id=1, source_target_pairs={{16,0},{24,8},{0,16},{8,24},{17,1},{25,9},{1,17},{9,25},{18,2},{26... | collective-permute-start | bytes 393224 | tf_op jit(solution)/shard_map/ppermute | solution.py:526
  25.3 10.2 %collective-permute-start = (f32[4,64,128]{2,1,0:T(8,128)S(1)}, f32[4,64,128]{2,1,0:T(8,128)S(1)}, u32[]{:S(2)}, u32[]{:S(2)}) collective-permute-start(f32[4,64,128]{2,1,0:T(8,128)S(1)} %get-tuple-element.33), channel_id=1, source_target_pairs={{24,0},{16,8},{8,16},{0,24},{25,1},{17,9},{9,17},{1,25},{26,2},{18... | collective-permute-start | bytes 393224 | tf_op jit(solution)/shard_map/ppermute | solution.py:526
  35.6 5.8 %collective-permute-start.6 = (f32[4,64,128]{2,1,0:T(8,128)S(1)}, f32[4,64,128]{2,1,0:T(8,128)S(1)}, u32[]{:S(2)}, u32[]{:S(2)}) collective-permute-start(f32[4,64,128]{2,1,0:T(8,128)S(1)} %multiply_subtract_fusion.own_ref.refs_0_), channel_id=1, source_target_pairs={{0,2},{1,3},{2,0},{3,1},{4,6},{5,7},{6,4},{7,5},{8,10},{9,11},{10,... | collective-permute-start | bytes 393224 | tf_op jit(solution)/shard_map/ppermute | solution.py:421
  36.1 5.3 %collective-permute-start.7 = (f32[4,64,128]{2,1,0:T(8,128)S(1)}, f32[4,64,128]{2,1,0:T(8,128)S(1)}, u32[]{:S(2)}, u32[]{:S(2)}) collective-permute-start(f32[4,64,128]{2,1,0:T(8,128)S(1)} %multiply_subtract_fusion.own_ref.refs_0_), channel_id=1, source_target_pairs={{0,0},{1,1},{2,4},{3,5},{4,2},{5,3},{6,6},{7,7},{8,8},{9,9},{10,12... | collective-permute-start | bytes 393224 | tf_op jit(solution)/shard_map/ppermute | solution.py:421
  41.5 3.6 %collective-permute-start.8 = (f32[2,4,64,128]{3,2,1,0:T(8,128)S(1)}, f32[2,4,64,128]{3,2,1,0:T(8,128)S(1)}, u32[]{:S(2)}, u32[]{:S(2)}) collective-permute-start(f32[2,4,64,128]{3,2,1,0:T(8,128)S(1)} %pad_maximum_fusion.1), channel_id=1, source_target_pairs={{0,1},{1,0},{2,3},{3,2},{4,5},{5,4},{6,7},{7,6},{8,9},{9,8},{10,11... | collective-permute-start | bytes 786440 | tf_op jit(solution)/shard_map/ppermute | solution.py:433
  41.5 7.3 %collective-permute-start.12 = (f32[4,64,128]{2,1,0:T(8,128)S(1)}, f32[4,64,128]{2,1,0:T(8,128)S(1)}, u32[]{:S(2)}, u32[]{:S(2)}) collective-permute-start(f32[4,64,128]{2,1,0:T(8,128)S(1)} %multiply_subtract_fusion.own_ref.refs_0_), channel_id=1, source_target_pairs={{24,0},{16,8},{8,16},{0,24},{25,1},{17,9},{9,17},{1,25},{26,2},{18... | collective-permute-start | bytes 393224 | tf_op jit(solution)/shard_map/ppermute | solution.py:427
  42.5 9.2 %collective-permute-start.13 = (f32[4,64,128]{2,1,0:T(8,128)S(1)}, f32[4,64,128]{2,1,0:T(8,128)S(1)}, u32[]{:S(2)}, u32[]{:S(2)}) collective-permute-start(f32[4,64,128]{2,1,0:T(8,128)S(1)} %multiply_subtract_fusion.own_ref.refs_0_), channel_id=1, source_target_pairs={{16,0},{24,8},{0,16},{8,24},{17,1},{25,9},{1,17},{9,25},{18,2},{26... | collective-permute-start | bytes 393224 | tf_op jit(solution)/shard_map/ppermute | solution.py:427
  44.0 7.7 %collective-permute-start.14 = (f32[4,64,128]{2,1,0:T(8,128)S(1)}, f32[4,64,128]{2,1,0:T(8,128)S(1)}, u32[]{:S(2)}, u32[]{:S(2)}) collective-permute-start(f32[4,64,128]{2,1,0:T(8,128)S(1)} %multiply_subtract_fusion.own_ref.refs_0_), channel_id=1, source_target_pairs={{8,0},{0,8},{24,16},{16,24},{9,1},{1,9},{25,17},{17,25},{10,2},{2,... | collective-permute-start | bytes 393224 | tf_op jit(solution)/shard_map/ppermute | solution.py:427
  46.4 10.9 %collective-permute-start.9 = (f32[4,64,128]{2,1,0:T(8,128)S(1)}, f32[4,64,128]{2,1,0:T(8,128)S(1)}, u32[]{:S(2)}, u32[]{:S(2)}) collective-permute-start(f32[4,64,128]{2,1,0:T(8,128)S(1)} %diffuse_adjoint.1.refs_0_), channel_id=1, source_target_pairs={{24,0},{16,8},{8,16},{0,24},{25,1},{17,9},{9,17},{1,25},{26,2},{18... | collective-permute-start | bytes 393224 | tf_op jit(solution)/shard_map/ppermute | solution.py:427
  47.4 10.0 %collective-permute-start.10 = (f32[4,64,128]{2,1,0:T(8,128)S(1)}, f32[4,64,128]{2,1,0:T(8,128)S(1)}, u32[]{:S(2)}, u32[]{:S(2)}) collective-permute-start(f32[4,64,128]{2,1,0:T(8,128)S(1)} %diffuse_adjoint.1.refs_0_), channel_id=1, source_target_pairs={{16,0},{24,8},{0,16},{8,24},{17,1},{25,9},{1,17},{9,25},{18,2},{26... | collective-permute-start | bytes 393224 | tf_op jit(solution)/shard_map/ppermute | solution.py:427
  48.9 8.5 %collective-permute-start.11 = (f32[4,64,128]{2,1,0:T(8,128)S(1)}, f32[4,64,128]{2,1,0:T(8,128)S(1)}, u32[]{:S(2)}, u32[]{:S(2)}) collective-permute-start(f32[4,64,128]{2,1,0:T(8,128)S(1)} %diffuse_adjoint.1.refs_0_), channel_id=1, source_target_pairs={{8,0},{0,8},{24,16},{16,24},{9,1},{1,9},{25,17},{17,25},{10,2},{2,... | collective-permute-start | bytes 393224 | tf_op jit(solution)/shard_map/ppermute | solution.py:427

commit v14 on v13

--- a/solution.py
+++ b/solution.py
@@ -92,8 +92,9 @@
     return count - d if count & (count - 1) else d
 
 
-def prepare_kernel(lev_share, root_ref, static_ref, north_ref, east_ref, out_ref):
+def prepare(root_ref, static_ref, north_ref, east_ref, out_ref):
     levels = static_ref.shape[0]
+    lev_share = out_ref.shape[0] - 2
     first = lax.axis_index("ens") * lev_share
     for j in range(lev_share):
         total = root_ref[first + j, 0] * static_ref[0]
@@ -144,17 +145,17 @@
     return jnp.concatenate([high, low, high], axis=0)
 
 
-def observe_kernel(n_cols, cap_rows, rows, lon, scale, *refs):
-    n_ens = len(refs) - 28
-    sources, (out_ref, row_ref, lane_ref), parts = refs[:8], refs[8:11], refs[11 : 11 + n_ens]
-    refs = refs[11 + n_ens :]
+def observe_kernel(n_cols, cap_rows, scale, *refs):
+    n_ens = len(refs) - 31
+    sources, (out_ref, packed_ref), parts = refs[:10], refs[10:12], refs[12 : 12 + n_ens]
+    refs = refs[12 + n_ens :]
     (acc_ref, fold_ref, matrix_ref, part_ref), landed, sems, slots = (
         refs[:4],
-        refs[4:12],
-        refs[12],
-        (refs[13:15], refs[15:17]),
+        refs[4:14],
+        refs[14],
+        (refs[15:17], refs[17:19]),
     )
-    slot_ref, weight_ref, innov_ref, index_ref, count_ref, local_ref, control_ref, pert_ref = landed
+    slot_ref, weight_ref, innov_ref, local_ref, control_ref, pert_ref, *static_refs = landed
     coarse = acc_ref.shape[1]
     obs_rows = slot_ref.shape[0]
     group = min(8, obs_rows)
@@ -207,7 +208,7 @@
             out_ref[e * n_cols + p, 1] = amounts[p * cap_rows : (p + 1) * cap_rows]
     for copy in copies[3:]:
         copy.wait()
-    list_cells(rows, lon, index_ref, count_ref, row_ref, lane_ref)
+    prepare(*static_refs, packed_ref)
     matrix_ref[...] = level_product(local_ref[...] * f32(scale), False)
     sum_members(matrix_ref, control_ref, pert_ref, part_ref)
     share = part_ref.shape[0] // n_ens
@@ -279,20 +280,16 @@
     return jnp.where(lane == 0, pltpu.roll(near, 1, 0), near)
 
 
-def rows_of(second_ref, first_ref, own_ref, other_ref, plane, rows):
+def rows_of(before_ref, after_ref, own_ref, other_ref, plane, rows):
     at = lax.axis_index("cols")
     count = lax.axis_size("cols")
-    core, chip = at % 2, at // 2 % 2
+    core = at % 2
     reads = [pl.ds(r, own_ref.shape[1] // rows, stride=rows) for r in range(rows)]
-    first = [first_ref[plane, r, :] for r in reads]
-    second = [second_ref[plane, r, :] for r in reads]
-    out = [jnp.where(jnp.logical_and(chip == 1, at >= 2), f, f32(0)) for f in first]
-    out = [jnp.where(jnp.logical_and(chip == 0, at >= 2), s, o) for s, o in zip(second, out)]
+    out = [jnp.where(at >= 2, before_ref[plane, r, :], f32(0)) for r in reads]
     out += [jnp.where(at >= 1, other_ref[1 - core, plane, r, :], f32(0)) for r in reads]
     out += [own_ref[plane, r, :] for r in reads]
     out += [jnp.where(at < count - 1, other_ref[core, plane, r, :], f32(0)) for r in reads]
-    last = [jnp.where(jnp.logical_and(chip == 0, at < count - 2), f, f32(0)) for f in first]
-    return out + [jnp.where(jnp.logical_and(chip == 1, at < count - 2), s, o) for s, o in zip(second, last)]
+    return out + [jnp.where(at < count - 2, after_ref[plane, r, :], f32(0)) for r in reads]
 
 
 def diffuse_rows(tiles, level, coef_ref, rows):
@@ -309,8 +306,13 @@
     return field
 
 
-def first_diffusion_kernel(lev_share, rows, second_ref, first_ref, own_ref, other_ref, out_ref, coef_ref):
-    tiles = (second_ref, first_ref, own_ref, other_ref)
+def first_diffusion_kernel(lev_share, rows, *refs):
+    before_ref, after_ref, own_ref, other_ref, *sources = refs[:6]
+    out_ref, coef_ref, row_ref, lane_ref, *landed, sems = refs[6:]
+    copies = [pltpu.make_async_copy(s, t, sems.at[i]) for i, (s, t) in enumerate(zip(sources, landed))]
+    for copy in copies:
+        copy.start()
+    tiles = (before_ref, after_ref, own_ref, other_ref)
     blocks = own_ref.shape[1] // rows
     side = 2
     north = rows_of(*tiles, lev_share, rows)
@@ -332,10 +334,13 @@
         return carry
 
     lax.fori_loop(0, lev_share, body, 0)
-
-
-def second_diffusion_kernel(rows, coef_ref, second_ref, first_ref, own_ref, other_ref, out_ref):
-    tiles = (second_ref, first_ref, own_ref, other_ref)
+    for copy in copies:
+        copy.wait()
+    list_cells(rows, blocks * LANES, *landed, row_ref, lane_ref)
+
+
+def second_diffusion_kernel(rows, coef_ref, before_ref, after_ref, own_ref, other_ref, out_ref):
+    tiles = (before_ref, after_ref, own_ref, other_ref)
     lev_share = out_ref.shape[0]
     blocks = own_ref.shape[1] // rows
 
@@ -409,17 +414,9 @@
             out_ref[:, at, :] = static_ref[:, at, :] + part.reshape(levels, 16, LANES)
 
 
-def exchanged(x, starts):
+def shifted(x):
     count = lax.axis_size("cols")
-    out = []
-    for start in starts:
-        pairs = []
-        for i in range(count):
-            chip, core = divmod(i, 2)
-            partner = (chip + start ^ 1) - start
-            pairs.append((i, 2 * partner + core if 0 <= 2 * partner + core < count else i))
-        out.append(lax.ppermute(x, "cols", pairs))
-    return out
+    return [lax.ppermute(x, "cols", [(i, (i + by) % count) for i in range(count)]) for by in (2, -2)]
 
 
 def from_peers(x):
@@ -427,9 +424,8 @@
     return [lax.ppermute(x, "ens", [(peer(i, d, count), i) for i in range(count)]) for d in range(count - 1, 0, -1)]
 
 
-def swapped(own, first, second):
-    at = lax.axis_index("cols")
-    pack = jnp.stack([own, jnp.where(at % 2 == at // 2 % 2, first, second)])
+def swapped(own, before, after):
+    pack = jnp.stack([own, jnp.where(lax.axis_index("cols") % 2 == 1, before, after)])
     return lax.ppermute(pack, "cols", [(i, i ^ 1) for i in range(lax.axis_size("cols"))])
 
 
@@ -470,15 +466,14 @@
     share_rows = obs_rows // n_ens
     coarse = n_cols * capacity // FINE
     size = levels * 16
-    slots, entry_row, entry_lane, *parts = pl.pallas_call(
-        functools.partial(observe_kernel, n_cols, cap_rows, rows, lon, member_scale),
+    slots, packed, *parts = pl.pallas_call(
+        functools.partial(observe_kernel, n_cols, cap_rows, member_scale),
         grid=(1,),
-        in_specs=[pl.BlockSpec(memory_space=pl.ANY)] * 8,
-        out_specs=[whole(n_ens * n_cols, 2, cap_rows, LANES)] + [VMEM] * (2 + n_ens),
+        in_specs=[pl.BlockSpec(memory_space=pl.ANY)] * 10,
+        out_specs=[whole(n_ens * n_cols, 2, cap_rows, LANES)] + [VMEM] * (1 + n_ens),
         out_shape=[
             pltpu.HBM((n_ens * n_cols, 2, cap_rows, LANES), f32),
-            pltpu.VMEM((entry_rows, LANES), jnp.int32),
-            pltpu.VMEM((entry_rows, LANES), jnp.int32),
+            pltpu.VMEM((lev_share + 2, per_level, LANES), f32),
         ]
         + [pltpu.VMEM((lev_share, per_level, LANES), f32)] * n_ens,
         scratch_shapes=[
@@ -489,12 +484,14 @@
             pltpu.VMEM((share_rows, LANES), jnp.int32),
             pltpu.VMEM((share_rows, LANES), f32),
             pltpu.VMEM((share_rows, LANES), f32),
-            pltpu.VMEM((lists, capacity), jnp.int32),
-            pltpu.SMEM((lists,), jnp.int32),
             pltpu.VMEM((levels, levels), f32),
             pltpu.VMEM(control.shape, f32),
             pltpu.VMEM(pert.shape, bf16),
-            pltpu.SemaphoreType.DMA((8,)),
+            pltpu.SMEM((levels, levels), f32),
+            pltpu.VMEM((levels, per_level, LANES), f32),
+            pltpu.VMEM((per_level, LANES), f32),
+            pltpu.VMEM((per_level, LANES), f32),
+            pltpu.SemaphoreType.DMA((10,)),
         ]
         + [pltpu.VMEM((coarse, 8 * LANES), bf16), pltpu.VMEM((4 * FINE, 8 * LANES), bf16)] * 2,
         compiler_params=params(24),
@@ -503,43 +500,41 @@
         in_hbm(obs_slot.reshape(obs_rows, LANES)),
         in_hbm(obs_weight.reshape(obs_rows, LANES)),
         in_hbm(innovation.reshape(obs_rows, LANES)),
-        in_hbm(send_index),
-        in_hbm(send_count),
         in_hbm(vertical_local),
         control,
         pert,
+        in_hbm(vertical_root),
+        static,
+        in_hbm(tiled(face_north)),
+        in_hbm(tiled(face_east)),
     )
-    slots, face_north, face_east = lax.optimization_barrier((slots, face_north, face_east))
-    packed = pl.pallas_call(
-        functools.partial(prepare_kernel, lev_share),
-        grid=(1,),
-        in_specs=[SMEM, whole(levels, per_level, LANES), whole(per_level, LANES), whole(per_level, LANES)],
-        out_specs=VMEM,
-        out_shape=pltpu.VMEM((lev_share + 2, per_level, LANES), f32),
-        compiler_params=params(8),
-        cost_estimate=pl.CostEstimate(flops=1 << 31, bytes_accessed=1 << 25, transcendentals=0),
-        name="prepare",
-    )(in_hbm(vertical_root), static, in_hbm(tiled(face_north)), in_hbm(tiled(face_east)))
     slots = lax.all_to_all(slots, ("ens", "cols"), split_axis=0, concat_axis=0, tiled=True)
-    second, first = exchanged(packed, (1, 0))
+    before, after = shifted(packed)
     sums = [parts[0]] + [
         lax.ppermute(parts[back(d, n_ens)], "ens", [(peer(i, d, n_ens), i) for i in range(n_ens)])
         for d in range(n_ens - 1, 0, -1)
     ]
-    other = swapped(packed, first, second)
-
-    increment, coefs = pl.pallas_call(
+    other = swapped(packed, before, after)
+
+    increment, coefs, entry_row, entry_lane = pl.pallas_call(
         functools.partial(first_diffusion_kernel, lev_share, rows),
-        in_specs=[VMEM] * 4,
-        out_specs=[VMEM] * 2,
+        in_specs=[VMEM] * 4 + [pl.BlockSpec(memory_space=pl.ANY)] * 2,
+        out_specs=[VMEM] * 4,
         out_shape=[
             pltpu.VMEM((lev_share, per_level, LANES), f32),
             pltpu.VMEM((3, 5 * rows, per_level // rows, LANES), f32),
+            pltpu.VMEM((entry_rows, LANES), jnp.int32),
+            pltpu.VMEM((entry_rows, LANES), jnp.int32),
+        ],
+        scratch_shapes=[
+            pltpu.VMEM((lists, capacity), jnp.int32),
+            pltpu.SMEM((lists,), jnp.int32),
+            pltpu.SemaphoreType.DMA((2,)),
         ],
         compiler_params=params(8),
         cost_estimate=pl.CostEstimate(flops=1 << 26, bytes_accessed=1 << 22, transcendentals=0),
         name="diffuse_forward",
-    )(second, first, packed, other)
+    )(before, after, packed, other, in_hbm(send_index), in_hbm(send_count))
 
     increment, coefs, slots = lax.optimization_barrier((increment, coefs, slots))
     slot_sums, static_here, control_here, pert_here = pl.pallas_call(
@@ -561,7 +556,7 @@
     slot_sums = slot_sums.reshape(2, lev_share, per_level, LANES)
     tile = functools.reduce(jnp.add, sums) + increment
     tile = tile * slot_sums[0] - slot_sums[1]
-    tile_first, tile_second = exchanged(tile, (0, 1))
+    tile_before, tile_after = shifted(tile)
     adjoints = [tile] + from_peers(tile)
     tile, vertical_local, vertical_root = lax.optimization_barrier((tile, vertical_local, vertical_root))
     from_local, from_root = pl.pallas_call(
@@ -573,10 +568,10 @@
         compiler_params=params(8),
         name="level_matrices",
     )(in_hbm(vertical_local), in_hbm(vertical_root))
-    tile_first, tile_second, from_local, from_root = lax.optimization_barrier(
-        (tile_first, tile_second, from_local, from_root)
+    tile_before, tile_after, from_local, from_root = lax.optimization_barrier(
+        (tile_before, tile_after, from_local, from_root)
     )
-    tile_other = swapped(tile, tile_first, tile_second)
+    tile_other = swapped(tile, tile_before, tile_after)
 
     smooth = pl.pallas_call(
         functools.partial(second_diffusion_kernel, rows),
@@ -585,7 +580,7 @@
         out_shape=pltpu.VMEM((lev_share, per_level, LANES), f32),
         compiler_params=params(8),
         name="diffuse_adjoint",
-    )(coefs, tile_second, tile_first, tile, tile_other)
+    )(coefs, tile_before, tile_after, tile, tile_other)
     smooth, from_local = lax.optimization_barrier((smooth, from_local))
     smooths = [smooth] + from_peers(smooth)
 

time: 59.5 us -> 61.1 us (1.027); the launches traced: 58.6 us -> 60.9 us
  starting transfers between devices: 22.2 us -> 23.9 us
  waiting for transfers between devices: 10.3 us -> 11.9 us
  Pallas kernels: 25.1 us -> 24.2 us
    ppermute x4, waiting for transfers between devices: 4.36 us -> 8.04 us  [shifted(): lax.ppermute(x, 'cols', [(i, (i + by) % count) for i in range(count)])]
    all_to_all x1, waiting for transfers between devices: 4.19 us -> 1.99 us  [local(): lax.all_to_all(slots, ('ens', 'cols'), split_axis=0, concat_axis=0, tiled...]
    ppermute x4, starting transfers between devices: 7.77 us -> 9.04 us  [shifted(): lax.ppermute(x, 'cols', [(i, (i + by) % count) for i in range(count)])]
    pallas_call x2 -> x1, Pallas kernels: 10.2 us -> 9.11 us  [local(): pl.pallas_call(functools.partial(observe_kernel, n_cols, cap_rows, member...]
    all_to_all x1, starting transfers between devices: 3.59 us -> 4.21 us  [local(): lax.all_to_all(slots, ('ens', 'cols'), split_axis=0, concat_axis=0, tiled...]
  transfers between devices with their start and end apart: 16 -> 16, of which waited for: 4 -> 6; matrix products, arithmetic and copies ran while one was open for 0% -> 0% of each run, Pallas kernels for 23% -> 23%
where the time goes in v14:
time: 61.1 us; the launch traced here: 60.9 us
  Pallas kernels  24.2 us (40%)
  starting transfers between devices  23.9 us (39%)
  waiting for transfers between devices  11.9 us (19%)
  between operations  0.78 us (1%)
    pallas_call x1, Pallas kernels, local(): pl.pallas_call(functools.partial(observe_kernel, n_cols, cap_rows, member...  9.11 us
    ppermute x4, starting transfers between devices, shifted(): lax.ppermute(x, 'cols', [(i, (i + by) % count) for i in range(count)])  9.04 us
    ppermute x4, waiting for transfers between devices, shifted(): lax.ppermute(x, 'cols', [(i, (i + by) % count) for i in range(count)])  8.04 us
    ppermute x6, starting transfers between devices, from_peers(): lax.ppermute(x, 'ens', [(peer(i, d, count), i) for i in range(count)])  6.97 us
    pallas_call x1, Pallas kernels, local(): pl.pallas_call(member_kernel, grid=(members // group,), in_specs=[VMEM] *...  5.65 us
    all_to_all x1, starting transfers between devices, local(): lax.all_to_all(slots, ('ens', 'cols'), split_axis=0, concat_axis=0, tiled...  4.21 us
    pallas_call x1, Pallas kernels, local(): pl.pallas_call(functools.partial(scatter_kernel, cap_rows), in_specs=[VME...  4 us
    ppermute x3, starting transfers between devices, local(): lax.ppermute(parts[back(d, n_ens)], 'ens', [(peer(i, d, n_ens), i) for i...  3.55 us
  transfers between devices with their start and end apart: 16, of which 6 were waited for; matrix products, arithmetic and copies ran while one was open for 0% of the time, Pallas kernels for 23%

profile of v14, /device:TPU:0, one launch (start us, length us, event | category | flops | bytes accessed | tf_op | source)
XLA Modules:
  0.0 60.9 jit_solution(13764227587795770849)
XLA Ops:
  0.6 9.1 %slot_sums_and_members.1 = (f32[32,2,8,128]{3,2,1,0:T(8,128)}, f32[6,64,128]{2,1,0:T(8,128)S(1)}, f32[4,64,128]{2,1,0:T(8,128)S(1)}, f32[4,64,128]{2,1,0:T(8,128...) custom-call(s32[512,128]{1,0:T(8,128)} %bitcast.58, f32[512,128]{1,0:T(8,128)} %bitcast.59, ...), custom_call_target="tpu_custom_call" | custom-call | tf_op jit(solution)/shard_map/slot_sums_and_members/pallas_call | solution.py:469
  9.7 3.1 %collective-permute-start.3 = (f32[6,64,128]{2,1,0:T(8,128)S(1)}, f32[6,64,128]{2,1,0:T(8,128)S(1)}, u32[]{:S(2)}, u32[]{:S(2)}) collective-permute-start(f32[6,64,128]{2,1,0:T(8,128)S(1)} %get-tuple-element.34.refs_2_), channel_id=1, source_target_pairs={{0,2},{1,3},{2,4},{3,5},{4,6},{5,7},{6,0},{7,1},{8,10},{9,11},{10,... | collective-permute-start | bytes 589832 | tf_op jit(solution)/shard_map/ppermute | solution.py:419
  12.8 2.1 %collective-permute-start.4 = (f32[6,64,128]{2,1,0:T(8,128)S(1)}, f32[6,64,128]{2,1,0:T(8,128)S(1)}, u32[]{:S(2)}, u32[]{:S(2)}) collective-permute-start(f32[6,64,128]{2,1,0:T(8,128)S(1)} %get-tuple-element.34.refs_2_), channel_id=1, source_target_pairs={{0,6},{1,7},{2,0},{3,1},{4,2},{5,3},{6,4},{7,5},{8,14},{9,15},{10,... | collective-permute-start | bytes 589832 | tf_op jit(solution)/shard_map/ppermute | solution.py:419
  14.9 4.2 %all-to-all-start = ((f32[32,2,8,128]{3,2,1,0:T(8,128)}), f32[32,2,8,128]{3,2,1,0:T(8,128)S(1)}, u32[]{:S(2)}, u32[]{:S(2)}) async-start(f32[32,2,8,128]{3,2,1,0:T(8,128)} %get-tuple-element.37), calls=%async_computation | async-start | bytes 524288 | tf_op jit(solution)/shard_map/all_to_all | solution.py:511
  19.1 1.5 %collective-permute-done.3.refs_0_ = f32[6,64,128]{2,1,0:T(8,128)S(1)} collective-permute-done((f32[6,64,128]{2,1,0:T(8,128)S(1)}, f32[6,64,128]{2,1,0:T(8,128)S(1)}, u32[]{:S(2)}, u32[]{:S(2)}) %collective-permute-start.3) | collective-permute-done | bytes 196640 | tf_op jit(solution)/shard_map/ppermute | solution.py:419
  20.6 3.5 %collective-permute-done.4.refs_1_ = f32[6,64,128]{2,1,0:T(8,128)S(1)} collective-permute-done((f32[6,64,128]{2,1,0:T(8,128)S(1)}, f32[6,64,128]{2,1,0:T(8,128)S(1)}, u32[]{:S(2)}, u32[]{:S(2)}) %collective-permute-start.4) | collective-permute-done | bytes 196640 | tf_op jit(solution)/shard_map/ppermute | solution.py:419
  24.2 0.1 collective-permute-start.5
  24.3 1.6 %collective-permute-start.2 = (f32[4,64,128]{2,1,0:T(8,128)S(1)}, f32[4,64,128]{2,1,0:T(8,128)S(1)}, u32[]{:S(2)}, u32[]{:S(2)}) collective-permute-start(f32[4,64,128]{2,1,0:T(8,128)S(1)} %get-tuple-element.33), channel_id=1, source_target_pairs={{8,0},{0,8},{24,16},{16,24},{9,1},{1,9},{25,17},{17,25},{10,2},{2,... | collective-permute-start | bytes 393224 | tf_op jit(solution)/shard_map/ppermute | solution.py:514
  25.8 1.5 %collective-permute-start.1 = (f32[4,64,128]{2,1,0:T(8,128)S(1)}, f32[4,64,128]{2,1,0:T(8,128)S(1)}, u32[]{:S(2)}, u32[]{:S(2)}) collective-permute-start(f32[4,64,128]{2,1,0:T(8,128)S(1)} %get-tuple-element.32), channel_id=1, source_target_pairs={{16,0},{24,8},{0,16},{8,24},{17,1},{25,9},{1,17},{9,25},{18,2},{26... | collective-permute-start | bytes 393224 | tf_op jit(solution)/shard_map/ppermute | solution.py:514
  27.3 0.5 collective-permute-start
  27.8 0.0 collective-permute-done.5.refs_3_
  27.8 1.6 %diffuse_forward.1 = (f32[4,64,128]{2,1,0:T(8,128)S(1)}, f32[3,10,32,128]{3,2,1,0:T(8,128)S(1)}, s32[64,128]{1,0:T(8,128)S(1)}, s32[64,128]{1,0:T(8,128)S(1)}) custom-call(f32[6,64,128]{2,1,0:T(8,128)S(1)} %collective-permute-done.3.refs_0_, f32[6,64,128]{2,1,0:T(8,128)S(1)} %collective-permute-done.4.refs_1_, f32[6,64,128]{2,1,0:T(8,128)S(1)} %get-tuple-element.34.refs_2_, ...), custom_call_target="tpu_custom_call" | custom-call | flops 67108864 | bytes 4194304 | tf_op jit(solution)/shard_map/diffuse_forward/pallas_call | solution.py:519
  29.4 2.0 %all-to-all-done.slots_ref = f32[32,2,8,128]{3,2,1,0:T(8,128)S(1)} async-done(((f32[32,2,8,128]{3,2,1,0:T(8,128)}), f32[32,2,8,128]{3,2,1,0:T(8,128)S(1)}, u32[]{:S(2)}, u32[]{:S(2)}) %all-to-all-start) | async-done | bytes 262176 | tf_op jit(solution)/shard_map/all_to_all | solution.py:511
  31.4 4.0 %scatter.1 = (f32[2,256,128]{2,1,0:T(8,128)S(1)}, f32[16,64,128]{2,1,0:T(8,128)S(1)}, f32[8,16,64,128]{3,2,1,0:T(8,128)S(1)}, bf16[8,16,64,128]{3,2,1,0:T(8,128)(2,1)S(1)}) custom-call(s32[64,128]{1,0:T(8,128)S(1)} %get-tuple-element.39.row_ref, s32[64,128]{1,0:T(8,128)S(1)} %get-tuple-element.40.lane_ref, f32[32,2,8,128]{3,2,1,0:T(8,128)S(1)} %all-to-all-done.slots_ref, ...), custom_call_target="tpu_custom_call" | custom-call | flops 2147483648 | bytes 8388608 | tf_op jit(solution)/shard_map/scatter/pallas_call | solution.py:540
  35.4 0.0 collective-permute-done
  35.4 0.1 multiply_subtract_fusion.own_ref.refs_0_
  35.5 0.2 collective-permute-start.6
  35.7 3.7 %collective-permute-start.7 = (f32[4,64,128]{2,1,0:T(8,128)S(1)}, f32[4,64,128]{2,1,0:T(8,128)S(1)}, u32[]{:S(2)}, u32[]{:S(2)}) collective-permute-start(f32[4,64,128]{2,1,0:T(8,128)S(1)} %multiply_subtract_fusion.own_ref.refs_0_), channel_id=1, source_target_pairs={{0,6},{1,7},{2,0},{3,1},{4,2},{5,3},{6,4},{7,5},{8,14},{9,15},{10,... | collective-permute-start | bytes 393224 | tf_op jit(solution)/shard_map/ppermute | solution.py:419
  39.4 1.2 %level_matrices.1 = (bf16[256,768]{1,0:T(8,128)(2,1)S(1)}, bf16[256,768]{1,0:T(8,128)(2,1)S(1)}) custom-call(f32[16,16]{1,0:T(8,128)} %local_ref, f32[16,16]{1,0:T(8,128)} %root_ref), custom_call_target="tpu_custom_call" | custom-call | tf_op jit(solution)/shard_map/level_matrices/pallas_call | solution.py:562
  40.6 3.1 %collective-permute-done.6.before_ref = f32[4,64,128]{2,1,0:T(8,128)S(1)} collective-permute-done((f32[4,64,128]{2,1,0:T(8,128)S(1)}, f32[4,64,128]{2,1,0:T(8,128)S(1)}, u32[]{:S(2)}, u32[]{:S(2)}) %collective-permute-start.6) | collective-permute-done | bytes 131104 | tf_op jit(solution)/shard_map/ppermute | solution.py:419
  43.7 0.1 collective-permute-start.8
  43.8 1.0 %collective-permute-start.12 = (f32[4,64,128]{2,1,0:T(8,128)S(1)}, f32[4,64,128]{2,1,0:T(8,128)S(1)}, u32[]{:S(2)}, u32[]{:S(2)}) collective-permute-start(f32[4,64,128]{2,1,0:T(8,128)S(1)} %multiply_subtract_fusion.own_ref.refs_0_), channel_id=1, source_target_pairs={{24,0},{16,8},{8,16},{0,24},{25,1},{17,9},{9,17},{1,25},{26,2},{18... | collective-permute-start | bytes 393224 | tf_op jit(solution)/shard_map/ppermute | solution.py:424
  44.8 1.3 %collective-permute-start.13 = (f32[4,64,128]{2,1,0:T(8,128)S(1)}, f32[4,64,128]{2,1,0:T(8,128)S(1)}, u32[]{:S(2)}, u32[]{:S(2)}) collective-permute-start(f32[4,64,128]{2,1,0:T(8,128)S(1)} %multiply_subtract_fusion.own_ref.refs_0_), channel_id=1, source_target_pairs={{16,0},{24,8},{0,16},{8,24},{17,1},{25,9},{1,17},{9,25},{18,2},{26... | collective-permute-start | bytes 393224 | tf_op jit(solution)/shard_map/ppermute | solution.py:424
  46.1 1.3 %collective-permute-start.14 = (f32[4,64,128]{2,1,0:T(8,128)S(1)}, f32[4,64,128]{2,1,0:T(8,128)S(1)}, u32[]{:S(2)}, u32[]{:S(2)}) collective-permute-start(f32[4,64,128]{2,1,0:T(8,128)S(1)} %multiply_subtract_fusion.own_ref.refs_0_), channel_id=1, source_target_pairs={{8,0},{0,8},{24,16},{16,24},{9,1},{1,9},{25,17},{17,25},{10,2},{2,... | collective-permute-start | bytes 393224 | tf_op jit(solution)/shard_map/ppermute | solution.py:424
  47.4 1.4 %diffuse_adjoint.1.refs_0_ = f32[4,64,128]{2,1,0:T(8,128)S(1)} custom-call(f32[3,10,32,128]{3,2,1,0:T(8,128)S(1)} %get-tuple-element.49.coef_ref, f32[4,64,128]{2,1,0:T(8,128)S(1)} %collective-permute-done.6.before_ref, f32[4,64,128]{2,1,0:T(8,128)S(1)} %collective-permute-done.7.after_ref, f32[4,64,128]{2,1,0:T(8,128)S(1)} %multiply_subtract_fusion.own_ref.refs_0_, ...), custom_call_target="tpu_custom_call" | custom-call | tf_op jit(solution)/shard_map/diffuse_adjoint/pallas_call | solution.py:576
  48.8 1.0 %collective-permute-start.9 = (f32[4,64,128]{2,1,0:T(8,128)S(1)}, f32[4,64,128]{2,1,0:T(8,128)S(1)}, u32[]{:S(2)}, u32[]{:S(2)}) collective-permute-start(f32[4,64,128]{2,1,0:T(8,128)S(1)} %diffuse_adjoint.1.refs_0_), channel_id=1, source_target_pairs={{24,0},{16,8},{8,16},{0,24},{25,1},{17,9},{9,17},{1,25},{26,2},{18... | collective-permute-start | bytes 393224 | tf_op jit(solution)/shard_map/ppermute | solution.py:424
  49.7 1.3 %collective-permute-start.10 = (f32[4,64,128]{2,1,0:T(8,128)S(1)}, f32[4,64,128]{2,1,0:T(8,128)S(1)}, u32[]{:S(2)}, u32[]{:S(2)}) collective-permute-start(f32[4,64,128]{2,1,0:T(8,128)S(1)} %diffuse_adjoint.1.refs_0_), channel_id=1, source_target_pairs={{16,0},{24,8},{0,16},{8,24},{17,1},{25,9},{1,17},{9,25},{18,2},{26... | collective-permute-start | bytes 393224 | tf_op jit(solution)/shard_map/ppermute | solution.py:424
  51.0 0.1 collective-permute-done.12.refs_1_
  51.1 1.2 %collective-permute-start.11 = (f32[4,64,128]{2,1,0:T(8,128)S(1)}, f32[4,64,128]{2,1,0:T(8,128)S(1)}, u32[]{:S(2)}, u32[]{:S(2)}) collective-permute-start(f32[4,64,128]{2,1,0:T(8,128)S(1)} %diffuse_adjoint.1.refs_0_), channel_id=1, source_target_pairs={{8,0},{0,8},{24,16},{16,24},{9,1},{1,9},{25,17},{17,25},{10,2},{2,... | collective-permute-start | bytes 393224 | tf_op jit(solution)/shard_map/ppermute | solution.py:424
  52.3 1.7 %collective-permute-done.13.refs_2_ = f32[4,64,128]{2,1,0:T(8,128)S(1)} collective-permute-done((f32[4,64,128]{2,1,0:T(8,128)S(1)}, f32[4,64,128]{2,1,0:T(8,128)S(1)}, u32[]{:S(2)}, u32[]{:S(2)}) %collective-permute-start.13) | collective-permute-done | bytes 131104 | tf_op jit(solution)/shard_map/ppermute | solution.py:424
  54.0 5.7 %members_gradient.1 = f32[8,16,64,128]{3,2,1,0:T(8,128)} custom-call(bf16[256,768]{1,0:T(8,128)(2,1)S(1)} %get-tuple-element.55.matrix_ref, f32[8,16,64,128]{3,2,1,0:T(8,128)S(1)} %get-tuple-element.56.control_ref, bf16[8,16,64,128]{3,2,1,0:T(8,128)(2,1)S(1)} %get-tuple-element.57.pert_ref, f32[4,64,128]{2,1,0:T(8,128)S(1)} %multiply_subtract_fusion.own_ref.refs_0_, ...), custom_call_target="tpu_custom_call" | custom-call | tf_op jit(solution)/shard_map/members_gradient/pallas_call | solution.py:588
  59.6 1.2 %static_gradient.1 = f32[16,64,128]{2,1,0:T(8,128)} custom-call(bf16[256,768]{1,0:T(8,128)(2,1)S(1)} %get-tuple-element.47.matrix_ref, f32[16,64,128]{2,1,0:T(8,128)S(1)} %get-tuple-element.48.static_ref, f32[4,64,128]{2,1,0:T(8,128)S(1)} %diffuse_adjoint.1.refs_0_, f32[4,64,128]{2,1,0:T(8,128)S(1)} %collective-permute-done.9.refs_1_, ...), custom_call_target="tpu_custom_call" | custom-call | tf_op jit(solution)/shard_map/static_gradient/pallas_call | solution.py:599
  (13 shorter events, 0.1 us)
Async XLA Ops:
  9.7 10.9 %collective-permute-start.3 = (f32[6,64,128]{2,1,0:T(8,128)S(1)}, f32[6,64,128]{2,1,0:T(8,128)S(1)}, u32[]{:S(2)}, u32[]{:S(2)}) collective-permute-start(f32[6,64,128]{2,1,0:T(8,128)S(1)} %get-tuple-element.34.refs_2_), channel_id=1, source_target_pairs={{0,2},{1,3},{2,4},{3,5},{4,6},{5,7},{6,0},{7,1},{8,10},{9,11},{10,... | collective-permute-start | bytes 589832 | tf_op jit(solution)/shard_map/ppermute | solution.py:419
  12.8 11.3 %collective-permute-start.4 = (f32[6,64,128]{2,1,0:T(8,128)S(1)}, f32[6,64,128]{2,1,0:T(8,128)S(1)}, u32[]{:S(2)}, u32[]{:S(2)}) collective-permute-start(f32[6,64,128]{2,1,0:T(8,128)S(1)} %get-tuple-element.34.refs_2_), channel_id=1, source_target_pairs={{0,6},{1,7},{2,0},{3,1},{4,2},{5,3},{6,4},{7,5},{8,14},{9,15},{10,... | collective-permute-start | bytes 589832 | tf_op jit(solution)/shard_map/ppermute | solution.py:419
  14.9 16.5 %all-to-all-start = ((f32[32,2,8,128]{3,2,1,0:T(8,128)}), f32[32,2,8,128]{3,2,1,0:T(8,128)S(1)}, u32[]{:S(2)}, u32[]{:S(2)}) async-start(f32[32,2,8,128]{3,2,1,0:T(8,128)} %get-tuple-element.37), calls=%async_computation | async-start | bytes 524288 | tf_op jit(solution)/shard_map/all_to_all | solution.py:511
  24.2 3.6 %collective-permute-start.5 = (f32[2,6,64,128]{3,2,1,0:T(8,128)S(1)}, f32[2,6,64,128]{3,2,1,0:T(8,128)S(1)}, u32[]{:S(2)}, u32[]{:S(2)}) collective-permute-start(f32[2,6,64,128]{3,2,1,0:T(8,128)S(1)} %pad_maximum_fusion), channel_id=1, source_target_pairs={{0,1},{1,0},{2,3},{3,2},{4,5},{5,4},{6,7},{7,6},{8,9},{9,8},{10,11... | collective-permute-start | bytes 1179656 | tf_op jit(solution)/shard_map/ppermute | solution.py:429
  24.3 11.2 %collective-permute-start.2 = (f32[4,64,128]{2,1,0:T(8,128)S(1)}, f32[4,64,128]{2,1,0:T(8,128)S(1)}, u32[]{:S(2)}, u32[]{:S(2)}) collective-permute-start(f32[4,64,128]{2,1,0:T(8,128)S(1)} %get-tuple-element.33), channel_id=1, source_target_pairs={{8,0},{0,8},{24,16},{16,24},{9,1},{1,9},{25,17},{17,25},{10,2},{2,... | collective-permute-start | bytes 393224 | tf_op jit(solution)/shard_map/ppermute | solution.py:514
  25.8 9.6 %collective-permute-start.1 = (f32[4,64,128]{2,1,0:T(8,128)S(1)}, f32[4,64,128]{2,1,0:T(8,128)S(1)}, u32[]{:S(2)}, u32[]{:S(2)}) collective-permute-start(f32[4,64,128]{2,1,0:T(8,128)S(1)} %get-tuple-element.32), channel_id=1, source_target_pairs={{16,0},{24,8},{0,16},{8,24},{17,1},{25,9},{1,17},{9,25},{18,2},{26... | collective-permute-start | bytes 393224 | tf_op jit(solution)/shard_map/ppermute | solution.py:514
  27.3 8.1 %collective-permute-start = (f32[4,64,128]{2,1,0:T(8,128)S(1)}, f32[4,64,128]{2,1,0:T(8,128)S(1)}, u32[]{:S(2)}, u32[]{:S(2)}) collective-permute-start(f32[4,64,128]{2,1,0:T(8,128)S(1)} %get-tuple-element.31), channel_id=1, source_target_pairs={{24,0},{16,8},{8,16},{0,24},{25,1},{17,9},{9,17},{1,25},{26,2},{18... | collective-permute-start | bytes 393224 | tf_op jit(solution)/shard_map/ppermute | solution.py:514
  35.5 8.2 %collective-permute-start.6 = (f32[4,64,128]{2,1,0:T(8,128)S(1)}, f32[4,64,128]{2,1,0:T(8,128)S(1)}, u32[]{:S(2)}, u32[]{:S(2)}) collective-permute-start(f32[4,64,128]{2,1,0:T(8,128)S(1)} %multiply_subtract_fusion.own_ref.refs_0_), channel_id=1, source_target_pairs={{0,2},{1,3},{2,4},{3,5},{4,6},{5,7},{6,0},{7,1},{8,10},{9,11},{10,... | collective-permute-start | bytes 393224 | tf_op jit(solution)/shard_map/ppermute | solution.py:419
  35.7 8.0 %collective-permute-start.7 = (f32[4,64,128]{2,1,0:T(8,128)S(1)}, f32[4,64,128]{2,1,0:T(8,128)S(1)}, u32[]{:S(2)}, u32[]{:S(2)}) collective-permute-start(f32[4,64,128]{2,1,0:T(8,128)S(1)} %multiply_subtract_fusion.own_ref.refs_0_), channel_id=1, source_target_pairs={{0,6},{1,7},{2,0},{3,1},{4,2},{5,3},{6,4},{7,5},{8,14},{9,15},{10,... | collective-permute-start | bytes 393224 | tf_op jit(solution)/shard_map/ppermute | solution.py:419
  43.7 3.6 %collective-permute-start.8 = (f32[2,4,64,128]{3,2,1,0:T(8,128)S(1)}, f32[2,4,64,128]{3,2,1,0:T(8,128)S(1)}, u32[]{:S(2)}, u32[]{:S(2)}) collective-permute-start(f32[2,4,64,128]{3,2,1,0:T(8,128)S(1)} %pad_maximum_fusion.1), channel_id=1, source_target_pairs={{0,1},{1,0},{2,3},{3,2},{4,5},{5,4},{6,7},{7,6},{8,9},{9,8},{10,11... | collective-permute-start | bytes 786440 | tf_op jit(solution)/shard_map/ppermute | solution.py:429
  43.8 7.3 %collective-permute-start.12 = (f32[4,64,128]{2,1,0:T(8,128)S(1)}, f32[4,64,128]{2,1,0:T(8,128)S(1)}, u32[]{:S(2)}, u32[]{:S(2)}) collective-permute-start(f32[4,64,128]{2,1,0:T(8,128)S(1)} %multiply_subtract_fusion.own_ref.refs_0_), channel_id=1, source_target_pairs={{24,0},{16,8},{8,16},{0,24},{25,1},{17,9},{9,17},{1,25},{26,2},{18... | collective-permute-start | bytes 393224 | tf_op jit(solution)/shard_map/ppermute | solution.py:424
  44.8 9.2 %collective-permute-start.13 = (f32[4,64,128]{2,1,0:T(8,128)S(1)}, f32[4,64,128]{2,1,0:T(8,128)S(1)}, u32[]{:S(2)}, u32[]{:S(2)}) collective-permute-start(f32[4,64,128]{2,1,0:T(8,128)S(1)} %multiply_subtract_fusion.own_ref.refs_0_), channel_id=1, source_target_pairs={{16,0},{24,8},{0,16},{8,24},{17,1},{25,9},{1,17},{9,25},{18,2},{26... | collective-permute-start | bytes 393224 | tf_op jit(solution)/shard_map/ppermute | solution.py:424
  46.1 7.9 %collective-permute-start.14 = (f32[4,64,128]{2,1,0:T(8,128)S(1)}, f32[4,64,128]{2,1,0:T(8,128)S(1)}, u32[]{:S(2)}, u32[]{:S(2)}) collective-permute-start(f32[4,64,128]{2,1,0:T(8,128)S(1)} %multiply_subtract_fusion.own_ref.refs_0_), channel_id=1, source_target_pairs={{8,0},{0,8},{24,16},{16,24},{9,1},{1,9},{25,17},{17,25},{10,2},{2,... | collective-permute-start | bytes 393224 | tf_op jit(solution)/shard_map/ppermute | solution.py:424
  48.8 10.9 %collective-permute-start.9 = (f32[4,64,128]{2,1,0:T(8,128)S(1)}, f32[4,64,128]{2,1,0:T(8,128)S(1)}, u32[]{:S(2)}, u32[]{:S(2)}) collective-permute-start(f32[4,64,128]{2,1,0:T(8,128)S(1)} %diffuse_adjoint.1.refs_0_), channel_id=1, source_target_pairs={{24,0},{16,8},{8,16},{0,24},{25,1},{17,9},{9,17},{1,25},{26,2},{18... | collective-permute-start | bytes 393224 | tf_op jit(solution)/shard_map/ppermute | solution.py:424
  49.7 9.9 %collective-permute-start.10 = (f32[4,64,128]{2,1,0:T(8,128)S(1)}, f32[4,64,128]{2,1,0:T(8,128)S(1)}, u32[]{:S(2)}, u32[]{:S(2)}) collective-permute-start(f32[4,64,128]{2,1,0:T(8,128)S(1)} %diffuse_adjoint.1.refs_0_), channel_id=1, source_target_pairs={{16,0},{24,8},{0,16},{8,24},{17,1},{25,9},{1,17},{9,25},{18,2},{26... | collective-permute-start | bytes 393224 | tf_op jit(solution)/shard_map/ppermute | solution.py:424
  51.1 8.5 %collective-permute-start.11 = (f32[4,64,128]{2,1,0:T(8,128)S(1)}, f32[4,64,128]{2,1,0:T(8,128)S(1)}, u32[]{:S(2)}, u32[]{:S(2)}) collective-permute-start(f32[4,64,128]{2,1,0:T(8,128)S(1)} %diffuse_adjoint.1.refs_0_), channel_id=1, source_target_pairs={{8,0},{0,8},{24,16},{16,24},{9,1},{1,9},{25,17},{17,25},{10,2},{2,... | collective-permute-start | bytes 393224 | tf_op jit(solution)/shard_map/ppermute | solution.py:424

commit v15 on v14

--- a/solution.py
+++ b/solution.py
@@ -146,14 +146,15 @@
 
 
 def observe_kernel(n_cols, cap_rows, scale, *refs):
-    n_ens = len(refs) - 31
+    n_ens = len(refs) - 32
     sources, (out_ref, packed_ref), parts = refs[:10], refs[10:12], refs[12 : 12 + n_ens]
     refs = refs[12 + n_ens :]
-    (acc_ref, fold_ref, matrix_ref, part_ref), landed, sems, slots = (
+    (acc_ref, fold_ref, matrix_ref, part_ref), landed, sems, slots, sums_ref = (
         refs[:4],
         refs[4:14],
         refs[14],
         (refs[15:17], refs[17:19]),
+        refs[19],
     )
     slot_ref, weight_ref, innov_ref, local_ref, control_ref, pert_ref, *static_refs = landed
     coarse = acc_ref.shape[1]
@@ -202,10 +203,15 @@
         )
         for t in range(2)
     )
-    for e in range(n_ens):
-        for p in range(n_cols):
-            out_ref[e * n_cols + p, 0] = weights[p * cap_rows : (p + 1) * cap_rows]
-            out_ref[e * n_cols + p, 1] = amounts[p * cap_rows : (p + 1) * cap_rows]
+    for p in range(n_cols):
+        sums_ref[p, 0] = weights[p * cap_rows : (p + 1) * cap_rows]
+        sums_ref[p, 1] = amounts[p * cap_rows : (p + 1) * cap_rows]
+    writes = [
+        pltpu.make_async_copy(sums_ref, out_ref.at[pl.ds(e * n_cols, n_cols)], sems.at[len(copies) + e])
+        for e in range(n_ens)
+    ]
+    for write in writes:
+        write.start()
     for copy in copies[3:]:
         copy.wait()
     prepare(*static_refs, packed_ref)
@@ -215,6 +221,8 @@
     for d, part in enumerate(parts):
         at = peer(lax.axis_index("ens"), d, n_ens) * share
         part[...] = part_ref[pl.ds(at, share)]
+    for write in writes:
+        write.wait()
 
 
 def sum_members(matrix_ref, control_ref, pert_ref, out_ref):
@@ -280,16 +288,20 @@
     return jnp.where(lane == 0, pltpu.roll(near, 1, 0), near)
 
 
-def rows_of(before_ref, after_ref, own_ref, other_ref, plane, rows):
+def rows_of(second_ref, first_ref, own_ref, other_ref, plane, rows):
     at = lax.axis_index("cols")
     count = lax.axis_size("cols")
-    core = at % 2
+    core, chip = at % 2, at // 2 % 2
     reads = [pl.ds(r, own_ref.shape[1] // rows, stride=rows) for r in range(rows)]
-    out = [jnp.where(at >= 2, before_ref[plane, r, :], f32(0)) for r in reads]
+    first = [first_ref[plane, r, :] for r in reads]
+    second = [second_ref[plane, r, :] for r in reads]
+    out = [jnp.where(jnp.logical_and(chip == 1, at >= 2), f, f32(0)) for f in first]
+    out = [jnp.where(jnp.logical_and(chip == 0, at >= 2), s, o) for s, o in zip(second, out)]
     out += [jnp.where(at >= 1, other_ref[1 - core, plane, r, :], f32(0)) for r in reads]
     out += [own_ref[plane, r, :] for r in reads]
     out += [jnp.where(at < count - 1, other_ref[core, plane, r, :], f32(0)) for r in reads]
-    return out + [jnp.where(at < count - 2, after_ref[plane, r, :], f32(0)) for r in reads]
+    last = [jnp.where(jnp.logical_and(chip == 0, at < count - 2), f, f32(0)) for f in first]
+    return out + [jnp.where(jnp.logical_and(chip == 1, at < count - 2), s, o) for s, o in zip(second, last)]
 
 
 def diffuse_rows(tiles, level, coef_ref, rows):
@@ -307,12 +319,12 @@
 
 
 def first_diffusion_kernel(lev_share, rows, *refs):
-    before_ref, after_ref, own_ref, other_ref, *sources = refs[:6]
+    second_ref, first_ref, own_ref, other_ref, *sources = refs[:6]
     out_ref, coef_ref, row_ref, lane_ref, *landed, sems = refs[6:]
     copies = [pltpu.make_async_copy(s, t, sems.at[i]) for i, (s, t) in enumerate(zip(sources, landed))]
     for copy in copies:
         copy.start()
-    tiles = (before_ref, after_ref, own_ref, other_ref)
+    tiles = (second_ref, first_ref, own_ref, other_ref)
     blocks = own_ref.shape[1] // rows
     side = 2
     north = rows_of(*tiles, lev_share, rows)
@@ -339,8 +351,8 @@
     list_cells(rows, blocks * LANES, *landed, row_ref, lane_ref)
 
 
-def second_diffusion_kernel(rows, coef_ref, before_ref, after_ref, own_ref, other_ref, out_ref):
-    tiles = (before_ref, after_ref, own_ref, other_ref)
+def second_diffusion_kernel(rows, coef_ref, second_ref, first_ref, own_ref, other_ref, out_ref):
+    tiles = (second_ref, first_ref, own_ref, other_ref)
     lev_share = out_ref.shape[0]
     blocks = own_ref.shape[1] // rows
 
@@ -414,9 +426,17 @@
             out_ref[:, at, :] = static_ref[:, at, :] + part.reshape(levels, 16, LANES)
 
 
-def shifted(x):
+def exchanged(x, starts):
     count = lax.axis_size("cols")
-    return [lax.ppermute(x, "cols", [(i, (i + by) % count) for i in range(count)]) for by in (2, -2)]
+    out = []
+    for start in starts:
+        pairs = []
+        for i in range(count):
+            chip, core = divmod(i, 2)
+            partner = (chip + start ^ 1) - start
+            pairs.append((i, 2 * partner + core if 0 <= 2 * partner + core < count else i))
+        out.append(lax.ppermute(x, "cols", pairs))
+    return out
 
 
 def from_peers(x):
@@ -424,8 +444,9 @@
     return [lax.ppermute(x, "ens", [(peer(i, d, count), i) for i in range(count)]) for d in range(count - 1, 0, -1)]
 
 
-def swapped(own, before, after):
-    pack = jnp.stack([own, jnp.where(lax.axis_index("cols") % 2 == 1, before, after)])
+def swapped(own, first, second):
+    at = lax.axis_index("cols")
+    pack = jnp.stack([own, jnp.where(at % 2 == at // 2 % 2, first, second)])
     return lax.ppermute(pack, "cols", [(i, i ^ 1) for i in range(lax.axis_size("cols"))])
 
 
@@ -470,7 +491,7 @@
         functools.partial(observe_kernel, n_cols, cap_rows, member_scale),
         grid=(1,),
         in_specs=[pl.BlockSpec(memory_space=pl.ANY)] * 10,
-        out_specs=[whole(n_ens * n_cols, 2, cap_rows, LANES)] + [VMEM] * (1 + n_ens),
+        out_specs=[pl.BlockSpec(memory_space=pl.ANY)] + [VMEM] * (1 + n_ens),
         out_shape=[
             pltpu.HBM((n_ens * n_cols, 2, cap_rows, LANES), f32),
             pltpu.VMEM((lev_share + 2, per_level, LANES), f32),
@@ -491,9 +512,10 @@
             pltpu.VMEM((levels, per_level, LANES), f32),
             pltpu.VMEM((per_level, LANES), f32),
             pltpu.VMEM((per_level, LANES), f32),
-            pltpu.SemaphoreType.DMA((10,)),
+            pltpu.SemaphoreType.DMA((10 + n_ens,)),
         ]
-        + [pltpu.VMEM((coarse, 8 * LANES), bf16), pltpu.VMEM((4 * FINE, 8 * LANES), bf16)] * 2,
+        + [pltpu.VMEM((coarse, 8 * LANES), bf16), pltpu.VMEM((4 * FINE, 8 * LANES), bf16)] * 2
+        + [pltpu.VMEM((n_cols, 2, cap_rows, LANES), f32)],
         compiler_params=params(24),
         name="slot_sums_and_members",
     )(
@@ -509,12 +531,12 @@
         in_hbm(tiled(face_east)),
     )
     slots = lax.all_to_all(slots, ("ens", "cols"), split_axis=0, concat_axis=0, tiled=True)
-    before, after = shifted(packed)
+    second, first = exchanged(packed, (1, 0))
     sums = [parts[0]] + [
         lax.ppermute(parts[back(d, n_ens)], "ens", [(peer(i, d, n_ens), i) for i in range(n_ens)])
         for d in range(n_ens - 1, 0, -1)
     ]
-    other = swapped(packed, before, after)
+    other = swapped(packed, first, second)
 
     increment, coefs, entry_row, entry_lane = pl.pallas_call(
         functools.partial(first_diffusion_kernel, lev_share, rows),
@@ -534,7 +556,7 @@
         compiler_params=params(8),
         cost_estimate=pl.CostEstimate(flops=1 << 26, bytes_accessed=1 << 22, transcendentals=0),
         name="diffuse_forward",
-    )(before, after, packed, other, in_hbm(send_index), in_hbm(send_count))
+    )(second, first, packed, other, in_hbm(send_index), in_hbm(send_count))
 
     increment, coefs, slots = lax.optimization_barrier((increment, coefs, slots))
     slot_sums, static_here, control_here, pert_here = pl.pallas_call(
@@ -556,7 +578,7 @@
     slot_sums = slot_sums.reshape(2, lev_share, per_level, LANES)
     tile = functools.reduce(jnp.add, sums) + increment
     tile = tile * slot_sums[0] - slot_sums[1]
-    tile_before, tile_after = shifted(tile)
+    tile_first, tile_second = exchanged(tile, (0, 1))
     adjoints = [tile] + from_peers(tile)
     tile, vertical_local, vertical_root = lax.optimization_barrier((tile, vertical_local, vertical_root))
     from_local, from_root = pl.pallas_call(
@@ -568,10 +590,10 @@
         compiler_params=params(8),
         name="level_matrices",
     )(in_hbm(vertical_local), in_hbm(vertical_root))
-    tile_before, tile_after, from_local, from_root = lax.optimization_barrier(
-        (tile_before, tile_after, from_local, from_root)
+    tile_first, tile_second, from_local, from_root = lax.optimization_barrier(
+        (tile_first, tile_second, from_local, from_root)
     )
-    tile_other = swapped(tile, tile_before, tile_after)
+    tile_other = swapped(tile, tile_first, tile_second)
 
     smooth = pl.pallas_call(
         functools.partial(second_diffusion_kernel, rows),
@@ -580,7 +602,7 @@
         out_shape=pltpu.VMEM((lev_share, per_level, LANES), f32),
         compiler_params=params(8),
         name="diffuse_adjoint",
-    )(coefs, tile_before, tile_after, tile, tile_other)
+    )(coefs, tile_second, tile_first, tile, tile_other)
     smooth, from_local = lax.optimization_barrier((smooth, from_local))
     smooths = [smooth] + from_peers(smooth)
 

time: 61.1 us -> 57.7 us (0.944); the launches traced: 60.9 us -> 56.8 us
  waiting for transfers between devices: 11.9 us -> 10.2 us
  starting transfers between devices: 23.9 us -> 22.2 us
  Pallas kernels: 24.2 us -> 23.5 us
    ppermute x4, waiting for transfers between devices: 8.04 us -> 4.36 us  [exchanged(): out.append(lax.ppermute(x, 'cols', pairs))]
    all_to_all x1, waiting for transfers between devices: 1.99 us -> 4.09 us  [local(): lax.all_to_all(slots, ('ens', 'cols'), split_axis=0, concat_axis=0, tiled...]
    ppermute x4, starting transfers between devices: 9.04 us -> 7.77 us  [exchanged(): out.append(lax.ppermute(x, 'cols', pairs))]
    pallas_call x1, Pallas kernels: 9.11 us -> 8.45 us  [local(): pl.pallas_call(functools.partial(observe_kernel, n_cols, cap_rows, member...]
    all_to_all x1, starting transfers between devices: 4.21 us -> 3.6 us  [local(): lax.all_to_all(slots, ('ens', 'cols'), split_axis=0, concat_axis=0, tiled...]
  transfers between devices with their start and end apart: 16 -> 16, of which waited for: 6 -> 4; matrix products, arithmetic and copies ran while one was open for 0% -> 0% of each run, Pallas kernels for 23% -> 24%
where the time goes in v15:
time: 57.7 us; the launch traced here: 56.8 us
  Pallas kernels  23.5 us (41%)
  starting transfers between devices  22.2 us (38%)
  waiting for transfers between devices  10.2 us (18%)
  between operations  0.81 us (1%)
    pallas_call x1, Pallas kernels, local(): pl.pallas_call(functools.partial(observe_kernel, n_cols, cap_rows, member...  8.45 us
    ppermute x4, starting transfers between devices, exchanged(): out.append(lax.ppermute(x, 'cols', pairs))  7.77 us
    ppermute x6, starting transfers between devices, from_peers(): lax.ppermute(x, 'ens', [(peer(i, d, count), i) for i in range(count)])  7.11 us
    pallas_call x1, Pallas kernels, local(): pl.pallas_call(member_kernel, grid=(members // group,), in_specs=[VMEM] *...  5.65 us
    ppermute x4, waiting for transfers between devices, exchanged(): out.append(lax.ppermute(x, 'cols', pairs))  4.36 us
    all_to_all x1, waiting for transfers between devices, local(): lax.all_to_all(slots, ('ens', 'cols'), split_axis=0, concat_axis=0, tiled...  4.09 us
    pallas_call x1, Pallas kernels, local(): pl.pallas_call(functools.partial(scatter_kernel, cap_rows), in_specs=[VME...  4 us
    all_to_all x1, starting transfers between devices, local(): lax.all_to_all(slots, ('ens', 'cols'), split_axis=0, concat_axis=0, tiled...  3.6 us
  transfers between devices with their start and end apart: 16, of which 4 were waited for; matrix products, arithmetic and copies ran while one was open for 0% of the time, Pallas kernels for 24%

profile of v15, /device:TPU:0, one launch (start us, length us, event | category | flops | bytes accessed | tf_op | source)
XLA Modules:
  0.0 56.8 jit_solution(14361441704288992389)
XLA Ops:
  0.6 8.4 %slot_sums_and_members.1 = (f32[32,2,8,128]{3,2,1,0:T(8,128)}, f32[6,64,128]{2,1,0:T(8,128)S(1)}, f32[4,64,128]{2,1,0:T(8,128)S(1)}, f32[4,64,128]{2,1,0:T(8,128...) custom-call(s32[512,128]{1,0:T(8,128)} %bitcast.58, f32[512,128]{1,0:T(8,128)} %bitcast.59, ...), custom_call_target="tpu_custom_call" | custom-call | tf_op jit(solution)/shard_map/slot_sums_and_members/pallas_call | solution.py:490
  9.1 0.7 %collective-permute-start.3 = (f32[6,64,128]{2,1,0:T(8,128)S(1)}, f32[6,64,128]{2,1,0:T(8,128)S(1)}, u32[]{:S(2)}, u32[]{:S(2)}) collective-permute-start(f32[6,64,128]{2,1,0:T(8,128)S(1)} %get-tuple-element.34.refs_2_), channel_id=1, source_target_pairs={{0,0},{1,1},{2,4},{3,5},{4,2},{5,3},{6,6},{7,7},{8,8},{9,9},{10,12... | collective-permute-start | bytes 589832 | tf_op jit(solution)/shard_map/ppermute | solution.py:438
  9.8 5.9 %collective-permute-start.4 = (f32[6,64,128]{2,1,0:T(8,128)S(1)}, f32[6,64,128]{2,1,0:T(8,128)S(1)}, u32[]{:S(2)}, u32[]{:S(2)}) collective-permute-start(f32[6,64,128]{2,1,0:T(8,128)S(1)} %get-tuple-element.34.refs_2_), channel_id=1, source_target_pairs={{0,2},{1,3},{2,0},{3,1},{4,6},{5,7},{6,4},{7,5},{8,10},{9,11},{10,... | collective-permute-start | bytes 589832 | tf_op jit(solution)/shard_map/ppermute | solution.py:438
  15.7 3.6 %all-to-all-start = ((f32[32,2,8,128]{3,2,1,0:T(8,128)}), f32[32,2,8,128]{3,2,1,0:T(8,128)S(1)}, u32[]{:S(2)}, u32[]{:S(2)}) async-start(f32[32,2,8,128]{3,2,1,0:T(8,128)} %get-tuple-element.37), calls=%async_computation | async-start | bytes 524288 | tf_op jit(solution)/shard_map/all_to_all | solution.py:533
  19.3 0.0 collective-permute-done.3.refs_0_
  19.3 1.0 %collective-permute-done.4.refs_1_ = f32[6,64,128]{2,1,0:T(8,128)S(1)} collective-permute-done((f32[6,64,128]{2,1,0:T(8,128)S(1)}, f32[6,64,128]{2,1,0:T(8,128)S(1)}, u32[]{:S(2)}, u32[]{:S(2)}) %collective-permute-start.4) | collective-permute-done | bytes 196640 | tf_op jit(solution)/shard_map/ppermute | solution.py:438
  20.4 0.1 collective-permute-start.5
  20.4 1.6 %collective-permute-start.2 = (f32[4,64,128]{2,1,0:T(8,128)S(1)}, f32[4,64,128]{2,1,0:T(8,128)S(1)}, u32[]{:S(2)}, u32[]{:S(2)}) collective-permute-start(f32[4,64,128]{2,1,0:T(8,128)S(1)} %get-tuple-element.33), channel_id=1, source_target_pairs={{8,0},{0,8},{24,16},{16,24},{9,1},{1,9},{25,17},{17,25},{10,2},{2,... | collective-permute-start | bytes 393224 | tf_op jit(solution)/shard_map/ppermute | solution.py:536
  22.0 1.5 %collective-permute-start.1 = (f32[4,64,128]{2,1,0:T(8,128)S(1)}, f32[4,64,128]{2,1,0:T(8,128)S(1)}, u32[]{:S(2)}, u32[]{:S(2)}) collective-permute-start(f32[4,64,128]{2,1,0:T(8,128)S(1)} %get-tuple-element.32), channel_id=1, source_target_pairs={{16,0},{24,8},{0,16},{8,24},{17,1},{25,9},{1,17},{9,25},{18,2},{26... | collective-permute-start | bytes 393224 | tf_op jit(solution)/shard_map/ppermute | solution.py:536
  23.5 0.5 collective-permute-start
  24.0 0.0 collective-permute-done.5.refs_3_
  24.0 1.6 %diffuse_forward.1 = (f32[4,64,128]{2,1,0:T(8,128)S(1)}, f32[3,10,32,128]{3,2,1,0:T(8,128)S(1)}, s32[64,128]{1,0:T(8,128)S(1)}, s32[64,128]{1,0:T(8,128)S(1)}) custom-call(f32[6,64,128]{2,1,0:T(8,128)S(1)} %collective-permute-done.3.refs_0_, f32[6,64,128]{2,1,0:T(8,128)S(1)} %collective-permute-done.4.refs_1_, f32[6,64,128]{2,1,0:T(8,128)S(1)} %get-tuple-element.34.refs_2_, ...), custom_call_target="tpu_custom_call" | custom-call | flops 67108864 | bytes 4194304 | tf_op jit(solution)/shard_map/diffuse_forward/pallas_call | solution.py:541
  25.6 4.1 %all-to-all-done.slots_ref = f32[32,2,8,128]{3,2,1,0:T(8,128)S(1)} async-done(((f32[32,2,8,128]{3,2,1,0:T(8,128)}), f32[32,2,8,128]{3,2,1,0:T(8,128)S(1)}, u32[]{:S(2)}, u32[]{:S(2)}) %all-to-all-start) | async-done | bytes 262176 | tf_op jit(solution)/shard_map/all_to_all | solution.py:533
  29.7 4.0 %scatter.1 = (f32[2,256,128]{2,1,0:T(8,128)S(1)}, f32[16,64,128]{2,1,0:T(8,128)S(1)}, f32[8,16,64,128]{3,2,1,0:T(8,128)S(1)}, bf16[8,16,64,128]{3,2,1,0:T(8,128)(2,1)S(1)}) custom-call(s32[64,128]{1,0:T(8,128)S(1)} %get-tuple-element.39.row_ref, s32[64,128]{1,0:T(8,128)S(1)} %get-tuple-element.40.lane_ref, f32[32,2,8,128]{3,2,1,0:T(8,128)S(1)} %all-to-all-done.slots_ref, ...), custom_call_target="tpu_custom_call" | custom-call | flops 2147483648 | bytes 8388608 | tf_op jit(solution)/shard_map/scatter/pallas_call | solution.py:562
  33.7 0.0 collective-permute-done
  33.7 0.1 multiply_subtract_fusion.own_ref.refs_0_
  33.8 0.5 collective-permute-start.6
  34.3 0.7 %collective-permute-start.7 = (f32[4,64,128]{2,1,0:T(8,128)S(1)}, f32[4,64,128]{2,1,0:T(8,128)S(1)}, u32[]{:S(2)}, u32[]{:S(2)}) collective-permute-start(f32[4,64,128]{2,1,0:T(8,128)S(1)} %multiply_subtract_fusion.own_ref.refs_0_), channel_id=1, source_target_pairs={{0,0},{1,1},{2,4},{3,5},{4,2},{5,3},{6,6},{7,7},{8,8},{9,9},{10,12... | collective-permute-start | bytes 393224 | tf_op jit(solution)/shard_map/ppermute | solution.py:438
  35.0 1.2 %level_matrices.1 = (bf16[256,768]{1,0:T(8,128)(2,1)S(1)}, bf16[256,768]{1,0:T(8,128)(2,1)S(1)}) custom-call(f32[16,16]{1,0:T(8,128)} %local_ref, f32[16,16]{1,0:T(8,128)} %root_ref), custom_call_target="tpu_custom_call" | custom-call | tf_op jit(solution)/shard_map/level_matrices/pallas_call | solution.py:584
  36.3 3.4 %collective-permute-done.6.first_ref = f32[4,64,128]{2,1,0:T(8,128)S(1)} collective-permute-done((f32[4,64,128]{2,1,0:T(8,128)S(1)}, f32[4,64,128]{2,1,0:T(8,128)S(1)}, u32[]{:S(2)}, u32[]{:S(2)}) %collective-permute-start.6) | collective-permute-done | bytes 131104 | tf_op jit(solution)/shard_map/ppermute | solution.py:438
  39.6 0.0 collective-permute-done.7.second_ref
  39.7 0.1 collective-permute-start.8
  39.8 1.0 %collective-permute-start.12 = (f32[4,64,128]{2,1,0:T(8,128)S(1)}, f32[4,64,128]{2,1,0:T(8,128)S(1)}, u32[]{:S(2)}, u32[]{:S(2)}) collective-permute-start(f32[4,64,128]{2,1,0:T(8,128)S(1)} %multiply_subtract_fusion.own_ref.refs_0_), channel_id=1, source_target_pairs={{24,0},{16,8},{8,16},{0,24},{25,1},{17,9},{9,17},{1,25},{26,2},{18... | collective-permute-start | bytes 393224 | tf_op jit(solution)/shard_map/ppermute | solution.py:444
  40.7 1.5 %collective-permute-start.13 = (f32[4,64,128]{2,1,0:T(8,128)S(1)}, f32[4,64,128]{2,1,0:T(8,128)S(1)}, u32[]{:S(2)}, u32[]{:S(2)}) collective-permute-start(f32[4,64,128]{2,1,0:T(8,128)S(1)} %multiply_subtract_fusion.own_ref.refs_0_), channel_id=1, source_target_pairs={{16,0},{24,8},{0,16},{8,24},{17,1},{25,9},{1,17},{9,25},{18,2},{26... | collective-permute-start | bytes 393224 | tf_op jit(solution)/shard_map/ppermute | solution.py:444
  42.2 1.1 %collective-permute-start.14 = (f32[4,64,128]{2,1,0:T(8,128)S(1)}, f32[4,64,128]{2,1,0:T(8,128)S(1)}, u32[]{:S(2)}, u32[]{:S(2)}) collective-permute-start(f32[4,64,128]{2,1,0:T(8,128)S(1)} %multiply_subtract_fusion.own_ref.refs_0_), channel_id=1, source_target_pairs={{8,0},{0,8},{24,16},{16,24},{9,1},{1,9},{25,17},{17,25},{10,2},{2,... | collective-permute-start | bytes 393224 | tf_op jit(solution)/shard_map/ppermute | solution.py:444
  43.3 1.3 %diffuse_adjoint.1.refs_0_ = f32[4,64,128]{2,1,0:T(8,128)S(1)} custom-call(f32[3,10,32,128]{3,2,1,0:T(8,128)S(1)} %get-tuple-element.49.coef_ref, f32[4,64,128]{2,1,0:T(8,128)S(1)} %collective-permute-done.7.second_ref, f32[4,64,128]{2,1,0:T(8,128)S(1)} %collective-permute-done.6.first_ref, f32[4,64,128]{2,1,0:T(8,128)S(1)} %multiply_subtract_fusion.own_ref.refs_0_, ...), custom_call_target="tpu_custom_call" | custom-call | tf_op jit(solution)/shard_map/diffuse_adjoint/pallas_call | solution.py:598
  44.7 1.0 %collective-permute-start.9 = (f32[4,64,128]{2,1,0:T(8,128)S(1)}, f32[4,64,128]{2,1,0:T(8,128)S(1)}, u32[]{:S(2)}, u32[]{:S(2)}) collective-permute-start(f32[4,64,128]{2,1,0:T(8,128)S(1)} %diffuse_adjoint.1.refs_0_), channel_id=1, source_target_pairs={{24,0},{16,8},{8,16},{0,24},{25,1},{17,9},{9,17},{1,25},{26,2},{18... | collective-permute-start | bytes 393224 | tf_op jit(solution)/shard_map/ppermute | solution.py:444
  45.6 1.5 %collective-permute-start.10 = (f32[4,64,128]{2,1,0:T(8,128)S(1)}, f32[4,64,128]{2,1,0:T(8,128)S(1)}, u32[]{:S(2)}, u32[]{:S(2)}) collective-permute-start(f32[4,64,128]{2,1,0:T(8,128)S(1)} %diffuse_adjoint.1.refs_0_), channel_id=1, source_target_pairs={{16,0},{24,8},{0,16},{8,24},{17,1},{25,9},{1,17},{9,25},{18,2},{26... | collective-permute-start | bytes 393224 | tf_op jit(solution)/shard_map/ppermute | solution.py:444
  47.1 1.1 %collective-permute-start.11 = (f32[4,64,128]{2,1,0:T(8,128)S(1)}, f32[4,64,128]{2,1,0:T(8,128)S(1)}, u32[]{:S(2)}, u32[]{:S(2)}) collective-permute-start(f32[4,64,128]{2,1,0:T(8,128)S(1)} %diffuse_adjoint.1.refs_0_), channel_id=1, source_target_pairs={{8,0},{0,8},{24,16},{16,24},{9,1},{1,9},{25,17},{17,25},{10,2},{2,... | collective-permute-start | bytes 393224 | tf_op jit(solution)/shard_map/ppermute | solution.py:444
  48.2 1.7 %collective-permute-done.13.refs_2_ = f32[4,64,128]{2,1,0:T(8,128)S(1)} collective-permute-done((f32[4,64,128]{2,1,0:T(8,128)S(1)}, f32[4,64,128]{2,1,0:T(8,128)S(1)}, u32[]{:S(2)}, u32[]{:S(2)}) %collective-permute-start.13) | collective-permute-done | bytes 131104 | tf_op jit(solution)/shard_map/ppermute | solution.py:444
  49.9 5.6 %members_gradient.1 = f32[8,16,64,128]{3,2,1,0:T(8,128)} custom-call(bf16[256,768]{1,0:T(8,128)(2,1)S(1)} %get-tuple-element.55.matrix_ref, f32[8,16,64,128]{3,2,1,0:T(8,128)S(1)} %get-tuple-element.56.control_ref, bf16[8,16,64,128]{3,2,1,0:T(8,128)(2,1)S(1)} %get-tuple-element.57.pert_ref, f32[4,64,128]{2,1,0:T(8,128)S(1)} %multiply_subtract_fusion.own_ref.refs_0_, ...), custom_call_target="tpu_custom_call" | custom-call | tf_op jit(solution)/shard_map/members_gradient/pallas_call | solution.py:610
  55.6 1.2 %static_gradient.1 = f32[16,64,128]{2,1,0:T(8,128)} custom-call(bf16[256,768]{1,0:T(8,128)(2,1)S(1)} %get-tuple-element.47.matrix_ref, f32[16,64,128]{2,1,0:T(8,128)S(1)} %get-tuple-element.48.static_ref, f32[4,64,128]{2,1,0:T(8,128)S(1)} %diffuse_adjoint.1.refs_0_, f32[4,64,128]{2,1,0:T(8,128)S(1)} %collective-permute-done.9.refs_1_, ...), custom_call_target="tpu_custom_call" | custom-call | tf_op jit(solution)/shard_map/static_gradient/pallas_call | solution.py:621
  (13 shorter events, 0.1 us)
Async XLA Ops:
  9.1 10.2 %collective-permute-start.3 = (f32[6,64,128]{2,1,0:T(8,128)S(1)}, f32[6,64,128]{2,1,0:T(8,128)S(1)}, u32[]{:S(2)}, u32[]{:S(2)}) collective-permute-start(f32[6,64,128]{2,1,0:T(8,128)S(1)} %get-tuple-element.34.refs_2_), channel_id=1, source_target_pairs={{0,0},{1,1},{2,4},{3,5},{4,2},{5,3},{6,6},{7,7},{8,8},{9,9},{10,12... | collective-permute-start | bytes 589832 | tf_op jit(solution)/shard_map/ppermute | solution.py:438
  9.8 10.5 %collective-permute-start.4 = (f32[6,64,128]{2,1,0:T(8,128)S(1)}, f32[6,64,128]{2,1,0:T(8,128)S(1)}, u32[]{:S(2)}, u32[]{:S(2)}) collective-permute-start(f32[6,64,128]{2,1,0:T(8,128)S(1)} %get-tuple-element.34.refs_2_), channel_id=1, source_target_pairs={{0,2},{1,3},{2,0},{3,1},{4,6},{5,7},{6,4},{7,5},{8,10},{9,11},{10,... | collective-permute-start | bytes 589832 | tf_op jit(solution)/shard_map/ppermute | solution.py:438
  15.7 14.0 %all-to-all-start = ((f32[32,2,8,128]{3,2,1,0:T(8,128)}), f32[32,2,8,128]{3,2,1,0:T(8,128)S(1)}, u32[]{:S(2)}, u32[]{:S(2)}) async-start(f32[32,2,8,128]{3,2,1,0:T(8,128)} %get-tuple-element.37), calls=%async_computation | async-start | bytes 524288 | tf_op jit(solution)/shard_map/all_to_all | solution.py:533
  20.4 3.6 %collective-permute-start.5 = (f32[2,6,64,128]{3,2,1,0:T(8,128)S(1)}, f32[2,6,64,128]{3,2,1,0:T(8,128)S(1)}, u32[]{:S(2)}, u32[]{:S(2)}) collective-permute-start(f32[2,6,64,128]{3,2,1,0:T(8,128)S(1)} %pad_maximum_fusion), channel_id=1, source_target_pairs={{0,1},{1,0},{2,3},{3,2},{4,5},{5,4},{6,7},{7,6},{8,9},{9,8},{10,11... | collective-permute-start | bytes 1179656 | tf_op jit(solution)/shard_map/ppermute | solution.py:450
  20.4 13.3 %collective-permute-start.2 = (f32[4,64,128]{2,1,0:T(8,128)S(1)}, f32[4,64,128]{2,1,0:T(8,128)S(1)}, u32[]{:S(2)}, u32[]{:S(2)}) collective-permute-start(f32[4,64,128]{2,1,0:T(8,128)S(1)} %get-tuple-element.33), channel_id=1, source_target_pairs={{8,0},{0,8},{24,16},{16,24},{9,1},{1,9},{25,17},{17,25},{10,2},{2,... | collective-permute-start | bytes 393224 | tf_op jit(solution)/shard_map/ppermute | solution.py:536
  22.0 11.7 %collective-permute-start.1 = (f32[4,64,128]{2,1,0:T(8,128)S(1)}, f32[4,64,128]{2,1,0:T(8,128)S(1)}, u32[]{:S(2)}, u32[]{:S(2)}) collective-permute-start(f32[4,64,128]{2,1,0:T(8,128)S(1)} %get-tuple-element.32), channel_id=1, source_target_pairs={{16,0},{24,8},{0,16},{8,24},{17,1},{25,9},{1,17},{9,25},{18,2},{26... | collective-permute-start | bytes 393224 | tf_op jit(solution)/shard_map/ppermute | solution.py:536
  23.5 10.2 %collective-permute-start = (f32[4,64,128]{2,1,0:T(8,128)S(1)}, f32[4,64,128]{2,1,0:T(8,128)S(1)}, u32[]{:S(2)}, u32[]{:S(2)}) collective-permute-start(f32[4,64,128]{2,1,0:T(8,128)S(1)} %get-tuple-element.31), channel_id=1, source_target_pairs={{24,0},{16,8},{8,16},{0,24},{25,1},{17,9},{9,17},{1,25},{26,2},{18... | collective-permute-start | bytes 393224 | tf_op jit(solution)/shard_map/ppermute | solution.py:536
  33.8 5.9 %collective-permute-start.6 = (f32[4,64,128]{2,1,0:T(8,128)S(1)}, f32[4,64,128]{2,1,0:T(8,128)S(1)}, u32[]{:S(2)}, u32[]{:S(2)}) collective-permute-start(f32[4,64,128]{2,1,0:T(8,128)S(1)} %multiply_subtract_fusion.own_ref.refs_0_), channel_id=1, source_target_pairs={{0,2},{1,3},{2,0},{3,1},{4,6},{5,7},{6,4},{7,5},{8,10},{9,11},{10,... | collective-permute-start | bytes 393224 | tf_op jit(solution)/shard_map/ppermute | solution.py:438
  34.3 5.3 %collective-permute-start.7 = (f32[4,64,128]{2,1,0:T(8,128)S(1)}, f32[4,64,128]{2,1,0:T(8,128)S(1)}, u32[]{:S(2)}, u32[]{:S(2)}) collective-permute-start(f32[4,64,128]{2,1,0:T(8,128)S(1)} %multiply_subtract_fusion.own_ref.refs_0_), channel_id=1, source_target_pairs={{0,0},{1,1},{2,4},{3,5},{4,2},{5,3},{6,6},{7,7},{8,8},{9,9},{10,12... | collective-permute-start | bytes 393224 | tf_op jit(solution)/shard_map/ppermute | solution.py:438
  39.7 3.6 %collective-permute-start.8 = (f32[2,4,64,128]{3,2,1,0:T(8,128)S(1)}, f32[2,4,64,128]{3,2,1,0:T(8,128)S(1)}, u32[]{:S(2)}, u32[]{:S(2)}) collective-permute-start(f32[2,4,64,128]{3,2,1,0:T(8,128)S(1)} %pad_maximum_fusion.1), channel_id=1, source_target_pairs={{0,1},{1,0},{2,3},{3,2},{4,5},{5,4},{6,7},{7,6},{8,9},{9,8},{10,11... | collective-permute-start | bytes 786440 | tf_op jit(solution)/shard_map/ppermute | solution.py:450
  39.8 7.3 %collective-permute-start.12 = (f32[4,64,128]{2,1,0:T(8,128)S(1)}, f32[4,64,128]{2,1,0:T(8,128)S(1)}, u32[]{:S(2)}, u32[]{:S(2)}) collective-permute-start(f32[4,64,128]{2,1,0:T(8,128)S(1)} %multiply_subtract_fusion.own_ref.refs_0_), channel_id=1, source_target_pairs={{24,0},{16,8},{8,16},{0,24},{25,1},{17,9},{9,17},{1,25},{26,2},{18... | collective-permute-start | bytes 393224 | tf_op jit(solution)/shard_map/ppermute | solution.py:444
  40.7 9.2 %collective-permute-start.13 = (f32[4,64,128]{2,1,0:T(8,128)S(1)}, f32[4,64,128]{2,1,0:T(8,128)S(1)}, u32[]{:S(2)}, u32[]{:S(2)}) collective-permute-start(f32[4,64,128]{2,1,0:T(8,128)S(1)} %multiply_subtract_fusion.own_ref.refs_0_), channel_id=1, source_target_pairs={{16,0},{24,8},{0,16},{8,24},{17,1},{25,9},{1,17},{9,25},{18,2},{26... | collective-permute-start | bytes 393224 | tf_op jit(solution)/shard_map/ppermute | solution.py:444
  42.2 7.7 %collective-permute-start.14 = (f32[4,64,128]{2,1,0:T(8,128)S(1)}, f32[4,64,128]{2,1,0:T(8,128)S(1)}, u32[]{:S(2)}, u32[]{:S(2)}) collective-permute-start(f32[4,64,128]{2,1,0:T(8,128)S(1)} %multiply_subtract_fusion.own_ref.refs_0_), channel_id=1, source_target_pairs={{8,0},{0,8},{24,16},{16,24},{9,1},{1,9},{25,17},{17,25},{10,2},{2,... | collective-permute-start | bytes 393224 | tf_op jit(solution)/shard_map/ppermute | solution.py:444
  44.7 10.9 %collective-permute-start.9 = (f32[4,64,128]{2,1,0:T(8,128)S(1)}, f32[4,64,128]{2,1,0:T(8,128)S(1)}, u32[]{:S(2)}, u32[]{:S(2)}) collective-permute-start(f32[4,64,128]{2,1,0:T(8,128)S(1)} %diffuse_adjoint.1.refs_0_), channel_id=1, source_target_pairs={{24,0},{16,8},{8,16},{0,24},{25,1},{17,9},{9,17},{1,25},{26,2},{18... | collective-permute-start | bytes 393224 | tf_op jit(solution)/shard_map/ppermute | solution.py:444
  45.6 10.0 %collective-permute-start.10 = (f32[4,64,128]{2,1,0:T(8,128)S(1)}, f32[4,64,128]{2,1,0:T(8,128)S(1)}, u32[]{:S(2)}, u32[]{:S(2)}) collective-permute-start(f32[4,64,128]{2,1,0:T(8,128)S(1)} %diffuse_adjoint.1.refs_0_), channel_id=1, source_target_pairs={{16,0},{24,8},{0,16},{8,24},{17,1},{25,9},{1,17},{9,25},{18,2},{26... | collective-permute-start | bytes 393224 | tf_op jit(solution)/shard_map/ppermute | solution.py:444
  47.1 8.5 %collective-permute-start.11 = (f32[4,64,128]{2,1,0:T(8,128)S(1)}, f32[4,64,128]{2,1,0:T(8,128)S(1)}, u32[]{:S(2)}, u32[]{:S(2)}) collective-permute-start(f32[4,64,128]{2,1,0:T(8,128)S(1)} %diffuse_adjoint.1.refs_0_), channel_id=1, source_target_pairs={{8,0},{0,8},{24,16},{16,24},{9,1},{1,9},{25,17},{17,25},{10,2},{2,... | collective-permute-start | bytes 393224 | tf_op jit(solution)/shard_map/ppermute | solution.py:444

commit v16 on v15

--- a/solution.py
+++ b/solution.py
@@ -59,7 +59,7 @@
     return jnp.where(where, amount, bf16(0)).reshape(count, index.shape[1])
 
 
-def in_turns(count, build, use, slots):
+def in_turns(count, build, use, slots, between, beside, chunks):
     build(0, slots[0])
 
     def step(i, carry):
@@ -69,9 +69,18 @@
         build(jnp.minimum(2 * i + 2, count - 1), slots[0])
         return carry
 
-    lax.fori_loop(0, count // 2, step, 0)
+    def last_step(i, carry):
+        beside(i - first)
+        return step(i, carry)
+
+    first = max(count // 2 - chunks, 0)
+    lax.fori_loop(0, first, step, 0)
+    between()
+    lax.fori_loop(first, count // 2, last_step, 0)
     if count % 2:
         use(count - 1, slots[0])
+    for j in range(count // 2 - first, chunks):
+        beside(j)
 
 
 def product_nt(left, right):
@@ -188,7 +197,15 @@
     def use(i, of):
         acc_ref[...] += product_nt(of[1][...], of[0][...])
 
-    in_turns(obs_rows // group, build, use, slots)
+    def fields():
+        for copy in copies[3:]:
+            copy.wait()
+        matrix_ref[...] = level_product(local_ref[...] * f32(scale), False)
+
+    def members(j):
+        sum_members(j, matrix_ref, control_ref, pert_ref, part_ref)
+
+    in_turns(obs_rows // group, build, use, slots, fields, members, part_ref.shape[1] // 16)
     for t in range(2):
         at = 2 * t * FINE
         terms = acc_ref[at : at + FINE, :] + acc_ref[at + FINE : at + 2 * FINE, :]
@@ -212,11 +229,7 @@
     ]
     for write in writes:
         write.start()
-    for copy in copies[3:]:
-        copy.wait()
     prepare(*static_refs, packed_ref)
-    matrix_ref[...] = level_product(local_ref[...] * f32(scale), False)
-    sum_members(matrix_ref, control_ref, pert_ref, part_ref)
     share = part_ref.shape[0] // n_ens
     for d, part in enumerate(parts):
         at = peer(lax.axis_index("ens"), d, n_ens) * share
@@ -225,23 +238,18 @@
         write.wait()
 
 
-def sum_members(matrix_ref, control_ref, pert_ref, out_ref):
-    members, levels, per_level, _ = control_ref.shape
+def sum_members(j, matrix_ref, control_ref, pert_ref, out_ref):
+    members, levels, _, _ = control_ref.shape
     group = 2 - members % 2
-
-    def chunk(j, carry):
-        at = pl.ds(pl.multiple_of(j * 16, 16), 16)
-        total = jnp.zeros((levels * 16, LANES), f32)
-        for k in range(0, members, group):
-            terms = [three_terms(control_ref[k + i, :, at, :].reshape(levels * 16, LANES)) for i in range(group)]
-            local = jnp.dot(matrix_ref[...], jnp.concatenate(terms, axis=1), preferred_element_type=f32)
-            for i in range(group):
-                pert = pert_ref[k + i, :, at, :].astype(f32).reshape(levels * 16, LANES)
-                total = total + pert * local[:, i * LANES : (i + 1) * LANES]
-        out_ref[:, at, :] = total.reshape(levels, 16, LANES)
-        return carry
-
-    lax.fori_loop(0, per_level // 16, chunk, 0)
+    at = pl.ds(pl.multiple_of(j * 16, 16), 16)
+    total = jnp.zeros((levels * 16, LANES), f32)
+    for k in range(0, members, group):
+        terms = [three_terms(control_ref[k + i, :, at, :].reshape(levels * 16, LANES)) for i in range(group)]
+        local = jnp.dot(matrix_ref[...], jnp.concatenate(terms, axis=1), preferred_element_type=f32)
+        for i in range(group):
+            pert = pert_ref[k + i, :, at, :].astype(f32).reshape(levels * 16, LANES)
+            total = total + pert * local[:, i * LANES : (i + 1) * LANES]
+    out_ref[:, at, :] = total.reshape(levels, 16, LANES)
 
 
 def gather_levels(parts, to_ref):

time: 57.7 us -> 57.4 us (level)
  no operation moved by 1% of the time
where the time goes in v16:
time: 57.4 us; the launch traced here: 56.6 us
  Pallas kernels  23.2 us (40%)
  starting transfers between devices  22.2 us (39%)
  waiting for transfers between devices  10.2 us (18%)
  between operations  0.81 us (1%)
    pallas_call x1, Pallas kernels, local(): pl.pallas_call(functools.partial(observe_kernel, n_cols, cap_rows, member...  8.18 us
    ppermute x4, starting transfers between devices, exchanged(): out.append(lax.ppermute(x, 'cols', pairs))  7.78 us
    ppermute x6, starting transfers between devices, from_peers(): lax.ppermute(x, 'ens', [(peer(i, d, count), i) for i in range(count)])  7.11 us
    pallas_call x1, Pallas kernels, local(): pl.pallas_call(member_kernel, grid=(members // group,), in_specs=[VMEM] *...  5.65 us
    ppermute x4, waiting for transfers between devices, exchanged(): out.append(lax.ppermute(x, 'cols', pairs))  4.36 us
    all_to_all x1, waiting for transfers between devices, local(): lax.all_to_all(slots, ('ens', 'cols'), split_axis=0, concat_axis=0, tiled...  4.09 us
    pallas_call x1, Pallas kernels, local(): pl.pallas_call(functools.partial(scatter_kernel, cap_rows), in_specs=[VME...  3.99 us
    all_to_all x1, starting transfers between devices, local(): lax.all_to_all(slots, ('ens', 'cols'), split_axis=0, concat_axis=0, tiled...  3.6 us
  transfers between devices with their start and end apart: 16, of which 4 were waited for; matrix products, arithmetic and copies ran while one was open for 0% of the time, Pallas kernels for 24%

profile of v16, /device:TPU:0, one launch (start us, length us, event | category | flops | bytes accessed | tf_op | source)
XLA Modules:
  0.0 56.6 jit_solution(12764687787872081542)
XLA Ops:
  0.6 8.2 %slot_sums_and_members.1 = (f32[32,2,8,128]{3,2,1,0:T(8,128)}, f32[6,64,128]{2,1,0:T(8,128)S(1)}, f32[4,64,128]{2,1,0:T(8,128)S(1)}, f32[4,64,128]{2,1,0:T(8,128...) custom-call(s32[512,128]{1,0:T(8,128)} %bitcast.58, f32[512,128]{1,0:T(8,128)} %bitcast.59, ...), custom_call_target="tpu_custom_call" | custom-call | tf_op jit(solution)/shard_map/slot_sums_and_members/pallas_call | solution.py:498
  8.8 0.7 %collective-permute-start.3 = (f32[6,64,128]{2,1,0:T(8,128)S(1)}, f32[6,64,128]{2,1,0:T(8,128)S(1)}, u32[]{:S(2)}, u32[]{:S(2)}) collective-permute-start(f32[6,64,128]{2,1,0:T(8,128)S(1)} %get-tuple-element.34.refs_2_), channel_id=1, source_target_pairs={{0,0},{1,1},{2,4},{3,5},{4,2},{5,3},{6,6},{7,7},{8,8},{9,9},{10,12... | collective-permute-start | bytes 589832 | tf_op jit(solution)/shard_map/ppermute | solution.py:446
  9.5 5.9 %collective-permute-start.4 = (f32[6,64,128]{2,1,0:T(8,128)S(1)}, f32[6,64,128]{2,1,0:T(8,128)S(1)}, u32[]{:S(2)}, u32[]{:S(2)}) collective-permute-start(f32[6,64,128]{2,1,0:T(8,128)S(1)} %get-tuple-element.34.refs_2_), channel_id=1, source_target_pairs={{0,2},{1,3},{2,0},{3,1},{4,6},{5,7},{6,4},{7,5},{8,10},{9,11},{10,... | collective-permute-start | bytes 589832 | tf_op jit(solution)/shard_map/ppermute | solution.py:446
  15.4 3.6 %all-to-all-start = ((f32[32,2,8,128]{3,2,1,0:T(8,128)}), f32[32,2,8,128]{3,2,1,0:T(8,128)S(1)}, u32[]{:S(2)}, u32[]{:S(2)}) async-start(f32[32,2,8,128]{3,2,1,0:T(8,128)} %get-tuple-element.37), calls=%async_computation | async-start | bytes 524288 | tf_op jit(solution)/shard_map/all_to_all | solution.py:541
  19.1 1.0 %collective-permute-done.4.refs_1_ = f32[6,64,128]{2,1,0:T(8,128)S(1)} collective-permute-done((f32[6,64,128]{2,1,0:T(8,128)S(1)}, f32[6,64,128]{2,1,0:T(8,128)S(1)}, u32[]{:S(2)}, u32[]{:S(2)}) %collective-permute-start.4) | collective-permute-done | bytes 196640 | tf_op jit(solution)/shard_map/ppermute | solution.py:446
  20.1 0.1 collective-permute-start.5
  20.2 1.6 %collective-permute-start.2 = (f32[4,64,128]{2,1,0:T(8,128)S(1)}, f32[4,64,128]{2,1,0:T(8,128)S(1)}, u32[]{:S(2)}, u32[]{:S(2)}) collective-permute-start(f32[4,64,128]{2,1,0:T(8,128)S(1)} %get-tuple-element.33), channel_id=1, source_target_pairs={{8,0},{0,8},{24,16},{16,24},{9,1},{1,9},{25,17},{17,25},{10,2},{2,... | collective-permute-start | bytes 393224 | tf_op jit(solution)/shard_map/ppermute | solution.py:544
  21.7 1.5 %collective-permute-start.1 = (f32[4,64,128]{2,1,0:T(8,128)S(1)}, f32[4,64,128]{2,1,0:T(8,128)S(1)}, u32[]{:S(2)}, u32[]{:S(2)}) collective-permute-start(f32[4,64,128]{2,1,0:T(8,128)S(1)} %get-tuple-element.32), channel_id=1, source_target_pairs={{16,0},{24,8},{0,16},{8,24},{17,1},{25,9},{1,17},{9,25},{18,2},{26... | collective-permute-start | bytes 393224 | tf_op jit(solution)/shard_map/ppermute | solution.py:544
  23.2 0.5 collective-permute-start
  23.7 1.6 %diffuse_forward.1 = (f32[4,64,128]{2,1,0:T(8,128)S(1)}, f32[3,10,32,128]{3,2,1,0:T(8,128)S(1)}, s32[64,128]{1,0:T(8,128)S(1)}, s32[64,128]{1,0:T(8,128)S(1)}) custom-call(f32[6,64,128]{2,1,0:T(8,128)S(1)} %collective-permute-done.3.refs_0_, f32[6,64,128]{2,1,0:T(8,128)S(1)} %collective-permute-done.4.refs_1_, f32[6,64,128]{2,1,0:T(8,128)S(1)} %get-tuple-element.34.refs_2_, ...), custom_call_target="tpu_custom_call" | custom-call | flops 67108864 | bytes 4194304 | tf_op jit(solution)/shard_map/diffuse_forward/pallas_call | solution.py:549
  25.3 4.1 %all-to-all-done.slots_ref = f32[32,2,8,128]{3,2,1,0:T(8,128)S(1)} async-done(((f32[32,2,8,128]{3,2,1,0:T(8,128)}), f32[32,2,8,128]{3,2,1,0:T(8,128)S(1)}, u32[]{:S(2)}, u32[]{:S(2)}) %all-to-all-start) | async-done | bytes 262176 | tf_op jit(solution)/shard_map/all_to_all | solution.py:541
  29.4 4.0 %scatter.1 = (f32[2,256,128]{2,1,0:T(8,128)S(1)}, f32[16,64,128]{2,1,0:T(8,128)S(1)}, f32[8,16,64,128]{3,2,1,0:T(8,128)S(1)}, bf16[8,16,64,128]{3,2,1,0:T(8,128)(2,1)S(1)}) custom-call(s32[64,128]{1,0:T(8,128)S(1)} %get-tuple-element.39.row_ref, s32[64,128]{1,0:T(8,128)S(1)} %get-tuple-element.40.lane_ref, f32[32,2,8,128]{3,2,1,0:T(8,128)S(1)} %all-to-all-done.slots_ref, ...), custom_call_target="tpu_custom_call" | custom-call | flops 2147483648 | bytes 8388608 | tf_op jit(solution)/shard_map/scatter/pallas_call | solution.py:570
  33.4 0.0 collective-permute-done.1
  33.4 0.0 collective-permute-done
  33.5 0.1 multiply_subtract_fusion.own_ref.refs_0_
  33.5 0.6 collective-permute-start.6
  34.1 0.7 %collective-permute-start.7 = (f32[4,64,128]{2,1,0:T(8,128)S(1)}, f32[4,64,128]{2,1,0:T(8,128)S(1)}, u32[]{:S(2)}, u32[]{:S(2)}) collective-permute-start(f32[4,64,128]{2,1,0:T(8,128)S(1)} %multiply_subtract_fusion.own_ref.refs_0_), channel_id=1, source_target_pairs={{0,0},{1,1},{2,4},{3,5},{4,2},{5,3},{6,6},{7,7},{8,8},{9,9},{10,12... | collective-permute-start | bytes 393224 | tf_op jit(solution)/shard_map/ppermute | solution.py:446
  34.7 1.2 %level_matrices.1 = (bf16[256,768]{1,0:T(8,128)(2,1)S(1)}, bf16[256,768]{1,0:T(8,128)(2,1)S(1)}) custom-call(f32[16,16]{1,0:T(8,128)} %local_ref, f32[16,16]{1,0:T(8,128)} %root_ref), custom_call_target="tpu_custom_call" | custom-call | tf_op jit(solution)/shard_map/level_matrices/pallas_call | solution.py:592
  36.0 3.4 %collective-permute-done.6.first_ref = f32[4,64,128]{2,1,0:T(8,128)S(1)} collective-permute-done((f32[4,64,128]{2,1,0:T(8,128)S(1)}, f32[4,64,128]{2,1,0:T(8,128)S(1)}, u32[]{:S(2)}, u32[]{:S(2)}) %collective-permute-start.6) | collective-permute-done | bytes 131104 | tf_op jit(solution)/shard_map/ppermute | solution.py:446
  39.4 0.0 collective-permute-done.7.second_ref
  39.4 0.1 collective-permute-start.8
  39.5 1.0 %collective-permute-start.12 = (f32[4,64,128]{2,1,0:T(8,128)S(1)}, f32[4,64,128]{2,1,0:T(8,128)S(1)}, u32[]{:S(2)}, u32[]{:S(2)}) collective-permute-start(f32[4,64,128]{2,1,0:T(8,128)S(1)} %multiply_subtract_fusion.own_ref.refs_0_), channel_id=1, source_target_pairs={{24,0},{16,8},{8,16},{0,24},{25,1},{17,9},{9,17},{1,25},{26,2},{18... | collective-permute-start | bytes 393224 | tf_op jit(solution)/shard_map/ppermute | solution.py:452
  40.5 1.5 %collective-permute-start.13 = (f32[4,64,128]{2,1,0:T(8,128)S(1)}, f32[4,64,128]{2,1,0:T(8,128)S(1)}, u32[]{:S(2)}, u32[]{:S(2)}) collective-permute-start(f32[4,64,128]{2,1,0:T(8,128)S(1)} %multiply_subtract_fusion.own_ref.refs_0_), channel_id=1, source_target_pairs={{16,0},{24,8},{0,16},{8,24},{17,1},{25,9},{1,17},{9,25},{18,2},{26... | collective-permute-start | bytes 393224 | tf_op jit(solution)/shard_map/ppermute | solution.py:452
  41.9 1.1 %collective-permute-start.14 = (f32[4,64,128]{2,1,0:T(8,128)S(1)}, f32[4,64,128]{2,1,0:T(8,128)S(1)}, u32[]{:S(2)}, u32[]{:S(2)}) collective-permute-start(f32[4,64,128]{2,1,0:T(8,128)S(1)} %multiply_subtract_fusion.own_ref.refs_0_), channel_id=1, source_target_pairs={{8,0},{0,8},{24,16},{16,24},{9,1},{1,9},{25,17},{17,25},{10,2},{2,... | collective-permute-start | bytes 393224 | tf_op jit(solution)/shard_map/ppermute | solution.py:452
  43.1 0.0 collective-permute-done.8.other_ref
  43.1 1.3 %diffuse_adjoint.1.refs_0_ = f32[4,64,128]{2,1,0:T(8,128)S(1)} custom-call(f32[3,10,32,128]{3,2,1,0:T(8,128)S(1)} %get-tuple-element.49.coef_ref, f32[4,64,128]{2,1,0:T(8,128)S(1)} %collective-permute-done.7.second_ref, f32[4,64,128]{2,1,0:T(8,128)S(1)} %collective-permute-done.6.first_ref, f32[4,64,128]{2,1,0:T(8,128)S(1)} %multiply_subtract_fusion.own_ref.refs_0_, ...), custom_call_target="tpu_custom_call" | custom-call | tf_op jit(solution)/shard_map/diffuse_adjoint/pallas_call | solution.py:606
  44.4 1.0 %collective-permute-start.9 = (f32[4,64,128]{2,1,0:T(8,128)S(1)}, f32[4,64,128]{2,1,0:T(8,128)S(1)}, u32[]{:S(2)}, u32[]{:S(2)}) collective-permute-start(f32[4,64,128]{2,1,0:T(8,128)S(1)} %diffuse_adjoint.1.refs_0_), channel_id=1, source_target_pairs={{24,0},{16,8},{8,16},{0,24},{25,1},{17,9},{9,17},{1,25},{26,2},{18... | collective-permute-start | bytes 393224 | tf_op jit(solution)/shard_map/ppermute | solution.py:452
  45.4 1.5 %collective-permute-start.10 = (f32[4,64,128]{2,1,0:T(8,128)S(1)}, f32[4,64,128]{2,1,0:T(8,128)S(1)}, u32[]{:S(2)}, u32[]{:S(2)}) collective-permute-start(f32[4,64,128]{2,1,0:T(8,128)S(1)} %diffuse_adjoint.1.refs_0_), channel_id=1, source_target_pairs={{16,0},{24,8},{0,16},{8,24},{17,1},{25,9},{1,17},{9,25},{18,2},{26... | collective-permute-start | bytes 393224 | tf_op jit(solution)/shard_map/ppermute | solution.py:452
  46.8 1.1 %collective-permute-start.11 = (f32[4,64,128]{2,1,0:T(8,128)S(1)}, f32[4,64,128]{2,1,0:T(8,128)S(1)}, u32[]{:S(2)}, u32[]{:S(2)}) collective-permute-start(f32[4,64,128]{2,1,0:T(8,128)S(1)} %diffuse_adjoint.1.refs_0_), channel_id=1, source_target_pairs={{8,0},{0,8},{24,16},{16,24},{9,1},{1,9},{25,17},{17,25},{10,2},{2,... | collective-permute-start | bytes 393224 | tf_op jit(solution)/shard_map/ppermute | solution.py:452
  48.0 1.7 %collective-permute-done.13.refs_2_ = f32[4,64,128]{2,1,0:T(8,128)S(1)} collective-permute-done((f32[4,64,128]{2,1,0:T(8,128)S(1)}, f32[4,64,128]{2,1,0:T(8,128)S(1)}, u32[]{:S(2)}, u32[]{:S(2)}) %collective-permute-start.13) | collective-permute-done | bytes 131104 | tf_op jit(solution)/shard_map/ppermute | solution.py:452
  49.7 5.6 %members_gradient.1 = f32[8,16,64,128]{3,2,1,0:T(8,128)} custom-call(bf16[256,768]{1,0:T(8,128)(2,1)S(1)} %get-tuple-element.55.matrix_ref, f32[8,16,64,128]{3,2,1,0:T(8,128)S(1)} %get-tuple-element.56.control_ref, bf16[8,16,64,128]{3,2,1,0:T(8,128)(2,1)S(1)} %get-tuple-element.57.pert_ref, f32[4,64,128]{2,1,0:T(8,128)S(1)} %multiply_subtract_fusion.own_ref.refs_0_, ...), custom_call_target="tpu_custom_call" | custom-call | tf_op jit(solution)/shard_map/members_gradient/pallas_call | solution.py:618
  55.3 1.2 %static_gradient.1 = f32[16,64,128]{2,1,0:T(8,128)} custom-call(bf16[256,768]{1,0:T(8,128)(2,1)S(1)} %get-tuple-element.47.matrix_ref, f32[16,64,128]{2,1,0:T(8,128)S(1)} %get-tuple-element.48.static_ref, f32[4,64,128]{2,1,0:T(8,128)S(1)} %diffuse_adjoint.1.refs_0_, f32[4,64,128]{2,1,0:T(8,128)S(1)} %collective-permute-done.9.refs_1_, ...), custom_call_target="tpu_custom_call" | custom-call | tf_op jit(solution)/shard_map/static_gradient/pallas_call | solution.py:629
  (13 shorter events, 0.1 us)
Async XLA Ops:
  8.8 10.2 %collective-permute-start.3 = (f32[6,64,128]{2,1,0:T(8,128)S(1)}, f32[6,64,128]{2,1,0:T(8,128)S(1)}, u32[]{:S(2)}, u32[]{:S(2)}) collective-permute-start(f32[6,64,128]{2,1,0:T(8,128)S(1)} %get-tuple-element.34.refs_2_), channel_id=1, source_target_pairs={{0,0},{1,1},{2,4},{3,5},{4,2},{5,3},{6,6},{7,7},{8,8},{9,9},{10,12... | collective-permute-start | bytes 589832 | tf_op jit(solution)/shard_map/ppermute | solution.py:446
  9.5 10.5 %collective-permute-start.4 = (f32[6,64,128]{2,1,0:T(8,128)S(1)}, f32[6,64,128]{2,1,0:T(8,128)S(1)}, u32[]{:S(2)}, u32[]{:S(2)}) collective-permute-start(f32[6,64,128]{2,1,0:T(8,128)S(1)} %get-tuple-element.34.refs_2_), channel_id=1, source_target_pairs={{0,2},{1,3},{2,0},{3,1},{4,6},{5,7},{6,4},{7,5},{8,10},{9,11},{10,... | collective-permute-start | bytes 589832 | tf_op jit(solution)/shard_map/ppermute | solution.py:446
  15.4 14.0 %all-to-all-start = ((f32[32,2,8,128]{3,2,1,0:T(8,128)}), f32[32,2,8,128]{3,2,1,0:T(8,128)S(1)}, u32[]{:S(2)}, u32[]{:S(2)}) async-start(f32[32,2,8,128]{3,2,1,0:T(8,128)} %get-tuple-element.37), calls=%async_computation | async-start | bytes 524288 | tf_op jit(solution)/shard_map/all_to_all | solution.py:541
  20.1 3.6 %collective-permute-start.5 = (f32[2,6,64,128]{3,2,1,0:T(8,128)S(1)}, f32[2,6,64,128]{3,2,1,0:T(8,128)S(1)}, u32[]{:S(2)}, u32[]{:S(2)}) collective-permute-start(f32[2,6,64,128]{3,2,1,0:T(8,128)S(1)} %pad_maximum_fusion), channel_id=1, source_target_pairs={{0,1},{1,0},{2,3},{3,2},{4,5},{5,4},{6,7},{7,6},{8,9},{9,8},{10,11... | collective-permute-start | bytes 1179656 | tf_op jit(solution)/shard_map/ppermute | solution.py:458
  20.2 13.3 %collective-permute-start.2 = (f32[4,64,128]{2,1,0:T(8,128)S(1)}, f32[4,64,128]{2,1,0:T(8,128)S(1)}, u32[]{:S(2)}, u32[]{:S(2)}) collective-permute-start(f32[4,64,128]{2,1,0:T(8,128)S(1)} %get-tuple-element.33), channel_id=1, source_target_pairs={{8,0},{0,8},{24,16},{16,24},{9,1},{1,9},{25,17},{17,25},{10,2},{2,... | collective-permute-start | bytes 393224 | tf_op jit(solution)/shard_map/ppermute | solution.py:544
  21.7 11.7 %collective-permute-start.1 = (f32[4,64,128]{2,1,0:T(8,128)S(1)}, f32[4,64,128]{2,1,0:T(8,128)S(1)}, u32[]{:S(2)}, u32[]{:S(2)}) collective-permute-start(f32[4,64,128]{2,1,0:T(8,128)S(1)} %get-tuple-element.32), channel_id=1, source_target_pairs={{16,0},{24,8},{0,16},{8,24},{17,1},{25,9},{1,17},{9,25},{18,2},{26... | collective-permute-start | bytes 393224 | tf_op jit(solution)/shard_map/ppermute | solution.py:544
  23.2 10.2 %collective-permute-start = (f32[4,64,128]{2,1,0:T(8,128)S(1)}, f32[4,64,128]{2,1,0:T(8,128)S(1)}, u32[]{:S(2)}, u32[]{:S(2)}) collective-permute-start(f32[4,64,128]{2,1,0:T(8,128)S(1)} %get-tuple-element.31), channel_id=1, source_target_pairs={{24,0},{16,8},{8,16},{0,24},{25,1},{17,9},{9,17},{1,25},{26,2},{18... | collective-permute-start | bytes 393224 | tf_op jit(solution)/shard_map/ppermute | solution.py:544
  33.5 5.9 %collective-permute-start.6 = (f32[4,64,128]{2,1,0:T(8,128)S(1)}, f32[4,64,128]{2,1,0:T(8,128)S(1)}, u32[]{:S(2)}, u32[]{:S(2)}) collective-permute-start(f32[4,64,128]{2,1,0:T(8,128)S(1)} %multiply_subtract_fusion.own_ref.refs_0_), channel_id=1, source_target_pairs={{0,2},{1,3},{2,0},{3,1},{4,6},{5,7},{6,4},{7,5},{8,10},{9,11},{10,... | collective-permute-start | bytes 393224 | tf_op jit(solution)/shard_map/ppermute | solution.py:446
  34.1 5.3 %collective-permute-start.7 = (f32[4,64,128]{2,1,0:T(8,128)S(1)}, f32[4,64,128]{2,1,0:T(8,128)S(1)}, u32[]{:S(2)}, u32[]{:S(2)}) collective-permute-start(f32[4,64,128]{2,1,0:T(8,128)S(1)} %multiply_subtract_fusion.own_ref.refs_0_), channel_id=1, source_target_pairs={{0,0},{1,1},{2,4},{3,5},{4,2},{5,3},{6,6},{7,7},{8,8},{9,9},{10,12... | collective-permute-start | bytes 393224 | tf_op jit(solution)/shard_map/ppermute | solution.py:446
  39.4 3.6 %collective-permute-start.8 = (f32[2,4,64,128]{3,2,1,0:T(8,128)S(1)}, f32[2,4,64,128]{3,2,1,0:T(8,128)S(1)}, u32[]{:S(2)}, u32[]{:S(2)}) collective-permute-start(f32[2,4,64,128]{3,2,1,0:T(8,128)S(1)} %pad_maximum_fusion.1), channel_id=1, source_target_pairs={{0,1},{1,0},{2,3},{3,2},{4,5},{5,4},{6,7},{7,6},{8,9},{9,8},{10,11... | collective-permute-start | bytes 786440 | tf_op jit(solution)/shard_map/ppermute | solution.py:458
  39.5 7.3 %collective-permute-start.12 = (f32[4,64,128]{2,1,0:T(8,128)S(1)}, f32[4,64,128]{2,1,0:T(8,128)S(1)}, u32[]{:S(2)}, u32[]{:S(2)}) collective-permute-start(f32[4,64,128]{2,1,0:T(8,128)S(1)} %multiply_subtract_fusion.own_ref.refs_0_), channel_id=1, source_target_pairs={{24,0},{16,8},{8,16},{0,24},{25,1},{17,9},{9,17},{1,25},{26,2},{18... | collective-permute-start | bytes 393224 | tf_op jit(solution)/shard_map/ppermute | solution.py:452
  40.5 9.2 %collective-permute-start.13 = (f32[4,64,128]{2,1,0:T(8,128)S(1)}, f32[4,64,128]{2,1,0:T(8,128)S(1)}, u32[]{:S(2)}, u32[]{:S(2)}) collective-permute-start(f32[4,64,128]{2,1,0:T(8,128)S(1)} %multiply_subtract_fusion.own_ref.refs_0_), channel_id=1, source_target_pairs={{16,0},{24,8},{0,16},{8,24},{17,1},{25,9},{1,17},{9,25},{18,2},{26... | collective-permute-start | bytes 393224 | tf_op jit(solution)/shard_map/ppermute | solution.py:452
  41.9 7.7 %collective-permute-start.14 = (f32[4,64,128]{2,1,0:T(8,128)S(1)}, f32[4,64,128]{2,1,0:T(8,128)S(1)}, u32[]{:S(2)}, u32[]{:S(2)}) collective-permute-start(f32[4,64,128]{2,1,0:T(8,128)S(1)} %multiply_subtract_fusion.own_ref.refs_0_), channel_id=1, source_target_pairs={{8,0},{0,8},{24,16},{16,24},{9,1},{1,9},{25,17},{17,25},{10,2},{2,... | collective-permute-start | bytes 393224 | tf_op jit(solution)/shard_map/ppermute | solution.py:452
  44.4 10.9 %collective-permute-start.9 = (f32[4,64,128]{2,1,0:T(8,128)S(1)}, f32[4,64,128]{2,1,0:T(8,128)S(1)}, u32[]{:S(2)}, u32[]{:S(2)}) collective-permute-start(f32[4,64,128]{2,1,0:T(8,128)S(1)} %diffuse_adjoint.1.refs_0_), channel_id=1, source_target_pairs={{24,0},{16,8},{8,16},{0,24},{25,1},{17,9},{9,17},{1,25},{26,2},{18... | collective-permute-start | bytes 393224 | tf_op jit(solution)/shard_map/ppermute | solution.py:452
  45.4 10.0 %collective-permute-start.10 = (f32[4,64,128]{2,1,0:T(8,128)S(1)}, f32[4,64,128]{2,1,0:T(8,128)S(1)}, u32[]{:S(2)}, u32[]{:S(2)}) collective-permute-start(f32[4,64,128]{2,1,0:T(8,128)S(1)} %diffuse_adjoint.1.refs_0_), channel_id=1, source_target_pairs={{16,0},{24,8},{0,16},{8,24},{17,1},{25,9},{1,17},{9,25},{18,2},{26... | collective-permute-start | bytes 393224 | tf_op jit(solution)/shard_map/ppermute | solution.py:452
  46.8 8.5 %collective-permute-start.11 = (f32[4,64,128]{2,1,0:T(8,128)S(1)}, f32[4,64,128]{2,1,0:T(8,128)S(1)}, u32[]{:S(2)}, u32[]{:S(2)}) collective-permute-start(f32[4,64,128]{2,1,0:T(8,128)S(1)} %diffuse_adjoint.1.refs_0_), channel_id=1, source_target_pairs={{8,0},{0,8},{24,16},{16,24},{9,1},{1,9},{25,17},{17,25},{10,2},{2,... | collective-permute-start | bytes 393224 | tf_op jit(solution)/shard_map/ppermute | solution.py:452

commit v17 on v16

--- a/solution.py
+++ b/solution.py
@@ -598,8 +598,8 @@
         compiler_params=params(8),
         name="level_matrices",
     )(in_hbm(vertical_local), in_hbm(vertical_root))
-    tile_first, tile_second, from_local, from_root = lax.optimization_barrier(
-        (tile_first, tile_second, from_local, from_root)
+    tile_first, tile_second, adjoints[-1], from_local, from_root = lax.optimization_barrier(
+        (tile_first, tile_second, adjoints[-1], from_local, from_root)
     )
     tile_other = swapped(tile, tile_first, tile_second)
 

time: 57.4 us -> 60.1 us (1.047)
  waiting for transfers between devices: 10.2 us -> 14 us
  starting transfers between devices: 22.2 us -> 21.5 us
    ppermute x6, waiting for transfers between devices: 1.71 us -> 5.95 us  [from_peers(): lax.ppermute(x, 'ens', [(peer(i, d, count), i) for i in range(count)])]
    ppermute x6, starting transfers between devices: 7.11 us -> 6.41 us  [from_peers(): lax.ppermute(x, 'ens', [(peer(i, d, count), i) for i in range(count)])]
  transfers between devices with their start and end apart: 16 -> 16, of which waited for: 4 -> 5; matrix products, arithmetic and copies ran while one was open for 0% -> 0% of each run, Pallas kernels for 24% -> 23%
where the time goes in v17:
time: 60.1 us; the launch traced here: 59.6 us
  Pallas kernels  23.2 us (39%)
  starting transfers between devices  21.5 us (36%)
  waiting for transfers between devices  14 us (23%)
  between operations  0.81 us (1%)
    pallas_call x1, Pallas kernels, local(): pl.pallas_call(functools.partial(observe_kernel, n_cols, cap_rows, member...  8.18 us
    ppermute x4, starting transfers between devices, exchanged(): out.append(lax.ppermute(x, 'cols', pairs))  7.78 us
    ppermute x6, starting transfers between devices, from_peers(): lax.ppermute(x, 'ens', [(peer(i, d, count), i) for i in range(count)])  6.41 us
    ppermute x6, waiting for transfers between devices, from_peers(): lax.ppermute(x, 'ens', [(peer(i, d, count), i) for i in range(count)])  5.95 us
    pallas_call x1, Pallas kernels, local(): pl.pallas_call(member_kernel, grid=(members // group,), in_specs=[VMEM] *...  5.65 us
    all_to_all x1, waiting for transfers between devices, local(): lax.all_to_all(slots, ('ens', 'cols'), split_axis=0, concat_axis=0, tiled...  4.09 us
    pallas_call x1, Pallas kernels, local(): pl.pallas_call(functools.partial(scatter_kernel, cap_rows), in_specs=[VME...  3.99 us
    ppermute x4, waiting for transfers between devices, exchanged(): out.append(lax.ppermute(x, 'cols', pairs))  3.93 us
  transfers between devices with their start and end apart: 16, of which 5 were waited for; matrix products, arithmetic and copies ran while one was open for 0% of the time, Pallas kernels for 23%

profile of v17, /device:TPU:0, one launch (start us, length us, event | category | flops | bytes accessed | tf_op | source)
XLA Modules:
  0.0 59.6 jit_solution(5851815554022488236)
XLA Ops:
  0.6 8.2 %slot_sums_and_members.1 = (f32[32,2,8,128]{3,2,1,0:T(8,128)}, f32[6,64,128]{2,1,0:T(8,128)S(1)}, f32[4,64,128]{2,1,0:T(8,128)S(1)}, f32[4,64,128]{2,1,0:T(8,128...) custom-call(s32[512,128]{1,0:T(8,128)} %bitcast.58, f32[512,128]{1,0:T(8,128)} %bitcast.59, ...), custom_call_target="tpu_custom_call" | custom-call | tf_op jit(solution)/shard_map/slot_sums_and_members/pallas_call | solution.py:498
  8.8 0.7 %collective-permute-start.3 = (f32[6,64,128]{2,1,0:T(8,128)S(1)}, f32[6,64,128]{2,1,0:T(8,128)S(1)}, u32[]{:S(2)}, u32[]{:S(2)}) collective-permute-start(f32[6,64,128]{2,1,0:T(8,128)S(1)} %get-tuple-element.35.refs_2_), channel_id=1, source_target_pairs={{0,0},{1,1},{2,4},{3,5},{4,2},{5,3},{6,6},{7,7},{8,8},{9,9},{10,12... | collective-permute-start | bytes 589832 | tf_op jit(solution)/shard_map/ppermute | solution.py:446
  9.5 5.9 %collective-permute-start.4 = (f32[6,64,128]{2,1,0:T(8,128)S(1)}, f32[6,64,128]{2,1,0:T(8,128)S(1)}, u32[]{:S(2)}, u32[]{:S(2)}) collective-permute-start(f32[6,64,128]{2,1,0:T(8,128)S(1)} %get-tuple-element.35.refs_2_), channel_id=1, source_target_pairs={{0,2},{1,3},{2,0},{3,1},{4,6},{5,7},{6,4},{7,5},{8,10},{9,11},{10,... | collective-permute-start | bytes 589832 | tf_op jit(solution)/shard_map/ppermute | solution.py:446
  15.4 3.6 %all-to-all-start = ((f32[32,2,8,128]{3,2,1,0:T(8,128)}), f32[32,2,8,128]{3,2,1,0:T(8,128)S(1)}, u32[]{:S(2)}, u32[]{:S(2)}) async-start(f32[32,2,8,128]{3,2,1,0:T(8,128)} %get-tuple-element.38), calls=%async_computation | async-start | bytes 524288 | tf_op jit(solution)/shard_map/all_to_all | solution.py:541
  19.1 1.0 %collective-permute-done.4.refs_1_ = f32[6,64,128]{2,1,0:T(8,128)S(1)} collective-permute-done((f32[6,64,128]{2,1,0:T(8,128)S(1)}, f32[6,64,128]{2,1,0:T(8,128)S(1)}, u32[]{:S(2)}, u32[]{:S(2)}) %collective-permute-start.4) | collective-permute-done | bytes 196640 | tf_op jit(solution)/shard_map/ppermute | solution.py:446
  20.1 0.1 collective-permute-start.5
  20.2 1.6 %collective-permute-start.2 = (f32[4,64,128]{2,1,0:T(8,128)S(1)}, f32[4,64,128]{2,1,0:T(8,128)S(1)}, u32[]{:S(2)}, u32[]{:S(2)}) collective-permute-start(f32[4,64,128]{2,1,0:T(8,128)S(1)} %get-tuple-element.34), channel_id=1, source_target_pairs={{8,0},{0,8},{24,16},{16,24},{9,1},{1,9},{25,17},{17,25},{10,2},{2,... | collective-permute-start | bytes 393224 | tf_op jit(solution)/shard_map/ppermute | solution.py:544
  21.7 1.5 %collective-permute-start.1 = (f32[4,64,128]{2,1,0:T(8,128)S(1)}, f32[4,64,128]{2,1,0:T(8,128)S(1)}, u32[]{:S(2)}, u32[]{:S(2)}) collective-permute-start(f32[4,64,128]{2,1,0:T(8,128)S(1)} %get-tuple-element.33), channel_id=1, source_target_pairs={{16,0},{24,8},{0,16},{8,24},{17,1},{25,9},{1,17},{9,25},{18,2},{26... | collective-permute-start | bytes 393224 | tf_op jit(solution)/shard_map/ppermute | solution.py:544
  23.2 0.5 collective-permute-start
  23.7 1.6 %diffuse_forward.1 = (f32[4,64,128]{2,1,0:T(8,128)S(1)}, f32[3,10,32,128]{3,2,1,0:T(8,128)S(1)}, s32[64,128]{1,0:T(8,128)S(1)}, s32[64,128]{1,0:T(8,128)S(1)}) custom-call(f32[6,64,128]{2,1,0:T(8,128)S(1)} %collective-permute-done.3.refs_0_, f32[6,64,128]{2,1,0:T(8,128)S(1)} %collective-permute-done.4.refs_1_, f32[6,64,128]{2,1,0:T(8,128)S(1)} %get-tuple-element.35.refs_2_, ...), custom_call_target="tpu_custom_call" | custom-call | flops 67108864 | bytes 4194304 | tf_op jit(solution)/shard_map/diffuse_forward/pallas_call | solution.py:549
  25.3 4.1 %all-to-all-done.slots_ref = f32[32,2,8,128]{3,2,1,0:T(8,128)S(1)} async-done(((f32[32,2,8,128]{3,2,1,0:T(8,128)}), f32[32,2,8,128]{3,2,1,0:T(8,128)S(1)}, u32[]{:S(2)}, u32[]{:S(2)}) %all-to-all-start) | async-done | bytes 262176 | tf_op jit(solution)/shard_map/all_to_all | solution.py:541
  29.4 4.0 %scatter.1 = (f32[2,256,128]{2,1,0:T(8,128)S(1)}, f32[16,64,128]{2,1,0:T(8,128)S(1)}, f32[8,16,64,128]{3,2,1,0:T(8,128)S(1)}, bf16[8,16,64,128]{3,2,1,0:T(8,128)(2,1)S(1)}) custom-call(s32[64,128]{1,0:T(8,128)S(1)} %get-tuple-element.40.row_ref, s32[64,128]{1,0:T(8,128)S(1)} %get-tuple-element.41.lane_ref, f32[32,2,8,128]{3,2,1,0:T(8,128)S(1)} %all-to-all-done.slots_ref, ...), custom_call_target="tpu_custom_call" | custom-call | flops 2147483648 | bytes 8388608 | tf_op jit(solution)/shard_map/scatter/pallas_call | solution.py:570
  33.4 0.0 collective-permute-done.1
  33.5 0.1 multiply_subtract_fusion.own_ref.refs_0_
  33.5 0.6 collective-permute-start.6
  34.1 0.7 %collective-permute-start.7 = (f32[4,64,128]{2,1,0:T(8,128)S(1)}, f32[4,64,128]{2,1,0:T(8,128)S(1)}, u32[]{:S(2)}, u32[]{:S(2)}) collective-permute-start(f32[4,64,128]{2,1,0:T(8,128)S(1)} %multiply_subtract_fusion.own_ref.refs_0_), channel_id=1, source_target_pairs={{0,0},{1,1},{2,4},{3,5},{4,2},{5,3},{6,6},{7,7},{8,8},{9,9},{10,12... | collective-permute-start | bytes 393224 | tf_op jit(solution)/shard_map/ppermute | solution.py:446
  34.7 0.4 collective-permute-start.8
  35.2 1.2 %level_matrices.1 = (bf16[256,768]{1,0:T(8,128)(2,1)S(1)}, bf16[256,768]{1,0:T(8,128)(2,1)S(1)}) custom-call(f32[16,16]{1,0:T(8,128)} %local_ref, f32[16,16]{1,0:T(8,128)} %root_ref), custom_call_target="tpu_custom_call" | custom-call | tf_op jit(solution)/shard_map/level_matrices/pallas_call | solution.py:592
  36.4 2.9 %collective-permute-done.6.first_ref = f32[4,64,128]{2,1,0:T(8,128)S(1)} collective-permute-done((f32[4,64,128]{2,1,0:T(8,128)S(1)}, f32[4,64,128]{2,1,0:T(8,128)S(1)}, u32[]{:S(2)}, u32[]{:S(2)}) %collective-permute-start.6) | collective-permute-done | bytes 131104 | tf_op jit(solution)/shard_map/ppermute | solution.py:446
  39.4 0.0 collective-permute-done.7.second_ref
  39.4 0.8 %collective-permute-done.8.refs_3_ = f32[4,64,128]{2,1,0:T(8,128)S(1)} collective-permute-done((f32[4,64,128]{2,1,0:T(8,128)S(1)}, f32[4,64,128]{2,1,0:T(8,128)S(1)}, u32[]{:S(2)}, u32[]{:S(2)}) %collective-permute-start.8) | collective-permute-done | bytes 131104 | tf_op jit(solution)/shard_map/ppermute | solution.py:452
  40.2 0.1 collective-permute-start.9
  40.3 1.3 %collective-permute-start.13 = (f32[4,64,128]{2,1,0:T(8,128)S(1)}, f32[4,64,128]{2,1,0:T(8,128)S(1)}, u32[]{:S(2)}, u32[]{:S(2)}) collective-permute-start(f32[4,64,128]{2,1,0:T(8,128)S(1)} %multiply_subtract_fusion.own_ref.refs_0_), channel_id=1, source_target_pairs={{24,0},{16,8},{8,16},{0,24},{25,1},{17,9},{9,17},{1,25},{26,2},{18... | collective-permute-start | bytes 393224 | tf_op jit(solution)/shard_map/ppermute | solution.py:452
  41.5 1.2 %collective-permute-start.14 = (f32[4,64,128]{2,1,0:T(8,128)S(1)}, f32[4,64,128]{2,1,0:T(8,128)S(1)}, u32[]{:S(2)}, u32[]{:S(2)}) collective-permute-start(f32[4,64,128]{2,1,0:T(8,128)S(1)} %multiply_subtract_fusion.own_ref.refs_0_), channel_id=1, source_target_pairs={{16,0},{24,8},{0,16},{8,24},{17,1},{25,9},{1,17},{9,25},{18,2},{26... | collective-permute-start | bytes 393224 | tf_op jit(solution)/shard_map/ppermute | solution.py:452
  42.7 0.0 collective-permute-done.9.other_ref
  42.7 1.3 %diffuse_adjoint.1.refs_0_ = f32[4,64,128]{2,1,0:T(8,128)S(1)} custom-call(f32[3,10,32,128]{3,2,1,0:T(8,128)S(1)} %get-tuple-element.50.coef_ref, f32[4,64,128]{2,1,0:T(8,128)S(1)} %collective-permute-done.7.second_ref, f32[4,64,128]{2,1,0:T(8,128)S(1)} %collective-permute-done.6.first_ref, f32[4,64,128]{2,1,0:T(8,128)S(1)} %multiply_subtract_fusion.own_ref.refs_0_, ...), custom_call_target="tpu_custom_call" | custom-call | tf_op jit(solution)/shard_map/diffuse_adjoint/pallas_call | solution.py:606
  44.0 1.5 %collective-permute-start.10 = (f32[4,64,128]{2,1,0:T(8,128)S(1)}, f32[4,64,128]{2,1,0:T(8,128)S(1)}, u32[]{:S(2)}, u32[]{:S(2)}) collective-permute-start(f32[4,64,128]{2,1,0:T(8,128)S(1)} %diffuse_adjoint.1.refs_0_), channel_id=1, source_target_pairs={{24,0},{16,8},{8,16},{0,24},{25,1},{17,9},{9,17},{1,25},{26,2},{18... | collective-permute-start | bytes 393224 | tf_op jit(solution)/shard_map/ppermute | solution.py:452
  45.5 1.2 %collective-permute-start.11 = (f32[4,64,128]{2,1,0:T(8,128)S(1)}, f32[4,64,128]{2,1,0:T(8,128)S(1)}, u32[]{:S(2)}, u32[]{:S(2)}) collective-permute-start(f32[4,64,128]{2,1,0:T(8,128)S(1)} %diffuse_adjoint.1.refs_0_), channel_id=1, source_target_pairs={{16,0},{24,8},{0,16},{8,24},{17,1},{25,9},{1,17},{9,25},{18,2},{26... | collective-permute-start | bytes 393224 | tf_op jit(solution)/shard_map/ppermute | solution.py:452
  46.7 0.9 %collective-permute-start.12 = (f32[4,64,128]{2,1,0:T(8,128)S(1)}, f32[4,64,128]{2,1,0:T(8,128)S(1)}, u32[]{:S(2)}, u32[]{:S(2)}) collective-permute-start(f32[4,64,128]{2,1,0:T(8,128)S(1)} %diffuse_adjoint.1.refs_0_), channel_id=1, source_target_pairs={{8,0},{0,8},{24,16},{16,24},{9,1},{1,9},{25,17},{17,25},{10,2},{2,... | collective-permute-start | bytes 393224 | tf_op jit(solution)/shard_map/ppermute | solution.py:452
  47.6 5.2 %collective-permute-done.14.refs_2_ = f32[4,64,128]{2,1,0:T(8,128)S(1)} collective-permute-done((f32[4,64,128]{2,1,0:T(8,128)S(1)}, f32[4,64,128]{2,1,0:T(8,128)S(1)}, u32[]{:S(2)}, u32[]{:S(2)}) %collective-permute-start.14) | collective-permute-done | bytes 131104 | tf_op jit(solution)/shard_map/ppermute | solution.py:452
  52.8 5.6 %members_gradient.1 = f32[8,16,64,128]{3,2,1,0:T(8,128)} custom-call(bf16[256,768]{1,0:T(8,128)(2,1)S(1)} %get-tuple-element.56.matrix_ref, f32[8,16,64,128]{3,2,1,0:T(8,128)S(1)} %get-tuple-element.57.control_ref, bf16[8,16,64,128]{3,2,1,0:T(8,128)(2,1)S(1)} %get-tuple-element.58.pert_ref, f32[4,64,128]{2,1,0:T(8,128)S(1)} %multiply_subtract_fusion.own_ref.refs_0_, ...), custom_call_target="tpu_custom_call" | custom-call | tf_op jit(solution)/shard_map/members_gradient/pallas_call | solution.py:618
  58.4 1.2 %static_gradient.1 = f32[16,64,128]{2,1,0:T(8,128)} custom-call(bf16[256,768]{1,0:T(8,128)(2,1)S(1)} %get-tuple-element.48.matrix_ref, f32[16,64,128]{2,1,0:T(8,128)S(1)} %get-tuple-element.49.static_ref, f32[4,64,128]{2,1,0:T(8,128)S(1)} %diffuse_adjoint.1.refs_0_, f32[4,64,128]{2,1,0:T(8,128)S(1)} %collective-permute-done.10.refs_1_, ...), custom_call_target="tpu_custom_call" | custom-call | tf_op jit(solution)/shard_map/static_gradient/pallas_call | solution.py:629
  (13 shorter events, 0.1 us)
Async XLA Ops:
  8.8 10.2 %collective-permute-start.3 = (f32[6,64,128]{2,1,0:T(8,128)S(1)}, f32[6,64,128]{2,1,0:T(8,128)S(1)}, u32[]{:S(2)}, u32[]{:S(2)}) collective-permute-start(f32[6,64,128]{2,1,0:T(8,128)S(1)} %get-tuple-element.35.refs_2_), channel_id=1, source_target_pairs={{0,0},{1,1},{2,4},{3,5},{4,2},{5,3},{6,6},{7,7},{8,8},{9,9},{10,12... | collective-permute-start | bytes 589832 | tf_op jit(solution)/shard_map/ppermute | solution.py:446
  9.5 10.5 %collective-permute-start.4 = (f32[6,64,128]{2,1,0:T(8,128)S(1)}, f32[6,64,128]{2,1,0:T(8,128)S(1)}, u32[]{:S(2)}, u32[]{:S(2)}) collective-permute-start(f32[6,64,128]{2,1,0:T(8,128)S(1)} %get-tuple-element.35.refs_2_), channel_id=1, source_target_pairs={{0,2},{1,3},{2,0},{3,1},{4,6},{5,7},{6,4},{7,5},{8,10},{9,11},{10,... | collective-permute-start | bytes 589832 | tf_op jit(solution)/shard_map/ppermute | solution.py:446
  15.4 14.0 %all-to-all-start = ((f32[32,2,8,128]{3,2,1,0:T(8,128)}), f32[32,2,8,128]{3,2,1,0:T(8,128)S(1)}, u32[]{:S(2)}, u32[]{:S(2)}) async-start(f32[32,2,8,128]{3,2,1,0:T(8,128)} %get-tuple-element.38), calls=%async_computation | async-start | bytes 524288 | tf_op jit(solution)/shard_map/all_to_all | solution.py:541
  20.1 3.6 %collective-permute-start.5 = (f32[2,6,64,128]{3,2,1,0:T(8,128)S(1)}, f32[2,6,64,128]{3,2,1,0:T(8,128)S(1)}, u32[]{:S(2)}, u32[]{:S(2)}) collective-permute-start(f32[2,6,64,128]{3,2,1,0:T(8,128)S(1)} %pad_maximum_fusion), channel_id=1, source_target_pairs={{0,1},{1,0},{2,3},{3,2},{4,5},{5,4},{6,7},{7,6},{8,9},{9,8},{10,11... | collective-permute-start | bytes 1179656 | tf_op jit(solution)/shard_map/ppermute | solution.py:458
  20.2 13.3 %collective-permute-start.2 = (f32[4,64,128]{2,1,0:T(8,128)S(1)}, f32[4,64,128]{2,1,0:T(8,128)S(1)}, u32[]{:S(2)}, u32[]{:S(2)}) collective-permute-start(f32[4,64,128]{2,1,0:T(8,128)S(1)} %get-tuple-element.34), channel_id=1, source_target_pairs={{8,0},{0,8},{24,16},{16,24},{9,1},{1,9},{25,17},{17,25},{10,2},{2,... | collective-permute-start | bytes 393224 | tf_op jit(solution)/shard_map/ppermute | solution.py:544
  21.7 11.7 %collective-permute-start.1 = (f32[4,64,128]{2,1,0:T(8,128)S(1)}, f32[4,64,128]{2,1,0:T(8,128)S(1)}, u32[]{:S(2)}, u32[]{:S(2)}) collective-permute-start(f32[4,64,128]{2,1,0:T(8,128)S(1)} %get-tuple-element.33), channel_id=1, source_target_pairs={{16,0},{24,8},{0,16},{8,24},{17,1},{25,9},{1,17},{9,25},{18,2},{26... | collective-permute-start | bytes 393224 | tf_op jit(solution)/shard_map/ppermute | solution.py:544
  23.2 10.2 %collective-permute-start = (f32[4,64,128]{2,1,0:T(8,128)S(1)}, f32[4,64,128]{2,1,0:T(8,128)S(1)}, u32[]{:S(2)}, u32[]{:S(2)}) collective-permute-start(f32[4,64,128]{2,1,0:T(8,128)S(1)} %get-tuple-element.32), channel_id=1, source_target_pairs={{24,0},{16,8},{8,16},{0,24},{25,1},{17,9},{9,17},{1,25},{26,2},{18... | collective-permute-start | bytes 393224 | tf_op jit(solution)/shard_map/ppermute | solution.py:544
  33.5 5.9 %collective-permute-start.6 = (f32[4,64,128]{2,1,0:T(8,128)S(1)}, f32[4,64,128]{2,1,0:T(8,128)S(1)}, u32[]{:S(2)}, u32[]{:S(2)}) collective-permute-start(f32[4,64,128]{2,1,0:T(8,128)S(1)} %multiply_subtract_fusion.own_ref.refs_0_), channel_id=1, source_target_pairs={{0,2},{1,3},{2,0},{3,1},{4,6},{5,7},{6,4},{7,5},{8,10},{9,11},{10,... | collective-permute-start | bytes 393224 | tf_op jit(solution)/shard_map/ppermute | solution.py:446
  34.1 5.3 %collective-permute-start.7 = (f32[4,64,128]{2,1,0:T(8,128)S(1)}, f32[4,64,128]{2,1,0:T(8,128)S(1)}, u32[]{:S(2)}, u32[]{:S(2)}) collective-permute-start(f32[4,64,128]{2,1,0:T(8,128)S(1)} %multiply_subtract_fusion.own_ref.refs_0_), channel_id=1, source_target_pairs={{0,0},{1,1},{2,4},{3,5},{4,2},{5,3},{6,6},{7,7},{8,8},{9,9},{10,12... | collective-permute-start | bytes 393224 | tf_op jit(solution)/shard_map/ppermute | solution.py:446
  34.7 5.4 %collective-permute-start.8 = (f32[4,64,128]{2,1,0:T(8,128)S(1)}, f32[4,64,128]{2,1,0:T(8,128)S(1)}, u32[]{:S(2)}, u32[]{:S(2)}) collective-permute-start(f32[4,64,128]{2,1,0:T(8,128)S(1)} %multiply_subtract_fusion.own_ref.refs_0_), channel_id=1, source_target_pairs={{8,0},{0,8},{24,16},{16,24},{9,1},{1,9},{25,17},{17,25},{10,2},{2,... | collective-permute-start | bytes 393224 | tf_op jit(solution)/shard_map/ppermute | solution.py:452
  40.2 2.5 %collective-permute-start.9 = (f32[2,4,64,128]{3,2,1,0:T(8,128)S(1)}, f32[2,4,64,128]{3,2,1,0:T(8,128)S(1)}, u32[]{:S(2)}, u32[]{:S(2)}) collective-permute-start(f32[2,4,64,128]{3,2,1,0:T(8,128)S(1)} %pad_maximum_fusion.1), channel_id=1, source_target_pairs={{0,1},{1,0},{2,3},{3,2},{4,5},{5,4},{6,7},{7,6},{8,9},{9,8},{10,11... | collective-permute-start | bytes 786440 | tf_op jit(solution)/shard_map/ppermute | solution.py:458
  40.3 7.3 %collective-permute-start.13 = (f32[4,64,128]{2,1,0:T(8,128)S(1)}, f32[4,64,128]{2,1,0:T(8,128)S(1)}, u32[]{:S(2)}, u32[]{:S(2)}) collective-permute-start(f32[4,64,128]{2,1,0:T(8,128)S(1)} %multiply_subtract_fusion.own_ref.refs_0_), channel_id=1, source_target_pairs={{24,0},{16,8},{8,16},{0,24},{25,1},{17,9},{9,17},{1,25},{26,2},{18... | collective-permute-start | bytes 393224 | tf_op jit(solution)/shard_map/ppermute | solution.py:452
  41.5 11.2 %collective-permute-start.14 = (f32[4,64,128]{2,1,0:T(8,128)S(1)}, f32[4,64,128]{2,1,0:T(8,128)S(1)}, u32[]{:S(2)}, u32[]{:S(2)}) collective-permute-start(f32[4,64,128]{2,1,0:T(8,128)S(1)} %multiply_subtract_fusion.own_ref.refs_0_), channel_id=1, source_target_pairs={{16,0},{24,8},{0,16},{8,24},{17,1},{25,9},{1,17},{9,25},{18,2},{26... | collective-permute-start | bytes 393224 | tf_op jit(solution)/shard_map/ppermute | solution.py:452
  44.0 14.4 %collective-permute-start.10 = (f32[4,64,128]{2,1,0:T(8,128)S(1)}, f32[4,64,128]{2,1,0:T(8,128)S(1)}, u32[]{:S(2)}, u32[]{:S(2)}) collective-permute-start(f32[4,64,128]{2,1,0:T(8,128)S(1)} %diffuse_adjoint.1.refs_0_), channel_id=1, source_target_pairs={{24,0},{16,8},{8,16},{0,24},{25,1},{17,9},{9,17},{1,25},{26,2},{18... | collective-permute-start | bytes 393224 | tf_op jit(solution)/shard_map/ppermute | solution.py:452
  45.5 12.9 %collective-permute-start.11 = (f32[4,64,128]{2,1,0:T(8,128)S(1)}, f32[4,64,128]{2,1,0:T(8,128)S(1)}, u32[]{:S(2)}, u32[]{:S(2)}) collective-permute-start(f32[4,64,128]{2,1,0:T(8,128)S(1)} %diffuse_adjoint.1.refs_0_), channel_id=1, source_target_pairs={{16,0},{24,8},{0,16},{8,24},{17,1},{25,9},{1,17},{9,25},{18,2},{26... | collective-permute-start | bytes 393224 | tf_op jit(solution)/shard_map/ppermute | solution.py:452
  46.7 11.7 %collective-permute-start.12 = (f32[4,64,128]{2,1,0:T(8,128)S(1)}, f32[4,64,128]{2,1,0:T(8,128)S(1)}, u32[]{:S(2)}, u32[]{:S(2)}) collective-permute-start(f32[4,64,128]{2,1,0:T(8,128)S(1)} %diffuse_adjoint.1.refs_0_), channel_id=1, source_target_pairs={{8,0},{0,8},{24,16},{16,24},{9,1},{1,9},{25,17},{17,25},{10,2},{2,... | collective-permute-start | bytes 393224 | tf_op jit(solution)/shard_map/ppermute | solution.py:452

commit v18 on v16

--- a/solution.py
+++ b/solution.py
@@ -252,10 +252,10 @@
     out_ref[:, at, :] = total.reshape(levels, 16, LANES)
 
 
-def gather_levels(parts, to_ref):
+def gather_levels(parts, to_ref, far_first):
     share = to_ref.shape[0] // len(parts)
     for i, part in enumerate(parts):
-        at = peer(lax.axis_index("ens"), (len(parts) - i) % len(parts), len(parts))
+        at = peer(lax.axis_index("ens"), (len(parts) - i) % len(parts) if far_first else i, len(parts))
         to_ref[pl.ds(at * share, share)] = part[...]
 
 
@@ -266,7 +266,7 @@
 
     @pl.when(pl.program_id(0) == 0)
     def _():
-        gather_levels(parts, adjoint_ref)
+        gather_levels(parts, adjoint_ref, True)
 
     def chunk(j, carry):
         at = pl.ds(pl.multiple_of(j * 16, 16), 16)
@@ -425,7 +425,7 @@
 def static_kernel(matrix_ref, static_ref, *refs):
     parts, (out_ref, smooth_ref) = refs[:-2], refs[-2:]
     levels, per_level, _ = static_ref.shape
-    gather_levels(parts, smooth_ref)
+    gather_levels(parts, smooth_ref, False)
     for j in range(0, per_level, 32):
         terms = [three_terms(smooth_ref[:, j + i : j + i + 16, :].reshape(levels * 16, LANES)) for i in (0, 16)]
         change = jnp.dot(matrix_ref[...], jnp.concatenate(terms, axis=1), preferred_element_type=f32)
@@ -612,7 +612,7 @@
         name="diffuse_adjoint",
     )(coefs, tile_second, tile_first, tile, tile_other)
     smooth, from_local = lax.optimization_barrier((smooth, from_local))
-    smooths = [smooth] + from_peers(smooth)
+    smooths = [smooth] + from_peers(smooth)[::-1]
 
     group = 2 - members % 2
     ensemble_grad = pl.pallas_call(

time: 57.4 us -> 57 us (level)
  starting transfers between devices: 22.2 us -> 21.3 us
    ppermute x6, starting transfers between devices: 7.11 us -> 6.22 us  [from_peers(): lax.ppermute(x, 'ens', [(peer(i, d, count), i) for i in range(count)])]
  transfers between devices with their start and end apart: 16 -> 16, of which waited for: 4 -> 5; matrix products, arithmetic and copies ran while one was open for 0% -> 0% of each run, Pallas kernels for 24% -> 25%
where the time goes in v18:
time: 57 us; the launch traced here: 56.1 us
  Pallas kernels  23.2 us (41%)
  starting transfers between devices  21.3 us (37%)
  waiting for transfers between devices  10.6 us (19%)
  between operations  0.81 us (1%)
    pallas_call x1, Pallas kernels, local(): pl.pallas_call(functools.partial(observe_kernel, n_cols, cap_rows, member...  8.18 us
    ppermute x4, starting transfers between devices, exchanged(): out.append(lax.ppermute(x, 'cols', pairs))  7.78 us
    ppermute x6, starting transfers between devices, from_peers(): lax.ppermute(x, 'ens', [(peer(i, d, count), i) for i in range(count)])  6.22 us
    pallas_call x1, Pallas kernels, local(): pl.pallas_call(member_kernel, grid=(members // group,), in_specs=[VMEM] *...  5.65 us
    ppermute x4, waiting for transfers between devices, exchanged(): out.append(lax.ppermute(x, 'cols', pairs))  4.36 us
    all_to_all x1, waiting for transfers between devices, local(): lax.all_to_all(slots, ('ens', 'cols'), split_axis=0, concat_axis=0, tiled...  4.09 us
    pallas_call x1, Pallas kernels, local(): pl.pallas_call(functools.partial(scatter_kernel, cap_rows), in_specs=[VME...  3.99 us
    all_to_all x1, starting transfers between devices, local(): lax.all_to_all(slots, ('ens', 'cols'), split_axis=0, concat_axis=0, tiled...  3.6 us
  transfers between devices with their start and end apart: 16, of which 5 were waited for; matrix products, arithmetic and copies ran while one was open for 0% of the time, Pallas kernels for 25%

profile of v18, /device:TPU:0, one launch (start us, length us, event | category | flops | bytes accessed | tf_op | source)
XLA Modules:
  0.0 56.1 jit_solution(14978888908392331128)
XLA Ops:
  0.6 8.2 %slot_sums_and_members.1 = (f32[32,2,8,128]{3,2,1,0:T(8,128)}, f32[6,64,128]{2,1,0:T(8,128)S(1)}, f32[4,64,128]{2,1,0:T(8,128)S(1)}, f32[4,64,128]{2,1,0:T(8,128...) custom-call(s32[512,128]{1,0:T(8,128)} %bitcast.58, f32[512,128]{1,0:T(8,128)} %bitcast.59, ...), custom_call_target="tpu_custom_call" | custom-call | tf_op jit(solution)/shard_map/slot_sums_and_members/pallas_call | solution.py:498
  8.8 0.7 %collective-permute-start.3 = (f32[6,64,128]{2,1,0:T(8,128)S(1)}, f32[6,64,128]{2,1,0:T(8,128)S(1)}, u32[]{:S(2)}, u32[]{:S(2)}) collective-permute-start(f32[6,64,128]{2,1,0:T(8,128)S(1)} %get-tuple-element.34.refs_2_), channel_id=1, source_target_pairs={{0,0},{1,1},{2,4},{3,5},{4,2},{5,3},{6,6},{7,7},{8,8},{9,9},{10,12... | collective-permute-start | bytes 589832 | tf_op jit(solution)/shard_map/ppermute | solution.py:446
  9.5 5.9 %collective-permute-start.4 = (f32[6,64,128]{2,1,0:T(8,128)S(1)}, f32[6,64,128]{2,1,0:T(8,128)S(1)}, u32[]{:S(2)}, u32[]{:S(2)}) collective-permute-start(f32[6,64,128]{2,1,0:T(8,128)S(1)} %get-tuple-element.34.refs_2_), channel_id=1, source_target_pairs={{0,2},{1,3},{2,0},{3,1},{4,6},{5,7},{6,4},{7,5},{8,10},{9,11},{10,... | collective-permute-start | bytes 589832 | tf_op jit(solution)/shard_map/ppermute | solution.py:446
  15.4 3.6 %all-to-all-start = ((f32[32,2,8,128]{3,2,1,0:T(8,128)}), f32[32,2,8,128]{3,2,1,0:T(8,128)S(1)}, u32[]{:S(2)}, u32[]{:S(2)}) async-start(f32[32,2,8,128]{3,2,1,0:T(8,128)} %get-tuple-element.37), calls=%async_computation | async-start | bytes 524288 | tf_op jit(solution)/shard_map/all_to_all | solution.py:541
  19.1 1.0 %collective-permute-done.4.refs_1_ = f32[6,64,128]{2,1,0:T(8,128)S(1)} collective-permute-done((f32[6,64,128]{2,1,0:T(8,128)S(1)}, f32[6,64,128]{2,1,0:T(8,128)S(1)}, u32[]{:S(2)}, u32[]{:S(2)}) %collective-permute-start.4) | collective-permute-done | bytes 196640 | tf_op jit(solution)/shard_map/ppermute | solution.py:446
  20.1 0.1 collective-permute-start.5
  20.2 1.6 %collective-permute-start.2 = (f32[4,64,128]{2,1,0:T(8,128)S(1)}, f32[4,64,128]{2,1,0:T(8,128)S(1)}, u32[]{:S(2)}, u32[]{:S(2)}) collective-permute-start(f32[4,64,128]{2,1,0:T(8,128)S(1)} %get-tuple-element.33), channel_id=1, source_target_pairs={{8,0},{0,8},{24,16},{16,24},{9,1},{1,9},{25,17},{17,25},{10,2},{2,... | collective-permute-start | bytes 393224 | tf_op jit(solution)/shard_map/ppermute | solution.py:544
  21.7 1.5 %collective-permute-start.1 = (f32[4,64,128]{2,1,0:T(8,128)S(1)}, f32[4,64,128]{2,1,0:T(8,128)S(1)}, u32[]{:S(2)}, u32[]{:S(2)}) collective-permute-start(f32[4,64,128]{2,1,0:T(8,128)S(1)} %get-tuple-element.32), channel_id=1, source_target_pairs={{16,0},{24,8},{0,16},{8,24},{17,1},{25,9},{1,17},{9,25},{18,2},{26... | collective-permute-start | bytes 393224 | tf_op jit(solution)/shard_map/ppermute | solution.py:544
  23.2 0.5 collective-permute-start
  23.7 1.6 %diffuse_forward.1 = (f32[4,64,128]{2,1,0:T(8,128)S(1)}, f32[3,10,32,128]{3,2,1,0:T(8,128)S(1)}, s32[64,128]{1,0:T(8,128)S(1)}, s32[64,128]{1,0:T(8,128)S(1)}) custom-call(f32[6,64,128]{2,1,0:T(8,128)S(1)} %collective-permute-done.3.refs_0_, f32[6,64,128]{2,1,0:T(8,128)S(1)} %collective-permute-done.4.refs_1_, f32[6,64,128]{2,1,0:T(8,128)S(1)} %get-tuple-element.34.refs_2_, ...), custom_call_target="tpu_custom_call" | custom-call | flops 67108864 | bytes 4194304 | tf_op jit(solution)/shard_map/diffuse_forward/pallas_call | solution.py:549
  25.3 4.1 %all-to-all-done.slots_ref = f32[32,2,8,128]{3,2,1,0:T(8,128)S(1)} async-done(((f32[32,2,8,128]{3,2,1,0:T(8,128)}), f32[32,2,8,128]{3,2,1,0:T(8,128)S(1)}, u32[]{:S(2)}, u32[]{:S(2)}) %all-to-all-start) | async-done | bytes 262176 | tf_op jit(solution)/shard_map/all_to_all | solution.py:541
  29.4 4.0 %scatter.1 = (f32[2,256,128]{2,1,0:T(8,128)S(1)}, f32[16,64,128]{2,1,0:T(8,128)S(1)}, f32[8,16,64,128]{3,2,1,0:T(8,128)S(1)}, bf16[8,16,64,128]{3,2,1,0:T(8,128)(2,1)S(1)}) custom-call(s32[64,128]{1,0:T(8,128)S(1)} %get-tuple-element.39.row_ref, s32[64,128]{1,0:T(8,128)S(1)} %get-tuple-element.40.lane_ref, f32[32,2,8,128]{3,2,1,0:T(8,128)S(1)} %all-to-all-done.slots_ref, ...), custom_call_target="tpu_custom_call" | custom-call | flops 2147483648 | bytes 8388608 | tf_op jit(solution)/shard_map/scatter/pallas_call | solution.py:570
  33.4 0.0 collective-permute-done.1
  33.4 0.0 collective-permute-done
  33.5 0.1 multiply_subtract_fusion.own_ref.refs_0_
  33.5 0.6 collective-permute-start.6
  34.1 0.7 %collective-permute-start.7 = (f32[4,64,128]{2,1,0:T(8,128)S(1)}, f32[4,64,128]{2,1,0:T(8,128)S(1)}, u32[]{:S(2)}, u32[]{:S(2)}) collective-permute-start(f32[4,64,128]{2,1,0:T(8,128)S(1)} %multiply_subtract_fusion.own_ref.refs_0_), channel_id=1, source_target_pairs={{0,0},{1,1},{2,4},{3,5},{4,2},{5,3},{6,6},{7,7},{8,8},{9,9},{10,12... | collective-permute-start | bytes 393224 | tf_op jit(solution)/shard_map/ppermute | solution.py:446
  34.7 1.2 %level_matrices.1 = (bf16[256,768]{1,0:T(8,128)(2,1)S(1)}, bf16[256,768]{1,0:T(8,128)(2,1)S(1)}) custom-call(f32[16,16]{1,0:T(8,128)} %local_ref, f32[16,16]{1,0:T(8,128)} %root_ref), custom_call_target="tpu_custom_call" | custom-call | tf_op jit(solution)/shard_map/level_matrices/pallas_call | solution.py:592
  36.0 3.4 %collective-permute-done.6.first_ref = f32[4,64,128]{2,1,0:T(8,128)S(1)} collective-permute-done((f32[4,64,128]{2,1,0:T(8,128)S(1)}, f32[4,64,128]{2,1,0:T(8,128)S(1)}, u32[]{:S(2)}, u32[]{:S(2)}) %collective-permute-start.6) | collective-permute-done | bytes 131104 | tf_op jit(solution)/shard_map/ppermute | solution.py:446
  39.4 0.0 collective-permute-done.7.second_ref
  39.4 0.1 collective-permute-start.8
  39.5 1.0 %collective-permute-start.12 = (f32[4,64,128]{2,1,0:T(8,128)S(1)}, f32[4,64,128]{2,1,0:T(8,128)S(1)}, u32[]{:S(2)}, u32[]{:S(2)}) collective-permute-start(f32[4,64,128]{2,1,0:T(8,128)S(1)} %multiply_subtract_fusion.own_ref.refs_0_), channel_id=1, source_target_pairs={{24,0},{16,8},{8,16},{0,24},{25,1},{17,9},{9,17},{1,25},{26,2},{18... | collective-permute-start | bytes 393224 | tf_op jit(solution)/shard_map/ppermute | solution.py:452
  40.5 1.5 %collective-permute-start.13 = (f32[4,64,128]{2,1,0:T(8,128)S(1)}, f32[4,64,128]{2,1,0:T(8,128)S(1)}, u32[]{:S(2)}, u32[]{:S(2)}) collective-permute-start(f32[4,64,128]{2,1,0:T(8,128)S(1)} %multiply_subtract_fusion.own_ref.refs_0_), channel_id=1, source_target_pairs={{16,0},{24,8},{0,16},{8,24},{17,1},{25,9},{1,17},{9,25},{18,2},{26... | collective-permute-start | bytes 393224 | tf_op jit(solution)/shard_map/ppermute | solution.py:452
  41.9 1.1 %collective-permute-start.14 = (f32[4,64,128]{2,1,0:T(8,128)S(1)}, f32[4,64,128]{2,1,0:T(8,128)S(1)}, u32[]{:S(2)}, u32[]{:S(2)}) collective-permute-start(f32[4,64,128]{2,1,0:T(8,128)S(1)} %multiply_subtract_fusion.own_ref.refs_0_), channel_id=1, source_target_pairs={{8,0},{0,8},{24,16},{16,24},{9,1},{1,9},{25,17},{17,25},{10,2},{2,... | collective-permute-start | bytes 393224 | tf_op jit(solution)/shard_map/ppermute | solution.py:452
  43.1 1.3 %diffuse_adjoint.1.refs_0_ = f32[4,64,128]{2,1,0:T(8,128)S(1)} custom-call(f32[3,10,32,128]{3,2,1,0:T(8,128)S(1)} %get-tuple-element.49.coef_ref, f32[4,64,128]{2,1,0:T(8,128)S(1)} %collective-permute-done.7.second_ref, f32[4,64,128]{2,1,0:T(8,128)S(1)} %collective-permute-done.6.first_ref, f32[4,64,128]{2,1,0:T(8,128)S(1)} %multiply_subtract_fusion.own_ref.refs_0_, ...), custom_call_target="tpu_custom_call" | custom-call | tf_op jit(solution)/shard_map/diffuse_adjoint/pallas_call | solution.py:606
  44.4 1.0 %collective-permute-start.9 = (f32[4,64,128]{2,1,0:T(8,128)S(1)}, f32[4,64,128]{2,1,0:T(8,128)S(1)}, u32[]{:S(2)}, u32[]{:S(2)}) collective-permute-start(f32[4,64,128]{2,1,0:T(8,128)S(1)} %diffuse_adjoint.1.refs_0_), channel_id=1, source_target_pairs={{8,0},{0,8},{24,16},{16,24},{9,1},{1,9},{25,17},{17,25},{10,2},{2,... | collective-permute-start | bytes 393224 | tf_op jit(solution)/shard_map/ppermute | solution.py:452
  45.4 0.6 %collective-permute-start.10 = (f32[4,64,128]{2,1,0:T(8,128)S(1)}, f32[4,64,128]{2,1,0:T(8,128)S(1)}, u32[]{:S(2)}, u32[]{:S(2)}) collective-permute-start(f32[4,64,128]{2,1,0:T(8,128)S(1)} %diffuse_adjoint.1.refs_0_), channel_id=1, source_target_pairs={{16,0},{24,8},{0,16},{8,24},{17,1},{25,9},{1,17},{9,25},{18,2},{26... | collective-permute-start | bytes 393224 | tf_op jit(solution)/shard_map/ppermute | solution.py:452
  45.9 0.9 %collective-permute-done.12.refs_1_ = f32[4,64,128]{2,1,0:T(8,128)S(1)} collective-permute-done((f32[4,64,128]{2,1,0:T(8,128)S(1)}, f32[4,64,128]{2,1,0:T(8,128)S(1)}, u32[]{:S(2)}, u32[]{:S(2)}) %collective-permute-start.12) | collective-permute-done | bytes 131104 | tf_op jit(solution)/shard_map/ppermute | solution.py:452
  46.8 1.1 %collective-permute-start.11 = (f32[4,64,128]{2,1,0:T(8,128)S(1)}, f32[4,64,128]{2,1,0:T(8,128)S(1)}, u32[]{:S(2)}, u32[]{:S(2)}) collective-permute-start(f32[4,64,128]{2,1,0:T(8,128)S(1)} %diffuse_adjoint.1.refs_0_), channel_id=1, source_target_pairs={{24,0},{16,8},{8,16},{0,24},{25,1},{17,9},{9,17},{1,25},{26,2},{18... | collective-permute-start | bytes 393224 | tf_op jit(solution)/shard_map/ppermute | solution.py:452
  48.0 1.2 %collective-permute-done.13.refs_2_ = f32[4,64,128]{2,1,0:T(8,128)S(1)} collective-permute-done((f32[4,64,128]{2,1,0:T(8,128)S(1)}, f32[4,64,128]{2,1,0:T(8,128)S(1)}, u32[]{:S(2)}, u32[]{:S(2)}) %collective-permute-start.13) | collective-permute-done | bytes 131104 | tf_op jit(solution)/shard_map/ppermute | solution.py:452
  49.2 5.6 %members_gradient.1 = f32[8,16,64,128]{3,2,1,0:T(8,128)} custom-call(bf16[256,768]{1,0:T(8,128)(2,1)S(1)} %get-tuple-element.55.matrix_ref, f32[8,16,64,128]{3,2,1,0:T(8,128)S(1)} %get-tuple-element.56.control_ref, bf16[8,16,64,128]{3,2,1,0:T(8,128)(2,1)S(1)} %get-tuple-element.57.pert_ref, f32[4,64,128]{2,1,0:T(8,128)S(1)} %multiply_subtract_fusion.own_ref.refs_0_, ...), custom_call_target="tpu_custom_call" | custom-call | tf_op jit(solution)/shard_map/members_gradient/pallas_call | solution.py:618
  54.9 1.2 %static_gradient.1 = f32[16,64,128]{2,1,0:T(8,128)} custom-call(bf16[256,768]{1,0:T(8,128)(2,1)S(1)} %get-tuple-element.47.matrix_ref, f32[16,64,128]{2,1,0:T(8,128)S(1)} %get-tuple-element.48.static_ref, f32[4,64,128]{2,1,0:T(8,128)S(1)} %diffuse_adjoint.1.refs_0_, f32[4,64,128]{2,1,0:T(8,128)S(1)} %collective-permute-done.9.refs_1_, ...), custom_call_target="tpu_custom_call" | custom-call | tf_op jit(solution)/shard_map/static_gradient/pallas_call | solution.py:629
  (13 shorter events, 0.1 us)
Async XLA Ops:
  8.8 10.2 %collective-permute-start.3 = (f32[6,64,128]{2,1,0:T(8,128)S(1)}, f32[6,64,128]{2,1,0:T(8,128)S(1)}, u32[]{:S(2)}, u32[]{:S(2)}) collective-permute-start(f32[6,64,128]{2,1,0:T(8,128)S(1)} %get-tuple-element.34.refs_2_), channel_id=1, source_target_pairs={{0,0},{1,1},{2,4},{3,5},{4,2},{5,3},{6,6},{7,7},{8,8},{9,9},{10,12... | collective-permute-start | bytes 589832 | tf_op jit(solution)/shard_map/ppermute | solution.py:446
  9.5 10.5 %collective-permute-start.4 = (f32[6,64,128]{2,1,0:T(8,128)S(1)}, f32[6,64,128]{2,1,0:T(8,128)S(1)}, u32[]{:S(2)}, u32[]{:S(2)}) collective-permute-start(f32[6,64,128]{2,1,0:T(8,128)S(1)} %get-tuple-element.34.refs_2_), channel_id=1, source_target_pairs={{0,2},{1,3},{2,0},{3,1},{4,6},{5,7},{6,4},{7,5},{8,10},{9,11},{10,... | collective-permute-start | bytes 589832 | tf_op jit(solution)/shard_map/ppermute | solution.py:446
  15.4 14.0 %all-to-all-start = ((f32[32,2,8,128]{3,2,1,0:T(8,128)}), f32[32,2,8,128]{3,2,1,0:T(8,128)S(1)}, u32[]{:S(2)}, u32[]{:S(2)}) async-start(f32[32,2,8,128]{3,2,1,0:T(8,128)} %get-tuple-element.37), calls=%async_computation | async-start | bytes 524288 | tf_op jit(solution)/shard_map/all_to_all | solution.py:541
  20.1 3.6 %collective-permute-start.5 = (f32[2,6,64,128]{3,2,1,0:T(8,128)S(1)}, f32[2,6,64,128]{3,2,1,0:T(8,128)S(1)}, u32[]{:S(2)}, u32[]{:S(2)}) collective-permute-start(f32[2,6,64,128]{3,2,1,0:T(8,128)S(1)} %pad_maximum_fusion), channel_id=1, source_target_pairs={{0,1},{1,0},{2,3},{3,2},{4,5},{5,4},{6,7},{7,6},{8,9},{9,8},{10,11... | collective-permute-start | bytes 1179656 | tf_op jit(solution)/shard_map/ppermute | solution.py:458
  20.2 13.3 %collective-permute-start.2 = (f32[4,64,128]{2,1,0:T(8,128)S(1)}, f32[4,64,128]{2,1,0:T(8,128)S(1)}, u32[]{:S(2)}, u32[]{:S(2)}) collective-permute-start(f32[4,64,128]{2,1,0:T(8,128)S(1)} %get-tuple-element.33), channel_id=1, source_target_pairs={{8,0},{0,8},{24,16},{16,24},{9,1},{1,9},{25,17},{17,25},{10,2},{2,... | collective-permute-start | bytes 393224 | tf_op jit(solution)/shard_map/ppermute | solution.py:544
  21.7 11.7 %collective-permute-start.1 = (f32[4,64,128]{2,1,0:T(8,128)S(1)}, f32[4,64,128]{2,1,0:T(8,128)S(1)}, u32[]{:S(2)}, u32[]{:S(2)}) collective-permute-start(f32[4,64,128]{2,1,0:T(8,128)S(1)} %get-tuple-element.32), channel_id=1, source_target_pairs={{16,0},{24,8},{0,16},{8,24},{17,1},{25,9},{1,17},{9,25},{18,2},{26... | collective-permute-start | bytes 393224 | tf_op jit(solution)/shard_map/ppermute | solution.py:544
  23.2 10.2 %collective-permute-start = (f32[4,64,128]{2,1,0:T(8,128)S(1)}, f32[4,64,128]{2,1,0:T(8,128)S(1)}, u32[]{:S(2)}, u32[]{:S(2)}) collective-permute-start(f32[4,64,128]{2,1,0:T(8,128)S(1)} %get-tuple-element.31), channel_id=1, source_target_pairs={{24,0},{16,8},{8,16},{0,24},{25,1},{17,9},{9,17},{1,25},{26,2},{18... | collective-permute-start | bytes 393224 | tf_op jit(solution)/shard_map/ppermute | solution.py:544
  33.5 5.9 %collective-permute-start.6 = (f32[4,64,128]{2,1,0:T(8,128)S(1)}, f32[4,64,128]{2,1,0:T(8,128)S(1)}, u32[]{:S(2)}, u32[]{:S(2)}) collective-permute-start(f32[4,64,128]{2,1,0:T(8,128)S(1)} %multiply_subtract_fusion.own_ref.refs_0_), channel_id=1, source_target_pairs={{0,2},{1,3},{2,0},{3,1},{4,6},{5,7},{6,4},{7,5},{8,10},{9,11},{10,... | collective-permute-start | bytes 393224 | tf_op jit(solution)/shard_map/ppermute | solution.py:446
  34.1 5.3 %collective-permute-start.7 = (f32[4,64,128]{2,1,0:T(8,128)S(1)}, f32[4,64,128]{2,1,0:T(8,128)S(1)}, u32[]{:S(2)}, u32[]{:S(2)}) collective-permute-start(f32[4,64,128]{2,1,0:T(8,128)S(1)} %multiply_subtract_fusion.own_ref.refs_0_), channel_id=1, source_target_pairs={{0,0},{1,1},{2,4},{3,5},{4,2},{5,3},{6,6},{7,7},{8,8},{9,9},{10,12... | collective-permute-start | bytes 393224 | tf_op jit(solution)/shard_map/ppermute | solution.py:446
  39.4 3.6 %collective-permute-start.8 = (f32[2,4,64,128]{3,2,1,0:T(8,128)S(1)}, f32[2,4,64,128]{3,2,1,0:T(8,128)S(1)}, u32[]{:S(2)}, u32[]{:S(2)}) collective-permute-start(f32[2,4,64,128]{3,2,1,0:T(8,128)S(1)} %pad_maximum_fusion.1), channel_id=1, source_target_pairs={{0,1},{1,0},{2,3},{3,2},{4,5},{5,4},{6,7},{7,6},{8,9},{9,8},{10,11... | collective-permute-start | bytes 786440 | tf_op jit(solution)/shard_map/ppermute | solution.py:458
  39.5 7.3 %collective-permute-start.12 = (f32[4,64,128]{2,1,0:T(8,128)S(1)}, f32[4,64,128]{2,1,0:T(8,128)S(1)}, u32[]{:S(2)}, u32[]{:S(2)}) collective-permute-start(f32[4,64,128]{2,1,0:T(8,128)S(1)} %multiply_subtract_fusion.own_ref.refs_0_), channel_id=1, source_target_pairs={{24,0},{16,8},{8,16},{0,24},{25,1},{17,9},{9,17},{1,25},{26,2},{18... | collective-permute-start | bytes 393224 | tf_op jit(solution)/shard_map/ppermute | solution.py:452
  40.5 8.7 %collective-permute-start.13 = (f32[4,64,128]{2,1,0:T(8,128)S(1)}, f32[4,64,128]{2,1,0:T(8,128)S(1)}, u32[]{:S(2)}, u32[]{:S(2)}) collective-permute-start(f32[4,64,128]{2,1,0:T(8,128)S(1)} %multiply_subtract_fusion.own_ref.refs_0_), channel_id=1, source_target_pairs={{16,0},{24,8},{0,16},{8,24},{17,1},{25,9},{1,17},{9,25},{18,2},{26... | collective-permute-start | bytes 393224 | tf_op jit(solution)/shard_map/ppermute | solution.py:452
  41.9 7.3 %collective-permute-start.14 = (f32[4,64,128]{2,1,0:T(8,128)S(1)}, f32[4,64,128]{2,1,0:T(8,128)S(1)}, u32[]{:S(2)}, u32[]{:S(2)}) collective-permute-start(f32[4,64,128]{2,1,0:T(8,128)S(1)} %multiply_subtract_fusion.own_ref.refs_0_), channel_id=1, source_target_pairs={{8,0},{0,8},{24,16},{16,24},{9,1},{1,9},{25,17},{17,25},{10,2},{2,... | collective-permute-start | bytes 393224 | tf_op jit(solution)/shard_map/ppermute | solution.py:452
  44.4 10.5 %collective-permute-start.9 = (f32[4,64,128]{2,1,0:T(8,128)S(1)}, f32[4,64,128]{2,1,0:T(8,128)S(1)}, u32[]{:S(2)}, u32[]{:S(2)}) collective-permute-start(f32[4,64,128]{2,1,0:T(8,128)S(1)} %diffuse_adjoint.1.refs_0_), channel_id=1, source_target_pairs={{8,0},{0,8},{24,16},{16,24},{9,1},{1,9},{25,17},{17,25},{10,2},{2,... | collective-permute-start | bytes 393224 | tf_op jit(solution)/shard_map/ppermute | solution.py:452
  45.4 9.5 %collective-permute-start.10 = (f32[4,64,128]{2,1,0:T(8,128)S(1)}, f32[4,64,128]{2,1,0:T(8,128)S(1)}, u32[]{:S(2)}, u32[]{:S(2)}) collective-permute-start(f32[4,64,128]{2,1,0:T(8,128)S(1)} %diffuse_adjoint.1.refs_0_), channel_id=1, source_target_pairs={{16,0},{24,8},{0,16},{8,24},{17,1},{25,9},{1,17},{9,25},{18,2},{26... | collective-permute-start | bytes 393224 | tf_op jit(solution)/shard_map/ppermute | solution.py:452
  46.8 8.0 %collective-permute-start.11 = (f32[4,64,128]{2,1,0:T(8,128)S(1)}, f32[4,64,128]{2,1,0:T(8,128)S(1)}, u32[]{:S(2)}, u32[]{:S(2)}) collective-permute-start(f32[4,64,128]{2,1,0:T(8,128)S(1)} %diffuse_adjoint.1.refs_0_), channel_id=1, source_target_pairs={{24,0},{16,8},{8,16},{0,24},{25,1},{17,9},{9,17},{1,25},{26,2},{18... | collective-permute-start | bytes 393224 | tf_op jit(solution)/shard_map/ppermute | solution.py:452

commit v19 on v18

--- a/solution.py
+++ b/solution.py
@@ -266,7 +266,7 @@
 
     @pl.when(pl.program_id(0) == 0)
     def _():
-        gather_levels(parts, adjoint_ref, True)
+        gather_levels(parts, adjoint_ref, False)
 
     def chunk(j, carry):
         at = pl.ds(pl.multiple_of(j * 16, 16), 16)
@@ -587,7 +587,7 @@
     tile = functools.reduce(jnp.add, sums) + increment
     tile = tile * slot_sums[0] - slot_sums[1]
     tile_first, tile_second = exchanged(tile, (0, 1))
-    adjoints = [tile] + from_peers(tile)
+    adjoints = [tile] + from_peers(tile)[::-1]
     tile, vertical_local, vertical_root = lax.optimization_barrier((tile, vertical_local, vertical_root))
     from_local, from_root = pl.pallas_call(
         functools.partial(matrices_kernel, member_scale),

time: 57 us -> 57 us (level)
  waiting for transfers between devices: 10.6 us -> 9.54 us
  starting transfers between devices: 21.3 us -> 22.2 us
    ppermute x6, waiting for transfers between devices: 2.14 us -> 1.08 us  [from_peers(): lax.ppermute(x, 'ens', [(peer(i, d, count), i) for i in range(count)])]
    ppermute x6, starting transfers between devices: 6.22 us -> 7.11 us  [from_peers(): lax.ppermute(x, 'ens', [(peer(i, d, count), i) for i in range(count)])]
  transfers between devices with their start and end apart: 16 -> 16, of which waited for: 5 -> 4; matrix products, arithmetic and copies ran while one was open for 0% -> 0% of each run, Pallas kernels for 25% -> 25%
where the time goes in v19:
time: 57 us; the launch traced here: 55.9 us
  Pallas kernels  23.2 us (41%)
  starting transfers between devices  22.2 us (39%)
  waiting for transfers between devices  9.54 us (17%)
  between operations  0.81 us (1%)
    pallas_call x1, Pallas kernels, local(): pl.pallas_call(functools.partial(observe_kernel, n_cols, cap_rows, member...  8.18 us
    ppermute x4, starting transfers between devices, exchanged(): out.append(lax.ppermute(x, 'cols', pairs))  7.78 us
    ppermute x6, starting transfers between devices, from_peers(): lax.ppermute(x, 'ens', [(peer(i, d, count), i) for i in range(count)])  7.11 us
    pallas_call x1, Pallas kernels, local(): pl.pallas_call(member_kernel, grid=(members // group,), in_specs=[VMEM] *...  5.65 us
    ppermute x4, waiting for transfers between devices, exchanged(): out.append(lax.ppermute(x, 'cols', pairs))  4.36 us
    all_to_all x1, waiting for transfers between devices, local(): lax.all_to_all(slots, ('ens', 'cols'), split_axis=0, concat_axis=0, tiled...  4.09 us
    pallas_call x1, Pallas kernels, local(): pl.pallas_call(functools.partial(scatter_kernel, cap_rows), in_specs=[VME...  3.99 us
    all_to_all x1, starting transfers between devices, local(): lax.all_to_all(slots, ('ens', 'cols'), split_axis=0, concat_axis=0, tiled...  3.6 us
  transfers between devices with their start and end apart: 16, of which 4 were waited for; matrix products, arithmetic and copies ran while one was open for 0% of the time, Pallas kernels for 25%

profile of v19, /device:TPU:0, one launch (start us, length us, event | category | flops | bytes accessed | tf_op | source)
XLA Modules:
  0.0 55.9 jit_solution(8836187598440437204)
XLA Ops:
  0.6 8.2 %slot_sums_and_members.1 = (f32[32,2,8,128]{3,2,1,0:T(8,128)}, f32[6,64,128]{2,1,0:T(8,128)S(1)}, f32[4,64,128]{2,1,0:T(8,128)S(1)}, f32[4,64,128]{2,1,0:T(8,128...) custom-call(s32[512,128]{1,0:T(8,128)} %bitcast.58, f32[512,128]{1,0:T(8,128)} %bitcast.59, ...), custom_call_target="tpu_custom_call" | custom-call | tf_op jit(solution)/shard_map/slot_sums_and_members/pallas_call | solution.py:498
  8.8 0.7 %collective-permute-start.3 = (f32[6,64,128]{2,1,0:T(8,128)S(1)}, f32[6,64,128]{2,1,0:T(8,128)S(1)}, u32[]{:S(2)}, u32[]{:S(2)}) collective-permute-start(f32[6,64,128]{2,1,0:T(8,128)S(1)} %get-tuple-element.34.refs_2_), channel_id=1, source_target_pairs={{0,0},{1,1},{2,4},{3,5},{4,2},{5,3},{6,6},{7,7},{8,8},{9,9},{10,12... | collective-permute-start | bytes 589832 | tf_op jit(solution)/shard_map/ppermute | solution.py:446
  9.5 5.9 %collective-permute-start.4 = (f32[6,64,128]{2,1,0:T(8,128)S(1)}, f32[6,64,128]{2,1,0:T(8,128)S(1)}, u32[]{:S(2)}, u32[]{:S(2)}) collective-permute-start(f32[6,64,128]{2,1,0:T(8,128)S(1)} %get-tuple-element.34.refs_2_), channel_id=1, source_target_pairs={{0,2},{1,3},{2,0},{3,1},{4,6},{5,7},{6,4},{7,5},{8,10},{9,11},{10,... | collective-permute-start | bytes 589832 | tf_op jit(solution)/shard_map/ppermute | solution.py:446
  15.4 3.6 %all-to-all-start = ((f32[32,2,8,128]{3,2,1,0:T(8,128)}), f32[32,2,8,128]{3,2,1,0:T(8,128)S(1)}, u32[]{:S(2)}, u32[]{:S(2)}) async-start(f32[32,2,8,128]{3,2,1,0:T(8,128)} %get-tuple-element.37), calls=%async_computation | async-start | bytes 524288 | tf_op jit(solution)/shard_map/all_to_all | solution.py:541
  19.0 0.0 collective-permute-done.3.refs_0_
  19.1 1.0 %collective-permute-done.4.refs_1_ = f32[6,64,128]{2,1,0:T(8,128)S(1)} collective-permute-done((f32[6,64,128]{2,1,0:T(8,128)S(1)}, f32[6,64,128]{2,1,0:T(8,128)S(1)}, u32[]{:S(2)}, u32[]{:S(2)}) %collective-permute-start.4) | collective-permute-done | bytes 196640 | tf_op jit(solution)/shard_map/ppermute | solution.py:446
  20.1 0.1 collective-permute-start.5
  20.2 1.6 %collective-permute-start.2 = (f32[4,64,128]{2,1,0:T(8,128)S(1)}, f32[4,64,128]{2,1,0:T(8,128)S(1)}, u32[]{:S(2)}, u32[]{:S(2)}) collective-permute-start(f32[4,64,128]{2,1,0:T(8,128)S(1)} %get-tuple-element.33), channel_id=1, source_target_pairs={{8,0},{0,8},{24,16},{16,24},{9,1},{1,9},{25,17},{17,25},{10,2},{2,... | collective-permute-start | bytes 393224 | tf_op jit(solution)/shard_map/ppermute | solution.py:544
  21.7 1.5 %collective-permute-start.1 = (f32[4,64,128]{2,1,0:T(8,128)S(1)}, f32[4,64,128]{2,1,0:T(8,128)S(1)}, u32[]{:S(2)}, u32[]{:S(2)}) collective-permute-start(f32[4,64,128]{2,1,0:T(8,128)S(1)} %get-tuple-element.32), channel_id=1, source_target_pairs={{16,0},{24,8},{0,16},{8,24},{17,1},{25,9},{1,17},{9,25},{18,2},{26... | collective-permute-start | bytes 393224 | tf_op jit(solution)/shard_map/ppermute | solution.py:544
  23.2 0.5 collective-permute-start
  23.7 1.6 %diffuse_forward.1 = (f32[4,64,128]{2,1,0:T(8,128)S(1)}, f32[3,10,32,128]{3,2,1,0:T(8,128)S(1)}, s32[64,128]{1,0:T(8,128)S(1)}, s32[64,128]{1,0:T(8,128)S(1)}) custom-call(f32[6,64,128]{2,1,0:T(8,128)S(1)} %collective-permute-done.3.refs_0_, f32[6,64,128]{2,1,0:T(8,128)S(1)} %collective-permute-done.4.refs_1_, f32[6,64,128]{2,1,0:T(8,128)S(1)} %get-tuple-element.34.refs_2_, ...), custom_call_target="tpu_custom_call" | custom-call | flops 67108864 | bytes 4194304 | tf_op jit(solution)/shard_map/diffuse_forward/pallas_call | solution.py:549
  25.3 4.1 %all-to-all-done.slots_ref = f32[32,2,8,128]{3,2,1,0:T(8,128)S(1)} async-done(((f32[32,2,8,128]{3,2,1,0:T(8,128)}), f32[32,2,8,128]{3,2,1,0:T(8,128)S(1)}, u32[]{:S(2)}, u32[]{:S(2)}) %all-to-all-start) | async-done | bytes 262176 | tf_op jit(solution)/shard_map/all_to_all | solution.py:541
  29.4 4.0 %scatter.1 = (f32[2,256,128]{2,1,0:T(8,128)S(1)}, f32[16,64,128]{2,1,0:T(8,128)S(1)}, f32[8,16,64,128]{3,2,1,0:T(8,128)S(1)}, bf16[8,16,64,128]{3,2,1,0:T(8,128)(2,1)S(1)}) custom-call(s32[64,128]{1,0:T(8,128)S(1)} %get-tuple-element.39.row_ref, s32[64,128]{1,0:T(8,128)S(1)} %get-tuple-element.40.lane_ref, f32[32,2,8,128]{3,2,1,0:T(8,128)S(1)} %all-to-all-done.slots_ref, ...), custom_call_target="tpu_custom_call" | custom-call | flops 2147483648 | bytes 8388608 | tf_op jit(solution)/shard_map/scatter/pallas_call | solution.py:570
  33.4 0.0 collective-permute-done.1
  33.4 0.0 collective-permute-done
  33.5 0.1 multiply_subtract_fusion.own_ref.refs_0_
  33.5 0.6 collective-permute-start.6
  34.1 0.7 %collective-permute-start.7 = (f32[4,64,128]{2,1,0:T(8,128)S(1)}, f32[4,64,128]{2,1,0:T(8,128)S(1)}, u32[]{:S(2)}, u32[]{:S(2)}) collective-permute-start(f32[4,64,128]{2,1,0:T(8,128)S(1)} %multiply_subtract_fusion.own_ref.refs_0_), channel_id=1, source_target_pairs={{0,0},{1,1},{2,4},{3,5},{4,2},{5,3},{6,6},{7,7},{8,8},{9,9},{10,12... | collective-permute-start | bytes 393224 | tf_op jit(solution)/shard_map/ppermute | solution.py:446
  34.7 1.2 %level_matrices.1 = (bf16[256,768]{1,0:T(8,128)(2,1)S(1)}, bf16[256,768]{1,0:T(8,128)(2,1)S(1)}) custom-call(f32[16,16]{1,0:T(8,128)} %local_ref, f32[16,16]{1,0:T(8,128)} %root_ref), custom_call_target="tpu_custom_call" | custom-call | tf_op jit(solution)/shard_map/level_matrices/pallas_call | solution.py:592
  36.0 3.4 %collective-permute-done.6.first_ref = f32[4,64,128]{2,1,0:T(8,128)S(1)} collective-permute-done((f32[4,64,128]{2,1,0:T(8,128)S(1)}, f32[4,64,128]{2,1,0:T(8,128)S(1)}, u32[]{:S(2)}, u32[]{:S(2)}) %collective-permute-start.6) | collective-permute-done | bytes 131104 | tf_op jit(solution)/shard_map/ppermute | solution.py:446
  39.4 0.0 collective-permute-done.7.second_ref
  39.4 0.1 collective-permute-start.8
  39.5 1.0 %collective-permute-start.12 = (f32[4,64,128]{2,1,0:T(8,128)S(1)}, f32[4,64,128]{2,1,0:T(8,128)S(1)}, u32[]{:S(2)}, u32[]{:S(2)}) collective-permute-start(f32[4,64,128]{2,1,0:T(8,128)S(1)} %multiply_subtract_fusion.own_ref.refs_0_), channel_id=1, source_target_pairs={{8,0},{0,8},{24,16},{16,24},{9,1},{1,9},{25,17},{17,25},{10,2},{2,... | collective-permute-start | bytes 393224 | tf_op jit(solution)/shard_map/ppermute | solution.py:452
  40.5 0.6 %collective-permute-start.13 = (f32[4,64,128]{2,1,0:T(8,128)S(1)}, f32[4,64,128]{2,1,0:T(8,128)S(1)}, u32[]{:S(2)}, u32[]{:S(2)}) collective-permute-start(f32[4,64,128]{2,1,0:T(8,128)S(1)} %multiply_subtract_fusion.own_ref.refs_0_), channel_id=1, source_target_pairs={{16,0},{24,8},{0,16},{8,24},{17,1},{25,9},{1,17},{9,25},{18,2},{26... | collective-permute-start | bytes 393224 | tf_op jit(solution)/shard_map/ppermute | solution.py:452
  41.0 2.0 %collective-permute-start.14 = (f32[4,64,128]{2,1,0:T(8,128)S(1)}, f32[4,64,128]{2,1,0:T(8,128)S(1)}, u32[]{:S(2)}, u32[]{:S(2)}) collective-permute-start(f32[4,64,128]{2,1,0:T(8,128)S(1)} %multiply_subtract_fusion.own_ref.refs_0_), channel_id=1, source_target_pairs={{24,0},{16,8},{8,16},{0,24},{25,1},{17,9},{9,17},{1,25},{26,2},{18... | collective-permute-start | bytes 393224 | tf_op jit(solution)/shard_map/ppermute | solution.py:452
  43.1 1.3 %diffuse_adjoint.1.refs_0_ = f32[4,64,128]{2,1,0:T(8,128)S(1)} custom-call(f32[3,10,32,128]{3,2,1,0:T(8,128)S(1)} %get-tuple-element.49.coef_ref, f32[4,64,128]{2,1,0:T(8,128)S(1)} %collective-permute-done.7.second_ref, f32[4,64,128]{2,1,0:T(8,128)S(1)} %collective-permute-done.6.first_ref, f32[4,64,128]{2,1,0:T(8,128)S(1)} %multiply_subtract_fusion.own_ref.refs_0_, ...), custom_call_target="tpu_custom_call" | custom-call | tf_op jit(solution)/shard_map/diffuse_adjoint/pallas_call | solution.py:606
  44.4 1.0 %collective-permute-start.9 = (f32[4,64,128]{2,1,0:T(8,128)S(1)}, f32[4,64,128]{2,1,0:T(8,128)S(1)}, u32[]{:S(2)}, u32[]{:S(2)}) collective-permute-start(f32[4,64,128]{2,1,0:T(8,128)S(1)} %diffuse_adjoint.1.refs_0_), channel_id=1, source_target_pairs={{8,0},{0,8},{24,16},{16,24},{9,1},{1,9},{25,17},{17,25},{10,2},{2,... | collective-permute-start | bytes 393224 | tf_op jit(solution)/shard_map/ppermute | solution.py:452
  45.4 0.6 %collective-permute-start.10 = (f32[4,64,128]{2,1,0:T(8,128)S(1)}, f32[4,64,128]{2,1,0:T(8,128)S(1)}, u32[]{:S(2)}, u32[]{:S(2)}) collective-permute-start(f32[4,64,128]{2,1,0:T(8,128)S(1)} %diffuse_adjoint.1.refs_0_), channel_id=1, source_target_pairs={{16,0},{24,8},{0,16},{8,24},{17,1},{25,9},{1,17},{9,25},{18,2},{26... | collective-permute-start | bytes 393224 | tf_op jit(solution)/shard_map/ppermute | solution.py:452
  45.9 2.0 %collective-permute-start.11 = (f32[4,64,128]{2,1,0:T(8,128)S(1)}, f32[4,64,128]{2,1,0:T(8,128)S(1)}, u32[]{:S(2)}, u32[]{:S(2)}) collective-permute-start(f32[4,64,128]{2,1,0:T(8,128)S(1)} %diffuse_adjoint.1.refs_0_), channel_id=1, source_target_pairs={{24,0},{16,8},{8,16},{0,24},{25,1},{17,9},{9,17},{1,25},{26,2},{18... | collective-permute-start | bytes 393224 | tf_op jit(solution)/shard_map/ppermute | solution.py:452
  48.0 1.1 %collective-permute-done.13.refs_2_ = f32[4,64,128]{2,1,0:T(8,128)S(1)} collective-permute-done((f32[4,64,128]{2,1,0:T(8,128)S(1)}, f32[4,64,128]{2,1,0:T(8,128)S(1)}, u32[]{:S(2)}, u32[]{:S(2)}) %collective-permute-start.13) | collective-permute-done | bytes 131104 | tf_op jit(solution)/shard_map/ppermute | solution.py:452
  49.0 5.7 %members_gradient.1 = f32[8,16,64,128]{3,2,1,0:T(8,128)} custom-call(bf16[256,768]{1,0:T(8,128)(2,1)S(1)} %get-tuple-element.55.matrix_ref, f32[8,16,64,128]{3,2,1,0:T(8,128)S(1)} %get-tuple-element.56.control_ref, bf16[8,16,64,128]{3,2,1,0:T(8,128)(2,1)S(1)} %get-tuple-element.57.pert_ref, f32[4,64,128]{2,1,0:T(8,128)S(1)} %multiply_subtract_fusion.own_ref.refs_0_, ...), custom_call_target="tpu_custom_call" | custom-call | tf_op jit(solution)/shard_map/members_gradient/pallas_call | solution.py:618
  54.7 1.2 %static_gradient.1 = f32[16,64,128]{2,1,0:T(8,128)} custom-call(bf16[256,768]{1,0:T(8,128)(2,1)S(1)} %get-tuple-element.47.matrix_ref, f32[16,64,128]{2,1,0:T(8,128)S(1)} %get-tuple-element.48.static_ref, f32[4,64,128]{2,1,0:T(8,128)S(1)} %diffuse_adjoint.1.refs_0_, f32[4,64,128]{2,1,0:T(8,128)S(1)} %collective-permute-done.9.refs_1_, ...), custom_call_target="tpu_custom_call" | custom-call | tf_op jit(solution)/shard_map/static_gradient/pallas_call | solution.py:629
  (13 shorter events, 0.1 us)
Async XLA Ops:
  8.8 10.2 %collective-permute-start.3 = (f32[6,64,128]{2,1,0:T(8,128)S(1)}, f32[6,64,128]{2,1,0:T(8,128)S(1)}, u32[]{:S(2)}, u32[]{:S(2)}) collective-permute-start(f32[6,64,128]{2,1,0:T(8,128)S(1)} %get-tuple-element.34.refs_2_), channel_id=1, source_target_pairs={{0,0},{1,1},{2,4},{3,5},{4,2},{5,3},{6,6},{7,7},{8,8},{9,9},{10,12... | collective-permute-start | bytes 589832 | tf_op jit(solution)/shard_map/ppermute | solution.py:446
  9.5 10.5 %collective-permute-start.4 = (f32[6,64,128]{2,1,0:T(8,128)S(1)}, f32[6,64,128]{2,1,0:T(8,128)S(1)}, u32[]{:S(2)}, u32[]{:S(2)}) collective-permute-start(f32[6,64,128]{2,1,0:T(8,128)S(1)} %get-tuple-element.34.refs_2_), channel_id=1, source_target_pairs={{0,2},{1,3},{2,0},{3,1},{4,6},{5,7},{6,4},{7,5},{8,10},{9,11},{10,... | collective-permute-start | bytes 589832 | tf_op jit(solution)/shard_map/ppermute | solution.py:446
  15.4 14.0 %all-to-all-start = ((f32[32,2,8,128]{3,2,1,0:T(8,128)}), f32[32,2,8,128]{3,2,1,0:T(8,128)S(1)}, u32[]{:S(2)}, u32[]{:S(2)}) async-start(f32[32,2,8,128]{3,2,1,0:T(8,128)} %get-tuple-element.37), calls=%async_computation | async-start | bytes 524288 | tf_op jit(solution)/shard_map/all_to_all | solution.py:541
  20.1 3.6 %collective-permute-start.5 = (f32[2,6,64,128]{3,2,1,0:T(8,128)S(1)}, f32[2,6,64,128]{3,2,1,0:T(8,128)S(1)}, u32[]{:S(2)}, u32[]{:S(2)}) collective-permute-start(f32[2,6,64,128]{3,2,1,0:T(8,128)S(1)} %pad_maximum_fusion), channel_id=1, source_target_pairs={{0,1},{1,0},{2,3},{3,2},{4,5},{5,4},{6,7},{7,6},{8,9},{9,8},{10,11... | collective-permute-start | bytes 1179656 | tf_op jit(solution)/shard_map/ppermute | solution.py:458
  20.2 13.3 %collective-permute-start.2 = (f32[4,64,128]{2,1,0:T(8,128)S(1)}, f32[4,64,128]{2,1,0:T(8,128)S(1)}, u32[]{:S(2)}, u32[]{:S(2)}) collective-permute-start(f32[4,64,128]{2,1,0:T(8,128)S(1)} %get-tuple-element.33), channel_id=1, source_target_pairs={{8,0},{0,8},{24,16},{16,24},{9,1},{1,9},{25,17},{17,25},{10,2},{2,... | collective-permute-start | bytes 393224 | tf_op jit(solution)/shard_map/ppermute | solution.py:544
  21.7 11.7 %collective-permute-start.1 = (f32[4,64,128]{2,1,0:T(8,128)S(1)}, f32[4,64,128]{2,1,0:T(8,128)S(1)}, u32[]{:S(2)}, u32[]{:S(2)}) collective-permute-start(f32[4,64,128]{2,1,0:T(8,128)S(1)} %get-tuple-element.32), channel_id=1, source_target_pairs={{16,0},{24,8},{0,16},{8,24},{17,1},{25,9},{1,17},{9,25},{18,2},{26... | collective-permute-start | bytes 393224 | tf_op jit(solution)/shard_map/ppermute | solution.py:544
  23.2 10.2 %collective-permute-start = (f32[4,64,128]{2,1,0:T(8,128)S(1)}, f32[4,64,128]{2,1,0:T(8,128)S(1)}, u32[]{:S(2)}, u32[]{:S(2)}) collective-permute-start(f32[4,64,128]{2,1,0:T(8,128)S(1)} %get-tuple-element.31), channel_id=1, source_target_pairs={{24,0},{16,8},{8,16},{0,24},{25,1},{17,9},{9,17},{1,25},{26,2},{18... | collective-permute-start | bytes 393224 | tf_op jit(solution)/shard_map/ppermute | solution.py:544
  33.5 5.9 %collective-permute-start.6 = (f32[4,64,128]{2,1,0:T(8,128)S(1)}, f32[4,64,128]{2,1,0:T(8,128)S(1)}, u32[]{:S(2)}, u32[]{:S(2)}) collective-permute-start(f32[4,64,128]{2,1,0:T(8,128)S(1)} %multiply_subtract_fusion.own_ref.refs_0_), channel_id=1, source_target_pairs={{0,2},{1,3},{2,0},{3,1},{4,6},{5,7},{6,4},{7,5},{8,10},{9,11},{10,... | collective-permute-start | bytes 393224 | tf_op jit(solution)/shard_map/ppermute | solution.py:446
  34.1 5.3 %collective-permute-start.7 = (f32[4,64,128]{2,1,0:T(8,128)S(1)}, f32[4,64,128]{2,1,0:T(8,128)S(1)}, u32[]{:S(2)}, u32[]{:S(2)}) collective-permute-start(f32[4,64,128]{2,1,0:T(8,128)S(1)} %multiply_subtract_fusion.own_ref.refs_0_), channel_id=1, source_target_pairs={{0,0},{1,1},{2,4},{3,5},{4,2},{5,3},{6,6},{7,7},{8,8},{9,9},{10,12... | collective-permute-start | bytes 393224 | tf_op jit(solution)/shard_map/ppermute | solution.py:446
  39.4 3.6 %collective-permute-start.8 = (f32[2,4,64,128]{3,2,1,0:T(8,128)S(1)}, f32[2,4,64,128]{3,2,1,0:T(8,128)S(1)}, u32[]{:S(2)}, u32[]{:S(2)}) collective-permute-start(f32[2,4,64,128]{3,2,1,0:T(8,128)S(1)} %pad_maximum_fusion.1), channel_id=1, source_target_pairs={{0,1},{1,0},{2,3},{3,2},{4,5},{5,4},{6,7},{7,6},{8,9},{9,8},{10,11... | collective-permute-start | bytes 786440 | tf_op jit(solution)/shard_map/ppermute | solution.py:458
  39.5 6.4 %collective-permute-start.12 = (f32[4,64,128]{2,1,0:T(8,128)S(1)}, f32[4,64,128]{2,1,0:T(8,128)S(1)}, u32[]{:S(2)}, u32[]{:S(2)}) collective-permute-start(f32[4,64,128]{2,1,0:T(8,128)S(1)} %multiply_subtract_fusion.own_ref.refs_0_), channel_id=1, source_target_pairs={{8,0},{0,8},{24,16},{16,24},{9,1},{1,9},{25,17},{17,25},{10,2},{2,... | collective-permute-start | bytes 393224 | tf_op jit(solution)/shard_map/ppermute | solution.py:452
  40.5 8.6 %collective-permute-start.13 = (f32[4,64,128]{2,1,0:T(8,128)S(1)}, f32[4,64,128]{2,1,0:T(8,128)S(1)}, u32[]{:S(2)}, u32[]{:S(2)}) collective-permute-start(f32[4,64,128]{2,1,0:T(8,128)S(1)} %multiply_subtract_fusion.own_ref.refs_0_), channel_id=1, source_target_pairs={{16,0},{24,8},{0,16},{8,24},{17,1},{25,9},{1,17},{9,25},{18,2},{26... | collective-permute-start | bytes 393224 | tf_op jit(solution)/shard_map/ppermute | solution.py:452
  41.0 8.0 %collective-permute-start.14 = (f32[4,64,128]{2,1,0:T(8,128)S(1)}, f32[4,64,128]{2,1,0:T(8,128)S(1)}, u32[]{:S(2)}, u32[]{:S(2)}) collective-permute-start(f32[4,64,128]{2,1,0:T(8,128)S(1)} %multiply_subtract_fusion.own_ref.refs_0_), channel_id=1, source_target_pairs={{24,0},{16,8},{8,16},{0,24},{25,1},{17,9},{9,17},{1,25},{26,2},{18... | collective-permute-start | bytes 393224 | tf_op jit(solution)/shard_map/ppermute | solution.py:452
  44.4 10.3 %collective-permute-start.9 = (f32[4,64,128]{2,1,0:T(8,128)S(1)}, f32[4,64,128]{2,1,0:T(8,128)S(1)}, u32[]{:S(2)}, u32[]{:S(2)}) collective-permute-start(f32[4,64,128]{2,1,0:T(8,128)S(1)} %diffuse_adjoint.1.refs_0_), channel_id=1, source_target_pairs={{8,0},{0,8},{24,16},{16,24},{9,1},{1,9},{25,17},{17,25},{10,2},{2,... | collective-permute-start | bytes 393224 | tf_op jit(solution)/shard_map/ppermute | solution.py:452
  45.4 9.3 %collective-permute-start.10 = (f32[4,64,128]{2,1,0:T(8,128)S(1)}, f32[4,64,128]{2,1,0:T(8,128)S(1)}, u32[]{:S(2)}, u32[]{:S(2)}) collective-permute-start(f32[4,64,128]{2,1,0:T(8,128)S(1)} %diffuse_adjoint.1.refs_0_), channel_id=1, source_target_pairs={{16,0},{24,8},{0,16},{8,24},{17,1},{25,9},{1,17},{9,25},{18,2},{26... | collective-permute-start | bytes 393224 | tf_op jit(solution)/shard_map/ppermute | solution.py:452
  45.9 8.8 %collective-permute-start.11 = (f32[4,64,128]{2,1,0:T(8,128)S(1)}, f32[4,64,128]{2,1,0:T(8,128)S(1)}, u32[]{:S(2)}, u32[]{:S(2)}) collective-permute-start(f32[4,64,128]{2,1,0:T(8,128)S(1)} %diffuse_adjoint.1.refs_0_), channel_id=1, source_target_pairs={{24,0},{16,8},{8,16},{0,24},{25,1},{17,9},{9,17},{1,25},{26,2},{18... | collective-permute-start | bytes 393224 | tf_op jit(solution)/shard_map/ppermute | solution.py:452
